TPU v7x, 32 devices: a whole 2x2x4 slice. The times are simulated.
32 devices in a mesh: parts: 2 (over x), domain: 8 (over z, y), batch: 2 (over core).
Axes of the slice: x: 2, y: 2, z: 4, core: 2. Of those that a mesh axis runs over, the one named last changes fastest.
Arguments:
- positions: float32 [4, 3, 2048], P(('parts', 'batch'), None, 'domain'), parts along dimension 0, may hold values from 0 to 2
- features: float32 [4, 2048, 256], P(('parts', 'batch'), 'domain'), parts along dimension 0, may hold values from -6 to 6
- species: int32 [4, 2048], P(('parts', 'batch'), 'domain'), parts along dimension 0, may hold values from 0 to 3
- ref_forces: float32 [4, 3, 2048], P(('parts', 'batch'), None, 'domain'), parts along dimension 0, may hold values from -6 to 6
- centre_tile: int32 [4, 16], P(('parts', 'batch'), 'domain'), parts along dimension 0, may hold values from 0 to 3
- other_tile: int32 [4, 16], P(('parts', 'batch'), 'domain'), parts along dimension 0, may hold values from 0 to 7
- pair_live: int32 [4, 16], P(('parts', 'batch'), 'domain'), parts along dimension 0, may hold values 0 or 1
- send_tiles: int32 [4, 32], P(('parts', 'batch'), 'domain'), parts along dimension 0, may hold values from 0 to 3
- radial_w: float32 [8, 256], replicated, may hold values from -2 to 2
- mix_w: float32 [768, 256], replicated, may hold values from -0.21875 to 0.21875
- species_w: float32 [4, 256], replicated, may hold values from -6 to 6
- out_w: float32 [256], replicated, may hold values from -0.375 to 0.375
Outputs:
- forces: float32 [4, 3, 2048], P(('parts', 'batch'), None, 'domain'), parts along dimension 0
- grad_radial: float32 [16, 256], P('parts'), parts along dimension 0
- grad_mix: float32 [1536, 256], P('parts'), parts along dimension 0
- grad_species: float32 [8, 256], P('parts'), parts along dimension 0
- grad_out: float32 [512], P('parts'), parts along dimension 0
There are 2 independent parts, one for each index of `parts`. A program takes and returns all parts, laid end to end along the dimension named above; an argument that names none is the same for every part. Nothing has to cross between parts.
All inputs are finite; a program needn't handle non-finite values. No bound on the sum of `pair_live` on one device may be relied on, other than what follows from the above.
Results may differ from a plain program's by a relative error of at most 0.0003.
Values sent between devices are 32-bit elements; how exact they have to be, the bound alone decides.
No kernel may reach another device: no remote copies, remote signals or barrier semaphores. Data moves between devices by JAX's collectives and lax.ppermute only.
A program may use at most 128 MiB of HBM per device.

v0:
```python
import math

import jax
import jax.numpy as jnp
from jax import lax
from jax.experimental import pallas as pl
from jax.experimental.pallas import tpu as pltpu
from jax.sharding import PartitionSpec as P

TA = 64
SEND = 2
PAIRS = 2
COMPS = 9
BASIS = 8
SPECIES = 4
CHUNK = 2 * TA

cutoff = 2.5
soften = 0.25
env_scale = 0.25
root_three = math.sqrt(3.0)
F32 = jnp.float32
BF16 = jnp.bfloat16
NN = (((1,), (0,)), ((), ()))
NT = (((1,), (1,)), ((), ()))
TN = (((0,), (0,)), ((), ()))
GROUP = (0, 1, 1, 1, 2, 2, 2, 2, 2)


def split(value):
    high = value.astype(BF16)
    return high, (value - high.astype(F32)).astype(BF16)


def product(left, right, dims):
    (lh, ll), (rh, rl) = left, right

    def one(x, y):
        return lax.dot_general(x, y, dims, preferred_element_type=F32)

    return one(lh, rh) + (one(lh, rl) + one(ll, rh))


def flag(condition):
    return jnp.where(condition, 1.0, 0.0).astype(F32)


def lane_half():
    lane = lax.broadcasted_iota(jnp.int32, (1, CHUNK), 1)
    low = flag(lane < TA)
    return low, 1.0 - low


def twice(chunk, half):
    low, high = lane_half()
    swapped = pltpu.roll(chunk, TA, 1)
    return chunk * low + swapped * high if half == 0 else swapped * low + chunk * high


def pick(chunks, position):
    total = None
    for q, chunk in enumerate(chunks):
        for half in range(2):
            term = twice(chunk, half) * flag(position == 2 * q + half)
            total = term if total is None else total + term
    return total


def paired(first, second):
    low, high = lane_half()
    return first * low + second * high


def chunk_mask(position, q):
    low, high = lane_half()
    return low * flag(position == 2 * q) + high * flag(position == 2 * q + 1)


def geometry(lane_rows, columns, sign, live, same):
    offset = [(row - column) * sign for row, column in zip(lane_rows, columns)]
    dist_sq = offset[0] * offset[0] + offset[1] * offset[1] + offset[2] * offset[2] + soften
    distance = jnp.sqrt(dist_sq)
    inverse = 1.0 / distance
    unit = [x * inverse for x in offset]
    row = lax.broadcasted_iota(jnp.int32, (TA, CHUNK), 0)
    lane = lax.broadcasted_iota(jnp.int32, (TA, CHUNK), 1)
    lane = jnp.where(lane >= TA, lane - TA, lane)
    mask = live * (1.0 - same * flag(row == lane))
    base = jnp.maximum(1.0 - dist_sq * (1.0 / (cutoff * cutoff)), 0.0)
    weight = base * base * base * mask * inverse
    slope = -(6.0 / (cutoff * cutoff)) * base * base * mask - weight * inverse
    angle = distance * (math.pi / cutoff)
    return unit, inverse, weight, slope, jnp.sin(angle), jnp.cos(angle)


def harmonics(v):
    x, y, z = v
    return [
        None,
        x,
        y,
        z,
        root_three * x * y,
        root_three * y * z,
        root_three * z * x,
        0.5 * root_three * (x * x - y * y),
        z * z - 0.5 * (x * x + y * y),
    ]


def harmonics_tangent(v, t):
    x, y, z = v
    a, b, c = t
    return [
        None,
        a,
        b,
        c,
        root_three * (a * y + x * b),
        root_three * (b * z + y * c),
        root_three * (c * x + z * a),
        root_three * (x * a - y * b),
        2.0 * z * c - (x * a + y * b),
    ]


def paired_orders(sine, cosine, weight, slope):
    low, high = lane_half()
    double_s, double_c = 2.0 * sine * cosine, 1.0 - 2.0 * sine * sine
    now_s = sine * low + double_s * high
    now_c = cosine * low + double_c * high
    old_s = -sine * low
    old_c = cosine * low + high
    values, slopes = [], []
    for k in range(BASIS // 2):
        order = ((2 * k + 1) * low + (2 * k + 2) * high) * (math.pi / cutoff)
        values.append(now_s * weight)
        slopes.append(now_c * (weight * order) + now_s * slope)
        now_s, old_s = 2.0 * double_c * now_s - old_s, now_s
        now_c, old_c = 2.0 * double_c * now_c - old_c, now_c
    return values, slopes


def single_orders(sine, cosine, weight, slope):
    now_s, now_c = sine, cosine
    old_s, old_c = jnp.zeros_like(sine), jnp.ones_like(cosine)
    values, slopes = [], []
    for n in range(1, BASIS + 1):
        values.append(now_s * weight)
        slopes.append(now_c * (weight * (n * math.pi / cutoff)) + now_s * slope)
        now_s, old_s = 2.0 * cosine * now_s - old_s, now_s
        now_c, old_c = 2.0 * cosine * now_c - old_c, now_c
    return values, slopes


def columns_of(rows, square, turned):
    square[...] = jnp.zeros_like(square)
    square[0 : rows.shape[0], :] = rows
    turned[...] = square[...].T


def pair_rows(first, p):
    return twice(first, p)


def radial_feat(feat, radial, p, high_ref, low_ref):
    own = feat[p * TA : (p + 1) * TA, :]
    for n in range(BASIS):
        hi, lo = split(own * radial[n : n + 1, :])
        high_ref[n * TA : (n + 1) * TA, :] = hi
        low_ref[n * TA : (n + 1) * TA, :] = lo


def gather_kernel(send, pos, feat, ref, to_low, to_high):
    position = [pos[0, :, q * CHUNK : (q + 1) * CHUNK] for q in range(2)]
    error = [ref[0, :, q * CHUNK : (q + 1) * CHUNK] for q in range(2)]
    low, high = lane_half()
    for out, first in ((to_low, 0), (to_high, SEND)):
        tiles = [send[0, first + j] for j in range(SEND)]
        for j in range(SEND):
            start = pl.multiple_of(tiles[j] * TA, TA)
            out[j * TA : (j + 1) * TA, :] = feat[0, pl.ds(start, TA), :]
        out[SEND * TA :, :] = jnp.zeros((16, out.shape[1]), F32)
        out[SEND * TA : SEND * TA + 3, 0:CHUNK] = paired(
            pick(position, tiles[0]), pick(position, tiles[1])
        )
        out[SEND * TA : SEND * TA + 3, CHUNK:] = paired(pick(error, tiles[0]), pick(error, tiles[1]))
        for other in range(2 * SEND):
            same = low * flag(send[0, other] == tiles[0]) + high * flag(send[0, other] == tiles[1])
            out[SEND * TA + 8 + other : SEND * TA + 9 + other, 0:CHUNK] = same


def force_kernel(
    centre, other, live, send, pos, feat, species, from_low, from_high, radial_w, mix_w, species_w, out_w,
    env, dinv, gate, curve, inv, rows, fsel, own, to_high, to_low,
    square, turned, th, tl, xh, xl, raw, mh, ml,
):
    ghost = SEND * TA
    chunks = [
        from_low[ghost : ghost + 3, 0:CHUNK],
        pos[0, :, 0:CHUNK],
        pos[0, :, CHUNK:],
        from_high[ghost : ghost + 3, 0:CHUNK],
    ]
    kinds = [species[:, q * CHUNK : (q + 1) * CHUNK].astype(F32) for q in range(2)]
    centres = [centre[0, p] for p in range(PAIRS)]
    others = [other[0, p] for p in range(PAIRS)]
    sames = [flag(others[p] == centres[p] + SEND) for p in range(PAIRS)]
    shared = flag(centres[0] == centres[1])
    rows[...] = jnp.zeros_like(rows)
    rows[0:3, :] = paired(*(pick(chunks, others[p]) for p in range(PAIRS)))
    rows[3:6, :] = paired(*(pick(chunks[1:3], centres[p]) for p in range(PAIRS)))
    rows[6:7, :] = paired(*(pick(kinds, centres[p]) for p in range(PAIRS)))
    columns_of(rows[...], square, turned)

    for p in range(PAIRS):
        o = others[p]
        below = pl.multiple_of(jnp.clip(o, 0, 1) * TA, TA)
        inside = pl.multiple_of(jnp.clip(o - SEND, 0, 3) * TA, TA)
        above = pl.multiple_of(jnp.clip(o - SEND - 4, 0, 1) * TA, TA)
        fsel[p * TA : (p + 1) * TA, :] = (
            from_low[pl.ds(below, TA), :] * flag(o < SEND)
            + feat[0, pl.ds(inside, TA), :] * flag((o >= SEND) & (o < SEND + 4))
            + from_high[pl.ds(above, TA), :] * flag(o >= SEND + 4)
        )

    shapes = []
    for p in range(PAIRS):
        lane_rows = [twice(rows[i : i + 1, :], p) for i in range(3)]
        columns = [turned[p * TA : (p + 1) * TA, 3 + i : 4 + i] for i in range(3)]
        unit, inverse, weight, slope, sine, cosine = geometry(
            lane_rows, columns, 1.0, live[0, p].astype(F32), sames[p]
        )
        angular = harmonics(unit)
        values, slopes = paired_orders(sine, cosine, weight, slope)
        shapes.append((unit, inverse, angular, values, slopes))
        for m in range(COMPS):
            for k in range(BASIS // 2):
                entry = values[k] if m == 0 else angular[m] * values[k]
                hi, lo = split(entry)
                th[m * TA : (m + 1) * TA, k * CHUNK : (k + 1) * CHUNK] = hi
                tl[m * TA : (m + 1) * TA, k * CHUNK : (k + 1) * CHUNK] = lo
        radial_feat(fsel, radial_w, p, xh.at[p], xl.at[p])
        raw[p * COMPS * TA : (p + 1) * COMPS * TA, 0:256] = product(
            (th[...], tl[...]), (xh[p], xl[p]), NN
        )

    for m in range(COMPS):
        first = raw[m * TA : (m + 1) * TA, 0:256]
        second = raw[(COMPS + m) * TA : (COMPS + m + 1) * TA, 0:256]
        env[m * TA : (m + 1) * TA, :] = env_scale * (first + shared * second)
        env[(COMPS + m) * TA : (COMPS + m + 1) * TA, :] = env_scale * (second + shared * first)
    for p in range(PAIRS):
        sums = [None] * 3
        for m in range(COMPS):
            block = env[(p * COMPS + m) * TA : (p * COMPS + m + 1) * TA, :]
            sums[GROUP[m]] = block * block if sums[GROUP[m]] is None else sums[GROUP[m]] + block * block
        for g in range(3):
            inv[p * TA : (p + 1) * TA, g * 256 : (g + 1) * 256] = sums[g]
    hi, lo = split(mix_w[...])
    mh[...] = hi
    ml[...] = lo
    hidden = product(split(inv[...]), (mh[...], ml[...]), NN)
    kind = turned[:, 6:7]
    for s in range(species_w.shape[0]):
        hidden = hidden + flag(kind == float(s)) * species_w[s : s + 1, :]
    sigma = 1.0 / (1.0 + jnp.exp(-hidden))
    first_order = sigma * (1.0 + hidden * (1.0 - sigma))
    gate[...] = first_order
    curve[...] = sigma * (1.0 - sigma) * (2.0 + hidden * (1.0 - 2.0 * sigma)) * out_w[...]
    dinv[...] = product(split(first_order * out_w[...]), (mh[...], ml[...]), NT)

    grads_low = [jnp.zeros((3, CHUNK), F32) for _ in range(4)]
    low, high = lane_half()
    for p in range(PAIRS):
        unit, inverse, angular, values, slopes = shapes[p]
        for m in range(COMPS):
            block = env[(p * COMPS + m) * TA : (p * COMPS + m + 1) * TA, :]
            part = dinv[p * TA : (p + 1) * TA, GROUP[m] * 256 : (GROUP[m] + 1) * 256]
            hi, lo = split((2.0 * env_scale) * block * part)
            th[m * TA : (m + 1) * TA, 0:256] = hi
            tl[m * TA : (m + 1) * TA, 0:256] = lo
        raw[0 : COMPS * TA, :] = product((th[:, 0:256], tl[:, 0:256]), (xh[p], xl[p]), NT)
        d_radius = None
        d_angular = []
        for m in range(COMPS):
            along, across = None, None
            for k in range(BASIS // 2):
                block = raw[m * TA : (m + 1) * TA, k * CHUNK : (k + 1) * CHUNK]
                along = block * slopes[k] if along is None else along + block * slopes[k]
                across = block * values[k] if across is None else across + block * values[k]
            d_angular.append(across)
            term = along if m == 0 else along * angular[m]
            d_radius = term if d_radius is None else d_radius + term
        x, y, z = unit
        g = d_angular
        toward = [
            g[1] + root_three * (y * g[4] + z * g[6] + x * g[7]) - x * g[8],
            g[2] + root_three * (x * g[4] + z * g[5] - y * g[7]) - y * g[8],
            g[3] + root_three * (y * g[5] + x * g[6]) + 2.0 * (z * g[8]),
        ]
        radial_part = d_radius - inverse * (toward[0] * x + toward[1] * y + toward[2] * z)
        other_rows, centre_rows = [], []
        for i in range(3):
            d_offset = inverse * toward[i] + unit[i] * radial_part
            summed = jnp.sum(d_offset, axis=0, keepdims=True)
            other_rows.append(summed + pltpu.roll(summed, TA, 1))
            square[0:TA, :] = d_offset
            square[TA:, :] = d_offset
            centre_rows.append(-jnp.sum(square[...].T, axis=0, keepdims=True))
        for i in range(3):
            for q in range(4):
                at = chunk_mask(others[p], q) * other_rows[i]
                if q in (1, 2):
                    at = at + chunk_mask(centres[p] + SEND, q) * centre_rows[i]
                grads_low[q] = grads_low[q] + at * flag(
                    lax.broadcasted_iota(jnp.int32, (3, CHUNK), 0) == i
                )
    own[...] = jnp.zeros_like(own)
    own[0:3, 0:CHUNK] = grads_low[1]
    own[0:3, CHUNK:] = grads_low[2]
    own[3:6, 0:CHUNK] = grads_low[0]
    own[3:6, CHUNK:] = grads_low[3]
    for out, first, ghost_grad in ((to_low, 0, grads_low[0]), (to_high, SEND, grads_low[3])):
        out[...] = jnp.zeros_like(out)
        out[0:3, :] = paired(*(pick(grads_low[1:3], send[0, first + j]) for j in range(SEND)))
        out[3:6, :] = ghost_grad


def tangent_kernel(
    scale, centre, other, live, send, ref, from_low, from_high, own, low_one, low_two, high_one, high_two,
    rows, fsel, env, dinv, gate, curve, inv, radial_w, mix_w, out_w,
    forces, grad_mix, small, envdot, curl, both,
    square, turned, th, tl, xh, xl, raw, left, right,
):
    ghost = SEND * TA
    low, high = lane_half()
    centres = [centre[0, p] for p in range(PAIRS)]
    others = [other[0, p] for p in range(PAIRS)]
    sames = [flag(others[p] == centres[p] + SEND) for p in range(PAIRS)]
    shared = flag(centres[0] == centres[1])
    mine = [own[0:3, 0:CHUNK], own[0:3, CHUNK:]]
    arrived = [twice(low_one[3:6, :], j) for j in range(SEND)]
    arrived += [twice(high_one[3:6, :], j) for j in range(SEND)]
    for j in range(2 * SEND):
        for q in range(2):
            mine[q] = mine[q] + chunk_mask(send[0, j], q) * arrived[j]
    below = low_one[0:3, :]
    above = high_one[0:3, :]
    to_below = [twice(low_two[3:6, :], j) for j in range(SEND)]
    to_below += [twice(own[3:6, 0:CHUNK], j) for j in range(SEND)]
    to_above = [twice(own[3:6, CHUNK:], j) for j in range(SEND)]
    to_above += [twice(high_two[3:6, :], j) for j in range(SEND)]
    for j in range(2 * SEND):
        below = below + from_low[ghost + 8 + j : ghost + 9 + j, 0:CHUNK] * to_below[j]
        above = above + from_high[ghost + 8 + j : ghost + 9 + j, 0:CHUNK] * to_above[j]
    for q in range(2):
        forces[0, :, q * CHUNK : (q + 1) * CHUNK] = -mine[q]
    error = [
        below + from_low[ghost : ghost + 3, CHUNK:],
        mine[0] + ref[0, :, 0:CHUNK],
        mine[1] + ref[0, :, CHUNK:],
        above + from_high[ghost : ghost + 3, CHUNK:],
    ]
    error = [part * scale[0] for part in error]
    both[...] = jnp.zeros_like(both)
    both[0:8, :] = rows[...]
    both[8:11, :] = paired(*(pick(error, others[p]) for p in range(PAIRS)))
    both[11:14, :] = paired(*(pick(error[1:3], centres[p]) for p in range(PAIRS)))
    columns_of(both[...], square, turned)

    for p in range(PAIRS):
        lane_rows = [twice(both[i : i + 1, :], p) for i in range(3)]
        lane_move = [twice(both[8 + i : 9 + i, :], p) for i in range(3)]
        columns = [turned[p * TA : (p + 1) * TA, 3 + i : 4 + i] for i in range(3)]
        column_move = [turned[p * TA : (p + 1) * TA, 11 + i : 12 + i] for i in range(3)]
        unit, inverse, weight, slope, sine, cosine = geometry(
            lane_rows, columns, 1.0, live[0, p].astype(F32), sames[p]
        )
        move = [a - b for a, b in zip(lane_move, column_move)]
        stretch = unit[0] * move[0] + unit[1] * move[1] + unit[2] * move[2]
        turn = [(m - v * stretch) * inverse for m, v in zip(move, unit)]
        angular, turning = harmonics(unit), harmonics_tangent(unit, turn)
        values, slopes = paired_orders(sine, cosine, weight, slope)
        slopes = [s * stretch for s in slopes]
        for m in range(COMPS):
            for k in range(BASIS // 2):
                entry = slopes[k] if m == 0 else angular[m] * slopes[k] + turning[m] * values[k]
                hi, lo = split(entry)
                th[m * TA : (m + 1) * TA, k * CHUNK : (k + 1) * CHUNK] = hi
                tl[m * TA : (m + 1) * TA, k * CHUNK : (k + 1) * CHUNK] = lo
        radial_feat(fsel, radial_w, p, xh, xl)
        raw[p * COMPS * TA : (p + 1) * COMPS * TA, :] = product((th[...], tl[...]), (xh[...], xl[...]), NN)

    for m in range(COMPS):
        first = raw[m * TA : (m + 1) * TA, :]
        second = raw[(COMPS + m) * TA : (COMPS + m + 1) * TA, :]
        envdot[m * TA : (m + 1) * TA, :] = env_scale * (first + shared * second)
        envdot[(COMPS + m) * TA : (COMPS + m + 1) * TA, :] = env_scale * (second + shared * first)
    invdot = left
    half = PAIRS * TA
    for p in range(PAIRS):
        sums = [None] * 3
        for m in range(COMPS):
            at = slice((p * COMPS + m) * TA, (p * COMPS + m + 1) * TA)
            term = 2.0 * env[at, :] * envdot[at, :]
            sums[GROUP[m]] = term if sums[GROUP[m]] is None else sums[GROUP[m]] + term
        for g in range(3):
            invdot[half + p * TA : half + (p + 1) * TA, g * 256 : (g + 1) * 256] = sums[g]
    invdot[0:half, :] = inv[...]
    hidden_move = product(split(invdot[half:, :]), split(mix_w[...]), NN)
    bend = curve[...] * hidden_move
    curl[...] = bend
    once = 1.0 - shared * flag(lax.broadcasted_iota(jnp.int32, (half, 1), 0) >= TA)
    right[0:half, :] = bend * once
    right[half:, :] = gate[...] * out_w[...] * once
    grad_mix[...] = product(split(left[...]), split(right[...]), TN)
    small[...] = jnp.zeros_like(small)
    kind = turned[:, 6:7]
    for s in range(SPECIES):
        small[s : s + 1, :] = jnp.sum(right[0:half, :] * flag(kind == float(s)), axis=0, keepdims=True)
    small[SPECIES : SPECIES + 1, :] = jnp.sum(gate[...] * hidden_move * once, axis=0, keepdims=True)


def radial_kernel(
    centre, other, live, both, fsel, env, envdot, dinv, curl, mix_w,
    grad_radial,
    square, turned, lh, ll, gh, gl, turn_inv, raw,
):
    centres = [centre[0, p] for p in range(PAIRS)]
    others = [other[0, p] for p in range(PAIRS)]
    sames = [flag(others[p] == centres[p] + SEND) for p in range(PAIRS)]
    low, high = lane_half()
    columns_of(both[...], square, turned)
    turn_inv[...] = product(split(curl[...]), split(mix_w[...]), NT)
    total = [None] * BASIS
    for p in range(PAIRS):
        lane_rows = [twice(both[3 + i : 4 + i, :], p) for i in range(3)]
        lane_move = [twice(both[11 + i : 12 + i, :], p) for i in range(3)]
        columns = [turned[p * TA : (p + 1) * TA, i : i + 1] for i in range(3)]
        column_move = [turned[p * TA : (p + 1) * TA, 8 + i : 9 + i] for i in range(3)]
        unit, inverse, weight, slope, sine, cosine = geometry(
            lane_rows, columns, -1.0, live[0, p].astype(F32), sames[p]
        )
        move = [b - a for a, b in zip(lane_move, column_move)]
        stretch = unit[0] * move[0] + unit[1] * move[1] + unit[2] * move[2]
        turn = [(m - v * stretch) * inverse for m, v in zip(move, unit)]
        angular, turning = harmonics(unit), harmonics_tangent(unit, turn)
        values, slopes = single_orders(sine, cosine, weight, slope)
        for m in range(COMPS):
            if m == 0:
                on_value, on_slope = low, high * stretch
            else:
                on_value = angular[m] * low + turning[m] * high
                on_slope = angular[m] * high * stretch
            for n in range(BASIS):
                hi, lo = split(on_value * values[n] + on_slope * slopes[n])
                lh[n * TA : (n + 1) * TA, m * CHUNK : (m + 1) * CHUNK] = hi
                ll[n * TA : (n + 1) * TA, m * CHUNK : (m + 1) * CHUNK] = lo
            at = slice((p * COMPS + m) * TA, (p * COMPS + m + 1) * TA)
            group = slice(GROUP[m] * 256, (GROUP[m] + 1) * 256)
            here = slice(p * TA, (p + 1) * TA)
            steady = (2.0 * env_scale) * dinv[here, group]
            bent = (2.0 * env_scale) * turn_inv[here, group]
            hi, lo = split(env[at, :] * bent + envdot[at, :] * steady)
            gh[m * CHUNK : m * CHUNK + TA, :] = hi
            gl[m * CHUNK : m * CHUNK + TA, :] = lo
            hi, lo = split(env[at, :] * steady)
            gh[m * CHUNK + TA : (m + 1) * CHUNK, :] = hi
            gl[m * CHUNK + TA : (m + 1) * CHUNK, :] = lo
        raw[...] = product((lh[...], ll[...]), (gh[...], gl[...]), NN)
        for n in range(BASIS):
            term = jnp.sum(
                raw[n * TA : (n + 1) * TA, :] * fsel[p * TA : (p + 1) * TA, :], axis=0, keepdims=True
            )
            total[n] = term if total[n] is None else total[n] + term
    for n in range(BASIS):
        grad_radial[n : n + 1, :] = total[n]


def vmem():
    return pl.BlockSpec(memory_space=pltpu.VMEM)


def smem():
    return pl.BlockSpec(memory_space=pltpu.SMEM)


def call(kernel, name, outs, scratch, scalars, *operands, flops=0):
    return pl.pallas_call(
        kernel,
        name=name,
        out_shape=[jax.ShapeDtypeStruct(shape, F32) for shape in outs],
        in_specs=[smem()] * scalars + [vmem()] * (len(operands) - scalars),
        out_specs=[vmem()] * len(outs),
        scratch_shapes=[pltpu.VMEM(shape, kind) for shape, kind in scratch],
        compiler_params=pltpu.CompilerParams(vmem_limit_bytes=48 * 1024 * 1024),
        cost_estimate=pl.CostEstimate(flops=flops, bytes_accessed=1 << 20, transcendentals=0),
    )(*operands)


def shifted(block, axis, by):
    count = lax.axis_size(axis)
    return lax.ppermute(block, axis, [(i, (i + by) % count) for i in range(count)])


def on_device(
    positions,
    features,
    species,
    ref_forces,
    centre_tile,
    other_tile,
    pair_live,
    send_tiles,
    radial_w,
    mix_w,
    species_w,
    out_w,
):
    atoms = positions.shape[2]
    channels = features.shape[2]
    table = (COMPS * TA, BASIS * TA)
    sent = (SEND * TA + 16, channels)
    slots = PAIRS * TA
    turning = [((CHUNK, CHUNK), F32)] * 2
    out_row = out_w.reshape(1, channels)

    to_low, to_high = call(
        gather_kernel, "gather", [sent, sent], [], 1, send_tiles, positions, features, ref_forces
    )
    from_low = shifted(to_high, "domain", 1)
    from_high = shifted(to_low, "domain", -1)

    env, dinv, gate, curve, inv, rows, fsel, own, grads_up, grads_down = call(
        force_kernel,
        "force",
        [
            (PAIRS * COMPS * TA, channels),
            (slots, 3 * channels),
            (slots, channels),
            (slots, channels),
            (slots, 3 * channels),
            (8, CHUNK),
            (slots, channels),
            (8, atoms),
            (8, CHUNK),
            (8, CHUNK),
        ],
        turning
        + [(table, BF16)] * 2
        + [((PAIRS, BASIS * TA, channels), BF16)] * 2
        + [((PAIRS * COMPS * TA, BASIS * TA), F32)]
        + [((3 * channels, channels), BF16)] * 2,
        4,
        centre_tile, other_tile, pair_live, send_tiles,
        positions, features, species, from_low, from_high, radial_w, mix_w, species_w, out_row,
        flops=1 << 31,
    )
    low_one = shifted(grads_up, "domain", 1)
    low_two = shifted(grads_up, "domain", 2)
    high_one = shifted(grads_down, "domain", -1)
    high_two = shifted(grads_down, "domain", -2)

    total_count = 3.0 * atoms * lax.axis_size("domain") * lax.axis_size("batch")
    scale = jnp.full((1,), 2.0 / math.sqrt(total_count), F32)
    forces, grad_mix, small, envdot, curl, both = call(
        tangent_kernel,
        "tangent",
        [
            (1, 3, atoms),
            (3 * channels, channels),
            (8, channels),
            (PAIRS * COMPS * TA, channels),
            (slots, channels),
            (16, CHUNK),
        ],
        turning
        + [(table, BF16)] * 2
        + [((BASIS * TA, channels), BF16)] * 2
        + [((PAIRS * COMPS * TA, channels), F32)]
        + [((2 * slots, 3 * channels), F32), ((2 * slots, channels), F32)],
        5,
        scale, centre_tile, other_tile, pair_live, send_tiles,
        ref_forces, from_low, from_high, own, low_one, low_two, high_one, high_two,
        rows, fsel, env, dinv, gate, curve, inv, radial_w, mix_w, out_row,
        flops=1 << 31,
    )
    (grad_radial,) = call(
        radial_kernel,
        "radial",
        [(BASIS, channels)],
        turning
        + [((BASIS * TA, COMPS * CHUNK), BF16)] * 2
        + [((COMPS * CHUNK, channels), BF16)] * 2
        + [((slots, 3 * channels), F32), ((BASIS * TA, channels), F32)],
        3,
        centre_tile, other_tile, pair_live,
        both, fsel, env, envdot, dinv, curl, mix_w,
        flops=1 << 31,
    )
    packed = jnp.concatenate([grad_mix, grad_radial, small], axis=0)
    packed = lax.psum(packed, ("domain", "batch"))
    rows_mix = 3 * channels
    return (
        forces,
        packed[rows_mix : rows_mix + BASIS],
        packed[:rows_mix],
        packed[rows_mix + BASIS : rows_mix + BASIS + SPECIES],
        packed[rows_mix + BASIS + SPECIES],
    )


def solution(mesh):
    return jax.shard_map(
        on_device,
        mesh=mesh,
        in_specs=(
            P(("parts", "batch"), None, "domain"),
            P(("parts", "batch"), "domain", None),
            P(("parts", "batch"), "domain"),
            P(("parts", "batch"), None, "domain"),
            P(("parts", "batch"), "domain"),
            P(("parts", "batch"), "domain"),
            P(("parts", "batch"), "domain"),
            P(("parts", "batch"), "domain"),
            P(),
            P(),
            P(),
            P(),
        ),
        out_specs=(
            P(("parts", "batch"), None, "domain"),
            P("parts", None),
            P("parts", None),
            P("parts", None),
            P("parts"),
        ),
        check_vma=False,
    )
```

profile of v0, /device:TPU:0, one launch (start us, length us, event | category | flops | bytes accessed | tf_op | source)
XLA Modules:
  0.0 159.6 jit_solution(18295570123812192691)
XLA Ops:
  7.2 0.7 copy.17.pos
  7.9 0.7 copy.20.ref
  8.6 0.9 copy-done
  9.5 0.7 copy-done.1
  10.2 0.6 gather.1
  10.8 3.0 %collective-permute-start = (f32[144,256]{1,0:T(8,128)S(1)}, f32[144,256]{1,0:T(8,128)S(1)}, u32[]{:S(2)}, u32[]{:S(2)}) collective-permute-start(f32[144,256]{1,0:T(8,128)S(1)} %get-tuple-element.23), channel_id=1, source_target_pairs={{0,2},{2,4},{4,6},{6,8},{8,10},{10,12},{12,14},{14,0},{1,3},{3,5},... | collective-permute-start | bytes 442376 | tf_op jit(solution)/shard_map/ppermute | solution.py:504
  13.8 3.1 %collective-permute-start.1 = (f32[144,256]{1,0:T(8,128)S(1)}, f32[144,256]{1,0:T(8,128)S(1)}, u32[]{:S(2)}, u32[]{:S(2)}) collective-permute-start(f32[144,256]{1,0:T(8,128)S(1)} %get-tuple-element.24), channel_id=1, source_target_pairs={{0,14},{2,0},{4,2},{6,4},{8,6},{10,8},{12,10},{14,12},{1,15},{3,1}... | collective-permute-start | bytes 442376 | tf_op jit(solution)/shard_map/ppermute | solution.py:504
  16.9 3.9 %collective-permute-done.from_low = f32[144,256]{1,0:T(8,128)S(1)} collective-permute-done((f32[144,256]{1,0:T(8,128)S(1)}, f32[144,256]{1,0:T(8,128)S(1)}, u32[]{:S(2)}, u32[]{:S(2)}) %collective-permute-start) | collective-permute-done | bytes 147488 | tf_op jit(solution)/shard_map/ppermute | solution.py:504
  20.8 1.5 collective-permute-done.1.from_high
  22.3 0.7 copy-done.2
  23.0 1.1 copy-done.3
  24.1 0.7 copy-done.5
  24.8 0.7 copy-done.6
  25.5 0.7 copy-done.7
  26.2 0.7 copy-done.8
  26.8 0.7 copy-done.10
  27.5 0.7 copy-done.11
  28.2 0.7 copy-done.12
  28.8 5.5 %force.1 = (f32[1152,256]{1,0:T(8,128)S(1)}, f32[128,768]{1,0:T(8,128)S(1)}, f32[128,256]{1,0:T(8,128)S(1)}, f32[128,256]{1,0:T(8,128)S(1)}, f32[128,768]{1,0:T(...) custom-call(s32[1,2]{1,0:T(1,128)S(1)} %copy-done.10, ...), custom_call_target="tpu_custom_call" | custom-call | flops 2147483648 | bytes 1048576 | tf_op jit(solution)/shard_map/force/pallas_call | solution.py:490
  34.3 1.3 collective-permute-start.3
  35.6 0.6 collective-permute-start.2
  36.2 2.2 %collective-permute-start.5 = (f32[8,128]{1,0:T(8,128)S(1)}, f32[8,128]{1,0:T(8,128)S(1)}, u32[]{:S(2)}, u32[]{:S(2)}) collective-permute-start(f32[8,128]{1,0:T(8,128)S(1)} %get-tuple-element.27), channel_id=1, source_target_pairs={{0,12},{2,14},{4,0},{6,2},{8,4},{10,6},{12,8},{14,10},{1,13},{3,15... | collective-permute-start | bytes 12296 | tf_op jit(solution)/shard_map/ppermute | solution.py:504
  38.4 2.6 %collective-permute-start.4 = (f32[8,128]{1,0:T(8,128)S(1)}, f32[8,128]{1,0:T(8,128)S(1)}, u32[]{:S(2)}, u32[]{:S(2)}) collective-permute-start(f32[8,128]{1,0:T(8,128)S(1)} %get-tuple-element.27), channel_id=1, source_target_pairs={{0,14},{2,0},{4,2},{6,4},{8,6},{10,8},{12,10},{14,12},{1,15},{3,1}... | collective-permute-start | bytes 12296 | tf_op jit(solution)/shard_map/ppermute | solution.py:504
  41.1 0.8 collective-permute-done.2.low_one
  42.4 4.6 %tangent.1 = (f32[1,3,256]{2,1,0:T(4,128)S(1)}, f32[768,256]{1,0:T(8,128)S(1)}, f32[8,256]{1,0:T(8,128)S(1)}, f32[1152,256]{1,0:T(8,128)S(1)}, f32[128,256]{1,0:T(8,128)S(1)}, /*index=5*/f32[16,128]{1,0:T(8,128)S(1)}) custom-call(f32[1]{0:T(128)} %constant.0.clone.1.scale, s32[1,2]{1,0:T(1,128)S(1)} %copy-done.10, s32[1,2]{1,0:T(1,128)S(1)} %copy-done.11, ...), custom_call_target="tpu_custom_call" | custom-call | flops 2147483648 | bytes 1048576 | tf_op jit(solution)/shard_map/tangent/pallas_call | solution.py:490
  47.1 5.4 %radial.1 = f32[8,256]{1,0:T(8,128)S(1)} custom-call(s32[1,2]{1,0:T(1,128)S(1)} %copy-done.10, s32[1,2]{1,0:T(1,128)S(1)} %copy-done.11, s32[1,2]{1,0:T(1,128)S(1)} %copy-done.13, f32[16,128]{1,0:T(8,128)S(1)} %get-tuple-element.37.both, f32[128,256]{1,0:T(8,128)S(1)} %get-tuple-element.29.fsel, f32[1152,256]{1,0:T(8,128)S(1)} %get-tuple-element.30.env, ...), custom_call_target="tpu_custom_call" | custom-call | flops 2147483648 | bytes 1048576 | tf_op jit(solution)/shard_map/radial/pallas_call | solution.py:490
  52.5 1.0 pad_maximum_fusion
  54.1 92.7 %all-reduce.2.cloned.1.call-done = f32[784,256]{1,0:T(8,128)} async-done(((f32[784,256]{1,0:T(8,128)}), f32[784,256]{1,0:T(8,128)}) %all-reduce.2.cloned.1.call-update) | async-done | bytes 802832 | tf_op jit(solution)/shard_map/psum | solution.py:603
  146.8 1.3 slice.19
  148.1 1.3 slice.18
  149.4 1.3 slice.16
  150.7 2.1 %slice.17 = f32[768,256]{1,0:T(8,128)} slice(f32[784,256]{1,0:T(8,128)} %all-reduce.2.cloned.1.call-done), slice={[0:768], [0:256]} | slice | bytes 1572864 | tf_op jit(solution)/shard_map/slice | solution.py:608
  (23 shorter events, 1.2 us)
Async XLA Ops:
  7.2 139.7 %all-reduce.2.cloned.1.call-start = ((), (), s32[]{:S(2)}) async-start(), calls=%async_computation | async-start | bytes 1605632 | tf_op jit(solution)/shard_map/psum | solution.py:603
  8.6 0.9 copy-start
  9.5 0.7 copy-start.1
  10.8 10.0 %collective-permute-start = (f32[144,256]{1,0:T(8,128)S(1)}, f32[144,256]{1,0:T(8,128)S(1)}, u32[]{:S(2)}, u32[]{:S(2)}) collective-permute-start(f32[144,256]{1,0:T(8,128)S(1)} %get-tuple-element.23), channel_id=1, source_target_pairs={{0,2},{2,4},{4,6},{6,8},{8,10},{10,12},{12,14},{14,0},{1,3},{3,5},... | collective-permute-start | bytes 442376 | tf_op jit(solution)/shard_map/ppermute | solution.py:504
  13.8 8.5 %collective-permute-start.1 = (f32[144,256]{1,0:T(8,128)S(1)}, f32[144,256]{1,0:T(8,128)S(1)}, u32[]{:S(2)}, u32[]{:S(2)}) collective-permute-start(f32[144,256]{1,0:T(8,128)S(1)} %get-tuple-element.24), channel_id=1, source_target_pairs={{0,14},{2,0},{4,2},{6,4},{8,6},{10,8},{12,10},{14,12},{1,15},{3,1}... | collective-permute-start | bytes 442376 | tf_op jit(solution)/shard_map/ppermute | solution.py:504
  22.3 0.7 copy-start.2
  23.0 1.1 copy-start.3
  24.1 0.7 copy-start.5
  24.8 0.7 copy-start.6
  25.5 0.7 copy-start.7
  26.2 0.7 copy-start.8
  26.8 0.7 copy-start.10
  27.5 0.7 copy-start.11
  28.1 0.7 copy-start.12
  28.8 13.6 %copy-start.4 = (f32[768,256]{1,0:T(8,128)S(1)}, f32[768,256]{1,0:T(8,128)}, u32[]{:S(2)}) copy-start(f32[768,256]{1,0:T(8,128)} %mix_w.5) | copy-start | bytes 2359300
  28.8 13.6 %copy-start.9 = (f32[256]{0:T(256)S(1)}, f32[256]{0:T(256)}, u32[]{:S(2)}) copy-start(f32[256]{0:T(256)} %param.23) | copy-start | bytes 3076
  34.3 6.8 %collective-permute-start.3 = (f32[8,128]{1,0:T(8,128)S(1)}, f32[8,128]{1,0:T(8,128)S(1)}, u32[]{:S(2)}, u32[]{:S(2)}) collective-permute-start(f32[8,128]{1,0:T(8,128)S(1)} %get-tuple-element.26), channel_id=1, source_target_pairs={{0,4},{2,6},{4,8},{6,10},{8,12},{10,14},{12,0},{14,2},{1,5},{3,7},... | collective-permute-start | bytes 12296 | tf_op jit(solution)/shard_map/ppermute | solution.py:504
  35.6 6.3 %collective-permute-start.2 = (f32[8,128]{1,0:T(8,128)S(1)}, f32[8,128]{1,0:T(8,128)S(1)}, u32[]{:S(2)}, u32[]{:S(2)}) collective-permute-start(f32[8,128]{1,0:T(8,128)S(1)} %get-tuple-element.26), channel_id=1, source_target_pairs={{0,2},{2,4},{4,6},{6,8},{8,10},{10,12},{12,14},{14,0},{1,3},{3,5},... | collective-permute-start | bytes 12296 | tf_op jit(solution)/shard_map/ppermute | solution.py:504
  36.2 5.7 %collective-permute-start.5 = (f32[8,128]{1,0:T(8,128)S(1)}, f32[8,128]{1,0:T(8,128)S(1)}, u32[]{:S(2)}, u32[]{:S(2)}) collective-permute-start(f32[8,128]{1,0:T(8,128)S(1)} %get-tuple-element.27), channel_id=1, source_target_pairs={{0,12},{2,14},{4,0},{6,2},{8,4},{10,6},{12,8},{14,10},{1,13},{3,15... | collective-permute-start | bytes 12296 | tf_op jit(solution)/shard_map/ppermute | solution.py:504
  38.4 4.0 %collective-permute-start.4 = (f32[8,128]{1,0:T(8,128)S(1)}, f32[8,128]{1,0:T(8,128)S(1)}, u32[]{:S(2)}, u32[]{:S(2)}) collective-permute-start(f32[8,128]{1,0:T(8,128)S(1)} %get-tuple-element.27), channel_id=1, source_target_pairs={{0,14},{2,0},{4,2},{6,4},{8,6},{10,8},{12,10},{14,12},{1,15},{3,1}... | collective-permute-start | bytes 12296 | tf_op jit(solution)/shard_map/ppermute | solution.py:504
  42.4 4.6 %copy-start.13 = (s32[1,2]{1,0:T(1,128)S(1)}, s32[1,2]{1,0:T(1,128)}, u32[]{:S(2)}) copy-start(s32[1,2]{1,0:T(1,128)} %live.5) | copy-start | bytes 28
Sparse Core Ops, SparseCore 0:
  53.6 93.1 all-reduce.1
where the time goes:
time: 160 us
  waiting for transfers between devices  99.5 us (62%)
  Pallas kernels  16.1 us (10%)
  local copies, waits for them, and re-layouts  16 us (10%)
  between operations  14.1 us (9%)
  starting transfers between devices  13 us (8%)
    psum x1, waiting for transfers between devices, on_device(): packed = lax.psum(packed, ('domain', 'batch'))  92.7 us
    pallas_call x4, Pallas kernels, call(): pl.pallas_call(kernel, name=name, out_shape=[jax.ShapeDtypeStruct(shape,...  16.1 us
    ppermute x6, starting transfers between devices, shifted(): lax.ppermute(block, axis, [(i, (i + by) % count) for i in range(count)])  12.9 us
    unnamed x31, local copies, waits for them, and re-layouts  10.1 us
    ppermute x6, waiting for transfers between devices, shifted(): lax.ppermute(block, axis, [(i, (i + by) % count) for i in range(count)])  6.72 us
  transfers between devices with their start and end apart: 7, of which 5 were waited for; matrix products, arithmetic and copies ran while one was open for 0% of the time, Pallas kernels for 0%

commit v1 on v0

--- a/solution.py
+++ b/solution.py
@@ -13,6 +13,7 @@
 COMPS = 9
 BASIS = 8
 SPECIES = 4
+HALF = 128
 CHUNK = 2 * TA
 
 cutoff = 2.5
@@ -330,7 +331,7 @@
 def tangent_kernel(
     scale, centre, other, live, send, ref, from_low, from_high, own, low_one, low_two, high_one, high_two,
     rows, fsel, env, dinv, gate, curve, inv, radial_w, mix_w, out_w,
-    forces, grad_mix, small, envdot, curl, both,
+    forces, keep, give, small, envdot, curl, both,
     square, turned, th, tl, xh, xl, raw, left, right,
 ):
     ghost = SEND * TA
@@ -414,7 +415,11 @@
     once = 1.0 - shared * flag(lax.broadcasted_iota(jnp.int32, (half, 1), 0) >= TA)
     right[0:half, :] = bend * once
     right[half:, :] = gate[...] * out_w[...] * once
-    grad_mix[...] = product(split(left[...]), split(right[...]), TN)
+    core = lax.axis_index("batch")
+    left_parts = split(left[...])
+    for out, part in ((keep, core), (give, 1 - core)):
+        lanes = pl.ds(pl.multiple_of(part * HALF, HALF), HALF)
+        out[...] = product(left_parts, split(right[:, lanes]), TN)
     small[...] = jnp.zeros_like(small)
     kind = turned[:, 6:7]
     for s in range(SPECIES):
@@ -478,6 +483,42 @@
         grad_radial[n : n + 1, :] = total[n]
 
 
+SMALL = 32
+
+
+def pack_kernel(keep, taken, radial, small, packed):
+    rows = keep.shape[0]
+    packed[0:rows, :] = keep[...] + taken[...]
+    packed[rows:, :] = jnp.zeros((packed.shape[0] - rows, HALF), F32)
+    for h in range(2):
+        lanes = slice(h * HALF, (h + 1) * HALF)
+        packed[rows + 16 * h : rows + 16 * h + 8, :] = radial[:, lanes]
+        packed[rows + 16 * h + 8 : rows + 16 * h + 16, :] = small[:, lanes]
+
+
+def sum_kernel(spread, summed):
+    count = lax.axis_size("domain")
+    piece = spread.shape[0] // count
+    total = spread[0:piece, :]
+    for i in range(1, count):
+        total = total + spread[i * piece : (i + 1) * piece, :]
+    for i in range(count):
+        summed[i * piece : (i + 1) * piece, :] = total
+
+
+def join_kernel(whole, facing, mix, radial, kinds, out):
+    rows = mix.shape[0]
+    core = lax.axis_index("batch")
+    for ref, part in ((whole, core), (facing, 1 - core)):
+        mix[:, pl.ds(pl.multiple_of(part * HALF, HALF), HALF)] = ref[0:rows, :]
+    for h in range(2):
+        lanes = slice(h * HALF, (h + 1) * HALF)
+        both = whole[rows + 16 * h : rows + 16 * h + 16, :] + facing[rows + 16 * h : rows + 16 * h + 16, :]
+        radial[:, lanes] = both[0:BASIS]
+        kinds[:, lanes] = both[BASIS : BASIS + SPECIES]
+        out[:, lanes] = both[BASIS + SPECIES : BASIS + SPECIES + 1]
+
+
 def vmem():
     return pl.BlockSpec(memory_space=pltpu.VMEM)
 
@@ -564,12 +605,13 @@
 
     total_count = 3.0 * atoms * lax.axis_size("domain") * lax.axis_size("batch")
     scale = jnp.full((1,), 2.0 / math.sqrt(total_count), F32)
-    forces, grad_mix, small, envdot, curl, both = call(
+    forces, keep, give, small, envdot, curl, both = call(
         tangent_kernel,
         "tangent",
         [
             (1, 3, atoms),
-            (3 * channels, channels),
+            (3 * channels, HALF),
+            (3 * channels, HALF),
             (8, channels),
             (PAIRS * COMPS * TA, channels),
             (slots, channels),
@@ -599,16 +641,25 @@
         both, fsel, env, envdot, dinv, curl, mix_w,
         flops=1 << 31,
     )
-    packed = jnp.concatenate([grad_mix, grad_radial, small], axis=0)
-    packed = lax.psum(packed, ("domain", "batch"))
+    count = lax.axis_size("domain")
     rows_mix = 3 * channels
-    return (
-        forces,
-        packed[rows_mix : rows_mix + BASIS],
-        packed[:rows_mix],
-        packed[rows_mix + BASIS : rows_mix + BASIS + SPECIES],
-        packed[rows_mix + BASIS + SPECIES],
+    piece = -(-(rows_mix + SMALL) // (8 * count)) * 8
+    taken = shifted(give, "batch", 1)
+    (packed,) = call(pack_kernel, "pack", [(count * piece, HALF)], [], 0, keep, taken, grad_radial, small)
+    spread = lax.all_to_all(packed, "domain", 0, 0, tiled=True)
+    (summed,) = call(sum_kernel, "sum", [(count * piece, HALF)], [], 0, spread)
+    whole = lax.all_to_all(summed, "domain", 0, 0, tiled=True)
+    facing = shifted(whole, "batch", 1)
+    mix, radial, kinds, out = call(
+        join_kernel,
+        "join",
+        [(rows_mix, channels), (BASIS, channels), (SPECIES, channels), (1, channels)],
+        [],
+        0,
+        whole,
+        facing,
     )
+    return forces, radial, mix, kinds, out.reshape(channels)
 
 
 def solution(mesh):

time: 160 us -> 84.7 us (0.53)
  waiting for transfers between devices: 99.5 us -> 7.9 us
  blocking collectives: 0 us -> 35.3 us
  between operations: 14.1 us -> 0.7 us
  local copies, waits for them, and re-layouts: 16 us -> 10.1 us
    psum x1 -> x0, waiting for transfers between devices: 92.7 us -> none  [on_device(): packed = lax.psum(packed, ('domain', 'batch'))]
    all_to_all x0 -> x2, blocking collectives: none -> 35.3 us  [the longest x1 19.3 us: on_device(): spread = lax.all_to_all(packed, 'domain', 0, 0, tiled=True)]
    slice x4 -> x0, local copies, waits for them, and re-layouts: 5.91 us -> none  [the longest x1 2.06 us: on_device(): packed[:rows_mix]]
    ppermute x6 -> x8, waiting for transfers between devices: 6.72 us -> 7.9 us  [shifted(): lax.ppermute(block, axis, [(i, (i + by) % count) for i in range(count)])]
    pallas_call x4 -> x7, Pallas kernels: 16.1 us -> 17.3 us  [call(): pl.pallas_call(kernel, name=name, out_shape=[jax.ShapeDtypeStruct(shape,...]
    ppermute x6 -> x8, starting transfers between devices: 12.9 us -> 13 us  [shifted(): lax.ppermute(block, axis, [(i, (i + by) % count) for i in range(count)])]
    unnamed x31 -> x29, local copies, waits for them, and re-layouts: 10.1 us -> 10.1 us
  transfers between devices with their start and end apart: 7 -> 8, of which waited for: 5 -> 5; matrix products, arithmetic and copies ran while one was open for 0% -> 1% of each run, Pallas kernels for 0% -> 6%
where the time goes in v1:
time: 84.7 us; the launch traced here: 84.3 us
  blocking collectives  35.3 us (42%)
  Pallas kernels  17.3 us (20%)
  starting transfers between devices  13 us (15%)
  local copies, waits for them, and re-layouts  10.1 us (12%)
  waiting for transfers between devices  7.9 us (9%)
    all_to_all x1, blocking collectives, on_device(): spread = lax.all_to_all(packed, 'domain', 0, 0, tiled=True)  19.3 us
    pallas_call x7, Pallas kernels, call(): pl.pallas_call(kernel, name=name, out_shape=[jax.ShapeDtypeStruct(shape,...  17.3 us
    all_to_all x1, blocking collectives, on_device(): whole = lax.all_to_all(summed, 'domain', 0, 0, tiled=True)  16 us
    ppermute x8, starting transfers between devices, shifted(): lax.ppermute(block, axis, [(i, (i + by) % count) for i in range(count)])  13 us
    unnamed x29, local copies, waits for them, and re-layouts  10.1 us
    ppermute x8, waiting for transfers between devices, shifted(): lax.ppermute(block, axis, [(i, (i + by) % count) for i in range(count)])  7.9 us
  transfers between devices with their start and end apart: 8, of which 5 were waited for; matrix products, arithmetic and copies ran while one was open for 1% of the time, Pallas kernels for 6%

profile of v1, /device:TPU:0, one launch (start us, length us, event | category | flops | bytes accessed | tf_op | source)
XLA Modules:
  0.0 84.3 jit_solution(3646671392375696695)
XLA Ops:
  0.6 0.7 copy.17.pos
  1.3 0.7 copy.20.ref
  2.0 0.9 %copy-done = f32[1,256,256]{2,1,0:T(8,128)S(1)} copy-done((f32[1,256,256]{2,1,0:T(8,128)S(1)}, f32[1,256,256]{2,1,0:T(8,128)}, u32[]{:S(2)}) %copy-start) | copy-done | bytes 262168
  3.0 0.7 copy-done.1
  3.6 0.6 gather.1
  4.2 3.0 %collective-permute-start = (f32[144,256]{1,0:T(8,128)S(1)}, f32[144,256]{1,0:T(8,128)S(1)}, u32[]{:S(2)}, u32[]{:S(2)}) collective-permute-start(f32[144,256]{1,0:T(8,128)S(1)} %get-tuple-element.28), channel_id=1, source_target_pairs={{0,2},{2,4},{4,6},{6,8},{8,10},{10,12},{12,14},{14,0},{1,3},{3,5},... | collective-permute-start | bytes 442376 | tf_op jit(solution)/shard_map/ppermute | solution.py:545
  7.3 3.1 %collective-permute-start.1 = (f32[144,256]{1,0:T(8,128)S(1)}, f32[144,256]{1,0:T(8,128)S(1)}, u32[]{:S(2)}, u32[]{:S(2)}) collective-permute-start(f32[144,256]{1,0:T(8,128)S(1)} %get-tuple-element.29), channel_id=1, source_target_pairs={{0,14},{2,0},{4,2},{6,4},{8,6},{10,8},{12,10},{14,12},{1,15},{3,1}... | collective-permute-start | bytes 442376 | tf_op jit(solution)/shard_map/ppermute | solution.py:545
  10.4 3.9 %collective-permute-done.from_low = f32[144,256]{1,0:T(8,128)S(1)} collective-permute-done((f32[144,256]{1,0:T(8,128)S(1)}, f32[144,256]{1,0:T(8,128)S(1)}, u32[]{:S(2)}, u32[]{:S(2)}) %collective-permute-start) | collective-permute-done | bytes 147488 | tf_op jit(solution)/shard_map/ppermute | solution.py:545
  14.2 1.5 %collective-permute-done.1.from_high = f32[144,256]{1,0:T(8,128)S(1)} collective-permute-done((f32[144,256]{1,0:T(8,128)S(1)}, f32[144,256]{1,0:T(8,128)S(1)}, u32[]{:S(2)}, u32[]{:S(2)}) %collective-permute-start.1) | collective-permute-done | bytes 147488 | tf_op jit(solution)/shard_map/ppermute | solution.py:545
  15.7 0.7 copy-done.2
  16.4 1.1 %copy-done.3 = f32[768,256]{1,0:T(8,128)S(1)} copy-done((f32[768,256]{1,0:T(8,128)S(1)}, f32[768,256]{1,0:T(8,128)}, u32[]{:S(2)}) %copy-start.3) | copy-done | bytes 786456
  17.5 0.7 copy-done.5
  18.2 0.7 copy-done.6
  18.9 0.7 copy-done.7
  19.6 0.7 copy-done.8
  20.3 0.7 copy-done.10
  20.9 0.7 copy-done.11
  21.6 0.7 copy-done.12
  22.2 5.4 %force.1 = (f32[1152,256]{1,0:T(8,128)S(1)}, f32[128,768]{1,0:T(8,128)S(1)}, f32[128,256]{1,0:T(8,128)S(1)}, f32[128,256]{1,0:T(8,128)S(1)}, f32[128,768]{1,0:T(...) custom-call(s32[1,2]{1,0:T(1,128)S(1)} %copy-done.10, ...), custom_call_target="tpu_custom_call" | custom-call | flops 2147483648 | bytes 1048576 | tf_op jit(solution)/shard_map/force/pallas_call | solution.py:531
  27.7 1.3 %collective-permute-start.3 = (f32[8,128]{1,0:T(8,128)S(1)}, f32[8,128]{1,0:T(8,128)S(1)}, u32[]{:S(2)}, u32[]{:S(2)}) collective-permute-start(f32[8,128]{1,0:T(8,128)S(1)} %get-tuple-element.31), channel_id=1, source_target_pairs={{0,4},{2,6},{4,8},{6,10},{8,12},{10,14},{12,0},{14,2},{1,5},{3,7},... | collective-permute-start | bytes 12296 | tf_op jit(solution)/shard_map/ppermute | solution.py:545
  29.0 0.6 collective-permute-start.2
  29.6 2.2 %collective-permute-start.5 = (f32[8,128]{1,0:T(8,128)S(1)}, f32[8,128]{1,0:T(8,128)S(1)}, u32[]{:S(2)}, u32[]{:S(2)}) collective-permute-start(f32[8,128]{1,0:T(8,128)S(1)} %get-tuple-element.32), channel_id=1, source_target_pairs={{0,12},{2,14},{4,0},{6,2},{8,4},{10,6},{12,8},{14,10},{1,13},{3,15... | collective-permute-start | bytes 12296 | tf_op jit(solution)/shard_map/ppermute | solution.py:545
  31.8 2.6 %collective-permute-start.4 = (f32[8,128]{1,0:T(8,128)S(1)}, f32[8,128]{1,0:T(8,128)S(1)}, u32[]{:S(2)}, u32[]{:S(2)}) collective-permute-start(f32[8,128]{1,0:T(8,128)S(1)} %get-tuple-element.32), channel_id=1, source_target_pairs={{0,14},{2,0},{4,2},{6,4},{8,6},{10,8},{12,10},{14,12},{1,15},{3,1}... | collective-permute-start | bytes 12296 | tf_op jit(solution)/shard_map/ppermute | solution.py:545
  34.5 0.8 collective-permute-done.2.low_one
  35.3 0.6 collective-permute-done.4.high_one
  35.8 4.7 %tangent.1 = (f32[1,3,256]{2,1,0:T(4,128)S(1)}, f32[768,128]{1,0:T(8,128)S(1)}, f32[768,128]{1,0:T(8,128)S(1)}, f32[8,256]{1,0:T(8,128)S(1)}, f32[1152,256]{1,0:...) custom-call(f32[1]{0:T(128)} %constant.0.clone.1.scale, s32[1,2]{1,0:T(1,128)S(1)} %copy-done.10, ...), custom_call_target="tpu_custom_call" | custom-call | flops 2147483648 | bytes 1048576 | tf_op jit(solution)/shard_map/tangent/pallas_call | solution.py:531
  40.6 5.4 %radial.1 = f32[8,256]{1,0:T(8,128)S(1)} custom-call(s32[1,2]{1,0:T(1,128)S(1)} %copy-done.10, s32[1,2]{1,0:T(1,128)S(1)} %copy-done.11, s32[1,2]{1,0:T(1,128)S(1)} %copy-done.12, f32[16,128]{1,0:T(8,128)S(1)} %get-tuple-element.43.both, f32[128,256]{1,0:T(8,128)S(1)} %get-tuple-element.34.fsel, f32[1152,256]{1,0:T(8,128)S(1)} %get-tuple-element.35.env, ...), custom_call_target="tpu_custom_call" | custom-call | flops 2147483648 | bytes 1048576 | tf_op jit(solution)/shard_map/radial/pallas_call | solution.py:531
  46.1 19.3 %all_to_all.22 = f32[8,104,128]{2,1,0:T(8,128)S(1)} all-to-all(f32[8,104,128]{2,1,0:T(8,128)S(1)} %bitcast.8), channel_id=1, replica_groups=mesh['parts'=2,'domain'=8,'batch'=2] {'domain'}, dimensions={0} | all-to-all | bytes 851968 | tf_op jit(solution)/shard_map/all_to_all | solution.py:649
  65.5 16.0 %all_to_all.23 = f32[8,104,128]{2,1,0:T(8,128)S(1)} all-to-all(f32[8,104,128]{2,1,0:T(8,128)S(1)} %bitcast.10), channel_id=1, replica_groups=mesh['parts'=2,'domain'=8,'batch'=2] {'domain'}, dimensions={0} | all-to-all | bytes 851968 | tf_op jit(solution)/shard_map/all_to_all | solution.py:651
  81.5 0.6 copy.21
  82.1 1.2 %collective-permute-done.7.facing = f32[832,128]{1,0:T(8,128)S(1)} collective-permute-done((f32[832,128]{1,0:T(8,128)S(1)}, f32[832,128]{1,0:T(8,128)S(1)}, u32[]{:S(2)}, u32[]{:S(2)}) %collective-permute-start.7) | collective-permute-done | bytes 426016 | tf_op jit(solution)/shard_map/ppermute | solution.py:545
  83.3 1.0 %join.1 = (f32[768,256]{1,0:T(8,128)}, f32[8,256]{1,0:T(8,128)}, f32[4,256]{1,0:T(4,128)}, f32[1,256]{1,0:T(1,128)}) custom-call(f32[832,128]{1,0:T(8,128)S(1)} %bitcast.7, f32[832,128]{1,0:T(8,128)S(1)} %collective-permute-done.7.facing), custom_call_target="tpu_custom_call" | custom-call | bytes 1048576 | tf_op jit(solution)/shard_map/join/pallas_call | solution.py:531
  (22 shorter events, 0.2 us)
Async XLA Ops:
  2.0 0.9 %copy-start = (f32[1,256,256]{2,1,0:T(8,128)S(1)}, f32[1,256,256]{2,1,0:T(8,128)}, u32[]{:S(2)}) copy-start(f32[1,256,256]{2,1,0:T(8,128)} %feat.3) | copy-start | bytes 786436
  3.0 0.7 copy-start.1
  4.2 10.0 %collective-permute-start = (f32[144,256]{1,0:T(8,128)S(1)}, f32[144,256]{1,0:T(8,128)S(1)}, u32[]{:S(2)}, u32[]{:S(2)}) collective-permute-start(f32[144,256]{1,0:T(8,128)S(1)} %get-tuple-element.28), channel_id=1, source_target_pairs={{0,2},{2,4},{4,6},{6,8},{8,10},{10,12},{12,14},{14,0},{1,3},{3,5},... | collective-permute-start | bytes 442376 | tf_op jit(solution)/shard_map/ppermute | solution.py:545
  7.3 8.5 %collective-permute-start.1 = (f32[144,256]{1,0:T(8,128)S(1)}, f32[144,256]{1,0:T(8,128)S(1)}, u32[]{:S(2)}, u32[]{:S(2)}) collective-permute-start(f32[144,256]{1,0:T(8,128)S(1)} %get-tuple-element.29), channel_id=1, source_target_pairs={{0,14},{2,0},{4,2},{6,4},{8,6},{10,8},{12,10},{14,12},{1,15},{3,1}... | collective-permute-start | bytes 442376 | tf_op jit(solution)/shard_map/ppermute | solution.py:545
  15.7 0.7 copy-start.2
  16.4 1.1 %copy-start.3 = (f32[768,256]{1,0:T(8,128)S(1)}, f32[768,256]{1,0:T(8,128)}, u32[]{:S(2)}) copy-start(f32[768,256]{1,0:T(8,128)} %mix_w.5) | copy-start | bytes 2359300
  17.5 0.7 copy-start.5
  18.2 0.7 copy-start.6
  18.9 0.7 copy-start.7
  19.6 0.7 copy-start.8
  20.3 0.7 copy-start.10
  20.9 0.7 copy-start.11
  21.6 0.7 copy-start.12
  22.2 13.6 %copy-start.4 = (f32[768,256]{1,0:T(8,128)S(1)}, f32[768,256]{1,0:T(8,128)}, u32[]{:S(2)}) copy-start(f32[768,256]{1,0:T(8,128)} %mix_w.5) | copy-start | bytes 2359300
  22.2 13.6 %copy-start.9 = (f32[256]{0:T(256)S(1)}, f32[256]{0:T(256)}, u32[]{:S(2)}) copy-start(f32[256]{0:T(256)} %param.23) | copy-start | bytes 3076
  27.7 6.8 %collective-permute-start.3 = (f32[8,128]{1,0:T(8,128)S(1)}, f32[8,128]{1,0:T(8,128)S(1)}, u32[]{:S(2)}, u32[]{:S(2)}) collective-permute-start(f32[8,128]{1,0:T(8,128)S(1)} %get-tuple-element.31), channel_id=1, source_target_pairs={{0,4},{2,6},{4,8},{6,10},{8,12},{10,14},{12,0},{14,2},{1,5},{3,7},... | collective-permute-start | bytes 12296 | tf_op jit(solution)/shard_map/ppermute | solution.py:545
  29.0 6.3 %collective-permute-start.2 = (f32[8,128]{1,0:T(8,128)S(1)}, f32[8,128]{1,0:T(8,128)S(1)}, u32[]{:S(2)}, u32[]{:S(2)}) collective-permute-start(f32[8,128]{1,0:T(8,128)S(1)} %get-tuple-element.31), channel_id=1, source_target_pairs={{0,2},{2,4},{4,6},{6,8},{8,10},{10,12},{12,14},{14,0},{1,3},{3,5},... | collective-permute-start | bytes 12296 | tf_op jit(solution)/shard_map/ppermute | solution.py:545
  29.6 5.7 %collective-permute-start.5 = (f32[8,128]{1,0:T(8,128)S(1)}, f32[8,128]{1,0:T(8,128)S(1)}, u32[]{:S(2)}, u32[]{:S(2)}) collective-permute-start(f32[8,128]{1,0:T(8,128)S(1)} %get-tuple-element.32), channel_id=1, source_target_pairs={{0,12},{2,14},{4,0},{6,2},{8,4},{10,6},{12,8},{14,10},{1,13},{3,15... | collective-permute-start | bytes 12296 | tf_op jit(solution)/shard_map/ppermute | solution.py:545
  31.8 4.0 %collective-permute-start.4 = (f32[8,128]{1,0:T(8,128)S(1)}, f32[8,128]{1,0:T(8,128)S(1)}, u32[]{:S(2)}, u32[]{:S(2)}) collective-permute-start(f32[8,128]{1,0:T(8,128)S(1)} %get-tuple-element.32), channel_id=1, source_target_pairs={{0,14},{2,0},{4,2},{6,4},{8,6},{10,8},{12,10},{14,12},{1,15},{3,1}... | collective-permute-start | bytes 12296 | tf_op jit(solution)/shard_map/ppermute | solution.py:545
  40.5 5.5 %collective-permute-start.6 = (f32[768,128]{1,0:T(8,128)S(1)}, f32[768,128]{1,0:T(8,128)S(1)}, u32[]{:S(2)}, u32[]{:S(2)}) collective-permute-start(f32[768,128]{1,0:T(8,128)S(1)} %get-tuple-element.42), channel_id=1, source_target_pairs={{0,1},{1,0},{2,3},{3,2},{4,5},{5,4},{6,7},{7,6},{8,9},{9,8},{10,11... | collective-permute-start | bytes 1179656 | tf_op jit(solution)/shard_map/ppermute | solution.py:545
  81.5 1.8 %collective-permute-start.7 = (f32[832,128]{1,0:T(8,128)S(1)}, f32[832,128]{1,0:T(8,128)S(1)}, u32[]{:S(2)}, u32[]{:S(2)}) collective-permute-start(f32[832,128]{1,0:T(8,128)S(1)} %bitcast.6), channel_id=1, source_target_pairs={{0,1},{1,0},{2,3},{3,2},{4,5},{5,4},{6,7},{7,6},{8,9},{9,8},{10,11... | collective-permute-start | bytes 1277960 | tf_op jit(solution)/shard_map/ppermute | solution.py:545

commit v2 on v1

--- a/solution.py
+++ b/solution.py
@@ -1,3 +1,4 @@
+import functools
 import math
 
 import jax
@@ -428,82 +429,114 @@
 
 
 def radial_kernel(
-    centre, other, live, both, fsel, env, envdot, dinv, curl, mix_w,
+    p, centre, other, live, both, fsel, env, envdot, dinv, curl, mix_w, after,
     grad_radial,
-    square, turned, lh, ll, gh, gl, turn_inv, raw,
+    square, turned, lh, ll, gh, gl, raw,
 ):
-    centres = [centre[0, p] for p in range(PAIRS)]
-    others = [other[0, p] for p in range(PAIRS)]
-    sames = [flag(others[p] == centres[p] + SEND) for p in range(PAIRS)]
+    same = flag(other[0, p] == centre[0, p] + SEND)
     low, high = lane_half()
     columns_of(both[...], square, turned)
-    turn_inv[...] = product(split(curl[...]), split(mix_w[...]), NT)
-    total = [None] * BASIS
-    for p in range(PAIRS):
-        lane_rows = [twice(both[3 + i : 4 + i, :], p) for i in range(3)]
-        lane_move = [twice(both[11 + i : 12 + i, :], p) for i in range(3)]
-        columns = [turned[p * TA : (p + 1) * TA, i : i + 1] for i in range(3)]
-        column_move = [turned[p * TA : (p + 1) * TA, 8 + i : 9 + i] for i in range(3)]
-        unit, inverse, weight, slope, sine, cosine = geometry(
-            lane_rows, columns, -1.0, live[0, p].astype(F32), sames[p]
+    here = slice(p * TA, (p + 1) * TA)
+    turn_inv = product(split(curl[here, :]), split(mix_w[...]), NT)
+    lane_rows = [twice(both[3 + i : 4 + i, :], p) for i in range(3)]
+    lane_move = [twice(both[11 + i : 12 + i, :], p) for i in range(3)]
+    columns = [turned[here, i : i + 1] for i in range(3)]
+    column_move = [turned[here, 8 + i : 9 + i] for i in range(3)]
+    unit, inverse, weight, slope, sine, cosine = geometry(
+        lane_rows, columns, -1.0, live[0, p].astype(F32), same
+    )
+    move = [b - a for a, b in zip(lane_move, column_move)]
+    stretch = unit[0] * move[0] + unit[1] * move[1] + unit[2] * move[2]
+    turn = [(m - v * stretch) * inverse for m, v in zip(move, unit)]
+    angular, turning = harmonics(unit), harmonics_tangent(unit, turn)
+    values, slopes = single_orders(sine, cosine, weight, slope)
+    for m in range(COMPS):
+        if m == 0:
+            on_value, on_slope = low, high * stretch
+        else:
+            on_value = angular[m] * low + turning[m] * high
+            on_slope = angular[m] * high * stretch
+        for n in range(BASIS):
+            hi, lo = split(on_value * values[n] + on_slope * slopes[n])
+            lh[n * TA : (n + 1) * TA, m * CHUNK : (m + 1) * CHUNK] = hi
+            ll[n * TA : (n + 1) * TA, m * CHUNK : (m + 1) * CHUNK] = lo
+        at = slice((p * COMPS + m) * TA, (p * COMPS + m + 1) * TA)
+        group = slice(GROUP[m] * 256, (GROUP[m] + 1) * 256)
+        steady = (2.0 * env_scale) * dinv[here, group]
+        bent = (2.0 * env_scale) * turn_inv[:, group]
+        hi, lo = split(env[at, :] * bent + envdot[at, :] * steady)
+        gh[m * CHUNK : m * CHUNK + TA, :] = hi
+        gl[m * CHUNK : m * CHUNK + TA, :] = lo
+        hi, lo = split(env[at, :] * steady)
+        gh[m * CHUNK + TA : (m + 1) * CHUNK, :] = hi
+        gl[m * CHUNK + TA : (m + 1) * CHUNK, :] = lo
+    raw[...] = product((lh[...], ll[...]), (gh[...], gl[...]), NN)
+    for n in range(BASIS):
+        grad_radial[n : n + 1, :] = jnp.sum(
+            raw[n * TA : (n + 1) * TA, :] * fsel[here, :], axis=0, keepdims=True
         )
-        move = [b - a for a, b in zip(lane_move, column_move)]
-        stretch = unit[0] * move[0] + unit[1] * move[1] + unit[2] * move[2]
-        turn = [(m - v * stretch) * inverse for m, v in zip(move, unit)]
-        angular, turning = harmonics(unit), harmonics_tangent(unit, turn)
-        values, slopes = single_orders(sine, cosine, weight, slope)
-        for m in range(COMPS):
-            if m == 0:
-                on_value, on_slope = low, high * stretch
-            else:
-                on_value = angular[m] * low + turning[m] * high
-                on_slope = angular[m] * high * stretch
-            for n in range(BASIS):
-                hi, lo = split(on_value * values[n] + on_slope * slopes[n])
-                lh[n * TA : (n + 1) * TA, m * CHUNK : (m + 1) * CHUNK] = hi
-                ll[n * TA : (n + 1) * TA, m * CHUNK : (m + 1) * CHUNK] = lo
-            at = slice((p * COMPS + m) * TA, (p * COMPS + m + 1) * TA)
-            group = slice(GROUP[m] * 256, (GROUP[m] + 1) * 256)
-            here = slice(p * TA, (p + 1) * TA)
-            steady = (2.0 * env_scale) * dinv[here, group]
-            bent = (2.0 * env_scale) * turn_inv[here, group]
-            hi, lo = split(env[at, :] * bent + envdot[at, :] * steady)
-            gh[m * CHUNK : m * CHUNK + TA, :] = hi
-            gl[m * CHUNK : m * CHUNK + TA, :] = lo
-            hi, lo = split(env[at, :] * steady)
-            gh[m * CHUNK + TA : (m + 1) * CHUNK, :] = hi
-            gl[m * CHUNK + TA : (m + 1) * CHUNK, :] = lo
-        raw[...] = product((lh[...], ll[...]), (gh[...], gl[...]), NN)
-        for n in range(BASIS):
-            term = jnp.sum(
-                raw[n * TA : (n + 1) * TA, :] * fsel[p * TA : (p + 1) * TA, :], axis=0, keepdims=True
-            )
-            total[n] = term if total[n] is None else total[n] + term
-    for n in range(BASIS):
-        grad_radial[n : n + 1, :] = total[n]
 
 
 SMALL = 32
 
 
-def pack_kernel(keep, taken, radial, small, packed):
-    rows = keep.shape[0]
-    packed[0:rows, :] = keep[...] + taken[...]
-    packed[rows:, :] = jnp.zeros((packed.shape[0] - rows, HALF), F32)
+def halves(rows):
+    return (rows // 2, True) if rows % 16 == 0 else (rows, False)
+
+
+def hand_on(total, bit, cut, keep_out, give_out):
+    rows = keep_out.shape[0]
+    if not cut:
+        keep_out[...] = total(pl.ds(0, rows))
+        give_out[0:rows, :] = total(pl.ds(0, rows))
+        return
+    mine = lax.bitwise_and(lax.shift_right_logical(lax.axis_index("domain"), bit), 1)
+    for out, part in ((keep_out, mine), (give_out, 1 - mine)):
+        out[0:rows, :] = total(pl.ds(pl.multiple_of(part * rows, 8), rows))
+
+
+def first_kernel(cut, keep, taken, keep_out, give_out, token):
+    hand_on(lambda at: keep[at, :] + taken[at, :], 0, cut, keep_out, give_out)
+    token[...] = jnp.zeros_like(token)
+
+
+def second_kernel(bit, cut, keep, taken, radial_0, radial_1, small, keep_out, give_out, tiny_out):
+    hand_on(lambda at: keep[at, :] + taken[at, :], bit, cut, keep_out, give_out)
+    rows = keep_out.shape[0]
     for h in range(2):
         lanes = slice(h * HALF, (h + 1) * HALF)
-        packed[rows + 16 * h : rows + 16 * h + 8, :] = radial[:, lanes]
-        packed[rows + 16 * h + 8 : rows + 16 * h + 16, :] = small[:, lanes]
-
-
-def sum_kernel(spread, summed):
-    count = lax.axis_size("domain")
-    piece = spread.shape[0] // count
-    total = spread[0:piece, :]
-    for i in range(1, count):
-        total = total + spread[i * piece : (i + 1) * piece, :]
-    for i in range(count):
-        summed[i * piece : (i + 1) * piece, :] = total
+        tiny_out[16 * h : 16 * h + 8, :] = radial_0[:, lanes] + radial_1[:, lanes]
+        tiny_out[16 * h + 8 : 16 * h + 16, :] = small[:, lanes]
+    give_out[rows:, :] = tiny_out[...]
+
+
+def later_kernel(bit, cut, keep, taken, tiny, keep_out, give_out, tiny_out):
+    hand_on(lambda at: keep[at, :] + taken[at, :], bit, cut, keep_out, give_out)
+    tiny_out[...] = tiny[...] + taken[keep.shape[0] :, :]
+    give_out[keep_out.shape[0] :, :] = tiny_out[...]
+
+
+def last_kernel(keep, taken, tiny, total, tiny_out):
+    rows = keep.shape[0]
+    total[...] = keep[...] + taken[0:rows, :]
+    tiny_out[...] = tiny[...] + taken[rows:, :]
+
+
+def grow_kernel(bit, tail, mine, theirs, tiny, grown):
+    rows = theirs.shape[0]
+    at = lax.bitwise_and(lax.shift_right_logical(lax.axis_index("domain"), bit), 1)
+    for ref, part in ((mine, at), (theirs, 1 - at)):
+        grown[pl.ds(pl.multiple_of(part * rows, 8), rows), :] = ref[...]
+    if tail:
+        grown[2 * rows :, :] = tiny[...]
+
+
+def grow_last_kernel(mine, theirs, grown):
+    rows = theirs.shape[0] - SMALL
+    at = lax.bitwise_and(lax.axis_index("domain"), 1)
+    for ref, part in ((mine, at), (theirs, 1 - at)):
+        grown[pl.ds(pl.multiple_of(part * rows, 8), rows), :] = ref[0:rows, :]
+    grown[2 * rows :, :] = mine[rows:, :] + theirs[rows:, :]
 
 
 def join_kernel(whole, facing, mix, radial, kinds, out):
@@ -628,29 +661,68 @@
         rows, fsel, env, dinv, gate, curve, inv, radial_w, mix_w, out_row,
         flops=1 << 31,
     )
-    (grad_radial,) = call(
-        radial_kernel,
-        "radial",
-        [(BASIS, channels)],
-        turning
-        + [((BASIS * TA, COMPS * CHUNK), BF16)] * 2
-        + [((COMPS * CHUNK, channels), BF16)] * 2
-        + [((slots, 3 * channels), F32), ((BASIS * TA, channels), F32)],
-        3,
-        centre_tile, other_tile, pair_live,
-        both, fsel, env, envdot, dinv, curl, mix_w,
-        flops=1 << 31,
+
+    def radial(p, after):
+        return call(
+            functools.partial(radial_kernel, p),
+            "radial",
+            [(BASIS, channels)],
+            turning
+            + [((BASIS * TA, COMPS * CHUNK), BF16)] * 2
+            + [((COMPS * CHUNK, channels), BF16)] * 2
+            + [((BASIS * TA, channels), F32)],
+            3,
+            centre_tile, other_tile, pair_live,
+            both, fsel, env, envdot, dinv, curl, mix_w, after,
+            flops=1 << 31,
+        )[0]
+
+    count = lax.axis_size("domain")
+    bits = count.bit_length() - 1
+    rows_mix = 3 * channels
+
+    def partner(block, bit):
+        return lax.ppermute(block, "domain", [(i, i ^ (1 << bit)) for i in range(count)])
+
+    taken = shifted(give, "batch", 1)
+    radial_0 = radial(0, both)
+    rows_now, cut = halves(rows_mix)
+    cuts = [cut]
+    keep, give, token = call(
+        functools.partial(first_kernel, cut), "first",
+        [(rows_now, HALF), (rows_now, HALF), (8, CHUNK)], [], 0, keep, taken,
     )
-    count = lax.axis_size("domain")
-    rows_mix = 3 * channels
-    piece = -(-(rows_mix + SMALL) // (8 * count)) * 8
-    taken = shifted(give, "batch", 1)
-    (packed,) = call(pack_kernel, "pack", [(count * piece, HALF)], [], 0, keep, taken, grad_radial, small)
-    spread = lax.all_to_all(packed, "domain", 0, 0, tiled=True)
-    (summed,) = call(sum_kernel, "sum", [(count * piece, HALF)], [], 0, spread)
-    whole = lax.all_to_all(summed, "domain", 0, 0, tiled=True)
+    taken = partner(give, 0)
+    radial_1 = radial(1, token)
+    tiny = None
+    for bit in range(1, bits):
+        rows_now, cut = halves(rows_now)
+        cuts.append(cut)
+        outs = [(rows_now, HALF), (rows_now + SMALL, HALF), (SMALL, HALF)]
+        if bit == 1:
+            keep, give, tiny = call(
+                functools.partial(second_kernel, bit, cut), "second", outs, [], 0,
+                keep, taken, radial_0, radial_1, small,
+            )
+        else:
+            keep, give, tiny = call(
+                functools.partial(later_kernel, bit, cut), "later", outs, [], 0, keep, taken, tiny
+            )
+        taken = partner(give, bit)
+    mine, tiny = call(last_kernel, "last", [(rows_now, HALF), (SMALL, HALF)], [], 0, keep, taken, tiny)
+    for bit in range(bits - 1, 0, -1):
+        if cuts[bit]:
+            theirs = partner(mine, bit)
+            rows_now = 2 * rows_now
+            tail = bit == 1
+            (mine,) = call(
+                functools.partial(grow_kernel, bit, tail), "grow",
+                [(rows_now + SMALL * tail, HALF)], [], 0, mine, theirs, tiny,
+            )
+    theirs = partner(mine, 0)
+    (whole,) = call(grow_last_kernel, "grow_last", [(rows_mix + SMALL, HALF)], [], 0, mine, theirs)
     facing = shifted(whole, "batch", 1)
-    mix, radial, kinds, out = call(
+    mix, radial_sum, kinds, out = call(
         join_kernel,
         "join",
         [(rows_mix, channels), (BASIS, channels), (SPECIES, channels), (1, channels)],
@@ -659,7 +731,7 @@
         whole,
         facing,
     )
-    return forces, radial, mix, kinds, out.reshape(channels)
+    return forces, radial_sum, mix, kinds, out.reshape(channels)
 
 
 def solution(mesh):

time: 84.7 us -> 82.1 us (0.969)
  blocking collectives: 35.3 us -> 0 us
  waiting for transfers between devices: 7.9 us -> 32.5 us
  starting transfers between devices: 13 us -> 20.5 us
    all_to_all x2 -> x0, blocking collectives: 35.3 us -> none  [the longest x1 19.3 us: on_device(): spread = lax.all_to_all(packed, 'domain', 0, 0, tiled=True)]
    ppermute x0 -> x6, waiting for transfers between devices: none -> 24.6 us  [partner(): lax.ppermute(block, 'domain', [(i, i ^ 1 << bit) for i in range(count)])]
    ppermute x0 -> x6, starting transfers between devices: none -> 7.41 us  [partner(): lax.ppermute(block, 'domain', [(i, i ^ 1 << bit) for i in range(count)])]
    pallas_call x7 -> x13, Pallas kernels: 17.3 us -> 18 us  [call(): pl.pallas_call(kernel, name=name, out_shape=[jax.ShapeDtypeStruct(shape,...]
  transfers between devices with their start and end apart: 8 -> 14, of which waited for: 5 -> 11; matrix products, arithmetic and copies ran while one was open for 1% -> 1% of each run, Pallas kernels for 6% -> 7%
where the time goes in v2:
time: 82.1 us; the launch traced here: 81.7 us
  waiting for transfers between devices  32.5 us (40%)
  starting transfers between devices  20.5 us (25%)
  Pallas kernels  18 us (22%)
  local copies, waits for them, and re-layouts  10.1 us (12%)
    ppermute x6, waiting for transfers between devices, partner(): lax.ppermute(block, 'domain', [(i, i ^ 1 << bit) for i in range(count)])  24.6 us
    pallas_call x13, Pallas kernels, call(): pl.pallas_call(kernel, name=name, out_shape=[jax.ShapeDtypeStruct(shape,...  18 us
    ppermute x8, starting transfers between devices, shifted(): lax.ppermute(block, axis, [(i, (i + by) % count) for i in range(count)])  13.1 us
    unnamed x29, local copies, waits for them, and re-layouts  10.1 us
    ppermute x8, waiting for transfers between devices, shifted(): lax.ppermute(block, axis, [(i, (i + by) % count) for i in range(count)])  7.87 us
    ppermute x6, starting transfers between devices, partner(): lax.ppermute(block, 'domain', [(i, i ^ 1 << bit) for i in range(count)])  7.41 us
  transfers between devices with their start and end apart: 14, of which 11 were waited for; matrix products, arithmetic and copies ran while one was open for 1% of the time, Pallas kernels for 7%

profile of v2, /device:TPU:0, one launch (start us, length us, event | category | flops | bytes accessed | tf_op | source)
XLA Modules:
  0.0 81.7 jit_solution(1363214694799792220)
XLA Ops:
  0.6 0.7 copy.17.pos
  1.3 0.7 copy.20.ref
  2.0 0.9 %copy-done = f32[1,256,256]{2,1,0:T(8,128)S(1)} copy-done((f32[1,256,256]{2,1,0:T(8,128)S(1)}, f32[1,256,256]{2,1,0:T(8,128)}, u32[]{:S(2)}) %copy-start) | copy-done | bytes 262168
  4.2 3.0 %collective-permute-start = (f32[144,256]{1,0:T(8,128)S(1)}, f32[144,256]{1,0:T(8,128)S(1)}, u32[]{:S(2)}, u32[]{:S(2)}) collective-permute-start(f32[144,256]{1,0:T(8,128)S(1)} %get-tuple-element.39), channel_id=1, source_target_pairs={{0,2},{2,4},{4,6},{6,8},{8,10},{10,12},{12,14},{14,0},{1,3},{3,5},... | collective-permute-start | bytes 442376 | tf_op jit(solution)/shard_map/ppermute | solution.py:578
  7.3 3.1 %collective-permute-start.1 = (f32[144,256]{1,0:T(8,128)S(1)}, f32[144,256]{1,0:T(8,128)S(1)}, u32[]{:S(2)}, u32[]{:S(2)}) collective-permute-start(f32[144,256]{1,0:T(8,128)S(1)} %get-tuple-element.40), channel_id=1, source_target_pairs={{0,14},{2,0},{4,2},{6,4},{8,6},{10,8},{12,10},{14,12},{1,15},{3,1}... | collective-permute-start | bytes 442376 | tf_op jit(solution)/shard_map/ppermute | solution.py:578
  10.4 3.9 %collective-permute-done.from_low = f32[144,256]{1,0:T(8,128)S(1)} collective-permute-done((f32[144,256]{1,0:T(8,128)S(1)}, f32[144,256]{1,0:T(8,128)S(1)}, u32[]{:S(2)}, u32[]{:S(2)}) %collective-permute-start) | collective-permute-done | bytes 147488 | tf_op jit(solution)/shard_map/ppermute | solution.py:578
  14.2 1.5 %collective-permute-done.1.from_high = f32[144,256]{1,0:T(8,128)S(1)} collective-permute-done((f32[144,256]{1,0:T(8,128)S(1)}, f32[144,256]{1,0:T(8,128)S(1)}, u32[]{:S(2)}, u32[]{:S(2)}) %collective-permute-start.1) | collective-permute-done | bytes 147488 | tf_op jit(solution)/shard_map/ppermute | solution.py:578
  16.4 1.1 %copy-done.3 = f32[768,256]{1,0:T(8,128)S(1)} copy-done((f32[768,256]{1,0:T(8,128)S(1)}, f32[768,256]{1,0:T(8,128)}, u32[]{:S(2)}) %copy-start.3) | copy-done | bytes 786456
  17.5 0.7 copy-done.5
  18.2 0.7 copy-done.6
  18.9 0.7 copy-done.7
  19.6 0.7 copy-done.8
  22.2 5.4 %force.1 = (f32[1152,256]{1,0:T(8,128)S(1)}, f32[128,768]{1,0:T(8,128)S(1)}, f32[128,256]{1,0:T(8,128)S(1)}, f32[128,256]{1,0:T(8,128)S(1)}, f32[128,768]{1,0:T(...) custom-call(s32[1,2]{1,0:T(1,128)S(1)} %copy-done.10, ...), custom_call_target="tpu_custom_call" | custom-call | flops 2147483648 | bytes 1048576 | tf_op jit(solution)/shard_map/force/pallas_call | solution.py:564
  27.7 1.3 %collective-permute-start.3 = (f32[8,128]{1,0:T(8,128)S(1)}, f32[8,128]{1,0:T(8,128)S(1)}, u32[]{:S(2)}, u32[]{:S(2)}) collective-permute-start(f32[8,128]{1,0:T(8,128)S(1)} %get-tuple-element.42), channel_id=1, source_target_pairs={{0,4},{2,6},{4,8},{6,10},{8,12},{10,14},{12,0},{14,2},{1,5},{3,7},... | collective-permute-start | bytes 12296 | tf_op jit(solution)/shard_map/ppermute | solution.py:578
  29.6 2.2 %collective-permute-start.5 = (f32[8,128]{1,0:T(8,128)S(1)}, f32[8,128]{1,0:T(8,128)S(1)}, u32[]{:S(2)}, u32[]{:S(2)}) collective-permute-start(f32[8,128]{1,0:T(8,128)S(1)} %get-tuple-element.43), channel_id=1, source_target_pairs={{0,12},{2,14},{4,0},{6,2},{8,4},{10,6},{12,8},{14,10},{1,13},{3,15... | collective-permute-start | bytes 12296 | tf_op jit(solution)/shard_map/ppermute | solution.py:578
  31.8 2.6 %collective-permute-start.4 = (f32[8,128]{1,0:T(8,128)S(1)}, f32[8,128]{1,0:T(8,128)S(1)}, u32[]{:S(2)}, u32[]{:S(2)}) collective-permute-start(f32[8,128]{1,0:T(8,128)S(1)} %get-tuple-element.43), channel_id=1, source_target_pairs={{0,14},{2,0},{4,2},{6,4},{8,6},{10,8},{12,10},{14,12},{1,15},{3,1}... | collective-permute-start | bytes 12296 | tf_op jit(solution)/shard_map/ppermute | solution.py:578
  34.5 0.8 collective-permute-done.2.low_one
  35.8 4.6 %tangent.1 = (f32[1,3,256]{2,1,0:T(4,128)S(1)}, f32[768,128]{1,0:T(8,128)S(1)}, f32[768,128]{1,0:T(8,128)S(1)}, f32[8,256]{1,0:T(8,128)S(1)}, f32[1152,256]{1,0:...) custom-call(f32[1]{0:T(128)} %constant.0.clone.1.scale, s32[1,2]{1,0:T(1,128)S(1)} %copy-done.10, ...), custom_call_target="tpu_custom_call" | custom-call | flops 2147483648 | bytes 1048576 | tf_op jit(solution)/shard_map/tangent/pallas_call | solution.py:564
  40.6 3.0 %radial.2.radial_0 = f32[8,256]{1,0:T(8,128)S(1)} custom-call(s32[1,2]{1,0:T(1,128)S(1)} %copy-done.10, s32[1,2]{1,0:T(1,128)S(1)} %copy-done.11, s32[1,2]{1,0:T(1,128)S(1)} %copy-done.12, f32[16,128]{1,0:T(8,128)S(1)} %get-tuple-element.56.both.after, f32[128,256]{1,0:T(8,128)S(1)} %get-tuple-element.45.fsel, f32[1152,256]{1,0:T(8,128)S(1)} %get-tuple-element.46.env, ...), custom_call_target="tpu_custom_call" | custom-call | flops 2147483648 | bytes 1048576 | tf_op jit(solution)/shard_map/radial/pallas_call | solution.py:564
  43.7 3.0 %collective-permute-start.7 = (f32[384,128]{1,0:T(8,128)S(1)}, f32[384,128]{1,0:T(8,128)S(1)}, u32[]{:S(2)}, u32[]{:S(2)}) collective-permute-start(f32[384,128]{1,0:T(8,128)S(1)} %get-tuple-element.55), channel_id=1, source_target_pairs={{0,2},{2,0},{4,6},{6,4},{8,10},{10,8},{12,14},{14,12},{1,3},{3,1},... | collective-permute-start | bytes 589832 | tf_op jit(solution)/shard_map/ppermute | solution.py:685
  46.7 3.0 %radial.3.radial_1 = f32[8,256]{1,0:T(8,128)S(1)} custom-call(s32[1,2]{1,0:T(1,128)S(1)} %copy-done.10, s32[1,2]{1,0:T(1,128)S(1)} %copy-done.11, s32[1,2]{1,0:T(1,128)S(1)} %copy-done.12, f32[16,128]{1,0:T(8,128)S(1)} %get-tuple-element.56.both.after, f32[128,256]{1,0:T(8,128)S(1)} %get-tuple-element.45.fsel, f32[1152,256]{1,0:T(8,128)S(1)} %get-tuple-element.46.env, ...), custom_call_target="tpu_custom_call" | custom-call | flops 2147483648 | bytes 1048576 | tf_op jit(solution)/shard_map/radial/pallas_call | solution.py:564
  49.7 2.5 %collective-permute-done.7.taken = f32[384,128]{1,0:T(8,128)S(1)} collective-permute-done((f32[384,128]{1,0:T(8,128)S(1)}, f32[384,128]{1,0:T(8,128)S(1)}, u32[]{:S(2)}, u32[]{:S(2)}) %collective-permute-start.7) | collective-permute-done | bytes 196640 | tf_op jit(solution)/shard_map/ppermute | solution.py:685
  52.4 4.9 %collective-permute-done.8.taken = f32[224,128]{1,0:T(8,128)S(1)} collective-permute-done((f32[224,128]{1,0:T(8,128)S(1)}, f32[224,128]{1,0:T(8,128)S(1)}, u32[]{:S(2)}, u32[]{:S(2)}) %collective-permute-start.8) | collective-permute-done | bytes 114720 | tf_op jit(solution)/shard_map/ppermute | solution.py:685
  57.3 1.5 %collective-permute-start.9 = (f32[128,128]{1,0:T(8,128)S(1)}, f32[128,128]{1,0:T(8,128)S(1)}, u32[]{:S(2)}, u32[]{:S(2)}) collective-permute-start(f32[128,128]{1,0:T(8,128)S(1)} %get-tuple-element.65), channel_id=1, source_target_pairs={{0,8},{2,10},{4,12},{6,14},{8,0},{10,2},{12,4},{14,6},{1,9},{3,11}... | collective-permute-start | bytes 196616 | tf_op jit(solution)/shard_map/ppermute | solution.py:685
  58.8 4.2 %collective-permute-done.9.taken = f32[128,128]{1,0:T(8,128)S(1)} collective-permute-done((f32[128,128]{1,0:T(8,128)S(1)}, f32[128,128]{1,0:T(8,128)S(1)}, u32[]{:S(2)}, u32[]{:S(2)}) %collective-permute-start.9) | collective-permute-done | bytes 65568 | tf_op jit(solution)/shard_map/ppermute | solution.py:685
  63.0 1.1 %collective-permute-start.10 = (f32[96,128]{1,0:T(8,128)S(1)}, f32[96,128]{1,0:T(8,128)S(1)}, u32[]{:S(2)}, u32[]{:S(2)}) collective-permute-start(f32[96,128]{1,0:T(8,128)S(1)} %get-tuple-element.67.mine), channel_id=1, source_target_pairs={{0,8},{2,10},{4,12},{6,14},{8,0},{10,2},{12,4},{14,6},{1,9},{3,11}... | collective-permute-start | bytes 147464 | tf_op jit(solution)/shard_map/ppermute | solution.py:685
  64.1 4.2 %collective-permute-done.10.theirs = f32[96,128]{1,0:T(8,128)S(1)} collective-permute-done((f32[96,128]{1,0:T(8,128)S(1)}, f32[96,128]{1,0:T(8,128)S(1)}, u32[]{:S(2)}, u32[]{:S(2)}) %collective-permute-start.10) | collective-permute-done | bytes 49184 | tf_op jit(solution)/shard_map/ppermute | solution.py:685
  68.4 4.6 %collective-permute-done.11.theirs = f32[192,128]{1,0:T(8,128)S(1)} collective-permute-done((f32[192,128]{1,0:T(8,128)S(1)}, f32[192,128]{1,0:T(8,128)S(1)}, u32[]{:S(2)}, u32[]{:S(2)}) %collective-permute-start.11) | collective-permute-done | bytes 98336 | tf_op jit(solution)/shard_map/ppermute | solution.py:685
  73.0 1.7 %collective-permute-start.12 = (f32[416,128]{1,0:T(8,128)S(1)}, f32[416,128]{1,0:T(8,128)S(1)}, u32[]{:S(2)}, u32[]{:S(2)}) collective-permute-start(f32[416,128]{1,0:T(8,128)S(1)} %grow.3.mine), channel_id=1, source_target_pairs={{0,2},{2,0},{4,6},{6,4},{8,10},{10,8},{12,14},{14,12},{1,3},{3,1},... | collective-permute-start | bytes 638984 | tf_op jit(solution)/shard_map/ppermute | solution.py:685
  74.6 4.3 %collective-permute-done.12.theirs = f32[416,128]{1,0:T(8,128)S(1)} collective-permute-done((f32[416,128]{1,0:T(8,128)S(1)}, f32[416,128]{1,0:T(8,128)S(1)}, u32[]{:S(2)}, u32[]{:S(2)}) %collective-permute-start.12) | collective-permute-done | bytes 213024 | tf_op jit(solution)/shard_map/ppermute | solution.py:685
  79.6 1.2 %collective-permute-done.13.facing = f32[800,128]{1,0:T(8,128)S(1)} collective-permute-done((f32[800,128]{1,0:T(8,128)S(1)}, f32[800,128]{1,0:T(8,128)S(1)}, u32[]{:S(2)}, u32[]{:S(2)}) %collective-permute-start.13) | collective-permute-done | bytes 409632 | tf_op jit(solution)/shard_map/ppermute | solution.py:578
  80.7 1.0 %join.1 = (f32[768,256]{1,0:T(8,128)}, f32[8,256]{1,0:T(8,128)}, f32[4,256]{1,0:T(4,128)}, f32[1,256]{1,0:T(1,128)}) custom-call(f32[800,128]{1,0:T(8,128)S(1)} %grow_last.1.whole, f32[800,128]{1,0:T(8,128)S(1)} %collective-permute-done.13.facing), custom_call_target="tpu_custom_call" | custom-call | bytes 1048576 | tf_op jit(solution)/shard_map/join/pallas_call | solution.py:564
  (38 shorter events, 6.2 us)
Async XLA Ops:
  2.0 0.9 %copy-start = (f32[1,256,256]{2,1,0:T(8,128)S(1)}, f32[1,256,256]{2,1,0:T(8,128)}, u32[]{:S(2)}) copy-start(f32[1,256,256]{2,1,0:T(8,128)} %feat.3) | copy-start | bytes 786436
  3.0 0.7 copy-start.1
  4.2 10.0 %collective-permute-start = (f32[144,256]{1,0:T(8,128)S(1)}, f32[144,256]{1,0:T(8,128)S(1)}, u32[]{:S(2)}, u32[]{:S(2)}) collective-permute-start(f32[144,256]{1,0:T(8,128)S(1)} %get-tuple-element.39), channel_id=1, source_target_pairs={{0,2},{2,4},{4,6},{6,8},{8,10},{10,12},{12,14},{14,0},{1,3},{3,5},... | collective-permute-start | bytes 442376 | tf_op jit(solution)/shard_map/ppermute | solution.py:578
  7.3 8.5 %collective-permute-start.1 = (f32[144,256]{1,0:T(8,128)S(1)}, f32[144,256]{1,0:T(8,128)S(1)}, u32[]{:S(2)}, u32[]{:S(2)}) collective-permute-start(f32[144,256]{1,0:T(8,128)S(1)} %get-tuple-element.40), channel_id=1, source_target_pairs={{0,14},{2,0},{4,2},{6,4},{8,6},{10,8},{12,10},{14,12},{1,15},{3,1}... | collective-permute-start | bytes 442376 | tf_op jit(solution)/shard_map/ppermute | solution.py:578
  15.7 0.7 copy-start.2
  16.4 1.1 %copy-start.3 = (f32[768,256]{1,0:T(8,128)S(1)}, f32[768,256]{1,0:T(8,128)}, u32[]{:S(2)}) copy-start(f32[768,256]{1,0:T(8,128)} %mix_w.7) | copy-start | bytes 2359300
  17.5 0.7 copy-start.5
  18.2 0.7 copy-start.6
  18.9 0.7 copy-start.7
  19.6 0.7 copy-start.8
  20.3 0.7 copy-start.10
  20.9 0.7 copy-start.11
  21.6 0.7 copy-start.12
  22.2 13.6 %copy-start.4 = (f32[768,256]{1,0:T(8,128)S(1)}, f32[768,256]{1,0:T(8,128)}, u32[]{:S(2)}) copy-start(f32[768,256]{1,0:T(8,128)} %mix_w.7) | copy-start | bytes 2359300
  22.2 13.6 %copy-start.9 = (f32[256]{0:T(256)S(1)}, f32[256]{0:T(256)}, u32[]{:S(2)}) copy-start(f32[256]{0:T(256)} %param.23) | copy-start | bytes 3076
  27.7 6.8 %collective-permute-start.3 = (f32[8,128]{1,0:T(8,128)S(1)}, f32[8,128]{1,0:T(8,128)S(1)}, u32[]{:S(2)}, u32[]{:S(2)}) collective-permute-start(f32[8,128]{1,0:T(8,128)S(1)} %get-tuple-element.42), channel_id=1, source_target_pairs={{0,4},{2,6},{4,8},{6,10},{8,12},{10,14},{12,0},{14,2},{1,5},{3,7},... | collective-permute-start | bytes 12296 | tf_op jit(solution)/shard_map/ppermute | solution.py:578
  29.0 6.3 %collective-permute-start.2 = (f32[8,128]{1,0:T(8,128)S(1)}, f32[8,128]{1,0:T(8,128)S(1)}, u32[]{:S(2)}, u32[]{:S(2)}) collective-permute-start(f32[8,128]{1,0:T(8,128)S(1)} %get-tuple-element.42), channel_id=1, source_target_pairs={{0,2},{2,4},{4,6},{6,8},{8,10},{10,12},{12,14},{14,0},{1,3},{3,5},... | collective-permute-start | bytes 12296 | tf_op jit(solution)/shard_map/ppermute | solution.py:578
  29.6 5.7 %collective-permute-start.5 = (f32[8,128]{1,0:T(8,128)S(1)}, f32[8,128]{1,0:T(8,128)S(1)}, u32[]{:S(2)}, u32[]{:S(2)}) collective-permute-start(f32[8,128]{1,0:T(8,128)S(1)} %get-tuple-element.43), channel_id=1, source_target_pairs={{0,12},{2,14},{4,0},{6,2},{8,4},{10,6},{12,8},{14,10},{1,13},{3,15... | collective-permute-start | bytes 12296 | tf_op jit(solution)/shard_map/ppermute | solution.py:578
  31.8 4.0 %collective-permute-start.4 = (f32[8,128]{1,0:T(8,128)S(1)}, f32[8,128]{1,0:T(8,128)S(1)}, u32[]{:S(2)}, u32[]{:S(2)}) collective-permute-start(f32[8,128]{1,0:T(8,128)S(1)} %get-tuple-element.43), channel_id=1, source_target_pairs={{0,14},{2,0},{4,2},{6,4},{8,6},{10,8},{12,10},{14,12},{1,15},{3,1}... | collective-permute-start | bytes 12296 | tf_op jit(solution)/shard_map/ppermute | solution.py:578
  40.5 3.1 %collective-permute-start.6 = (f32[768,128]{1,0:T(8,128)S(1)}, f32[768,128]{1,0:T(8,128)S(1)}, u32[]{:S(2)}, u32[]{:S(2)}) collective-permute-start(f32[768,128]{1,0:T(8,128)S(1)} %get-tuple-element.53), channel_id=1, source_target_pairs={{0,1},{1,0},{2,3},{3,2},{4,5},{5,4},{6,7},{7,6},{8,9},{9,8},{10,11... | collective-permute-start | bytes 1179656 | tf_op jit(solution)/shard_map/ppermute | solution.py:578
  43.7 8.5 %collective-permute-start.7 = (f32[384,128]{1,0:T(8,128)S(1)}, f32[384,128]{1,0:T(8,128)S(1)}, u32[]{:S(2)}, u32[]{:S(2)}) collective-permute-start(f32[384,128]{1,0:T(8,128)S(1)} %get-tuple-element.55), channel_id=1, source_target_pairs={{0,2},{2,0},{4,6},{6,4},{8,10},{10,8},{12,14},{14,12},{1,3},{3,1},... | collective-permute-start | bytes 589832 | tf_op jit(solution)/shard_map/ppermute | solution.py:685
  52.3 5.0 %collective-permute-start.8 = (f32[224,128]{1,0:T(8,128)S(1)}, f32[224,128]{1,0:T(8,128)S(1)}, u32[]{:S(2)}, u32[]{:S(2)}) collective-permute-start(f32[224,128]{1,0:T(8,128)S(1)} %get-tuple-element.62), channel_id=1, source_target_pairs={{0,4},{2,6},{4,0},{6,2},{8,12},{10,14},{12,8},{14,10},{1,5},{3,7},... | collective-permute-start | bytes 344072 | tf_op jit(solution)/shard_map/ppermute | solution.py:685
  57.3 5.7 %collective-permute-start.9 = (f32[128,128]{1,0:T(8,128)S(1)}, f32[128,128]{1,0:T(8,128)S(1)}, u32[]{:S(2)}, u32[]{:S(2)}) collective-permute-start(f32[128,128]{1,0:T(8,128)S(1)} %get-tuple-element.65), channel_id=1, source_target_pairs={{0,8},{2,10},{4,12},{6,14},{8,0},{10,2},{12,4},{14,6},{1,9},{3,11}... | collective-permute-start | bytes 196616 | tf_op jit(solution)/shard_map/ppermute | solution.py:685
  63.0 5.2 %collective-permute-start.10 = (f32[96,128]{1,0:T(8,128)S(1)}, f32[96,128]{1,0:T(8,128)S(1)}, u32[]{:S(2)}, u32[]{:S(2)}) collective-permute-start(f32[96,128]{1,0:T(8,128)S(1)} %get-tuple-element.67.mine), channel_id=1, source_target_pairs={{0,8},{2,10},{4,12},{6,14},{8,0},{10,2},{12,4},{14,6},{1,9},{3,11}... | collective-permute-start | bytes 147464 | tf_op jit(solution)/shard_map/ppermute | solution.py:685
  68.2 4.7 %collective-permute-start.11 = (f32[192,128]{1,0:T(8,128)S(1)}, f32[192,128]{1,0:T(8,128)S(1)}, u32[]{:S(2)}, u32[]{:S(2)}) collective-permute-start(f32[192,128]{1,0:T(8,128)S(1)} %grow.2.mine), channel_id=1, source_target_pairs={{0,4},{2,6},{4,0},{6,2},{8,12},{10,14},{12,8},{14,10},{1,5},{3,7},... | collective-permute-start | bytes 294920 | tf_op jit(solution)/shard_map/ppermute | solution.py:685
  73.0 5.9 %collective-permute-start.12 = (f32[416,128]{1,0:T(8,128)S(1)}, f32[416,128]{1,0:T(8,128)S(1)}, u32[]{:S(2)}, u32[]{:S(2)}) collective-permute-start(f32[416,128]{1,0:T(8,128)S(1)} %grow.3.mine), channel_id=1, source_target_pairs={{0,2},{2,0},{4,6},{6,4},{8,10},{10,8},{12,14},{14,12},{1,3},{3,1},... | collective-permute-start | bytes 638984 | tf_op jit(solution)/shard_map/ppermute | solution.py:685
  78.9 1.8 %collective-permute-start.13 = (f32[800,128]{1,0:T(8,128)S(1)}, f32[800,128]{1,0:T(8,128)S(1)}, u32[]{:S(2)}, u32[]{:S(2)}) collective-permute-start(f32[800,128]{1,0:T(8,128)S(1)} %grow_last.1.whole), channel_id=1, source_target_pairs={{0,1},{1,0},{2,3},{3,2},{4,5},{5,4},{6,7},{7,6},{8,9},{9,8},{10,11... | collective-permute-start | bytes 1228808 | tf_op jit(solution)/shard_map/ppermute | solution.py:578

commit v3 on v2

v3 whole, which is shorter than its diff:
```python
import functools
import math

import jax
import jax.numpy as jnp
from jax import lax
from jax.experimental import pallas as pl
from jax.experimental.pallas import tpu as pltpu
from jax.sharding import PartitionSpec as P

TA = 64
SEND = 2
PAIRS = 2
COMPS = 9
BASIS = 8
SPECIES = 4
HALF = 128
CHUNK = 2 * TA

cutoff = 2.5
soften = 0.25
env_scale = 0.25
root_three = math.sqrt(3.0)
F32 = jnp.float32
BF16 = jnp.bfloat16
NN = (((1,), (0,)), ((), ()))
NT = (((1,), (1,)), ((), ()))
TN = (((0,), (0,)), ((), ()))
GROUP = (0, 1, 1, 1, 2, 2, 2, 2, 2)


def split(value):
    high = value.astype(BF16)
    return high, (value - high.astype(F32)).astype(BF16)


def product(left, right, dims):
    (lh, ll), (rh, rl) = left, right

    def one(x, y):
        return lax.dot_general(x, y, dims, preferred_element_type=F32)

    return one(lh, rh) + (one(lh, rl) + one(ll, rh))


def flag(condition):
    return jnp.where(condition, 1.0, 0.0).astype(F32)


def lane_half():
    lane = lax.broadcasted_iota(jnp.int32, (1, CHUNK), 1)
    low = flag(lane < TA)
    return low, 1.0 - low


def twice(chunk, half):
    low, high = lane_half()
    swapped = pltpu.roll(chunk, TA, 1)
    return chunk * low + swapped * high if half == 0 else swapped * low + chunk * high


def pick(chunks, position):
    total = None
    for q, chunk in enumerate(chunks):
        for half in range(2):
            term = twice(chunk, half) * flag(position == 2 * q + half)
            total = term if total is None else total + term
    return total


def paired(first, second):
    low, high = lane_half()
    return first * low + second * high


def chunk_mask(position, q):
    low, high = lane_half()
    return low * flag(position == 2 * q) + high * flag(position == 2 * q + 1)


def geometry(lane_rows, columns, sign, live, same):
    offset = [(row - column) * sign for row, column in zip(lane_rows, columns)]
    dist_sq = offset[0] * offset[0] + offset[1] * offset[1] + offset[2] * offset[2] + soften
    distance = jnp.sqrt(dist_sq)
    inverse = 1.0 / distance
    unit = [x * inverse for x in offset]
    row = lax.broadcasted_iota(jnp.int32, (TA, CHUNK), 0)
    lane = lax.broadcasted_iota(jnp.int32, (TA, CHUNK), 1)
    lane = jnp.where(lane >= TA, lane - TA, lane)
    mask = live * (1.0 - same * flag(row == lane))
    base = jnp.maximum(1.0 - dist_sq * (1.0 / (cutoff * cutoff)), 0.0)
    weight = base * base * base * mask * inverse
    slope = -(6.0 / (cutoff * cutoff)) * base * base * mask - weight * inverse
    angle = distance * (math.pi / cutoff)
    return unit, inverse, weight, slope, jnp.sin(angle), jnp.cos(angle)


def harmonics(v):
    x, y, z = v
    return [
        None,
        x,
        y,
        z,
        root_three * x * y,
        root_three * y * z,
        root_three * z * x,
        0.5 * root_three * (x * x - y * y),
        z * z - 0.5 * (x * x + y * y),
    ]


def harmonics_tangent(v, t):
    x, y, z = v
    a, b, c = t
    return [
        None,
        a,
        b,
        c,
        root_three * (a * y + x * b),
        root_three * (b * z + y * c),
        root_three * (c * x + z * a),
        root_three * (x * a - y * b),
        2.0 * z * c - (x * a + y * b),
    ]


def paired_orders(sine, cosine, weight, slope):
    low, high = lane_half()
    double_s, double_c = 2.0 * sine * cosine, 1.0 - 2.0 * sine * sine
    now_s = sine * low + double_s * high
    now_c = cosine * low + double_c * high
    old_s = -sine * low
    old_c = cosine * low + high
    values, slopes = [], []
    for k in range(BASIS // 2):
        order = ((2 * k + 1) * low + (2 * k + 2) * high) * (math.pi / cutoff)
        values.append(now_s * weight)
        slopes.append(now_c * (weight * order) + now_s * slope)
        now_s, old_s = 2.0 * double_c * now_s - old_s, now_s
        now_c, old_c = 2.0 * double_c * now_c - old_c, now_c
    return values, slopes


def single_orders(sine, cosine, weight, slope):
    now_s, now_c = sine, cosine
    old_s, old_c = jnp.zeros_like(sine), jnp.ones_like(cosine)
    values, slopes = [], []
    for n in range(1, BASIS + 1):
        values.append(now_s * weight)
        slopes.append(now_c * (weight * (n * math.pi / cutoff)) + now_s * slope)
        now_s, old_s = 2.0 * cosine * now_s - old_s, now_s
        now_c, old_c = 2.0 * cosine * now_c - old_c, now_c
    return values, slopes


def columns_of(rows, square, turned):
    square[...] = jnp.zeros_like(square)
    square[0 : rows.shape[0], :] = rows
    turned[...] = square[...].T


def pair_rows(first, p):
    return twice(first, p)


def radial_feat(feat, radial, p, high_ref, low_ref):
    own = feat[p * TA : (p + 1) * TA, :]
    for n in range(BASIS):
        hi, lo = split(own * radial[n : n + 1, :])
        high_ref[n * TA : (n + 1) * TA, :] = hi
        low_ref[n * TA : (n + 1) * TA, :] = lo


OTHER, CENTRE, LIVE, SAME, SHARED, SENT = 0, 2, 4, 6, 8, 9


def fetch(pairs, sems):
    copies = [pltpu.make_async_copy(src, dst, sems.at[i]) for i, (src, dst) in enumerate(pairs)]
    for copy in copies:
        copy.start()
    return copies


def gather_kernel(send, pos, feat, ref, to_low, to_high, token, send_v, pos_v, feat_v, ref_v, sems):
    copies = fetch([(send, send_v), (pos, pos_v), (ref, ref_v), (feat, feat_v)], sems)
    for copy in copies[:3]:
        copy.wait()
    low, high = lane_half()
    sent = [send_v[0:1, j : j + 1].astype(F32) for j in range(2 * SEND)]
    for out, first in ((to_low, 0), (to_high, SEND)):
        tiles = sent[first : first + SEND]
        out[SEND * TA :, :] = jnp.zeros((16, out.shape[1]), F32)
        for i in range(3):
            at = SEND * TA + i
            for lanes, source in ((slice(0, CHUNK), pos_v), (slice(CHUNK, 2 * CHUNK), ref_v)):
                chunks = [source[i, :, q * CHUNK : (q + 1) * CHUNK] for q in range(2)]
                out[at : at + 1, lanes] = paired(pick(chunks, tiles[0]), pick(chunks, tiles[1]))
        for other in range(2 * SEND):
            same = low * flag(sent[other] == tiles[0]) + high * flag(sent[other] == tiles[1])
            out[SEND * TA + 8 + other : SEND * TA + 9 + other, 0:CHUNK] = same
    token[...] = jnp.zeros_like(token)
    copies[3].wait()
    for out, first in ((to_low, 0), (to_high, SEND)):
        for j in range(SEND):
            out[j * TA : (j + 1) * TA, :] = pick_rows(feat_v.at[0], sent[first + j], 0)


def pick_rows(ref, position, first):
    total = None
    for t in range(ref.shape[0] // TA):
        term = ref[t * TA : (t + 1) * TA, :] * flag(position == float(first + t))
        total = term if total is None else total + term
    return total


def stage_kernel(
    centre, other, live, send, pos, ref, species, feat, radial_w, mix_w, species_w, out_w, after,
    flags, atoms, own_feat, weights, mh, ml,
    centre_v, other_v, live_v, send_v, pos_v, ref_v, species_v, radial_v, mix_v, species_w_v, out_v, sems,
):
    copies = fetch(
        [
            (centre, centre_v), (other, other_v), (live, live_v), (send, send_v), (pos, pos_v), (ref, ref_v),
            (species, species_v), (radial_w, radial_v), (species_w, species_w_v), (out_w, out_v),
            (feat.at[0], own_feat), (mix_w, mix_v),
        ],
        sems,
    )
    for copy in copies[:-1]:
        copy.wait()
    flags[...] = jnp.zeros_like(flags)
    centres = [centre_v[0:1, p : p + 1].astype(F32) for p in range(PAIRS)]
    others = [other_v[0:1, p : p + 1].astype(F32) for p in range(PAIRS)]
    for p in range(PAIRS):
        for row, value in (
            (OTHER, others[p]),
            (CENTRE, centres[p]),
            (LIVE, live_v[0:1, p : p + 1].astype(F32)),
            (SAME, flag(others[p] == centres[p] + SEND)),
        ):
            flags[row + p : row + p + 1, :] = jnp.broadcast_to(value, (1, CHUNK))
    flags[SHARED : SHARED + 1, :] = jnp.broadcast_to(flag(centres[0] == centres[1]), (1, CHUNK))
    for j in range(2 * SEND):
        value = send_v[0:1, j : j + 1].astype(F32)
        flags[SENT + j : SENT + j + 1, :] = jnp.broadcast_to(value, (1, CHUNK))
    atoms[...] = jnp.zeros_like(atoms)
    for i in range(3):
        atoms[i : i + 1, :] = pos_v[i]
        atoms[4 + i : 5 + i, :] = ref_v[i]
    atoms[3:4, :] = species_v[...].astype(F32)
    weights[...] = jnp.zeros_like(weights)
    weights[0:BASIS, :] = radial_v[...]
    weights[BASIS : BASIS + SPECIES, :] = species_w_v[...]
    weights[BASIS + SPECIES : BASIS + SPECIES + 1, :] = out_v[...]
    copies[-1].wait()
    hi, lo = split(mix_v[...])
    mh[...] = hi
    ml[...] = lo


def force_kernel(
    flags, atoms, feat, weights, mh, ml, from_low, from_high,
    env, dinv, gate, curve, inv, rows, fsel, own, to_high, to_low, shape_store, xh, xl,
    square, turned, th, tl, eh, el, raw, back,
):
    ghost = SEND * TA
    chunks = [
        from_low[ghost : ghost + 3, 0:CHUNK],
        atoms[0:3, 0:CHUNK],
        atoms[0:3, CHUNK:],
        from_high[ghost : ghost + 3, 0:CHUNK],
    ]
    kinds = [atoms[3:4, q * CHUNK : (q + 1) * CHUNK] for q in range(2)]

    def number(row):
        return flags[row : row + 1, :]

    centres = [number(CENTRE + p) for p in range(PAIRS)]
    others = [number(OTHER + p) for p in range(PAIRS)]
    shared = flags[SHARED : SHARED + 1, 0:1]
    rows[...] = jnp.zeros_like(rows)
    rows[0:3, :] = paired(*(pick(chunks, others[p]) for p in range(PAIRS)))
    rows[3:6, :] = paired(*(pick(chunks[1:3], centres[p]) for p in range(PAIRS)))
    rows[6:7, :] = paired(*(pick(kinds, centres[p]) for p in range(PAIRS)))
    columns_of(rows[...], square, turned)

    for p in range(PAIRS):
        o = flags[OTHER + p : OTHER + p + 1, 0:1]
        fsel[p * TA : (p + 1) * TA, :] = (
            pick_rows(from_low.at[0:ghost], o, 0)
            + pick_rows(feat, o, SEND)
            + pick_rows(from_high.at[0:ghost], o, SEND + 4)
        )

    shapes = []
    for p in range(PAIRS):
        lane_rows = [twice(rows[i : i + 1, :], p) for i in range(3)]
        columns = [turned[p * TA : (p + 1) * TA, 3 + i : 4 + i] for i in range(3)]
        unit, inverse, weight, slope, sine, cosine = geometry(
            lane_rows, columns, 1.0, number(LIVE + p), number(SAME + p)
        )
        angular = harmonics(unit)
        values, slopes = paired_orders(sine, cosine, weight, slope)
        shapes.append((unit, inverse, angular, values, slopes))
        for i, part in enumerate(unit + [inverse] + values + slopes):
            shape_store[p, i] = part
        for m in range(COMPS):
            for k in range(BASIS // 2):
                entry = values[k] if m == 0 else angular[m] * values[k]
                hi, lo = split(entry)
                th[p, m * TA : (m + 1) * TA, k * CHUNK : (k + 1) * CHUNK] = hi
                tl[p, m * TA : (m + 1) * TA, k * CHUNK : (k + 1) * CHUNK] = lo
        radial_feat(fsel, weights, p, xh.at[p], xl.at[p])
        raw[p * COMPS * TA : (p + 1) * COMPS * TA, :] = product((th[p], tl[p]), (xh[p], xl[p]), NN)

    for m in range(COMPS):
        first = raw[m * TA : (m + 1) * TA, :]
        second = raw[(COMPS + m) * TA : (COMPS + m + 1) * TA, :]
        env[m * TA : (m + 1) * TA, :] = env_scale * (first + shared * second)
        env[(COMPS + m) * TA : (COMPS + m + 1) * TA, :] = env_scale * (second + shared * first)
    for p in range(PAIRS):
        sums = [None] * 3
        for m in range(COMPS):
            block = env[(p * COMPS + m) * TA : (p * COMPS + m + 1) * TA, :]
            sums[GROUP[m]] = block * block if sums[GROUP[m]] is None else sums[GROUP[m]] + block * block
        for g in range(3):
            inv[p * TA : (p + 1) * TA, g * 256 : (g + 1) * 256] = sums[g]
    hidden = product(split(inv[...]), (mh[...], ml[...]), NN)
    kind = turned[:, 6:7]
    for s in range(SPECIES):
        hidden = hidden + flag(kind == float(s)) * weights[BASIS + s : BASIS + s + 1, :]
    out_row = weights[BASIS + SPECIES : BASIS + SPECIES + 1, :]
    sigma = 1.0 / (1.0 + jnp.exp(-hidden))
    first_order = sigma * (1.0 + hidden * (1.0 - sigma))
    gate[...] = first_order
    curve[...] = sigma * (1.0 - sigma) * (2.0 + hidden * (1.0 - 2.0 * sigma)) * out_row
    dinv[...] = product(split(first_order * out_row), (mh[...], ml[...]), NT)

    tile_grads = [jnp.zeros((3, CHUNK), F32) for _ in range(4)]
    for p in range(PAIRS):
        unit, inverse, angular, values, slopes = shapes[p]
        for m in range(COMPS):
            block = env[(p * COMPS + m) * TA : (p * COMPS + m + 1) * TA, :]
            part = dinv[p * TA : (p + 1) * TA, GROUP[m] * 256 : (GROUP[m] + 1) * 256]
            hi, lo = split((2.0 * env_scale) * block * part)
            eh[p, m * TA : (m + 1) * TA, :] = hi
            el[p, m * TA : (m + 1) * TA, :] = lo
        back[p] = product((eh[p], el[p]), (xh[p], xl[p]), NT)
        d_radius = None
        d_angular = []
        for m in range(COMPS):
            along, across = None, None
            for k in range(BASIS // 2):
                block = back[p, m * TA : (m + 1) * TA, k * CHUNK : (k + 1) * CHUNK]
                along = block * slopes[k] if along is None else along + block * slopes[k]
                across = block * values[k] if across is None else across + block * values[k]
            d_angular.append(across)
            term = along if m == 0 else along * angular[m]
            d_radius = term if d_radius is None else d_radius + term
        x, y, z = unit
        g = d_angular
        toward = [
            g[1] + root_three * (y * g[4] + z * g[6] + x * g[7]) - x * g[8],
            g[2] + root_three * (x * g[4] + z * g[5] - y * g[7]) - y * g[8],
            g[3] + root_three * (y * g[5] + x * g[6]) + 2.0 * (z * g[8]),
        ]
        radial_part = d_radius - inverse * (toward[0] * x + toward[1] * y + toward[2] * z)
        for i in range(3):
            d_offset = inverse * toward[i] + unit[i] * radial_part
            summed = jnp.sum(d_offset, axis=0, keepdims=True)
            other_row = summed + pltpu.roll(summed, TA, 1)
            square[0:TA, :] = d_offset
            square[TA:, :] = d_offset
            centre_row = -jnp.sum(square[...].T, axis=0, keepdims=True)
            component = flag(lax.broadcasted_iota(jnp.int32, (3, CHUNK), 0) == i)
            for q in range(4):
                at = chunk_mask(others[p], q) * other_row
                if q in (1, 2):
                    at = at + chunk_mask(centres[p] + SEND, q) * centre_row
                tile_grads[q] = tile_grads[q] + at * component
    own[...] = jnp.zeros_like(own)
    own[0:3, 0:CHUNK] = tile_grads[1]
    own[0:3, CHUNK:] = tile_grads[2]
    own[3:6, 0:CHUNK] = tile_grads[0]
    own[3:6, CHUNK:] = tile_grads[3]
    for out, first, ghost_grad in ((to_low, 0, tile_grads[0]), (to_high, SEND, tile_grads[3])):
        out[...] = jnp.zeros_like(out)
        out[0:3, :] = paired(*(pick(tile_grads[1:3], number(SENT + first + j)) for j in range(SEND)))
        out[3:6, :] = ghost_grad


def tangent_kernel(
    scale, flags, atoms, weights, mh, ml, from_low, from_high, own, low_one, low_two, high_one, high_two,
    rows, env, gate, curve, inv, shape_store, xh, xl,
    forces, keep, give, small, envdot, curl, both,
    square, turned, th, tl, raw, left, right,
):
    ghost = SEND * TA
    def number(row):
        return flags[row : row + 1, :]

    centres = [number(CENTRE + p) for p in range(PAIRS)]
    others = [number(OTHER + p) for p in range(PAIRS)]
    shared = flags[SHARED : SHARED + 1, 0:1]
    mine = [own[0:3, 0:CHUNK], own[0:3, CHUNK:]]
    arrived = [twice(low_one[3:6, :], j) for j in range(SEND)]
    arrived += [twice(high_one[3:6, :], j) for j in range(SEND)]
    for j in range(2 * SEND):
        for q in range(2):
            mine[q] = mine[q] + chunk_mask(number(SENT + j), q) * arrived[j]
    below = low_one[0:3, :]
    above = high_one[0:3, :]
    to_below = [twice(low_two[3:6, :], j) for j in range(SEND)]
    to_below += [twice(own[3:6, 0:CHUNK], j) for j in range(SEND)]
    to_above = [twice(own[3:6, CHUNK:], j) for j in range(SEND)]
    to_above += [twice(high_two[3:6, :], j) for j in range(SEND)]
    for j in range(2 * SEND):
        below = below + from_low[ghost + 8 + j : ghost + 9 + j, 0:CHUNK] * to_below[j]
        above = above + from_high[ghost + 8 + j : ghost + 9 + j, 0:CHUNK] * to_above[j]
    for q in range(2):
        for i in range(3):
            forces[i, :, q * CHUNK : (q + 1) * CHUNK] = -mine[q][i : i + 1, :]
    error = [
        below + from_low[ghost : ghost + 3, CHUNK:],
        mine[0] + atoms[4:7, 0:CHUNK],
        mine[1] + atoms[4:7, CHUNK:],
        above + from_high[ghost : ghost + 3, CHUNK:],
    ]
    error = [part * scale for part in error]
    both[...] = jnp.zeros_like(both)
    both[0:8, :] = rows[...]
    both[8:11, :] = paired(*(pick(error, others[p]) for p in range(PAIRS)))
    both[11:14, :] = paired(*(pick(error[1:3], centres[p]) for p in range(PAIRS)))
    columns_of(both[...], square, turned)

    for p in range(PAIRS):
        lane_move = [twice(both[8 + i : 9 + i, :], p) for i in range(3)]
        column_move = [turned[p * TA : (p + 1) * TA, 11 + i : 12 + i] for i in range(3)]
        unit = [shape_store[p, i] for i in range(3)]
        inverse = shape_store[p, 3]
        values = [shape_store[p, 4 + k] for k in range(BASIS // 2)]
        slopes = [shape_store[p, 8 + k] for k in range(BASIS // 2)]
        move = [a - b for a, b in zip(lane_move, column_move)]
        stretch = unit[0] * move[0] + unit[1] * move[1] + unit[2] * move[2]
        turn = [(m - v * stretch) * inverse for m, v in zip(move, unit)]
        angular, turning = harmonics(unit), harmonics_tangent(unit, turn)
        slopes = [s * stretch for s in slopes]
        for m in range(COMPS):
            for k in range(BASIS // 2):
                entry = slopes[k] if m == 0 else angular[m] * slopes[k] + turning[m] * values[k]
                hi, lo = split(entry)
                th[p, m * TA : (m + 1) * TA, k * CHUNK : (k + 1) * CHUNK] = hi
                tl[p, m * TA : (m + 1) * TA, k * CHUNK : (k + 1) * CHUNK] = lo
        raw[p * COMPS * TA : (p + 1) * COMPS * TA, :] = product((th[p], tl[p]), (xh[p], xl[p]), NN)

    for m in range(COMPS):
        first = raw[m * TA : (m + 1) * TA, :]
        second = raw[(COMPS + m) * TA : (COMPS + m + 1) * TA, :]
        envdot[m * TA : (m + 1) * TA, :] = env_scale * (first + shared * second)
        envdot[(COMPS + m) * TA : (COMPS + m + 1) * TA, :] = env_scale * (second + shared * first)
    invdot = left
    half = PAIRS * TA
    for p in range(PAIRS):
        sums = [None] * 3
        for m in range(COMPS):
            at = slice((p * COMPS + m) * TA, (p * COMPS + m + 1) * TA)
            term = 2.0 * env[at, :] * envdot[at, :]
            sums[GROUP[m]] = term if sums[GROUP[m]] is None else sums[GROUP[m]] + term
        for g in range(3):
            invdot[half + p * TA : half + (p + 1) * TA, g * 256 : (g + 1) * 256] = sums[g]
    invdot[0:half, :] = inv[...]
    hidden_move = product(split(invdot[half:, :]), (mh[...], ml[...]), NN)
    bend = curve[...] * hidden_move
    curl[...] = bend
    once = 1.0 - shared * flag(lax.broadcasted_iota(jnp.int32, (half, 1), 0) >= TA)
    right[0:half, :] = bend * once
    right[half:, :] = gate[...] * weights[BASIS + SPECIES : BASIS + SPECIES + 1, :] * once
    core = lax.axis_index("batch")
    left_parts = split(left[...])
    for out, part in ((keep, core), (give, 1 - core)):
        lanes = pl.ds(pl.multiple_of(part * HALF, HALF), HALF)
        out[...] = product(left_parts, split(right[:, lanes]), TN)
    small[...] = jnp.zeros_like(small)
    kind = turned[:, 6:7]
    for s in range(SPECIES):
        small[s : s + 1, :] = jnp.sum(right[0:half, :] * flag(kind == float(s)), axis=0, keepdims=True)
    small[SPECIES : SPECIES + 1, :] = jnp.sum(gate[...] * hidden_move * once, axis=0, keepdims=True)


def radial_kernel(
    p, flags, both, fsel, env, envdot, dinv, curl, mh, ml, after,
    grad_radial,
    square, turned, lh, ll, gh, gl, raw,
):
    low, high = lane_half()
    columns_of(both[...], square, turned)
    here = slice(p * TA, (p + 1) * TA)
    turn_inv = product(split(curl[here, :]), (mh[...], ml[...]), NT)
    lane_rows = [twice(both[3 + i : 4 + i, :], p) for i in range(3)]
    lane_move = [twice(both[11 + i : 12 + i, :], p) for i in range(3)]
    columns = [turned[here, i : i + 1] for i in range(3)]
    column_move = [turned[here, 8 + i : 9 + i] for i in range(3)]
    unit, inverse, weight, slope, sine, cosine = geometry(
        lane_rows, columns, -1.0, flags[LIVE + p : LIVE + p + 1, :], flags[SAME + p : SAME + p + 1, :]
    )
    move = [b - a for a, b in zip(lane_move, column_move)]
    stretch = unit[0] * move[0] + unit[1] * move[1] + unit[2] * move[2]
    turn = [(m - v * stretch) * inverse for m, v in zip(move, unit)]
    angular, turning = harmonics(unit), harmonics_tangent(unit, turn)
    values, slopes = single_orders(sine, cosine, weight, slope)
    for m in range(COMPS):
        if m == 0:
            on_value, on_slope = low, high * stretch
        else:
            on_value = angular[m] * low + turning[m] * high
            on_slope = angular[m] * high * stretch
        for n in range(BASIS):
            hi, lo = split(on_value * values[n] + on_slope * slopes[n])
            lh[n * TA : (n + 1) * TA, m * CHUNK : (m + 1) * CHUNK] = hi
            ll[n * TA : (n + 1) * TA, m * CHUNK : (m + 1) * CHUNK] = lo
        at = slice((p * COMPS + m) * TA, (p * COMPS + m + 1) * TA)
        group = slice(GROUP[m] * 256, (GROUP[m] + 1) * 256)
        steady = (2.0 * env_scale) * dinv[here, group]
        bent = (2.0 * env_scale) * turn_inv[:, group]
        hi, lo = split(env[at, :] * bent + envdot[at, :] * steady)
        gh[m * CHUNK : m * CHUNK + TA, :] = hi
        gl[m * CHUNK : m * CHUNK + TA, :] = lo
        hi, lo = split(env[at, :] * steady)
        gh[m * CHUNK + TA : (m + 1) * CHUNK, :] = hi
        gl[m * CHUNK + TA : (m + 1) * CHUNK, :] = lo
    raw[...] = product((lh[...], ll[...]), (gh[...], gl[...]), NN)
    for n in range(BASIS):
        grad_radial[n : n + 1, :] = jnp.sum(
            raw[n * TA : (n + 1) * TA, :] * fsel[here, :], axis=0, keepdims=True
        )


SMALL = 32
LEVEL = 3


def place(shift, width):
    return lax.bitwise_and(lax.shift_right_logical(lax.axis_index("domain"), shift), width - 1)


def block_of(part, rows):
    return pl.ds(pl.multiple_of(part * rows, 8), rows)


def total_of(refs, at):
    total = refs[0][at, :]
    for ref in refs[1:]:
        total = total + ref[at, :]
    return total


def spread_kernel(shift, width, count, *refs):
    terms, outs = refs[:count], refs[count:]
    me = place(shift, width)
    for k in range(width - 1, -1, -1):
        outs[k][...] = total_of(terms, block_of(lax.bitwise_xor(me, k), outs[k].shape[0]))


def tail_kernel(count, *refs):
    terms, (radial_0, radial_1, small, out) = refs[:count], refs[count:]
    rows = terms[0].shape[0]
    out[0:rows, :] = total_of(terms, slice(0, rows))
    for h in range(2):
        lanes = slice(h * HALF, (h + 1) * HALF)
        at = rows + 16 * h
        out[at : at + 8, :] = radial_0[:, lanes] + radial_1[:, lanes]
        out[at + 8 : at + 16, :] = small[:, lanes]


def grow_kernel(shift, width, *refs):
    parts, out, tails = refs[:width], refs[width], refs[width + 1]
    rows = parts[0].shape[0] - SMALL
    me = place(shift, width)
    for k, ref in enumerate(parts):
        to = lax.bitwise_xor(me, k)
        out[block_of(to, rows), :] = ref[0:rows, :]
        tails[block_of(to, SMALL), :] = ref[rows:, :]
    total = tails[0:SMALL, :]
    for j in range(1, width):
        total = total + tails[j * SMALL : (j + 1) * SMALL, :]
    out[width * rows :, :] = total


def whole_kernel(shift, width, *refs):
    parts, out, held = refs[:width], refs[width], refs[width + 1]
    rows = parts[0].shape[0]
    me = place(shift, width)
    for k, ref in enumerate(parts):
        held[block_of(lax.bitwise_xor(me, k), rows), :] = ref[...]
    out[...] = total_of([held.at[j * rows : (j + 1) * rows] for j in range(width)], slice(0, rows))


def join_kernel(whole, facing, mix, radial, kinds, out):
    rows = mix.shape[0]
    core = lax.axis_index("batch")
    for ref, part in ((whole, core), (facing, 1 - core)):
        mix[:, pl.ds(pl.multiple_of(part * HALF, HALF), HALF)] = ref[0:rows, :]
    for h in range(2):
        lanes = slice(h * HALF, (h + 1) * HALF)
        both = whole[rows + 16 * h : rows + 16 * h + 16, :] + facing[rows + 16 * h : rows + 16 * h + 16, :]
        radial[:, lanes] = both[0:BASIS]
        kinds[:, lanes] = both[BASIS : BASIS + SPECIES]
        out[:, lanes] = both[BASIS + SPECIES : BASIS + SPECIES + 1]


def spec(space):
    return pl.BlockSpec(memory_space=space)


def call(kernel, name, outs, scratch, *operands, space=pltpu.VMEM, after=(), flops=0):
    if space is pltpu.HBM:
        operands = [pltpu.with_memory_space_constraint(operand, space) for operand in operands]
    outs = [out if len(out) == 2 and isinstance(out[0], tuple) else (out, F32) for out in outs]
    return pl.pallas_call(
        kernel,
        name=name,
        out_shape=[jax.ShapeDtypeStruct(*out) for out in outs],
        in_specs=[spec(space)] * len(operands) + [spec(pltpu.VMEM)] * len(after),
        out_specs=[spec(pltpu.VMEM)] * len(outs),
        scratch_shapes=[pltpu.VMEM(*item) if isinstance(item, tuple) else item for item in scratch],
        compiler_params=pltpu.CompilerParams(vmem_limit_bytes=28 * 1024 * 1024),
        cost_estimate=pl.CostEstimate(flops=flops, bytes_accessed=1 << 20, transcendentals=0),
    )(*operands, *after)


def shifted(block, axis, by):
    count = lax.axis_size(axis)
    return lax.ppermute(block, axis, [(i, (i + by) % count) for i in range(count)])


def partner(block, mask):
    return lax.ppermute(block, "domain", [(i, i ^ mask) for i in range(lax.axis_size("domain"))])


def on_device(
    positions,
    features,
    species,
    ref_forces,
    centre_tile,
    other_tile,
    pair_live,
    send_tiles,
    radial_w,
    mix_w,
    species_w,
    out_w,
):
    atoms_here = positions.shape[2]
    channels = features.shape[2]
    table = (COMPS * TA, BASIS * TA)
    sent = (SEND * TA + 16, channels)
    slots = PAIRS * TA
    line = (3, 1, atoms_here)
    turning = [((CHUNK, CHUNK), F32)] * 2
    out_row = out_w.reshape(1, channels)
    positions = positions.transpose(1, 0, 2)
    ref_forces = ref_forces.transpose(1, 0, 2)
    ints = [((1, n), jnp.int32) for n in (PAIRS, PAIRS, PAIRS, 2 * SEND)]

    to_low, to_high, token = call(
        gather_kernel,
        "gather",
        [sent, sent, (8, CHUNK)],
        [
            ints[3],
            (line, F32),
            ((1, atoms_here, channels), F32),
            (line, F32),
            pltpu.SemaphoreType.DMA((4,)),
        ],
        send_tiles, positions, features, ref_forces,
        space=pltpu.HBM,
    )
    from_low = shifted(to_high, "domain", 1)
    from_high = shifted(to_low, "domain", -1)
    flags, atoms, own_feat, weights, mh, ml = call(
        stage_kernel,
        "stage",
        [
            (16, CHUNK),
            (8, atoms_here),
            (atoms_here, channels),
            (16, channels),
            (mix_w.shape, BF16),
            (mix_w.shape, BF16),
        ],
        ints
        + [(line, F32), (line, F32), ((1, atoms_here), jnp.int32)]
        + [(radial_w.shape, F32), (mix_w.shape, F32), (species_w.shape, F32), (out_row.shape, F32)]
        + [pltpu.SemaphoreType.DMA((12,))],
        centre_tile, other_tile, pair_live, send_tiles, positions, ref_forces, species, features,
        radial_w, mix_w, species_w, out_row,
        space=pltpu.HBM,
        after=(token,),
    )

    factors = (PAIRS, BASIS * TA, channels)
    env, dinv, gate, curve, inv, rows, fsel, own, grads_up, grads_down, shape_store, xh, xl = call(
        force_kernel,
        "force",
        [
            (PAIRS * COMPS * TA, channels),
            (slots, 3 * channels),
            (slots, channels),
            (slots, channels),
            (slots, 3 * channels),
            (8, CHUNK),
            (slots, channels),
            (8, atoms_here),
            (8, CHUNK),
            (8, CHUNK),
            (PAIRS, 4 + BASIS, TA, CHUNK),
            (factors, BF16),
            (factors, BF16),
        ],
        turning
        + [((PAIRS, *table), BF16)] * 2
        + [((PAIRS, COMPS * TA, channels), BF16)] * 2
        + [((PAIRS * COMPS * TA, channels), F32), ((PAIRS, *table), F32)],
        flags, atoms, own_feat, weights, mh, ml, from_low, from_high,
        flops=1 << 31,
    )
    low_one = shifted(grads_up, "domain", 1)
    low_two = shifted(grads_up, "domain", 2)
    high_one = shifted(grads_down, "domain", -1)
    high_two = shifted(grads_down, "domain", -2)

    rows_mix = 3 * channels
    total_count = 3.0 * atoms_here * lax.axis_size("domain") * lax.axis_size("batch")
    forces, keep, give, small, envdot, curl, both = call(
        functools.partial(tangent_kernel, 2.0 / math.sqrt(total_count)),
        "tangent",
        [
            line,
            (rows_mix, HALF),
            (rows_mix, HALF),
            (8, channels),
            (PAIRS * COMPS * TA, channels),
            (slots, channels),
            (16, CHUNK),
        ],
        turning
        + [((PAIRS, *table), BF16)] * 2
        + [((PAIRS * COMPS * TA, channels), F32)]
        + [((2 * slots, 3 * channels), F32), ((2 * slots, channels), F32)],
        flags, atoms, weights, mh, ml, from_low, from_high, own, low_one, low_two, high_one, high_two,
        rows, env, gate, curve, inv, shape_store, xh, xl,
        flops=1 << 31,
    )

    def radial(p, after):
        return call(
            functools.partial(radial_kernel, p),
            "radial",
            [(BASIS, channels)],
            turning
            + [((BASIS * TA, COMPS * CHUNK), BF16)] * 2
            + [((COMPS * CHUNK, channels), BF16)] * 2
            + [((BASIS * TA, channels), F32)],
            flags, both, fsel, env, envdot, dinv, curl, mh, ml, after,
            flops=1 << 31,
        )[0]

    bits = lax.axis_size("domain").bit_length() - 1
    levels = [(shift, 1 << min(LEVEL, bits - shift)) for shift in range(0, bits, LEVEL)]
    terms = [keep, shifted(give, "batch", 1)]
    radials = [radial(0, both)]
    rows_now = rows_mix
    cut = []
    for shift, width in levels:
        if rows_now % (8 * width):
            break
        rows_now //= width
        cut.append((shift, width))
        blocks = call(
            functools.partial(spread_kernel, shift, width, len(terms)),
            "spread", [(rows_now, HALF)] * width, [], *terms,
        )
        terms = [blocks[0]] + [partner(blocks[k], k << shift) for k in range(width - 1, 0, -1)]
        if len(radials) < PAIRS:
            radials.append(radial(1, blocks[0]))
    (mine,) = call(
        functools.partial(tail_kernel, len(terms)),
        "tail", [(rows_now + SMALL, HALF)], [], *terms, *radials, small,
    )
    for shift, width in levels[len(cut) :]:
        parts = [mine] + [partner(mine, k << shift) for k in range(1, width)]
        (mine,) = call(
            functools.partial(whole_kernel, shift, width),
            "whole", [(rows_now + SMALL, HALF)], [((width * (rows_now + SMALL), HALF), F32)], *parts,
        )
    for shift, width in reversed(cut):
        parts = [mine] + [partner(mine, k << shift) for k in range(1, width)]
        rows_now *= width
        (mine,) = call(
            functools.partial(grow_kernel, shift, width),
            "grow", [(rows_now + SMALL, HALF)], [((width * SMALL, HALF), F32)], *parts,
        )
    facing = shifted(mine, "batch", 1)
    mix, radial_sum, kinds, out = call(
        join_kernel,
        "join",
        [(rows_mix, channels), (BASIS, channels), (SPECIES, channels), (1, channels)],
        [],
        mine,
        facing,
    )
    return forces.transpose(1, 0, 2), radial_sum, mix, kinds, out.reshape(channels)


def solution(mesh):
    return jax.shard_map(
        on_device,
        mesh=mesh,
        in_specs=(
            P(("parts", "batch"), None, "domain"),
            P(("parts", "batch"), "domain", None),
            P(("parts", "batch"), "domain"),
            P(("parts", "batch"), None, "domain"),
            P(("parts", "batch"), "domain"),
            P(("parts", "batch"), "domain"),
            P(("parts", "batch"), "domain"),
            P(("parts", "batch"), "domain"),
            P(),
            P(),
            P(),
            P(),
        ),
        out_specs=(
            P(("parts", "batch"), None, "domain"),
            P("parts", None),
            P("parts", None),
            P("parts", None),
            P("parts"),
        ),
        check_vma=False,
    )
```

time: 82.1 us -> 67.8 us (0.83)
  waiting for transfers between devices: 32.5 us -> 13.2 us
  starting transfers between devices: 20.5 us -> 36.4 us
  local copies, waits for them, and re-layouts: 10.1 us -> 0 us
    ppermute x6 -> x14, waiting for transfers between devices: 24.6 us -> 4.59 us  [partner(): lax.ppermute(block, 'domain', [(i, i ^ mask) for i in range(lax.axis_size...]
    ppermute x6 -> x14, starting transfers between devices: 7.41 us -> 23.4 us  [partner(): lax.ppermute(block, 'domain', [(i, i ^ mask) for i in range(lax.axis_size...]
    unnamed x29 -> x0, local copies, waits for them, and re-layouts: 10.1 us -> none
    pallas_call x13 -> x10, Pallas kernels: 18 us -> 17.3 us  [call(): pl.pallas_call(kernel, name=name, out_shape=[jax.ShapeDtypeStruct(*out) f...]
  transfers between devices with their start and end apart: 14 -> 22, of which waited for: 11 -> 12; matrix products, arithmetic and copies ran while one was open for 1% -> 0% of each run, Pallas kernels for 7% -> 10%
where the time goes in v3:
time: 67.8 us; the launch traced here: 67.6 us
  starting transfers between devices  36.4 us (54%)
  Pallas kernels  17.3 us (26%)
  waiting for transfers between devices  13.2 us (19%)
  between operations  0.74 us (1%)
    ppermute x14, starting transfers between devices, partner(): lax.ppermute(block, 'domain', [(i, i ^ mask) for i in range(lax.axis_size...  23.4 us
    pallas_call x10, Pallas kernels, call(): pl.pallas_call(kernel, name=name, out_shape=[jax.ShapeDtypeStruct(*out) f...  17.3 us
    ppermute x8, starting transfers between devices, shifted(): lax.ppermute(block, axis, [(i, (i + by) % count) for i in range(count)])  13 us
    ppermute x8, waiting for transfers between devices, shifted(): lax.ppermute(block, axis, [(i, (i + by) % count) for i in range(count)])  8.56 us
    ppermute x14, waiting for transfers between devices, partner(): lax.ppermute(block, 'domain', [(i, i ^ mask) for i in range(lax.axis_size...  4.59 us
  transfers between devices with their start and end apart: 22, of which 12 were waited for; matrix products, arithmetic and copies ran while one was open for 0% of the time, Pallas kernels for 10%

profile of v3, /device:TPU:0, one launch (start us, length us, event | category | flops | bytes accessed | tf_op | source)
XLA Modules:
  0.0 67.6 jit_solution(5650792036246827788)
XLA Ops:
  0.6 1.2 %gather.1 = (f32[144,256]{1,0:T(8,128)S(1)}, f32[144,256]{1,0:T(8,128)S(1)}, f32[8,128]{1,0:T(8,128)S(1)}) custom-call(s32[1,4]{1,0:T(1,128)} %send.3, f32[3,1,256]{2,1,0:T(1,128)} %bitcast.5, f32[1,256,256]{2,1,0:T(8,128)} %feat.3, f32[3,1,256]{2,1,0:T(1,128)} %bitcast.7), custom_call_target="tpu_custom_call" | custom-call | bytes 1048576 | tf_op jit(solution)/shard_map/gather/pallas_call | solution.py:621
  1.8 3.0 %collective-permute-start = (f32[144,256]{1,0:T(8,128)S(1)}, f32[144,256]{1,0:T(8,128)S(1)}, u32[]{:S(2)}, u32[]{:S(2)}) collective-permute-start(f32[144,256]{1,0:T(8,128)S(1)} %get-tuple-element.52), channel_id=1, source_target_pairs={{0,2},{2,4},{4,6},{6,8},{8,10},{10,12},{12,14},{14,0},{1,3},{3,5},... | collective-permute-start | bytes 442376 | tf_op jit(solution)/shard_map/ppermute | solution.py:635
  4.8 3.1 %collective-permute-start.1 = (f32[144,256]{1,0:T(8,128)S(1)}, f32[144,256]{1,0:T(8,128)S(1)}, u32[]{:S(2)}, u32[]{:S(2)}) collective-permute-start(f32[144,256]{1,0:T(8,128)S(1)} %get-tuple-element.53), channel_id=1, source_target_pairs={{0,14},{2,0},{4,2},{6,4},{8,6},{10,8},{12,10},{14,12},{1,15},{3,1}... | collective-permute-start | bytes 442376 | tf_op jit(solution)/shard_map/ppermute | solution.py:635
  7.9 1.6 %stage.1 = (f32[16,128]{1,0:T(8,128)S(1)}, f32[8,256]{1,0:T(8,128)S(1)}, f32[256,256]{1,0:T(8,128)S(1)}, f32[16,256]{1,0:T(8,128)S(1)}, bf16[768,256]{1,0:T(8,128)(2,1)S(1)}, /*index=5*/bf16[768,256]{1,0:T(8,128)(2,1)S(1)}) custom-call(s32[1,2]{1,0:T(1,128)} %centre.1, s32[1,2]{1,0:T(1,128)} %other.1, s32[1,2]{1,0:T(1,128)} %live.1, s32[1,4]{1,0:T(1,128)} %send.3, ...), custom_call_target="tpu_custom_call" | custom-call | bytes 1048576 | tf_op jit(solution)/shard_map/stage/pallas_call | solution.py:621
  9.5 2.3 %collective-permute-done.from_low = f32[144,256]{1,0:T(8,128)S(1)} collective-permute-done((f32[144,256]{1,0:T(8,128)S(1)}, f32[144,256]{1,0:T(8,128)S(1)}, u32[]{:S(2)}, u32[]{:S(2)}) %collective-permute-start) | collective-permute-done | bytes 147488 | tf_op jit(solution)/shard_map/ppermute | solution.py:635
  11.8 1.5 %collective-permute-done.1.from_high = f32[144,256]{1,0:T(8,128)S(1)} collective-permute-done((f32[144,256]{1,0:T(8,128)S(1)}, f32[144,256]{1,0:T(8,128)S(1)}, u32[]{:S(2)}, u32[]{:S(2)}) %collective-permute-start.1) | collective-permute-done | bytes 147488 | tf_op jit(solution)/shard_map/ppermute | solution.py:635
  13.3 5.0 %force.1 = (f32[1152,256]{1,0:T(8,128)S(1)}, f32[128,768]{1,0:T(8,128)S(1)}, f32[128,256]{1,0:T(8,128)S(1)}, f32[128,256]{1,0:T(8,128)S(1)}, f32[128,768]{1,0:T(...) custom-call(f32[16,128]{1,0:T(8,128)S(1)} %get-tuple-element.47.flag, ...), custom_call_target="tpu_custom_call" | custom-call | flops 2147483648 | bytes 1048576 | tf_op jit(solution)/shard_map/force/pallas_call | solution.py:621
  18.3 1.3 %collective-permute-start.3 = (f32[8,128]{1,0:T(8,128)S(1)}, f32[8,128]{1,0:T(8,128)S(1)}, u32[]{:S(2)}, u32[]{:S(2)}) collective-permute-start(f32[8,128]{1,0:T(8,128)S(1)} %get-tuple-element.56), channel_id=1, source_target_pairs={{0,4},{2,6},{4,8},{6,10},{8,12},{10,14},{12,0},{14,2},{1,5},{3,7},... | collective-permute-start | bytes 12296 | tf_op jit(solution)/shard_map/ppermute | solution.py:635
  19.6 0.6 collective-permute-start.2
  20.2 2.2 %collective-permute-start.5 = (f32[8,128]{1,0:T(8,128)S(1)}, f32[8,128]{1,0:T(8,128)S(1)}, u32[]{:S(2)}, u32[]{:S(2)}) collective-permute-start(f32[8,128]{1,0:T(8,128)S(1)} %get-tuple-element.57), channel_id=1, source_target_pairs={{0,12},{2,14},{4,0},{6,2},{8,4},{10,6},{12,8},{14,10},{1,13},{3,15... | collective-permute-start | bytes 12296 | tf_op jit(solution)/shard_map/ppermute | solution.py:635
  22.4 2.6 %collective-permute-start.4 = (f32[8,128]{1,0:T(8,128)S(1)}, f32[8,128]{1,0:T(8,128)S(1)}, u32[]{:S(2)}, u32[]{:S(2)}) collective-permute-start(f32[8,128]{1,0:T(8,128)S(1)} %get-tuple-element.57), channel_id=1, source_target_pairs={{0,14},{2,0},{4,2},{6,4},{8,6},{10,8},{12,10},{14,12},{1,15},{3,1}... | collective-permute-start | bytes 12296 | tf_op jit(solution)/shard_map/ppermute | solution.py:635
  25.1 0.8 %collective-permute-done.2.low_one = f32[8,128]{1,0:T(8,128)S(1)} collective-permute-done((f32[8,128]{1,0:T(8,128)S(1)}, f32[8,128]{1,0:T(8,128)S(1)}, u32[]{:S(2)}, u32[]{:S(2)}) %collective-permute-start.2) | collective-permute-done | bytes 4128 | tf_op jit(solution)/shard_map/ppermute | solution.py:635
  25.9 0.6 collective-permute-done.4.high_one
  26.4 3.4 %tangent.1 = (f32[3,1,256]{2,1,0:T(1,128)}, f32[768,128]{1,0:T(8,128)S(1)}, f32[768,128]{1,0:T(8,128)S(1)}, f32[8,256]{1,0:T(8,128)S(1)}, f32[1152,256]{1,0:T(8,...) custom-call(f32[16,128]{1,0:T(8,128)S(1)} %get-tuple-element.47.flags, f32[8,256]{1,0:T(8,128)S(1)} %get-tuple-element.48.atoms, ...), custom_call_target="tpu_custom_call" | custom-call | flops 2147483648 | bytes 1048576 | tf_op jit(solution)/shard_map/tangent/pallas_call | solution.py:621
  29.9 1.7 %collective-permute-done.6.refs_1_ = f32[768,128]{1,0:T(8,128)S(1)} collective-permute-done((f32[768,128]{1,0:T(8,128)S(1)}, f32[768,128]{1,0:T(8,128)S(1)}, u32[]{:S(2)}, u32[]{:S(2)}) %collective-permute-start.6) | collective-permute-done | bytes 393248 | tf_op jit(solution)/shard_map/ppermute | solution.py:635
  31.7 5.0 %collective-permute-start.7 = (f32[96,128]{1,0:T(8,128)S(1)}, f32[96,128]{1,0:T(8,128)S(1)}, u32[]{:S(2)}, u32[]{:S(2)}) collective-permute-start(f32[96,128]{1,0:T(8,128)S(1)} %get-tuple-element.70), channel_id=1, source_target_pairs={{0,14},{2,12},{4,10},{6,8},{8,6},{10,4},{12,2},{14,0},{1,15},{3,13... | collective-permute-start | bytes 147464 | tf_op jit(solution)/shard_map/ppermute | solution.py:639
  36.7 1.2 %collective-permute-start.8 = (f32[96,128]{1,0:T(8,128)S(1)}, f32[96,128]{1,0:T(8,128)S(1)}, u32[]{:S(2)}, u32[]{:S(2)}) collective-permute-start(f32[96,128]{1,0:T(8,128)S(1)} %get-tuple-element.71), channel_id=1, source_target_pairs={{0,12},{2,14},{4,8},{6,10},{8,4},{10,6},{12,0},{14,2},{1,13},{3,15... | collective-permute-start | bytes 147464 | tf_op jit(solution)/shard_map/ppermute | solution.py:639
  37.9 2.5 %radial.2.refs_8_ = f32[8,256]{1,0:T(8,128)S(1)} custom-call(f32[16,128]{1,0:T(8,128)S(1)} %get-tuple-element.47.flags, f32[16,128]{1,0:T(8,128)S(1)} %get-tuple-element.77.both.after, f32[128,256]{1,0:T(8,128)S(1)} %get-tuple-element.78.fsel, f32[1152,256]{1,0:T(8,128)S(1)} %get-tuple-element.59.env, f32[1152,256]{1,0:T(8,128)S(1)} %get-tuple-element.79.envdot, ...), custom_call_target="tpu_custom_call" | custom-call | flops 2147483648 | bytes 1048576 | tf_op jit(solution)/shard_map/radial/pallas_call | solution.py:621
  40.5 1.8 %collective-permute-start.10 = (f32[96,128]{1,0:T(8,128)S(1)}, f32[96,128]{1,0:T(8,128)S(1)}, u32[]{:S(2)}, u32[]{:S(2)}) collective-permute-start(f32[96,128]{1,0:T(8,128)S(1)} %get-tuple-element.73), channel_id=1, source_target_pairs={{0,8},{2,10},{4,12},{6,14},{8,0},{10,2},{12,4},{14,6},{1,9},{3,11}... | collective-permute-start | bytes 147464 | tf_op jit(solution)/shard_map/ppermute | solution.py:639
  42.3 2.3 %collective-permute-start.11 = (f32[96,128]{1,0:T(8,128)S(1)}, f32[96,128]{1,0:T(8,128)S(1)}, u32[]{:S(2)}, u32[]{:S(2)}) collective-permute-start(f32[96,128]{1,0:T(8,128)S(1)} %get-tuple-element.74), channel_id=1, source_target_pairs={{0,6},{2,4},{4,2},{6,0},{8,14},{10,12},{12,10},{14,8},{1,7},{3,5},... | collective-permute-start | bytes 147464 | tf_op jit(solution)/shard_map/ppermute | solution.py:639
  44.6 1.8 %collective-permute-start.12 = (f32[96,128]{1,0:T(8,128)S(1)}, f32[96,128]{1,0:T(8,128)S(1)}, u32[]{:S(2)}, u32[]{:S(2)}) collective-permute-start(f32[96,128]{1,0:T(8,128)S(1)} %get-tuple-element.75), channel_id=1, source_target_pairs={{0,4},{2,6},{4,0},{6,2},{8,12},{10,14},{12,8},{14,10},{1,5},{3,7},... | collective-permute-start | bytes 147464 | tf_op jit(solution)/shard_map/ppermute | solution.py:639
  46.4 2.5 %radial.3.refs_9_ = f32[8,256]{1,0:T(8,128)S(1)} custom-call(f32[16,128]{1,0:T(8,128)S(1)} %get-tuple-element.47.flags, f32[16,128]{1,0:T(8,128)S(1)} %get-tuple-element.77.both.after, f32[128,256]{1,0:T(8,128)S(1)} %get-tuple-element.78.fsel, f32[1152,256]{1,0:T(8,128)S(1)} %get-tuple-element.59.env, f32[1152,256]{1,0:T(8,128)S(1)} %get-tuple-element.79.envdot, ...), custom_call_target="tpu_custom_call" | custom-call | flops 2147483648 | bytes 1048576 | tf_op jit(solution)/shard_map/radial/pallas_call | solution.py:621
  49.3 1.1 %collective-permute-done.13.refs_7_ = f32[96,128]{1,0:T(8,128)S(1)} collective-permute-done((f32[96,128]{1,0:T(8,128)S(1)}, f32[96,128]{1,0:T(8,128)S(1)}, u32[]{:S(2)}, u32[]{:S(2)}) %collective-permute-start.13) | collective-permute-done | bytes 49184 | tf_op jit(solution)/shard_map/ppermute | solution.py:639
  50.5 2.6 %collective-permute-start.20 = (f32[128,128]{1,0:T(8,128)S(1)}, f32[128,128]{1,0:T(8,128)S(1)}, u32[]{:S(2)}, u32[]{:S(2)}) collective-permute-start(f32[128,128]{1,0:T(8,128)S(1)} %tail.1.refs_0_), channel_id=1, source_target_pairs={{0,14},{2,12},{4,10},{6,8},{8,6},{10,4},{12,2},{14,0},{1,15},{3,13... | collective-permute-start | bytes 196616 | tf_op jit(solution)/shard_map/ppermute | solution.py:639
  53.1 1.2 %collective-permute-start.19 = (f32[128,128]{1,0:T(8,128)S(1)}, f32[128,128]{1,0:T(8,128)S(1)}, u32[]{:S(2)}, u32[]{:S(2)}) collective-permute-start(f32[128,128]{1,0:T(8,128)S(1)} %tail.1.refs_0_), channel_id=1, source_target_pairs={{0,12},{2,14},{4,8},{6,10},{8,4},{10,6},{12,0},{14,2},{1,13},{3,15... | collective-permute-start | bytes 196616 | tf_op jit(solution)/shard_map/ppermute | solution.py:639
  54.7 3.5 %collective-permute-start.17 = (f32[128,128]{1,0:T(8,128)S(1)}, f32[128,128]{1,0:T(8,128)S(1)}, u32[]{:S(2)}, u32[]{:S(2)}) collective-permute-start(f32[128,128]{1,0:T(8,128)S(1)} %tail.1.refs_0_), channel_id=1, source_target_pairs={{0,8},{2,10},{4,12},{6,14},{8,0},{10,2},{12,4},{14,6},{1,9},{3,11}... | collective-permute-start | bytes 196616 | tf_op jit(solution)/shard_map/ppermute | solution.py:639
  58.4 1.7 %collective-permute-start.15 = (f32[128,128]{1,0:T(8,128)S(1)}, f32[128,128]{1,0:T(8,128)S(1)}, u32[]{:S(2)}, u32[]{:S(2)}) collective-permute-start(f32[128,128]{1,0:T(8,128)S(1)} %tail.1.refs_0_), channel_id=1, source_target_pairs={{0,4},{2,6},{4,0},{6,2},{8,12},{10,14},{12,8},{14,10},{1,5},{3,7},... | collective-permute-start | bytes 196616 | tf_op jit(solution)/shard_map/ppermute | solution.py:639
  60.2 1.5 %collective-permute-start.14 = (f32[128,128]{1,0:T(8,128)S(1)}, f32[128,128]{1,0:T(8,128)S(1)}, u32[]{:S(2)}, u32[]{:S(2)}) collective-permute-start(f32[128,128]{1,0:T(8,128)S(1)} %tail.1.refs_0_), channel_id=1, source_target_pairs={{0,2},{2,0},{4,6},{6,4},{8,10},{10,8},{12,14},{14,12},{1,3},{3,1},... | collective-permute-start | bytes 196616 | tf_op jit(solution)/shard_map/ppermute | solution.py:639
  61.7 1.6 %collective-permute-done.18.refs_5_ = f32[128,128]{1,0:T(8,128)S(1)} collective-permute-done((f32[128,128]{1,0:T(8,128)S(1)}, f32[128,128]{1,0:T(8,128)S(1)}, u32[]{:S(2)}, u32[]{:S(2)}) %collective-permute-start.18) | collective-permute-done | bytes 65568 | tf_op jit(solution)/shard_map/ppermute | solution.py:639
  63.8 0.6 collective-permute-done.16.refs_3_
  64.9 1.7 %collective-permute-done.21.facing = f32[800,128]{1,0:T(8,128)S(1)} collective-permute-done((f32[800,128]{1,0:T(8,128)S(1)}, f32[800,128]{1,0:T(8,128)S(1)}, u32[]{:S(2)}, u32[]{:S(2)}) %collective-permute-start.21) | collective-permute-done | bytes 409632 | tf_op jit(solution)/shard_map/ppermute | solution.py:635
  66.6 1.0 %join.1 = (f32[768,256]{1,0:T(8,128)}, f32[8,256]{1,0:T(8,128)}, f32[4,256]{1,0:T(4,128)}, f32[1,256]{1,0:T(1,128)}) custom-call(f32[800,128]{1,0:T(8,128)S(1)} %grow.1.whole, f32[800,128]{1,0:T(8,128)S(1)} %collective-permute-done.21.facing), custom_call_target="tpu_custom_call" | custom-call | bytes 1048576 | tf_op jit(solution)/shard_map/join/pallas_call | solution.py:621
  (22 shorter events, 2.2 us)
Async XLA Ops:
  1.8 10.0 %collective-permute-start = (f32[144,256]{1,0:T(8,128)S(1)}, f32[144,256]{1,0:T(8,128)S(1)}, u32[]{:S(2)}, u32[]{:S(2)}) collective-permute-start(f32[144,256]{1,0:T(8,128)S(1)} %get-tuple-element.52), channel_id=1, source_target_pairs={{0,2},{2,4},{4,6},{6,8},{8,10},{10,12},{12,14},{14,0},{1,3},{3,5},... | collective-permute-start | bytes 442376 | tf_op jit(solution)/shard_map/ppermute | solution.py:635
  4.8 8.5 %collective-permute-start.1 = (f32[144,256]{1,0:T(8,128)S(1)}, f32[144,256]{1,0:T(8,128)S(1)}, u32[]{:S(2)}, u32[]{:S(2)}) collective-permute-start(f32[144,256]{1,0:T(8,128)S(1)} %get-tuple-element.53), channel_id=1, source_target_pairs={{0,14},{2,0},{4,2},{6,4},{8,6},{10,8},{12,10},{14,12},{1,15},{3,1}... | collective-permute-start | bytes 442376 | tf_op jit(solution)/shard_map/ppermute | solution.py:635
  18.3 6.8 %collective-permute-start.3 = (f32[8,128]{1,0:T(8,128)S(1)}, f32[8,128]{1,0:T(8,128)S(1)}, u32[]{:S(2)}, u32[]{:S(2)}) collective-permute-start(f32[8,128]{1,0:T(8,128)S(1)} %get-tuple-element.56), channel_id=1, source_target_pairs={{0,4},{2,6},{4,8},{6,10},{8,12},{10,14},{12,0},{14,2},{1,5},{3,7},... | collective-permute-start | bytes 12296 | tf_op jit(solution)/shard_map/ppermute | solution.py:635
  19.6 6.3 %collective-permute-start.2 = (f32[8,128]{1,0:T(8,128)S(1)}, f32[8,128]{1,0:T(8,128)S(1)}, u32[]{:S(2)}, u32[]{:S(2)}) collective-permute-start(f32[8,128]{1,0:T(8,128)S(1)} %get-tuple-element.56), channel_id=1, source_target_pairs={{0,2},{2,4},{4,6},{6,8},{8,10},{10,12},{12,14},{14,0},{1,3},{3,5},... | collective-permute-start | bytes 12296 | tf_op jit(solution)/shard_map/ppermute | solution.py:635
  20.2 5.7 %collective-permute-start.5 = (f32[8,128]{1,0:T(8,128)S(1)}, f32[8,128]{1,0:T(8,128)S(1)}, u32[]{:S(2)}, u32[]{:S(2)}) collective-permute-start(f32[8,128]{1,0:T(8,128)S(1)} %get-tuple-element.57), channel_id=1, source_target_pairs={{0,12},{2,14},{4,0},{6,2},{8,4},{10,6},{12,8},{14,10},{1,13},{3,15... | collective-permute-start | bytes 12296 | tf_op jit(solution)/shard_map/ppermute | solution.py:635
  22.4 4.0 %collective-permute-start.4 = (f32[8,128]{1,0:T(8,128)S(1)}, f32[8,128]{1,0:T(8,128)S(1)}, u32[]{:S(2)}, u32[]{:S(2)}) collective-permute-start(f32[8,128]{1,0:T(8,128)S(1)} %get-tuple-element.57), channel_id=1, source_target_pairs={{0,14},{2,0},{4,2},{6,4},{8,6},{10,8},{12,10},{14,12},{1,15},{3,1}... | collective-permute-start | bytes 12296 | tf_op jit(solution)/shard_map/ppermute | solution.py:635
  29.8 1.8 %collective-permute-start.6 = (f32[768,128]{1,0:T(8,128)S(1)}, f32[768,128]{1,0:T(8,128)S(1)}, u32[]{:S(2)}, u32[]{:S(2)}) collective-permute-start(f32[768,128]{1,0:T(8,128)S(1)} %get-tuple-element.68), channel_id=1, source_target_pairs={{0,1},{1,0},{2,3},{3,2},{4,5},{5,4},{6,7},{7,6},{8,9},{9,8},{10,11... | collective-permute-start | bytes 1179656 | tf_op jit(solution)/shard_map/ppermute | solution.py:635
  31.7 12.9 %collective-permute-start.7 = (f32[96,128]{1,0:T(8,128)S(1)}, f32[96,128]{1,0:T(8,128)S(1)}, u32[]{:S(2)}, u32[]{:S(2)}) collective-permute-start(f32[96,128]{1,0:T(8,128)S(1)} %get-tuple-element.70), channel_id=1, source_target_pairs={{0,14},{2,12},{4,10},{6,8},{8,6},{10,4},{12,2},{14,0},{1,15},{3,13... | collective-permute-start | bytes 147464 | tf_op jit(solution)/shard_map/ppermute | solution.py:639
  36.7 9.7 %collective-permute-start.8 = (f32[96,128]{1,0:T(8,128)S(1)}, f32[96,128]{1,0:T(8,128)S(1)}, u32[]{:S(2)}, u32[]{:S(2)}) collective-permute-start(f32[96,128]{1,0:T(8,128)S(1)} %get-tuple-element.71), channel_id=1, source_target_pairs={{0,12},{2,14},{4,8},{6,10},{8,4},{10,6},{12,0},{14,2},{1,13},{3,15... | collective-permute-start | bytes 147464 | tf_op jit(solution)/shard_map/ppermute | solution.py:639
  40.4 8.4 %collective-permute-start.9 = (f32[96,128]{1,0:T(8,128)S(1)}, f32[96,128]{1,0:T(8,128)S(1)}, u32[]{:S(2)}, u32[]{:S(2)}) collective-permute-start(f32[96,128]{1,0:T(8,128)S(1)} %get-tuple-element.72), channel_id=1, source_target_pairs={{0,10},{2,8},{4,14},{6,12},{8,2},{10,0},{12,6},{14,4},{1,11},{3,9}... | collective-permute-start | bytes 147464 | tf_op jit(solution)/shard_map/ppermute | solution.py:639
  40.5 8.4 %collective-permute-start.10 = (f32[96,128]{1,0:T(8,128)S(1)}, f32[96,128]{1,0:T(8,128)S(1)}, u32[]{:S(2)}, u32[]{:S(2)}) collective-permute-start(f32[96,128]{1,0:T(8,128)S(1)} %get-tuple-element.73), channel_id=1, source_target_pairs={{0,8},{2,10},{4,12},{6,14},{8,0},{10,2},{12,4},{14,6},{1,9},{3,11}... | collective-permute-start | bytes 147464 | tf_op jit(solution)/shard_map/ppermute | solution.py:639
  42.3 6.6 %collective-permute-start.11 = (f32[96,128]{1,0:T(8,128)S(1)}, f32[96,128]{1,0:T(8,128)S(1)}, u32[]{:S(2)}, u32[]{:S(2)}) collective-permute-start(f32[96,128]{1,0:T(8,128)S(1)} %get-tuple-element.74), channel_id=1, source_target_pairs={{0,6},{2,4},{4,2},{6,0},{8,14},{10,12},{12,10},{14,8},{1,7},{3,5},... | collective-permute-start | bytes 147464 | tf_op jit(solution)/shard_map/ppermute | solution.py:639
  44.6 4.8 %collective-permute-start.12 = (f32[96,128]{1,0:T(8,128)S(1)}, f32[96,128]{1,0:T(8,128)S(1)}, u32[]{:S(2)}, u32[]{:S(2)}) collective-permute-start(f32[96,128]{1,0:T(8,128)S(1)} %get-tuple-element.75), channel_id=1, source_target_pairs={{0,4},{2,6},{4,0},{6,2},{8,12},{10,14},{12,8},{14,10},{1,5},{3,7},... | collective-permute-start | bytes 147464 | tf_op jit(solution)/shard_map/ppermute | solution.py:639
  46.4 4.1 %collective-permute-start.13 = (f32[96,128]{1,0:T(8,128)S(1)}, f32[96,128]{1,0:T(8,128)S(1)}, u32[]{:S(2)}, u32[]{:S(2)}) collective-permute-start(f32[96,128]{1,0:T(8,128)S(1)} %get-tuple-element.76), channel_id=1, source_target_pairs={{0,2},{2,0},{4,6},{6,4},{8,10},{10,8},{12,14},{14,12},{1,3},{3,1},... | collective-permute-start | bytes 147464 | tf_op jit(solution)/shard_map/ppermute | solution.py:639
  50.5 7.9 %collective-permute-start.20 = (f32[128,128]{1,0:T(8,128)S(1)}, f32[128,128]{1,0:T(8,128)S(1)}, u32[]{:S(2)}, u32[]{:S(2)}) collective-permute-start(f32[128,128]{1,0:T(8,128)S(1)} %tail.1.refs_0_), channel_id=1, source_target_pairs={{0,14},{2,12},{4,10},{6,8},{8,6},{10,4},{12,2},{14,0},{1,15},{3,13... | collective-permute-start | bytes 196616 | tf_op jit(solution)/shard_map/ppermute | solution.py:639
  53.1 7.1 %collective-permute-start.19 = (f32[128,128]{1,0:T(8,128)S(1)}, f32[128,128]{1,0:T(8,128)S(1)}, u32[]{:S(2)}, u32[]{:S(2)}) collective-permute-start(f32[128,128]{1,0:T(8,128)S(1)} %tail.1.refs_0_), channel_id=1, source_target_pairs={{0,12},{2,14},{4,8},{6,10},{8,4},{10,6},{12,0},{14,2},{1,13},{3,15... | collective-permute-start | bytes 196616 | tf_op jit(solution)/shard_map/ppermute | solution.py:639
  54.3 8.9 %collective-permute-start.18 = (f32[128,128]{1,0:T(8,128)S(1)}, f32[128,128]{1,0:T(8,128)S(1)}, u32[]{:S(2)}, u32[]{:S(2)}) collective-permute-start(f32[128,128]{1,0:T(8,128)S(1)} %tail.1.refs_0_), channel_id=1, source_target_pairs={{0,10},{2,8},{4,14},{6,12},{8,2},{10,0},{12,6},{14,4},{1,11},{3,9}... | collective-permute-start | bytes 196616 | tf_op jit(solution)/shard_map/ppermute | solution.py:639
  54.7 9.1 %collective-permute-start.17 = (f32[128,128]{1,0:T(8,128)S(1)}, f32[128,128]{1,0:T(8,128)S(1)}, u32[]{:S(2)}, u32[]{:S(2)}) collective-permute-start(f32[128,128]{1,0:T(8,128)S(1)} %tail.1.refs_0_), channel_id=1, source_target_pairs={{0,8},{2,10},{4,12},{6,14},{8,0},{10,2},{12,4},{14,6},{1,9},{3,11}... | collective-permute-start | bytes 196616 | tf_op jit(solution)/shard_map/ppermute | solution.py:639
  58.2 6.2 %collective-permute-start.16 = (f32[128,128]{1,0:T(8,128)S(1)}, f32[128,128]{1,0:T(8,128)S(1)}, u32[]{:S(2)}, u32[]{:S(2)}) collective-permute-start(f32[128,128]{1,0:T(8,128)S(1)} %tail.1.refs_0_), channel_id=1, source_target_pairs={{0,6},{2,4},{4,2},{6,0},{8,14},{10,12},{12,10},{14,8},{1,7},{3,5},... | collective-permute-start | bytes 196616 | tf_op jit(solution)/shard_map/ppermute | solution.py:639
  58.4 6.0 %collective-permute-start.15 = (f32[128,128]{1,0:T(8,128)S(1)}, f32[128,128]{1,0:T(8,128)S(1)}, u32[]{:S(2)}, u32[]{:S(2)}) collective-permute-start(f32[128,128]{1,0:T(8,128)S(1)} %tail.1.refs_0_), channel_id=1, source_target_pairs={{0,4},{2,6},{4,0},{6,2},{8,12},{10,14},{12,8},{14,10},{1,5},{3,7},... | collective-permute-start | bytes 196616 | tf_op jit(solution)/shard_map/ppermute | solution.py:639
  60.2 4.6 %collective-permute-start.14 = (f32[128,128]{1,0:T(8,128)S(1)}, f32[128,128]{1,0:T(8,128)S(1)}, u32[]{:S(2)}, u32[]{:S(2)}) collective-permute-start(f32[128,128]{1,0:T(8,128)S(1)} %tail.1.refs_0_), channel_id=1, source_target_pairs={{0,2},{2,0},{4,6},{6,4},{8,10},{10,8},{12,14},{14,12},{1,3},{3,1},... | collective-permute-start | bytes 196616 | tf_op jit(solution)/shard_map/ppermute | solution.py:639
  64.8 1.8 %collective-permute-start.21 = (f32[800,128]{1,0:T(8,128)S(1)}, f32[800,128]{1,0:T(8,128)S(1)}, u32[]{:S(2)}, u32[]{:S(2)}) collective-permute-start(f32[800,128]{1,0:T(8,128)S(1)} %grow.1.whole), channel_id=1, source_target_pairs={{0,1},{1,0},{2,3},{3,2},{4,5},{5,4},{6,7},{7,6},{8,9},{9,8},{10,11... | collective-permute-start | bytes 1228808 | tf_op jit(solution)/shard_map/ppermute | solution.py:635

commit v4 on v3

--- a/solution.py
+++ b/solution.py
@@ -45,6 +45,10 @@
 
 def flag(condition):
     return jnp.where(condition, 1.0, 0.0).astype(F32)
+
+
+def place(shift, width):
+    return lax.bitwise_and(lax.shift_right_logical(lax.axis_index("domain"), shift), width - 1)
 
 
 def lane_half():
@@ -174,6 +178,7 @@
 
 
 OTHER, CENTRE, LIVE, SAME, SHARED, SENT = 0, 2, 4, 6, 8, 9
+GHOST_ROWS = 8
 
 
 def fetch(pairs, sems):
@@ -183,15 +188,26 @@
     return copies
 
 
-def gather_kernel(send, pos, feat, ref, to_low, to_high, token, send_v, pos_v, feat_v, ref_v, sems):
+def upward(shift):
+    return 1.0 - flag(place(shift, 2) == 1)
+
+
+def either(choice, first, second):
+    return first * choice + second * (1.0 - choice)
+
+
+def gather_kernel(send, pos, feat, ref, to_first, to_second, token, send_v, pos_v, feat_v, ref_v, sems):
     copies = fetch([(send, send_v), (pos, pos_v), (ref, ref_v), (feat, feat_v)], sems)
     for copy in copies[:3]:
         copy.wait()
     low, high = lane_half()
+    up = upward(0)
     sent = [send_v[0:1, j : j + 1].astype(F32) for j in range(2 * SEND)]
-    for out, first in ((to_low, 0), (to_high, SEND)):
-        tiles = sent[first : first + SEND]
-        out[SEND * TA :, :] = jnp.zeros((16, out.shape[1]), F32)
+    tiles_of = []
+    for out, choice in ((to_first, 1.0 - up), (to_second, up)):
+        tiles = [either(choice, sent[j], sent[SEND + j]) for j in range(SEND)]
+        tiles_of.append(tiles)
+        out[SEND * TA :, :] = jnp.zeros((GHOST_ROWS, out.shape[1]), F32)
         for i in range(3):
             at = SEND * TA + i
             for lanes, source in ((slice(0, CHUNK), pos_v), (slice(CHUNK, 2 * CHUNK), ref_v)):
@@ -199,18 +215,18 @@
                 out[at : at + 1, lanes] = paired(pick(chunks, tiles[0]), pick(chunks, tiles[1]))
         for other in range(2 * SEND):
             same = low * flag(sent[other] == tiles[0]) + high * flag(sent[other] == tiles[1])
-            out[SEND * TA + 8 + other : SEND * TA + 9 + other, 0:CHUNK] = same
+            out[SEND * TA + 3 + other : SEND * TA + 4 + other, 0:CHUNK] = same
     token[...] = jnp.zeros_like(token)
     copies[3].wait()
-    for out, first in ((to_low, 0), (to_high, SEND)):
+    for out, tiles in zip((to_first, to_second), tiles_of):
         for j in range(SEND):
-            out[j * TA : (j + 1) * TA, :] = pick_rows(feat_v.at[0], sent[first + j], 0)
+            out[j * TA : (j + 1) * TA, :] = pick_rows(feat_v.at[0], tiles[j], 0.0)
 
 
 def pick_rows(ref, position, first):
     total = None
     for t in range(ref.shape[0] // TA):
-        term = ref[t * TA : (t + 1) * TA, :] * flag(position == float(first + t))
+        term = ref[t * TA : (t + 1) * TA, :] * flag(position == first + float(t))
         total = term if total is None else total + term
     return total
 
@@ -261,17 +277,14 @@
 
 
 def force_kernel(
-    flags, atoms, feat, weights, mh, ml, from_low, from_high,
-    env, dinv, gate, curve, inv, rows, fsel, own, to_high, to_low, shape_store, xh, xl,
+    flags, atoms, feat, weights, mh, ml, from_first, from_second,
+    env, dinv, gate, curve, inv, rows, fsel, own, one_first, one_second, two_first, two_second, shape_store, xh, xl,
     square, turned, th, tl, eh, el, raw, back,
 ):
     ghost = SEND * TA
-    chunks = [
-        from_low[ghost : ghost + 3, 0:CHUNK],
-        atoms[0:3, 0:CHUNK],
-        atoms[0:3, CHUNK:],
-        from_high[ghost : ghost + 3, 0:CHUNK],
-    ]
+    up = upward(0)
+    near, far = from_first[ghost : ghost + 3, 0:CHUNK], from_second[ghost : ghost + 3, 0:CHUNK]
+    chunks = [either(up, far, near), atoms[0:3, 0:CHUNK], atoms[0:3, CHUNK:], either(up, near, far)]
     kinds = [atoms[3:4, q * CHUNK : (q + 1) * CHUNK] for q in range(2)]
 
     def number(row):
@@ -289,9 +302,9 @@
     for p in range(PAIRS):
         o = flags[OTHER + p : OTHER + p + 1, 0:1]
         fsel[p * TA : (p + 1) * TA, :] = (
-            pick_rows(from_low.at[0:ghost], o, 0)
-            + pick_rows(feat, o, SEND)
-            + pick_rows(from_high.at[0:ghost], o, SEND + 4)
+            pick_rows(from_first.at[0:ghost], o, (SEND + 4) * up)
+            + pick_rows(feat, o, float(SEND))
+            + pick_rows(from_second.at[0:ghost], o, (SEND + 4) * (1.0 - up))
         )
 
     shapes = []
@@ -385,14 +398,20 @@
     own[0:3, CHUNK:] = tile_grads[2]
     own[3:6, 0:CHUNK] = tile_grads[0]
     own[3:6, CHUNK:] = tile_grads[3]
-    for out, first, ghost_grad in ((to_low, 0, tile_grads[0]), (to_high, SEND, tile_grads[3])):
-        out[...] = jnp.zeros_like(out)
-        out[0:3, :] = paired(*(pick(tile_grads[1:3], number(SENT + first + j)) for j in range(SEND)))
-        out[3:6, :] = ghost_grad
+    leaving = []
+    for first, ghost_grad in ((0, tile_grads[0]), (SEND, tile_grads[3])):
+        listed = paired(*(pick(tile_grads[1:3], number(SENT + first + j)) for j in range(SEND)))
+        leaving.append((listed, ghost_grad))
+    for shift, outs in ((0, (one_first, one_second)), (1, (two_first, two_second))):
+        choice = upward(shift)
+        for out, above in zip(outs, (choice, 1.0 - choice)):
+            out[...] = jnp.zeros_like(out)
+            out[0:3, :] = either(above, leaving[1][0], leaving[0][0])
+            out[3:6, :] = either(above, leaving[1][1], leaving[0][1])
 
 
 def tangent_kernel(
-    scale, flags, atoms, weights, mh, ml, from_low, from_high, own, low_one, low_two, high_one, high_two,
+    scale, flags, atoms, weights, mh, ml, from_first, from_second, own, one_first, one_second, two_first, two_second,
     rows, env, gate, curve, inv, shape_store, xh, xl,
     forces, keep, give, small, envdot, curl, both,
     square, turned, th, tl, raw, left, right,
@@ -405,6 +424,13 @@
     others = [number(OTHER + p) for p in range(PAIRS)]
     shared = flags[SHARED : SHARED + 1, 0:1]
     mine = [own[0:3, 0:CHUNK], own[0:3, CHUNK:]]
+    up, up_two = upward(0), upward(1)
+    low_one = either(up, one_second[...], one_first[...])
+    high_one = either(up, one_first[...], one_second[...])
+    low_two = either(up_two, two_second[...], two_first[...])
+    high_two = either(up_two, two_first[...], two_second[...])
+    low_tail = either(up, from_second[ghost:, :], from_first[ghost:, :])
+    high_tail = either(up, from_first[ghost:, :], from_second[ghost:, :])
     arrived = [twice(low_one[3:6, :], j) for j in range(SEND)]
     arrived += [twice(high_one[3:6, :], j) for j in range(SEND)]
     for j in range(2 * SEND):
@@ -417,16 +443,16 @@
     to_above = [twice(own[3:6, CHUNK:], j) for j in range(SEND)]
     to_above += [twice(high_two[3:6, :], j) for j in range(SEND)]
     for j in range(2 * SEND):
-        below = below + from_low[ghost + 8 + j : ghost + 9 + j, 0:CHUNK] * to_below[j]
-        above = above + from_high[ghost + 8 + j : ghost + 9 + j, 0:CHUNK] * to_above[j]
+        below = below + low_tail[3 + j : 4 + j, 0:CHUNK] * to_below[j]
+        above = above + high_tail[3 + j : 4 + j, 0:CHUNK] * to_above[j]
     for q in range(2):
         for i in range(3):
             forces[i, :, q * CHUNK : (q + 1) * CHUNK] = -mine[q][i : i + 1, :]
     error = [
-        below + from_low[ghost : ghost + 3, CHUNK:],
+        below + low_tail[0:3, CHUNK:],
         mine[0] + atoms[4:7, 0:CHUNK],
         mine[1] + atoms[4:7, CHUNK:],
-        above + from_high[ghost : ghost + 3, CHUNK:],
+        above + high_tail[0:3, CHUNK:],
     ]
     error = [part * scale for part in error]
     both[...] = jnp.zeros_like(both)
@@ -538,11 +564,7 @@
 
 
 SMALL = 32
-LEVEL = 3
-
-
-def place(shift, width):
-    return lax.bitwise_and(lax.shift_right_logical(lax.axis_index("domain"), shift), width - 1)
+FOUR = 4
 
 
 def block_of(part, rows):
@@ -556,45 +578,47 @@
     return total
 
 
-def spread_kernel(shift, width, count, *refs):
-    terms, outs = refs[:count], refs[count:]
-    me = place(shift, width)
-    for k in range(width - 1, -1, -1):
-        outs[k][...] = total_of(terms, block_of(lax.bitwise_xor(me, k), outs[k].shape[0]))
-
-
-def tail_kernel(count, *refs):
-    terms, (radial_0, radial_1, small, out) = refs[:count], refs[count:]
-    rows = terms[0].shape[0]
-    out[0:rows, :] = total_of(terms, slice(0, rows))
+def halve_kernel(keep, taken, keep_out, give_out):
+    me = place(0, 2)
+    for out, part in ((keep_out, me), (give_out, 1 - me)):
+        out[...] = total_of([keep, taken], block_of(part, out.shape[0]))
+
+
+def spread_kernel(keep, taken, radial_0, radial_1, small, *refs):
+    outs, tiny = refs[:FOUR], refs[FOUR]
     for h in range(2):
         lanes = slice(h * HALF, (h + 1) * HALF)
-        at = rows + 16 * h
-        out[at : at + 8, :] = radial_0[:, lanes] + radial_1[:, lanes]
-        out[at + 8 : at + 16, :] = small[:, lanes]
-
-
-def grow_kernel(shift, width, *refs):
-    parts, out, tails = refs[:width], refs[width], refs[width + 1]
-    rows = parts[0].shape[0] - SMALL
-    me = place(shift, width)
+        tiny[16 * h : 16 * h + 8, :] = radial_0[:, lanes] + radial_1[:, lanes]
+        tiny[16 * h + 8 : 16 * h + 16, :] = small[:, lanes]
+    me = place(1, FOUR)
+    for k, out in enumerate(outs):
+        rows, few = out.shape[0] - SMALL // FOUR, SMALL // FOUR
+        to = lax.bitwise_xor(me, k)
+        out[0:rows, :] = total_of([keep, taken], block_of(to, rows))
+        out[rows:, :] = tiny[block_of(to, few), :]
+
+
+def total_kernel(*refs):
+    refs[-1][...] = total_of(refs[:-1], slice(None))
+
+
+def grow_kernel(*refs):
+    parts, out = refs[:FOUR], refs[FOUR]
+    few = SMALL // FOUR
+    rows = parts[0].shape[0] - few
+    me = place(1, FOUR)
     for k, ref in enumerate(parts):
         to = lax.bitwise_xor(me, k)
         out[block_of(to, rows), :] = ref[0:rows, :]
-        tails[block_of(to, SMALL), :] = ref[rows:, :]
-    total = tails[0:SMALL, :]
-    for j in range(1, width):
-        total = total + tails[j * SMALL : (j + 1) * SMALL, :]
-    out[width * rows :, :] = total
-
-
-def whole_kernel(shift, width, *refs):
-    parts, out, held = refs[:width], refs[width], refs[width + 1]
-    rows = parts[0].shape[0]
-    me = place(shift, width)
-    for k, ref in enumerate(parts):
-        held[block_of(lax.bitwise_xor(me, k), rows), :] = ref[...]
-    out[...] = total_of([held.at[j * rows : (j + 1) * rows] for j in range(width)], slice(0, rows))
+        out[pl.ds(pl.multiple_of(FOUR * rows + to * few, 8), few), :] = ref[rows:, :]
+
+
+def pair_kernel(mine, theirs, out):
+    rows = mine.shape[0] - SMALL
+    me = place(0, 2)
+    for ref, part in ((mine, me), (theirs, 1 - me)):
+        out[block_of(part, rows), :] = ref[0:rows, :]
+    out[2 * rows :, :] = mine[rows:, :] + theirs[rows:, :]
 
 
 def join_kernel(whole, facing, mix, radial, kinds, out):
@@ -633,6 +657,12 @@
 def shifted(block, axis, by):
     count = lax.axis_size(axis)
     return lax.ppermute(block, axis, [(i, (i + by) % count) for i in range(count)])
+
+
+def exchanged(block, shift, first):
+    count, step = lax.axis_size("domain"), 1 << shift
+    up = [((i >> shift) & 1 == 0) == first for i in range(count)]
+    return lax.ppermute(block, "domain", [(i, (i + step if up[i] else i - step) % count) for i in range(count)])
 
 
 def partner(block, mask):
@@ -656,7 +686,7 @@
     atoms_here = positions.shape[2]
     channels = features.shape[2]
     table = (COMPS * TA, BASIS * TA)
-    sent = (SEND * TA + 16, channels)
+    sent = (SEND * TA + GHOST_ROWS, channels)
     slots = PAIRS * TA
     line = (3, 1, atoms_here)
     turning = [((CHUNK, CHUNK), F32)] * 2
@@ -665,7 +695,7 @@
     ref_forces = ref_forces.transpose(1, 0, 2)
     ints = [((1, n), jnp.int32) for n in (PAIRS, PAIRS, PAIRS, 2 * SEND)]
 
-    to_low, to_high, token = call(
+    to_first, to_second, token = call(
         gather_kernel,
         "gather",
         [sent, sent, (8, CHUNK)],
@@ -679,8 +709,8 @@
         send_tiles, positions, features, ref_forces,
         space=pltpu.HBM,
     )
-    from_low = shifted(to_high, "domain", 1)
-    from_high = shifted(to_low, "domain", -1)
+    from_first = exchanged(to_first, 0, True)
+    from_second = exchanged(to_second, 0, False)
     flags, atoms, own_feat, weights, mh, ml = call(
         stage_kernel,
         "stage",
@@ -703,7 +733,7 @@
     )
 
     factors = (PAIRS, BASIS * TA, channels)
-    env, dinv, gate, curve, inv, rows, fsel, own, grads_up, grads_down, shape_store, xh, xl = call(
+    env, dinv, gate, curve, inv, rows, fsel, own, *leaving, shape_store, xh, xl = call(
         force_kernel,
         "force",
         [
@@ -717,6 +747,8 @@
             (8, atoms_here),
             (8, CHUNK),
             (8, CHUNK),
+            (8, CHUNK),
+            (8, CHUNK),
             (PAIRS, 4 + BASIS, TA, CHUNK),
             (factors, BF16),
             (factors, BF16),
@@ -725,13 +757,11 @@
         + [((PAIRS, *table), BF16)] * 2
         + [((PAIRS, COMPS * TA, channels), BF16)] * 2
         + [((PAIRS * COMPS * TA, channels), F32), ((PAIRS, *table), F32)],
-        flags, atoms, own_feat, weights, mh, ml, from_low, from_high,
+        flags, atoms, own_feat, weights, mh, ml, from_first, from_second,
         flops=1 << 31,
     )
-    low_one = shifted(grads_up, "domain", 1)
-    low_two = shifted(grads_up, "domain", 2)
-    high_one = shifted(grads_down, "domain", -1)
-    high_two = shifted(grads_down, "domain", -2)
+    arriving = [exchanged(leaving[i], i // 2, i % 2 == 0) for i in (0, 2, 1, 3)]
+    arriving = [arriving[i] for i in (0, 2, 1, 3)]
 
     rows_mix = 3 * channels
     total_count = 3.0 * atoms_here * lax.axis_size("domain") * lax.axis_size("batch")
@@ -751,7 +781,7 @@
         + [((PAIRS, *table), BF16)] * 2
         + [((PAIRS * COMPS * TA, channels), F32)]
         + [((2 * slots, 3 * channels), F32), ((2 * slots, channels), F32)],
-        flags, atoms, weights, mh, ml, from_low, from_high, own, low_one, low_two, high_one, high_two,
+        flags, atoms, weights, mh, ml, from_first, from_second, own, *arriving,
         rows, env, gate, curve, inv, shape_store, xh, xl,
         flops=1 << 31,
     )
@@ -769,41 +799,25 @@
             flops=1 << 31,
         )[0]
 
-    bits = lax.axis_size("domain").bit_length() - 1
-    levels = [(shift, 1 << min(LEVEL, bits - shift)) for shift in range(0, bits, LEVEL)]
-    terms = [keep, shifted(give, "batch", 1)]
-    radials = [radial(0, both)]
-    rows_now = rows_mix
-    cut = []
-    for shift, width in levels:
-        if rows_now % (8 * width):
-            break
-        rows_now //= width
-        cut.append((shift, width))
-        blocks = call(
-            functools.partial(spread_kernel, shift, width, len(terms)),
-            "spread", [(rows_now, HALF)] * width, [], *terms,
-        )
-        terms = [blocks[0]] + [partner(blocks[k], k << shift) for k in range(width - 1, 0, -1)]
-        if len(radials) < PAIRS:
-            radials.append(radial(1, blocks[0]))
-    (mine,) = call(
-        functools.partial(tail_kernel, len(terms)),
-        "tail", [(rows_now + SMALL, HALF)], [], *terms, *radials, small,
-    )
-    for shift, width in levels[len(cut) :]:
-        parts = [mine] + [partner(mine, k << shift) for k in range(1, width)]
-        (mine,) = call(
-            functools.partial(whole_kernel, shift, width),
-            "whole", [(rows_now + SMALL, HALF)], [((width * (rows_now + SMALL), HALF), F32)], *parts,
-        )
-    for shift, width in reversed(cut):
-        parts = [mine] + [partner(mine, k << shift) for k in range(1, width)]
-        rows_now *= width
-        (mine,) = call(
-            functools.partial(grow_kernel, shift, width),
-            "grow", [(rows_now + SMALL, HALF)], [((width * SMALL, HALF), F32)], *parts,
-        )
+    keep, give = call(
+        halve_kernel, "halve", [(rows_mix // 2, HALF)] * 2, [], keep, shifted(give, "batch", 1)
+    )
+    taken = partner(give, 1)
+    radials = [radial(p, keep) for p in range(PAIRS)]
+    piece = rows_mix // (2 * FOUR) + SMALL // FOUR
+    blocks = call(
+        spread_kernel, "spread", [(piece, HALF)] * FOUR, [((SMALL, HALF), F32)],
+        keep, taken, *radials, small,
+    )
+    terms = [blocks[0]] + [partner(blocks[k], 2 * k) for k in range(1, FOUR)]
+    (mine,) = call(total_kernel, "total", [(piece, HALF)], [], *terms)
+    bit = 2 * FOUR
+    while bit < lax.axis_size("domain"):
+        (mine,) = call(total_kernel, "total", [(piece, HALF)], [], mine, partner(mine, bit))
+        bit *= 2
+    parts = [mine] + [partner(mine, 2 * k) for k in range(1, FOUR)]
+    (mine,) = call(grow_kernel, "grow", [(rows_mix // 2 + SMALL, HALF)], [], *parts)
+    (mine,) = call(pair_kernel, "pair", [(rows_mix + SMALL, HALF)], [], mine, partner(mine, 1))
     facing = shifted(mine, "batch", 1)
     mix, radial_sum, kinds, out = call(
         join_kernel,

time: 67.8 us -> 64.3 us (0.948)
  starting transfers between devices: 36.4 us -> 23.7 us
  waiting for transfers between devices: 13.2 us -> 22.3 us
    ppermute x8 -> x2, starting transfers between devices: 13 us -> 0.14 us  [shifted(): lax.ppermute(block, axis, [(i, (i + by) % count) for i in range(count)])]
    ppermute x0 -> x6, starting transfers between devices: none -> 11.7 us  [exchanged(): lax.ppermute(block, 'domain', [(i, (i + step if up[i] else i - step) % co...]
    ppermute x14 -> x8, starting transfers between devices: 23.4 us -> 11.9 us  [partner(): lax.ppermute(block, 'domain', [(i, i ^ mask) for i in range(lax.axis_size...]
    ppermute x0 -> x6, waiting for transfers between devices: none -> 7.19 us  [exchanged(): lax.ppermute(block, 'domain', [(i, (i + step if up[i] else i - step) % co...]
    ppermute x14 -> x8, waiting for transfers between devices: 4.59 us -> 11.6 us  [partner(): lax.ppermute(block, 'domain', [(i, i ^ mask) for i in range(lax.axis_size...]
    ppermute x8 -> x2, waiting for transfers between devices: 8.56 us -> 3.44 us  [shifted(): lax.ppermute(block, axis, [(i, (i + by) % count) for i in range(count)])]
    pallas_call x10 -> x12, Pallas kernels: 17.3 us -> 17.5 us  [call(): pl.pallas_call(kernel, name=name, out_shape=[jax.ShapeDtypeStruct(*out) f...]
  transfers between devices with their start and end apart: 22 -> 16, of which waited for: 12 -> 13; matrix products, arithmetic and copies ran while one was open for 0% -> 0% of each run, Pallas kernels for 10% -> 10%
where the time goes in v4:
time: 64.3 us; the launch traced here: 64.1 us
  starting transfers between devices  23.7 us (37%)
  waiting for transfers between devices  22.3 us (35%)
  Pallas kernels  17.5 us (27%)
  between operations  0.72 us (1%)
    pallas_call x12, Pallas kernels, call(): pl.pallas_call(kernel, name=name, out_shape=[jax.ShapeDtypeStruct(*out) f...  17.5 us
    ppermute x8, starting transfers between devices, partner(): lax.ppermute(block, 'domain', [(i, i ^ mask) for i in range(lax.axis_size...  11.9 us
    ppermute x6, starting transfers between devices, exchanged(): lax.ppermute(block, 'domain', [(i, (i + step if up[i] else i - step) % co...  11.7 us
    ppermute x8, waiting for transfers between devices, partner(): lax.ppermute(block, 'domain', [(i, i ^ mask) for i in range(lax.axis_size...  11.6 us
    ppermute x6, waiting for transfers between devices, exchanged(): lax.ppermute(block, 'domain', [(i, (i + step if up[i] else i - step) % co...  7.19 us
    ppermute x2, waiting for transfers between devices, shifted(): lax.ppermute(block, axis, [(i, (i + by) % count) for i in range(count)])  3.44 us
  transfers between devices with their start and end apart: 16, of which 13 were waited for; matrix products, arithmetic and copies ran while one was open for 0% of the time, Pallas kernels for 10%

profile of v4, /device:TPU:0, one launch (start us, length us, event | category | flops | bytes accessed | tf_op | source)
XLA Modules:
  0.0 64.1 jit_solution(10517431960844676440)
XLA Ops:
  0.6 1.2 %gather.1 = (f32[136,256]{1,0:T(8,128)S(1)}, f32[136,256]{1,0:T(8,128)S(1)}, f32[8,128]{1,0:T(8,128)S(1)}) custom-call(s32[1,4]{1,0:T(1,128)} %send.3, f32[3,1,256]{2,1,0:T(1,128)} %bitcast.5, f32[1,256,256]{2,1,0:T(8,128)} %feat.3, f32[3,1,256]{2,1,0:T(1,128)} %bitcast.7), custom_call_target="tpu_custom_call" | custom-call | bytes 1048576 | tf_op jit(solution)/shard_map/gather/pallas_call | solution.py:645
  1.8 3.0 %collective-permute-start = (f32[136,256]{1,0:T(8,128)S(1)}, f32[136,256]{1,0:T(8,128)S(1)}, u32[]{:S(2)}, u32[]{:S(2)}) collective-permute-start(f32[136,256]{1,0:T(8,128)S(1)} %get-tuple-element.52), channel_id=1, source_target_pairs={{0,2},{2,0},{4,6},{6,4},{8,10},{10,8},{12,14},{14,12},{1,3},{3,1},... | collective-permute-start | bytes 417800 | tf_op jit(solution)/shard_map/ppermute | solution.py:665
  4.8 3.5 %collective-permute-start.1 = (f32[136,256]{1,0:T(8,128)S(1)}, f32[136,256]{1,0:T(8,128)S(1)}, u32[]{:S(2)}, u32[]{:S(2)}) collective-permute-start(f32[136,256]{1,0:T(8,128)S(1)} %get-tuple-element.53), channel_id=1, source_target_pairs={{0,14},{2,4},{4,2},{6,8},{8,6},{10,12},{12,10},{14,0},{1,15},{3,5}... | collective-permute-start | bytes 417800 | tf_op jit(solution)/shard_map/ppermute | solution.py:665
  8.4 1.6 %stage.1 = (f32[16,128]{1,0:T(8,128)S(1)}, f32[8,256]{1,0:T(8,128)S(1)}, f32[256,256]{1,0:T(8,128)S(1)}, f32[16,256]{1,0:T(8,128)S(1)}, bf16[768,256]{1,0:T(8,128)(2,1)S(1)}, /*index=5*/bf16[768,256]{1,0:T(8,128)(2,1)S(1)}) custom-call(s32[1,2]{1,0:T(1,128)} %centre.1, s32[1,2]{1,0:T(1,128)} %other.1, s32[1,2]{1,0:T(1,128)} %live.1, s32[1,4]{1,0:T(1,128)} %send.3, ...), custom_call_target="tpu_custom_call" | custom-call | bytes 1048576 | tf_op jit(solution)/shard_map/stage/pallas_call | solution.py:645
  10.0 0.8 %collective-permute-done.from_first = f32[136,256]{1,0:T(8,128)S(1)} collective-permute-done((f32[136,256]{1,0:T(8,128)S(1)}, f32[136,256]{1,0:T(8,128)S(1)}, u32[]{:S(2)}, u32[]{:S(2)}) %collective-permute-start) | collective-permute-done | bytes 139296 | tf_op jit(solution)/shard_map/ppermute | solution.py:665
  10.8 1.9 %collective-permute-done.1.from_second = f32[136,256]{1,0:T(8,128)S(1)} collective-permute-done((f32[136,256]{1,0:T(8,128)S(1)}, f32[136,256]{1,0:T(8,128)S(1)}, u32[]{:S(2)}, u32[]{:S(2)}) %collective-permute-start.1) | collective-permute-done | bytes 139296 | tf_op jit(solution)/shard_map/ppermute | solution.py:665
  12.7 5.1 %force.1 = (f32[1152,256]{1,0:T(8,128)S(1)}, f32[128,768]{1,0:T(8,128)S(1)}, f32[128,256]{1,0:T(8,128)S(1)}, f32[128,256]{1,0:T(8,128)S(1)}, f32[128,768]{1,0:T(...) custom-call(f32[16,128]{1,0:T(8,128)S(1)} %get-tuple-element.47.flag, ...), custom_call_target="tpu_custom_call" | custom-call | flops 2147483648 | bytes 1048576 | tf_op jit(solution)/shard_map/force/pallas_call | solution.py:645
  17.8 0.6 collective-permute-start.2
  18.4 3.5 %collective-permute-start.3 = (f32[8,128]{1,0:T(8,128)S(1)}, f32[8,128]{1,0:T(8,128)S(1)}, u32[]{:S(2)}, u32[]{:S(2)}) collective-permute-start(f32[8,128]{1,0:T(8,128)S(1)} %get-tuple-element.57), channel_id=1, source_target_pairs={{0,14},{2,4},{4,2},{6,8},{8,6},{10,12},{12,10},{14,0},{1,15},{3,5}... | collective-permute-start | bytes 12296 | tf_op jit(solution)/shard_map/ppermute | solution.py:665
  22.0 0.9 %collective-permute-start.5 = (f32[8,128]{1,0:T(8,128)S(1)}, f32[8,128]{1,0:T(8,128)S(1)}, u32[]{:S(2)}, u32[]{:S(2)}) collective-permute-start(f32[8,128]{1,0:T(8,128)S(1)} %get-tuple-element.59), channel_id=1, source_target_pairs={{0,12},{2,14},{4,8},{6,10},{8,4},{10,6},{12,0},{14,2},{1,13},{3,15... | collective-permute-start | bytes 12296 | tf_op jit(solution)/shard_map/ppermute | solution.py:665
  22.9 1.9 %collective-permute-done.3.one_second = f32[8,128]{1,0:T(8,128)S(1)} collective-permute-done((f32[8,128]{1,0:T(8,128)S(1)}, f32[8,128]{1,0:T(8,128)S(1)}, u32[]{:S(2)}, u32[]{:S(2)}) %collective-permute-start.3) | collective-permute-done | bytes 4128 | tf_op jit(solution)/shard_map/ppermute | solution.py:665
  24.7 0.8 %collective-permute-done.4.two_first = f32[8,128]{1,0:T(8,128)S(1)} collective-permute-done((f32[8,128]{1,0:T(8,128)S(1)}, f32[8,128]{1,0:T(8,128)S(1)}, u32[]{:S(2)}, u32[]{:S(2)}) %collective-permute-start.4) | collective-permute-done | bytes 4128 | tf_op jit(solution)/shard_map/ppermute | solution.py:665
  25.6 1.8 %collective-permute-done.5.two_second = f32[8,128]{1,0:T(8,128)S(1)} collective-permute-done((f32[8,128]{1,0:T(8,128)S(1)}, f32[8,128]{1,0:T(8,128)S(1)}, u32[]{:S(2)}, u32[]{:S(2)}) %collective-permute-start.5) | collective-permute-done | bytes 4128 | tf_op jit(solution)/shard_map/ppermute | solution.py:665
  27.4 3.4 %tangent.1 = (f32[3,1,256]{2,1,0:T(1,128)}, f32[768,128]{1,0:T(8,128)S(1)}, f32[768,128]{1,0:T(8,128)S(1)}, f32[8,256]{1,0:T(8,128)S(1)}, f32[1152,256]{1,0:T(8,...) custom-call(f32[16,128]{1,0:T(8,128)S(1)} %get-tuple-element.47.flags, f32[8,256]{1,0:T(8,128)S(1)} %get-tuple-element.48.atoms, ...), custom_call_target="tpu_custom_call" | custom-call | flops 2147483648 | bytes 1048576 | tf_op jit(solution)/shard_map/tangent/pallas_call | solution.py:645
  30.9 1.7 %collective-permute-done.6.taken = f32[768,128]{1,0:T(8,128)S(1)} collective-permute-done((f32[768,128]{1,0:T(8,128)S(1)}, f32[768,128]{1,0:T(8,128)S(1)}, u32[]{:S(2)}, u32[]{:S(2)}) %collective-permute-start.6) | collective-permute-done | bytes 393248 | tf_op jit(solution)/shard_map/ppermute | solution.py:659
  32.7 1.1 %collective-permute-start.7 = (f32[384,128]{1,0:T(8,128)S(1)}, f32[384,128]{1,0:T(8,128)S(1)}, u32[]{:S(2)}, u32[]{:S(2)}) collective-permute-start(f32[384,128]{1,0:T(8,128)S(1)} %get-tuple-element.72), channel_id=1, source_target_pairs={{0,2},{2,0},{4,6},{6,4},{8,10},{10,8},{12,14},{14,12},{1,3},{3,1},... | collective-permute-start | bytes 589832 | tf_op jit(solution)/shard_map/ppermute | solution.py:669
  33.8 2.5 %radial.3.radial_1 = f32[8,256]{1,0:T(8,128)S(1)} custom-call(f32[16,128]{1,0:T(8,128)S(1)} %get-tuple-element.47.flags, f32[16,128]{1,0:T(8,128)S(1)} %get-tuple-element.73.both, f32[128,256]{1,0:T(8,128)S(1)} %get-tuple-element.74.fsel, f32[1152,256]{1,0:T(8,128)S(1)} %get-tuple-element.61.env, f32[1152,256]{1,0:T(8,128)S(1)} %get-tuple-element.75.envdot, ...), custom_call_target="tpu_custom_call" | custom-call | flops 2147483648 | bytes 1048576 | tf_op jit(solution)/shard_map/radial/pallas_call | solution.py:645
  36.3 2.5 %radial.2.radial_0 = f32[8,256]{1,0:T(8,128)S(1)} custom-call(f32[16,128]{1,0:T(8,128)S(1)} %get-tuple-element.47.flags, f32[16,128]{1,0:T(8,128)S(1)} %get-tuple-element.73.both, f32[128,256]{1,0:T(8,128)S(1)} %get-tuple-element.74.fsel, f32[1152,256]{1,0:T(8,128)S(1)} %get-tuple-element.61.env, f32[1152,256]{1,0:T(8,128)S(1)} %get-tuple-element.75.envdot, ...), custom_call_target="tpu_custom_call" | custom-call | flops 2147483648 | bytes 1048576 | tf_op jit(solution)/shard_map/radial/pallas_call | solution.py:645
  38.8 0.8 %collective-permute-done.7.taken = f32[384,128]{1,0:T(8,128)S(1)} collective-permute-done((f32[384,128]{1,0:T(8,128)S(1)}, f32[384,128]{1,0:T(8,128)S(1)}, u32[]{:S(2)}, u32[]{:S(2)}) %collective-permute-start.7) | collective-permute-done | bytes 196640 | tf_op jit(solution)/shard_map/ppermute | solution.py:669
  39.7 0.3 collective-permute-start.8
  40.0 2.1 %collective-permute-start.9 = (f32[104,128]{1,0:T(8,128)S(1)}, f32[104,128]{1,0:T(8,128)S(1)}, u32[]{:S(2)}, u32[]{:S(2)}) collective-permute-start(f32[104,128]{1,0:T(8,128)S(1)} %get-tuple-element.81), channel_id=1, source_target_pairs={{0,8},{2,10},{4,12},{6,14},{8,0},{10,2},{12,4},{14,6},{1,9},{3,11}... | collective-permute-start | bytes 159752 | tf_op jit(solution)/shard_map/ppermute | solution.py:669
  42.2 2.0 %collective-permute-start.10 = (f32[104,128]{1,0:T(8,128)S(1)}, f32[104,128]{1,0:T(8,128)S(1)}, u32[]{:S(2)}, u32[]{:S(2)}) collective-permute-start(f32[104,128]{1,0:T(8,128)S(1)} %get-tuple-element.82), channel_id=1, source_target_pairs={{0,12},{2,14},{4,8},{6,10},{8,4},{10,6},{12,0},{14,2},{1,13},{3,15... | collective-permute-start | bytes 159752 | tf_op jit(solution)/shard_map/ppermute | solution.py:669
  44.2 1.2 %collective-permute-done.9.refs_2_ = f32[104,128]{1,0:T(8,128)S(1)} collective-permute-done((f32[104,128]{1,0:T(8,128)S(1)}, f32[104,128]{1,0:T(8,128)S(1)}, u32[]{:S(2)}, u32[]{:S(2)}) %collective-permute-start.9) | collective-permute-done | bytes 53280 | tf_op jit(solution)/shard_map/ppermute | solution.py:669
  45.4 2.7 %collective-permute-done.10.refs_3_ = f32[104,128]{1,0:T(8,128)S(1)} collective-permute-done((f32[104,128]{1,0:T(8,128)S(1)}, f32[104,128]{1,0:T(8,128)S(1)}, u32[]{:S(2)}, u32[]{:S(2)}) %collective-permute-start.10) | collective-permute-done | bytes 53280 | tf_op jit(solution)/shard_map/ppermute | solution.py:669
  48.2 2.2 %collective-permute-start.13 = (f32[104,128]{1,0:T(8,128)S(1)}, f32[104,128]{1,0:T(8,128)S(1)}, u32[]{:S(2)}, u32[]{:S(2)}) collective-permute-start(f32[104,128]{1,0:T(8,128)S(1)} %total.1.refs_0_), channel_id=1, source_target_pairs={{0,12},{2,14},{4,8},{6,10},{8,4},{10,6},{12,0},{14,2},{1,13},{3,15... | collective-permute-start | bytes 159752 | tf_op jit(solution)/shard_map/ppermute | solution.py:669
  50.3 2.3 %collective-permute-start.11 = (f32[104,128]{1,0:T(8,128)S(1)}, f32[104,128]{1,0:T(8,128)S(1)}, u32[]{:S(2)}, u32[]{:S(2)}) collective-permute-start(f32[104,128]{1,0:T(8,128)S(1)} %total.1.refs_0_), channel_id=1, source_target_pairs={{0,4},{2,6},{4,0},{6,2},{8,12},{10,14},{12,8},{14,10},{1,5},{3,7},... | collective-permute-start | bytes 159752 | tf_op jit(solution)/shard_map/ppermute | solution.py:669
  52.6 1.5 %collective-permute-done.13.refs_3_ = f32[104,128]{1,0:T(8,128)S(1)} collective-permute-done((f32[104,128]{1,0:T(8,128)S(1)}, f32[104,128]{1,0:T(8,128)S(1)}, u32[]{:S(2)}, u32[]{:S(2)}) %collective-permute-start.13) | collective-permute-done | bytes 53280 | tf_op jit(solution)/shard_map/ppermute | solution.py:669
  54.1 1.2 %collective-permute-done.12.refs_2_ = f32[104,128]{1,0:T(8,128)S(1)} collective-permute-done((f32[104,128]{1,0:T(8,128)S(1)}, f32[104,128]{1,0:T(8,128)S(1)}, u32[]{:S(2)}, u32[]{:S(2)}) %collective-permute-start.12) | collective-permute-done | bytes 53280 | tf_op jit(solution)/shard_map/ppermute | solution.py:669
  55.4 1.8 %collective-permute-start.14 = (f32[416,128]{1,0:T(8,128)S(1)}, f32[416,128]{1,0:T(8,128)S(1)}, u32[]{:S(2)}, u32[]{:S(2)}) collective-permute-start(f32[416,128]{1,0:T(8,128)S(1)} %grow.1.mine), channel_id=1, source_target_pairs={{0,2},{2,0},{4,6},{6,4},{8,10},{10,8},{12,14},{14,12},{1,3},{3,1},... | collective-permute-start | bytes 638984 | tf_op jit(solution)/shard_map/ppermute | solution.py:669
  57.2 4.1 %collective-permute-done.14.theirs = f32[416,128]{1,0:T(8,128)S(1)} collective-permute-done((f32[416,128]{1,0:T(8,128)S(1)}, f32[416,128]{1,0:T(8,128)S(1)}, u32[]{:S(2)}, u32[]{:S(2)}) %collective-permute-start.14) | collective-permute-done | bytes 213024 | tf_op jit(solution)/shard_map/ppermute | solution.py:669
  61.4 1.7 %collective-permute-done.15.facing = f32[800,128]{1,0:T(8,128)S(1)} collective-permute-done((f32[800,128]{1,0:T(8,128)S(1)}, f32[800,128]{1,0:T(8,128)S(1)}, u32[]{:S(2)}, u32[]{:S(2)}) %collective-permute-start.15) | collective-permute-done | bytes 409632 | tf_op jit(solution)/shard_map/ppermute | solution.py:659
  63.1 1.0 %join.1 = (f32[768,256]{1,0:T(8,128)}, f32[8,256]{1,0:T(8,128)}, f32[4,256]{1,0:T(4,128)}, f32[1,256]{1,0:T(1,128)}) custom-call(f32[800,128]{1,0:T(8,128)S(1)} %pair.1.whole, f32[800,128]{1,0:T(8,128)S(1)} %collective-permute-done.15.facing), custom_call_target="tpu_custom_call" | custom-call | bytes 1048576 | tf_op jit(solution)/shard_map/join/pallas_call | solution.py:645
  (12 shorter events, 0.3 us)
Async XLA Ops:
  1.8 8.9 %collective-permute-start = (f32[136,256]{1,0:T(8,128)S(1)}, f32[136,256]{1,0:T(8,128)S(1)}, u32[]{:S(2)}, u32[]{:S(2)}) collective-permute-start(f32[136,256]{1,0:T(8,128)S(1)} %get-tuple-element.52), channel_id=1, source_target_pairs={{0,2},{2,0},{4,6},{6,4},{8,10},{10,8},{12,14},{14,12},{1,3},{3,1},... | collective-permute-start | bytes 417800 | tf_op jit(solution)/shard_map/ppermute | solution.py:665
  4.8 7.8 %collective-permute-start.1 = (f32[136,256]{1,0:T(8,128)S(1)}, f32[136,256]{1,0:T(8,128)S(1)}, u32[]{:S(2)}, u32[]{:S(2)}) collective-permute-start(f32[136,256]{1,0:T(8,128)S(1)} %get-tuple-element.53), channel_id=1, source_target_pairs={{0,14},{2,4},{4,2},{6,8},{8,6},{10,12},{12,10},{14,0},{1,15},{3,5}... | collective-permute-start | bytes 417800 | tf_op jit(solution)/shard_map/ppermute | solution.py:665
  17.8 5.1 %collective-permute-start.2 = (f32[8,128]{1,0:T(8,128)S(1)}, f32[8,128]{1,0:T(8,128)S(1)}, u32[]{:S(2)}, u32[]{:S(2)}) collective-permute-start(f32[8,128]{1,0:T(8,128)S(1)} %get-tuple-element.56), channel_id=1, source_target_pairs={{0,2},{2,0},{4,6},{6,4},{8,10},{10,8},{12,14},{14,12},{1,3},{3,1},... | collective-permute-start | bytes 12296 | tf_op jit(solution)/shard_map/ppermute | solution.py:665
  18.4 6.3 %collective-permute-start.3 = (f32[8,128]{1,0:T(8,128)S(1)}, f32[8,128]{1,0:T(8,128)S(1)}, u32[]{:S(2)}, u32[]{:S(2)}) collective-permute-start(f32[8,128]{1,0:T(8,128)S(1)} %get-tuple-element.57), channel_id=1, source_target_pairs={{0,14},{2,4},{4,2},{6,8},{8,6},{10,12},{12,10},{14,0},{1,15},{3,5}... | collective-permute-start | bytes 12296 | tf_op jit(solution)/shard_map/ppermute | solution.py:665
  22.0 3.6 %collective-permute-start.4 = (f32[8,128]{1,0:T(8,128)S(1)}, f32[8,128]{1,0:T(8,128)S(1)}, u32[]{:S(2)}, u32[]{:S(2)}) collective-permute-start(f32[8,128]{1,0:T(8,128)S(1)} %get-tuple-element.58), channel_id=1, source_target_pairs={{0,4},{2,6},{4,0},{6,2},{8,12},{10,14},{12,8},{14,10},{1,5},{3,7},... | collective-permute-start | bytes 12296 | tf_op jit(solution)/shard_map/ppermute | solution.py:665
  22.0 5.4 %collective-permute-start.5 = (f32[8,128]{1,0:T(8,128)S(1)}, f32[8,128]{1,0:T(8,128)S(1)}, u32[]{:S(2)}, u32[]{:S(2)}) collective-permute-start(f32[8,128]{1,0:T(8,128)S(1)} %get-tuple-element.59), channel_id=1, source_target_pairs={{0,12},{2,14},{4,8},{6,10},{8,4},{10,6},{12,0},{14,2},{1,13},{3,15... | collective-permute-start | bytes 12296 | tf_op jit(solution)/shard_map/ppermute | solution.py:665
  30.8 1.8 %collective-permute-start.6 = (f32[768,128]{1,0:T(8,128)S(1)}, f32[768,128]{1,0:T(8,128)S(1)}, u32[]{:S(2)}, u32[]{:S(2)}) collective-permute-start(f32[768,128]{1,0:T(8,128)S(1)} %get-tuple-element.70), channel_id=1, source_target_pairs={{0,1},{1,0},{2,3},{3,2},{4,5},{5,4},{6,7},{7,6},{8,9},{9,8},{10,11... | collective-permute-start | bytes 1179656 | tf_op jit(solution)/shard_map/ppermute | solution.py:659
  32.7 7.0 %collective-permute-start.7 = (f32[384,128]{1,0:T(8,128)S(1)}, f32[384,128]{1,0:T(8,128)S(1)}, u32[]{:S(2)}, u32[]{:S(2)}) collective-permute-start(f32[384,128]{1,0:T(8,128)S(1)} %get-tuple-element.72), channel_id=1, source_target_pairs={{0,2},{2,0},{4,6},{6,4},{8,10},{10,8},{12,14},{14,12},{1,3},{3,1},... | collective-permute-start | bytes 589832 | tf_op jit(solution)/shard_map/ppermute | solution.py:669
  39.7 4.5 %collective-permute-start.8 = (f32[104,128]{1,0:T(8,128)S(1)}, f32[104,128]{1,0:T(8,128)S(1)}, u32[]{:S(2)}, u32[]{:S(2)}) collective-permute-start(f32[104,128]{1,0:T(8,128)S(1)} %get-tuple-element.80), channel_id=1, source_target_pairs={{0,4},{2,6},{4,0},{6,2},{8,12},{10,14},{12,8},{14,10},{1,5},{3,7},... | collective-permute-start | bytes 159752 | tf_op jit(solution)/shard_map/ppermute | solution.py:669
  40.0 5.4 %collective-permute-start.9 = (f32[104,128]{1,0:T(8,128)S(1)}, f32[104,128]{1,0:T(8,128)S(1)}, u32[]{:S(2)}, u32[]{:S(2)}) collective-permute-start(f32[104,128]{1,0:T(8,128)S(1)} %get-tuple-element.81), channel_id=1, source_target_pairs={{0,8},{2,10},{4,12},{6,14},{8,0},{10,2},{12,4},{14,6},{1,9},{3,11}... | collective-permute-start | bytes 159752 | tf_op jit(solution)/shard_map/ppermute | solution.py:669
  42.2 6.0 %collective-permute-start.10 = (f32[104,128]{1,0:T(8,128)S(1)}, f32[104,128]{1,0:T(8,128)S(1)}, u32[]{:S(2)}, u32[]{:S(2)}) collective-permute-start(f32[104,128]{1,0:T(8,128)S(1)} %get-tuple-element.82), channel_id=1, source_target_pairs={{0,12},{2,14},{4,8},{6,10},{8,4},{10,6},{12,0},{14,2},{1,13},{3,15... | collective-permute-start | bytes 159752 | tf_op jit(solution)/shard_map/ppermute | solution.py:669
  48.2 6.0 %collective-permute-start.13 = (f32[104,128]{1,0:T(8,128)S(1)}, f32[104,128]{1,0:T(8,128)S(1)}, u32[]{:S(2)}, u32[]{:S(2)}) collective-permute-start(f32[104,128]{1,0:T(8,128)S(1)} %total.1.refs_0_), channel_id=1, source_target_pairs={{0,12},{2,14},{4,8},{6,10},{8,4},{10,6},{12,0},{14,2},{1,13},{3,15... | collective-permute-start | bytes 159752 | tf_op jit(solution)/shard_map/ppermute | solution.py:669
  50.3 5.0 %collective-permute-start.12 = (f32[104,128]{1,0:T(8,128)S(1)}, f32[104,128]{1,0:T(8,128)S(1)}, u32[]{:S(2)}, u32[]{:S(2)}) collective-permute-start(f32[104,128]{1,0:T(8,128)S(1)} %total.1.refs_0_), channel_id=1, source_target_pairs={{0,8},{2,10},{4,12},{6,14},{8,0},{10,2},{12,4},{14,6},{1,9},{3,11}... | collective-permute-start | bytes 159752 | tf_op jit(solution)/shard_map/ppermute | solution.py:669
  50.3 5.0 %collective-permute-start.11 = (f32[104,128]{1,0:T(8,128)S(1)}, f32[104,128]{1,0:T(8,128)S(1)}, u32[]{:S(2)}, u32[]{:S(2)}) collective-permute-start(f32[104,128]{1,0:T(8,128)S(1)} %total.1.refs_0_), channel_id=1, source_target_pairs={{0,4},{2,6},{4,0},{6,2},{8,12},{10,14},{12,8},{14,10},{1,5},{3,7},... | collective-permute-start | bytes 159752 | tf_op jit(solution)/shard_map/ppermute | solution.py:669
  55.4 5.9 %collective-permute-start.14 = (f32[416,128]{1,0:T(8,128)S(1)}, f32[416,128]{1,0:T(8,128)S(1)}, u32[]{:S(2)}, u32[]{:S(2)}) collective-permute-start(f32[416,128]{1,0:T(8,128)S(1)} %grow.1.mine), channel_id=1, source_target_pairs={{0,2},{2,0},{4,6},{6,4},{8,10},{10,8},{12,14},{14,12},{1,3},{3,1},... | collective-permute-start | bytes 638984 | tf_op jit(solution)/shard_map/ppermute | solution.py:669
  61.3 1.8 %collective-permute-start.15 = (f32[800,128]{1,0:T(8,128)S(1)}, f32[800,128]{1,0:T(8,128)S(1)}, u32[]{:S(2)}, u32[]{:S(2)}) collective-permute-start(f32[800,128]{1,0:T(8,128)S(1)} %pair.1.whole), channel_id=1, source_target_pairs={{0,1},{1,0},{2,3},{3,2},{4,5},{5,4},{6,7},{7,6},{8,9},{9,8},{10,11... | collective-permute-start | bytes 1228808 | tf_op jit(solution)/shard_map/ppermute | solution.py:659

commit v5 on v4

--- a/solution.py
+++ b/solution.py
@@ -196,7 +196,7 @@
     return first * choice + second * (1.0 - choice)
 
 
-def gather_kernel(send, pos, feat, ref, to_first, to_second, token, send_v, pos_v, feat_v, ref_v, sems):
+def gather_kernel(send, pos, feat, ref, to_second, to_first, token, send_v, pos_v, feat_v, ref_v, sems):
     copies = fetch([(send, send_v), (pos, pos_v), (ref, ref_v), (feat, feat_v)], sems)
     for copy in copies[:3]:
         copy.wait()
@@ -277,7 +277,7 @@
 
 
 def force_kernel(
-    flags, atoms, feat, weights, mh, ml, from_first, from_second,
+    flags, atoms, feat, weights, mh, ml, from_second, from_first,
     env, dinv, gate, curve, inv, rows, fsel, own, one_first, one_second, two_first, two_second, shape_store, xh, xl,
     square, turned, th, tl, eh, el, raw, back,
 ):
@@ -411,7 +411,7 @@
 
 
 def tangent_kernel(
-    scale, flags, atoms, weights, mh, ml, from_first, from_second, own, one_first, one_second, two_first, two_second,
+    scale, flags, atoms, weights, mh, ml, from_first, from_second, own, one_second, two_second, one_first, two_first,
     rows, env, gate, curve, inv, shape_store, xh, xl,
     forces, keep, give, small, envdot, curl, both,
     square, turned, th, tl, raw, left, right,
@@ -571,6 +571,10 @@
     return pl.ds(pl.multiple_of(part * rows, 8), rows)
 
 
+def block_of_lanes(part):
+    return pl.ds(pl.multiple_of(part * HALF, HALF), HALF)
+
+
 def total_of(refs, at):
     total = refs[0][at, :]
     for ref in refs[1:]:
@@ -613,25 +617,20 @@
         out[pl.ds(pl.multiple_of(FOUR * rows + to * few, 8), few), :] = ref[rows:, :]
 
 
-def pair_kernel(mine, theirs, out):
+def join_kernel(mine, theirs, facing_mine, facing_theirs, mix, radial, kinds, out):
     rows = mine.shape[0] - SMALL
-    me = place(0, 2)
-    for ref, part in ((mine, me), (theirs, 1 - me)):
-        out[block_of(part, rows), :] = ref[0:rows, :]
-    out[2 * rows :, :] = mine[rows:, :] + theirs[rows:, :]
-
-
-def join_kernel(whole, facing, mix, radial, kinds, out):
-    rows = mix.shape[0]
-    core = lax.axis_index("batch")
-    for ref, part in ((whole, core), (facing, 1 - core)):
-        mix[:, pl.ds(pl.multiple_of(part * HALF, HALF), HALF)] = ref[0:rows, :]
+    me, core = place(0, 2), lax.axis_index("batch")
+    for lane_part, pair in ((core, (mine, theirs)), (1 - core, (facing_mine, facing_theirs))):
+        lanes = block_of_lanes(lane_part)
+        for ref, part in zip(pair, (me, 1 - me)):
+            mix[block_of(part, rows), lanes] = ref[0:rows, :]
+    both = (mine[rows:, :] + theirs[rows:, :]) + (facing_mine[rows:, :] + facing_theirs[rows:, :])
     for h in range(2):
         lanes = slice(h * HALF, (h + 1) * HALF)
-        both = whole[rows + 16 * h : rows + 16 * h + 16, :] + facing[rows + 16 * h : rows + 16 * h + 16, :]
-        radial[:, lanes] = both[0:BASIS]
-        kinds[:, lanes] = both[BASIS : BASIS + SPECIES]
-        out[:, lanes] = both[BASIS + SPECIES : BASIS + SPECIES + 1]
+        few = both[16 * h : 16 * h + 16, :]
+        radial[:, lanes] = few[0:BASIS]
+        kinds[:, lanes] = few[BASIS : BASIS + SPECIES]
+        out[:, lanes] = few[BASIS + SPECIES : BASIS + SPECIES + 1]
 
 
 def spec(space):
@@ -695,7 +694,7 @@
     ref_forces = ref_forces.transpose(1, 0, 2)
     ints = [((1, n), jnp.int32) for n in (PAIRS, PAIRS, PAIRS, 2 * SEND)]
 
-    to_first, to_second, token = call(
+    to_second, to_first, token = call(
         gather_kernel,
         "gather",
         [sent, sent, (8, CHUNK)],
@@ -709,8 +708,8 @@
         send_tiles, positions, features, ref_forces,
         space=pltpu.HBM,
     )
+    from_second = exchanged(to_second, 0, False)
     from_first = exchanged(to_first, 0, True)
-    from_second = exchanged(to_second, 0, False)
     flags, atoms, own_feat, weights, mh, ml = call(
         stage_kernel,
         "stage",
@@ -757,11 +756,10 @@
         + [((PAIRS, *table), BF16)] * 2
         + [((PAIRS, COMPS * TA, channels), BF16)] * 2
         + [((PAIRS * COMPS * TA, channels), F32), ((PAIRS, *table), F32)],
-        flags, atoms, own_feat, weights, mh, ml, from_first, from_second,
+        flags, atoms, own_feat, weights, mh, ml, from_second, from_first,
         flops=1 << 31,
     )
-    arriving = [exchanged(leaving[i], i // 2, i % 2 == 0) for i in (0, 2, 1, 3)]
-    arriving = [arriving[i] for i in (0, 2, 1, 3)]
+    arriving = [exchanged(leaving[i], i // 2, i % 2 == 0) for i in (1, 3, 0, 2)]
 
     rows_mix = 3 * channels
     total_count = 3.0 * atoms_here * lax.axis_size("domain") * lax.axis_size("batch")
@@ -809,7 +807,7 @@
         spread_kernel, "spread", [(piece, HALF)] * FOUR, [((SMALL, HALF), F32)],
         keep, taken, *radials, small,
     )
-    terms = [blocks[0]] + [partner(blocks[k], 2 * k) for k in range(1, FOUR)]
+    terms = [blocks[0]] + [partner(blocks[k], 2 * k) for k in range(FOUR - 1, 0, -1)]
     (mine,) = call(total_kernel, "total", [(piece, HALF)], [], *terms)
     bit = 2 * FOUR
     while bit < lax.axis_size("domain"):
@@ -817,15 +815,16 @@
         bit *= 2
     parts = [mine] + [partner(mine, 2 * k) for k in range(1, FOUR)]
     (mine,) = call(grow_kernel, "grow", [(rows_mix // 2 + SMALL, HALF)], [], *parts)
-    (mine,) = call(pair_kernel, "pair", [(rows_mix + SMALL, HALF)], [], mine, partner(mine, 1))
-    facing = shifted(mine, "batch", 1)
+    theirs = partner(mine, 1)
+    facing = [shifted(part, "batch", 1) for part in (mine, theirs)]
     mix, radial_sum, kinds, out = call(
         join_kernel,
         "join",
         [(rows_mix, channels), (BASIS, channels), (SPECIES, channels), (1, channels)],
         [],
         mine,
-        facing,
+        theirs,
+        *facing,
     )
     return forces.transpose(1, 0, 2), radial_sum, mix, kinds, out.reshape(channels)
 

time: 64.3 us -> 64.4 us (level)
  waiting for transfers between devices: 22.3 us -> 23.3 us
  starting transfers between devices: 23.7 us -> 22.8 us
    ppermute x8, waiting for transfers between devices: 11.6 us -> 13.7 us  [partner(): lax.ppermute(block, 'domain', [(i, i ^ mask) for i in range(lax.axis_size...]
    ppermute x8, starting transfers between devices: 11.9 us -> 10.8 us  [partner(): lax.ppermute(block, 'domain', [(i, i ^ mask) for i in range(lax.axis_size...]
    ppermute x6, waiting for transfers between devices: 7.19 us -> 6.41 us  [exchanged(): lax.ppermute(block, 'domain', [(i, (i + step if up[i] else i - step) % co...]
    ppermute x2 -> x3, waiting for transfers between devices: 3.44 us -> 3.17 us  [shifted(): lax.ppermute(block, axis, [(i, (i + by) % count) for i in range(count)])]
    pallas_call x12 -> x11, Pallas kernels: 17.5 us -> 17.4 us  [call(): pl.pallas_call(kernel, name=name, out_shape=[jax.ShapeDtypeStruct(*out) f...]
  transfers between devices with their start and end apart: 16 -> 17, of which waited for: 13 -> 12; matrix products, arithmetic and copies ran while one was open for 0% -> 0% of each run, Pallas kernels for 10% -> 10%
where the time goes in v5:
time: 64.4 us; the launch traced here: 64.2 us
  waiting for transfers between devices  23.3 us (36%)
  starting transfers between devices  22.8 us (35%)
  Pallas kernels  17.4 us (27%)
  between operations  0.71 us (1%)
    pallas_call x11, Pallas kernels, call(): pl.pallas_call(kernel, name=name, out_shape=[jax.ShapeDtypeStruct(*out) f...  17.4 us
    ppermute x8, waiting for transfers between devices, partner(): lax.ppermute(block, 'domain', [(i, i ^ mask) for i in range(lax.axis_size...  13.7 us
    ppermute x6, starting transfers between devices, exchanged(): lax.ppermute(block, 'domain', [(i, (i + step if up[i] else i - step) % co...  11.9 us
    ppermute x8, starting transfers between devices, partner(): lax.ppermute(block, 'domain', [(i, i ^ mask) for i in range(lax.axis_size...  10.8 us
    ppermute x6, waiting for transfers between devices, exchanged(): lax.ppermute(block, 'domain', [(i, (i + step if up[i] else i - step) % co...  6.41 us
    ppermute x3, waiting for transfers between devices, shifted(): lax.ppermute(block, axis, [(i, (i + by) % count) for i in range(count)])  3.17 us
  transfers between devices with their start and end apart: 17, of which 12 were waited for; matrix products, arithmetic and copies ran while one was open for 0% of the time, Pallas kernels for 10%

profile of v5, /device:TPU:0, one launch (start us, length us, event | category | flops | bytes accessed | tf_op | source)
XLA Modules:
  0.0 64.2 jit_solution(16203886068143614820)
XLA Ops:
  0.6 1.2 %gather.1 = (f32[136,256]{1,0:T(8,128)S(1)}, f32[136,256]{1,0:T(8,128)S(1)}, f32[8,128]{1,0:T(8,128)S(1)}) custom-call(s32[1,4]{1,0:T(1,128)} %send.3, f32[3,1,256]{2,1,0:T(1,128)} %bitcast.5, f32[1,256,256]{2,1,0:T(8,128)} %feat.3, f32[3,1,256]{2,1,0:T(1,128)} %bitcast.7), custom_call_target="tpu_custom_call" | custom-call | bytes 1048576 | tf_op jit(solution)/shard_map/gather/pallas_call | solution.py:644
  1.8 3.0 %collective-permute-start = (f32[136,256]{1,0:T(8,128)S(1)}, f32[136,256]{1,0:T(8,128)S(1)}, u32[]{:S(2)}, u32[]{:S(2)}) collective-permute-start(f32[136,256]{1,0:T(8,128)S(1)} %get-tuple-element.52), channel_id=1, source_target_pairs={{0,2},{2,0},{4,6},{6,4},{8,10},{10,8},{12,14},{14,12},{1,3},{3,1},... | collective-permute-start | bytes 417800 | tf_op jit(solution)/shard_map/ppermute | solution.py:664
  4.8 3.5 %collective-permute-start.1 = (f32[136,256]{1,0:T(8,128)S(1)}, f32[136,256]{1,0:T(8,128)S(1)}, u32[]{:S(2)}, u32[]{:S(2)}) collective-permute-start(f32[136,256]{1,0:T(8,128)S(1)} %get-tuple-element.53), channel_id=1, source_target_pairs={{0,14},{2,4},{4,2},{6,8},{8,6},{10,12},{12,10},{14,0},{1,15},{3,5}... | collective-permute-start | bytes 417800 | tf_op jit(solution)/shard_map/ppermute | solution.py:664
  8.4 1.6 %stage.1 = (f32[16,128]{1,0:T(8,128)S(1)}, f32[8,256]{1,0:T(8,128)S(1)}, f32[256,256]{1,0:T(8,128)S(1)}, f32[16,256]{1,0:T(8,128)S(1)}, bf16[768,256]{1,0:T(8,128)(2,1)S(1)}, /*index=5*/bf16[768,256]{1,0:T(8,128)(2,1)S(1)}) custom-call(s32[1,2]{1,0:T(1,128)} %centre.1, s32[1,2]{1,0:T(1,128)} %other.1, s32[1,2]{1,0:T(1,128)} %live.1, s32[1,4]{1,0:T(1,128)} %send.3, ...), custom_call_target="tpu_custom_call" | custom-call | bytes 1048576 | tf_op jit(solution)/shard_map/stage/pallas_call | solution.py:644
  10.0 0.8 %collective-permute-done.from_first = f32[136,256]{1,0:T(8,128)S(1)} collective-permute-done((f32[136,256]{1,0:T(8,128)S(1)}, f32[136,256]{1,0:T(8,128)S(1)}, u32[]{:S(2)}, u32[]{:S(2)}) %collective-permute-start) | collective-permute-done | bytes 139296 | tf_op jit(solution)/shard_map/ppermute | solution.py:664
  10.8 1.9 %collective-permute-done.1.from_second = f32[136,256]{1,0:T(8,128)S(1)} collective-permute-done((f32[136,256]{1,0:T(8,128)S(1)}, f32[136,256]{1,0:T(8,128)S(1)}, u32[]{:S(2)}, u32[]{:S(2)}) %collective-permute-start.1) | collective-permute-done | bytes 139296 | tf_op jit(solution)/shard_map/ppermute | solution.py:664
  12.7 5.1 %force.1 = (f32[1152,256]{1,0:T(8,128)S(1)}, f32[128,768]{1,0:T(8,128)S(1)}, f32[128,256]{1,0:T(8,128)S(1)}, f32[128,256]{1,0:T(8,128)S(1)}, f32[128,768]{1,0:T(...) custom-call(f32[16,128]{1,0:T(8,128)S(1)} %get-tuple-element.47.flag, ...), custom_call_target="tpu_custom_call" | custom-call | flops 2147483648 | bytes 1048576 | tf_op jit(solution)/shard_map/force/pallas_call | solution.py:644
  17.8 3.7 %collective-permute-start.2 = (f32[8,128]{1,0:T(8,128)S(1)}, f32[8,128]{1,0:T(8,128)S(1)}, u32[]{:S(2)}, u32[]{:S(2)}) collective-permute-start(f32[8,128]{1,0:T(8,128)S(1)} %get-tuple-element.56), channel_id=1, source_target_pairs={{0,14},{2,4},{4,2},{6,8},{8,6},{10,12},{12,10},{14,0},{1,15},{3,5}... | collective-permute-start | bytes 12296 | tf_op jit(solution)/shard_map/ppermute | solution.py:664
  21.5 0.5 collective-permute-start.3
  21.9 1.2 %collective-permute-start.4 = (f32[8,128]{1,0:T(8,128)S(1)}, f32[8,128]{1,0:T(8,128)S(1)}, u32[]{:S(2)}, u32[]{:S(2)}) collective-permute-start(f32[8,128]{1,0:T(8,128)S(1)} %get-tuple-element.58), channel_id=1, source_target_pairs={{0,2},{2,0},{4,6},{6,4},{8,10},{10,8},{12,14},{14,12},{1,3},{3,1},... | collective-permute-start | bytes 12296 | tf_op jit(solution)/shard_map/ppermute | solution.py:664
  23.2 1.0 %collective-permute-done.2.one_second = f32[8,128]{1,0:T(8,128)S(1)} collective-permute-done((f32[8,128]{1,0:T(8,128)S(1)}, f32[8,128]{1,0:T(8,128)S(1)}, u32[]{:S(2)}, u32[]{:S(2)}) %collective-permute-start.2) | collective-permute-done | bytes 4128 | tf_op jit(solution)/shard_map/ppermute | solution.py:664
  24.2 2.7 %collective-permute-done.3.two_second = f32[8,128]{1,0:T(8,128)S(1)} collective-permute-done((f32[8,128]{1,0:T(8,128)S(1)}, f32[8,128]{1,0:T(8,128)S(1)}, u32[]{:S(2)}, u32[]{:S(2)}) %collective-permute-start.3) | collective-permute-done | bytes 4128 | tf_op jit(solution)/shard_map/ppermute | solution.py:664
  26.9 3.4 %tangent.1 = (f32[3,1,256]{2,1,0:T(1,128)}, f32[768,128]{1,0:T(8,128)S(1)}, f32[768,128]{1,0:T(8,128)S(1)}, f32[8,256]{1,0:T(8,128)S(1)}, f32[1152,256]{1,0:T(8,...) custom-call(f32[16,128]{1,0:T(8,128)S(1)} %get-tuple-element.47.flags, f32[8,256]{1,0:T(8,128)S(1)} %get-tuple-element.48.atoms, ...), custom_call_target="tpu_custom_call" | custom-call | flops 2147483648 | bytes 1048576 | tf_op jit(solution)/shard_map/tangent/pallas_call | solution.py:644
  30.3 0.1 collective-permute-start.6
  30.4 1.7 %collective-permute-done.6.taken = f32[768,128]{1,0:T(8,128)S(1)} collective-permute-done((f32[768,128]{1,0:T(8,128)S(1)}, f32[768,128]{1,0:T(8,128)S(1)}, u32[]{:S(2)}, u32[]{:S(2)}) %collective-permute-start.6) | collective-permute-done | bytes 393248 | tf_op jit(solution)/shard_map/ppermute | solution.py:658
  32.2 0.7 %collective-permute-start.7 = (f32[384,128]{1,0:T(8,128)S(1)}, f32[384,128]{1,0:T(8,128)S(1)}, u32[]{:S(2)}, u32[]{:S(2)}) collective-permute-start(f32[384,128]{1,0:T(8,128)S(1)} %get-tuple-element.72), channel_id=1, source_target_pairs={{0,2},{2,0},{4,6},{6,4},{8,10},{10,8},{12,14},{14,12},{1,3},{3,1},... | collective-permute-start | bytes 589832 | tf_op jit(solution)/shard_map/ppermute | solution.py:668
  32.9 2.5 %radial.3.radial_1 = f32[8,256]{1,0:T(8,128)S(1)} custom-call(f32[16,128]{1,0:T(8,128)S(1)} %get-tuple-element.47.flags, f32[16,128]{1,0:T(8,128)S(1)} %get-tuple-element.73.both, f32[128,256]{1,0:T(8,128)S(1)} %get-tuple-element.74.fsel, f32[1152,256]{1,0:T(8,128)S(1)} %get-tuple-element.61.env, f32[1152,256]{1,0:T(8,128)S(1)} %get-tuple-element.75.envdot, ...), custom_call_target="tpu_custom_call" | custom-call | flops 2147483648 | bytes 1048576 | tf_op jit(solution)/shard_map/radial/pallas_call | solution.py:644
  35.4 2.5 %radial.2.radial_0 = f32[8,256]{1,0:T(8,128)S(1)} custom-call(f32[16,128]{1,0:T(8,128)S(1)} %get-tuple-element.47.flags, f32[16,128]{1,0:T(8,128)S(1)} %get-tuple-element.73.both, f32[128,256]{1,0:T(8,128)S(1)} %get-tuple-element.74.fsel, f32[1152,256]{1,0:T(8,128)S(1)} %get-tuple-element.61.env, f32[1152,256]{1,0:T(8,128)S(1)} %get-tuple-element.75.envdot, ...), custom_call_target="tpu_custom_call" | custom-call | flops 2147483648 | bytes 1048576 | tf_op jit(solution)/shard_map/radial/pallas_call | solution.py:644
  37.9 1.2 %collective-permute-done.7.taken = f32[384,128]{1,0:T(8,128)S(1)} collective-permute-done((f32[384,128]{1,0:T(8,128)S(1)}, f32[384,128]{1,0:T(8,128)S(1)}, u32[]{:S(2)}, u32[]{:S(2)}) %collective-permute-start.7) | collective-permute-done | bytes 196640 | tf_op jit(solution)/shard_map/ppermute | solution.py:668
  39.2 2.4 %collective-permute-start.8 = (f32[104,128]{1,0:T(8,128)S(1)}, f32[104,128]{1,0:T(8,128)S(1)}, u32[]{:S(2)}, u32[]{:S(2)}) collective-permute-start(f32[104,128]{1,0:T(8,128)S(1)} %get-tuple-element.80), channel_id=1, source_target_pairs={{0,12},{2,14},{4,8},{6,10},{8,4},{10,6},{12,0},{14,2},{1,13},{3,15... | collective-permute-start | bytes 159752 | tf_op jit(solution)/shard_map/ppermute | solution.py:668
  41.6 2.1 %collective-permute-start.10 = (f32[104,128]{1,0:T(8,128)S(1)}, f32[104,128]{1,0:T(8,128)S(1)}, u32[]{:S(2)}, u32[]{:S(2)}) collective-permute-start(f32[104,128]{1,0:T(8,128)S(1)} %get-tuple-element.82), channel_id=1, source_target_pairs={{0,4},{2,6},{4,0},{6,2},{8,12},{10,14},{12,8},{14,10},{1,5},{3,7},... | collective-permute-start | bytes 159752 | tf_op jit(solution)/shard_map/ppermute | solution.py:668
  43.7 1.7 %collective-permute-done.8.refs_1_ = f32[104,128]{1,0:T(8,128)S(1)} collective-permute-done((f32[104,128]{1,0:T(8,128)S(1)}, f32[104,128]{1,0:T(8,128)S(1)}, u32[]{:S(2)}, u32[]{:S(2)}) %collective-permute-start.8) | collective-permute-done | bytes 53280 | tf_op jit(solution)/shard_map/ppermute | solution.py:668
  45.3 1.5 %collective-permute-done.9.refs_2_ = f32[104,128]{1,0:T(8,128)S(1)} collective-permute-done((f32[104,128]{1,0:T(8,128)S(1)}, f32[104,128]{1,0:T(8,128)S(1)}, u32[]{:S(2)}, u32[]{:S(2)}) %collective-permute-start.9) | collective-permute-done | bytes 53280 | tf_op jit(solution)/shard_map/ppermute | solution.py:668
  46.8 2.3 %collective-permute-start.13 = (f32[104,128]{1,0:T(8,128)S(1)}, f32[104,128]{1,0:T(8,128)S(1)}, u32[]{:S(2)}, u32[]{:S(2)}) collective-permute-start(f32[104,128]{1,0:T(8,128)S(1)} %total.1.refs_0_), channel_id=1, source_target_pairs={{0,12},{2,14},{4,8},{6,10},{8,4},{10,6},{12,0},{14,2},{1,13},{3,15... | collective-permute-start | bytes 159752 | tf_op jit(solution)/shard_map/ppermute | solution.py:668
  49.1 0.2 collective-permute-start.12
  49.4 1.9 %collective-permute-start.11 = (f32[104,128]{1,0:T(8,128)S(1)}, f32[104,128]{1,0:T(8,128)S(1)}, u32[]{:S(2)}, u32[]{:S(2)}) collective-permute-start(f32[104,128]{1,0:T(8,128)S(1)} %total.1.refs_0_), channel_id=1, source_target_pairs={{0,4},{2,6},{4,0},{6,2},{8,12},{10,14},{12,8},{14,10},{1,5},{3,7},... | collective-permute-start | bytes 159752 | tf_op jit(solution)/shard_map/ppermute | solution.py:668
  51.3 2.1 %collective-permute-done.13.refs_3_ = f32[104,128]{1,0:T(8,128)S(1)} collective-permute-done((f32[104,128]{1,0:T(8,128)S(1)}, f32[104,128]{1,0:T(8,128)S(1)}, u32[]{:S(2)}, u32[]{:S(2)}) %collective-permute-start.13) | collective-permute-done | bytes 53280 | tf_op jit(solution)/shard_map/ppermute | solution.py:668
  53.3 1.5 %collective-permute-done.12.refs_2_ = f32[104,128]{1,0:T(8,128)S(1)} collective-permute-done((f32[104,128]{1,0:T(8,128)S(1)}, f32[104,128]{1,0:T(8,128)S(1)}, u32[]{:S(2)}, u32[]{:S(2)}) %collective-permute-start.12) | collective-permute-done | bytes 53280 | tf_op jit(solution)/shard_map/ppermute | solution.py:668
  54.9 1.2 %collective-permute-start.14 = (f32[416,128]{1,0:T(8,128)S(1)}, f32[416,128]{1,0:T(8,128)S(1)}, u32[]{:S(2)}, u32[]{:S(2)}) collective-permute-start(f32[416,128]{1,0:T(8,128)S(1)} %grow.1.mine), channel_id=1, source_target_pairs={{0,2},{2,0},{4,6},{6,4},{8,10},{10,8},{12,14},{14,12},{1,3},{3,1},... | collective-permute-start | bytes 638984 | tf_op jit(solution)/shard_map/ppermute | solution.py:668
  56.1 5.7 %collective-permute-done.14.theirs = f32[416,128]{1,0:T(8,128)S(1)} collective-permute-done((f32[416,128]{1,0:T(8,128)S(1)}, f32[416,128]{1,0:T(8,128)S(1)}, u32[]{:S(2)}, u32[]{:S(2)}) %collective-permute-start.14) | collective-permute-done | bytes 213024 | tf_op jit(solution)/shard_map/ppermute | solution.py:668
  61.8 1.5 %collective-permute-done.16.facing_theirs = f32[416,128]{1,0:T(8,128)S(1)} collective-permute-done((f32[416,128]{1,0:T(8,128)S(1)}, f32[416,128]{1,0:T(8,128)S(1)}, u32[]{:S(2)}, u32[]{:S(2)}) %collective-permute-start.16) | collective-permute-done | bytes 213024 | tf_op jit(solution)/shard_map/ppermute | solution.py:658
  63.3 1.0 %join.1 = (f32[768,256]{1,0:T(8,128)}, f32[8,256]{1,0:T(8,128)}, f32[4,256]{1,0:T(4,128)}, f32[1,256]{1,0:T(1,128)}) custom-call(f32[416,128]{1,0:T(8,128)S(1)} %grow.1.mine, f32[416,128]{1,0:T(8,128)S(1)} %collective-permute-done.14.theirs, f32[416,128]{1,0:T(8,128)S(1)} %collective-permute-done.15.facing_mine, ...), custom_call_target="tpu_custom_call" | custom-call | bytes 1048576 | tf_op jit(solution)/shard_map/join/pallas_call | solution.py:644
  (13 shorter events, 0.2 us)
Async XLA Ops:
  1.8 8.9 %collective-permute-start = (f32[136,256]{1,0:T(8,128)S(1)}, f32[136,256]{1,0:T(8,128)S(1)}, u32[]{:S(2)}, u32[]{:S(2)}) collective-permute-start(f32[136,256]{1,0:T(8,128)S(1)} %get-tuple-element.52), channel_id=1, source_target_pairs={{0,2},{2,0},{4,6},{6,4},{8,10},{10,8},{12,14},{14,12},{1,3},{3,1},... | collective-permute-start | bytes 417800 | tf_op jit(solution)/shard_map/ppermute | solution.py:664
  4.8 7.8 %collective-permute-start.1 = (f32[136,256]{1,0:T(8,128)S(1)}, f32[136,256]{1,0:T(8,128)S(1)}, u32[]{:S(2)}, u32[]{:S(2)}) collective-permute-start(f32[136,256]{1,0:T(8,128)S(1)} %get-tuple-element.53), channel_id=1, source_target_pairs={{0,14},{2,4},{4,2},{6,8},{8,6},{10,12},{12,10},{14,0},{1,15},{3,5}... | collective-permute-start | bytes 417800 | tf_op jit(solution)/shard_map/ppermute | solution.py:664
  17.8 6.4 %collective-permute-start.2 = (f32[8,128]{1,0:T(8,128)S(1)}, f32[8,128]{1,0:T(8,128)S(1)}, u32[]{:S(2)}, u32[]{:S(2)}) collective-permute-start(f32[8,128]{1,0:T(8,128)S(1)} %get-tuple-element.56), channel_id=1, source_target_pairs={{0,14},{2,4},{4,2},{6,8},{8,6},{10,12},{12,10},{14,0},{1,15},{3,5}... | collective-permute-start | bytes 12296 | tf_op jit(solution)/shard_map/ppermute | solution.py:664
  21.5 5.4 %collective-permute-start.3 = (f32[8,128]{1,0:T(8,128)S(1)}, f32[8,128]{1,0:T(8,128)S(1)}, u32[]{:S(2)}, u32[]{:S(2)}) collective-permute-start(f32[8,128]{1,0:T(8,128)S(1)} %get-tuple-element.57), channel_id=1, source_target_pairs={{0,12},{2,14},{4,8},{6,10},{8,4},{10,6},{12,0},{14,2},{1,13},{3,15... | collective-permute-start | bytes 12296 | tf_op jit(solution)/shard_map/ppermute | solution.py:664
  21.9 5.0 %collective-permute-start.4 = (f32[8,128]{1,0:T(8,128)S(1)}, f32[8,128]{1,0:T(8,128)S(1)}, u32[]{:S(2)}, u32[]{:S(2)}) collective-permute-start(f32[8,128]{1,0:T(8,128)S(1)} %get-tuple-element.58), channel_id=1, source_target_pairs={{0,2},{2,0},{4,6},{6,4},{8,10},{10,8},{12,14},{14,12},{1,3},{3,1},... | collective-permute-start | bytes 12296 | tf_op jit(solution)/shard_map/ppermute | solution.py:664
  23.2 3.7 %collective-permute-start.5 = (f32[8,128]{1,0:T(8,128)S(1)}, f32[8,128]{1,0:T(8,128)S(1)}, u32[]{:S(2)}, u32[]{:S(2)}) collective-permute-start(f32[8,128]{1,0:T(8,128)S(1)} %get-tuple-element.59), channel_id=1, source_target_pairs={{0,4},{2,6},{4,0},{6,2},{8,12},{10,14},{12,8},{14,10},{1,5},{3,7},... | collective-permute-start | bytes 12296 | tf_op jit(solution)/shard_map/ppermute | solution.py:664
  30.3 1.8 %collective-permute-start.6 = (f32[768,128]{1,0:T(8,128)S(1)}, f32[768,128]{1,0:T(8,128)S(1)}, u32[]{:S(2)}, u32[]{:S(2)}) collective-permute-start(f32[768,128]{1,0:T(8,128)S(1)} %get-tuple-element.70), channel_id=1, source_target_pairs={{0,1},{1,0},{2,3},{3,2},{4,5},{5,4},{6,7},{7,6},{8,9},{9,8},{10,11... | collective-permute-start | bytes 1179656 | tf_op jit(solution)/shard_map/ppermute | solution.py:658
  32.2 7.0 %collective-permute-start.7 = (f32[384,128]{1,0:T(8,128)S(1)}, f32[384,128]{1,0:T(8,128)S(1)}, u32[]{:S(2)}, u32[]{:S(2)}) collective-permute-start(f32[384,128]{1,0:T(8,128)S(1)} %get-tuple-element.72), channel_id=1, source_target_pairs={{0,2},{2,0},{4,6},{6,4},{8,10},{10,8},{12,14},{14,12},{1,3},{3,1},... | collective-permute-start | bytes 589832 | tf_op jit(solution)/shard_map/ppermute | solution.py:668
  39.2 6.1 %collective-permute-start.8 = (f32[104,128]{1,0:T(8,128)S(1)}, f32[104,128]{1,0:T(8,128)S(1)}, u32[]{:S(2)}, u32[]{:S(2)}) collective-permute-start(f32[104,128]{1,0:T(8,128)S(1)} %get-tuple-element.80), channel_id=1, source_target_pairs={{0,12},{2,14},{4,8},{6,10},{8,4},{10,6},{12,0},{14,2},{1,13},{3,15... | collective-permute-start | bytes 159752 | tf_op jit(solution)/shard_map/ppermute | solution.py:668
  41.6 5.2 %collective-permute-start.9 = (f32[104,128]{1,0:T(8,128)S(1)}, f32[104,128]{1,0:T(8,128)S(1)}, u32[]{:S(2)}, u32[]{:S(2)}) collective-permute-start(f32[104,128]{1,0:T(8,128)S(1)} %get-tuple-element.81), channel_id=1, source_target_pairs={{0,8},{2,10},{4,12},{6,14},{8,0},{10,2},{12,4},{14,6},{1,9},{3,11}... | collective-permute-start | bytes 159752 | tf_op jit(solution)/shard_map/ppermute | solution.py:668
  41.6 5.2 %collective-permute-start.10 = (f32[104,128]{1,0:T(8,128)S(1)}, f32[104,128]{1,0:T(8,128)S(1)}, u32[]{:S(2)}, u32[]{:S(2)}) collective-permute-start(f32[104,128]{1,0:T(8,128)S(1)} %get-tuple-element.82), channel_id=1, source_target_pairs={{0,4},{2,6},{4,0},{6,2},{8,12},{10,14},{12,8},{14,10},{1,5},{3,7},... | collective-permute-start | bytes 159752 | tf_op jit(solution)/shard_map/ppermute | solution.py:668
  46.8 6.5 %collective-permute-start.13 = (f32[104,128]{1,0:T(8,128)S(1)}, f32[104,128]{1,0:T(8,128)S(1)}, u32[]{:S(2)}, u32[]{:S(2)}) collective-permute-start(f32[104,128]{1,0:T(8,128)S(1)} %total.1.refs_0_), channel_id=1, source_target_pairs={{0,12},{2,14},{4,8},{6,10},{8,4},{10,6},{12,0},{14,2},{1,13},{3,15... | collective-permute-start | bytes 159752 | tf_op jit(solution)/shard_map/ppermute | solution.py:668
  49.1 5.7 %collective-permute-start.12 = (f32[104,128]{1,0:T(8,128)S(1)}, f32[104,128]{1,0:T(8,128)S(1)}, u32[]{:S(2)}, u32[]{:S(2)}) collective-permute-start(f32[104,128]{1,0:T(8,128)S(1)} %total.1.refs_0_), channel_id=1, source_target_pairs={{0,8},{2,10},{4,12},{6,14},{8,0},{10,2},{12,4},{14,6},{1,9},{3,11}... | collective-permute-start | bytes 159752 | tf_op jit(solution)/shard_map/ppermute | solution.py:668
  49.4 5.5 %collective-permute-start.11 = (f32[104,128]{1,0:T(8,128)S(1)}, f32[104,128]{1,0:T(8,128)S(1)}, u32[]{:S(2)}, u32[]{:S(2)}) collective-permute-start(f32[104,128]{1,0:T(8,128)S(1)} %total.1.refs_0_), channel_id=1, source_target_pairs={{0,4},{2,6},{4,0},{6,2},{8,12},{10,14},{12,8},{14,10},{1,5},{3,7},... | collective-permute-start | bytes 159752 | tf_op jit(solution)/shard_map/ppermute | solution.py:668
  54.9 6.9 %collective-permute-start.14 = (f32[416,128]{1,0:T(8,128)S(1)}, f32[416,128]{1,0:T(8,128)S(1)}, u32[]{:S(2)}, u32[]{:S(2)}) collective-permute-start(f32[416,128]{1,0:T(8,128)S(1)} %grow.1.mine), channel_id=1, source_target_pairs={{0,2},{2,0},{4,6},{6,4},{8,10},{10,8},{12,14},{14,12},{1,3},{3,1},... | collective-permute-start | bytes 638984 | tf_op jit(solution)/shard_map/ppermute | solution.py:668
  56.1 5.7 %collective-permute-start.15 = (f32[416,128]{1,0:T(8,128)S(1)}, f32[416,128]{1,0:T(8,128)S(1)}, u32[]{:S(2)}, u32[]{:S(2)}) collective-permute-start(f32[416,128]{1,0:T(8,128)S(1)} %grow.1.mine), channel_id=1, source_target_pairs={{0,1},{1,0},{2,3},{3,2},{4,5},{5,4},{6,7},{7,6},{8,9},{9,8},{10,11... | collective-permute-start | bytes 638984 | tf_op jit(solution)/shard_map/ppermute | solution.py:658
  61.8 1.5 %collective-permute-start.16 = (f32[416,128]{1,0:T(8,128)S(1)}, f32[416,128]{1,0:T(8,128)S(1)}, u32[]{:S(2)}, u32[]{:S(2)}) collective-permute-start(f32[416,128]{1,0:T(8,128)S(1)} %collective-permute-done.14.theirs), channel_id=1, source_target_pairs={{0,1},{1,0},{2,3},{3,2},{4,5},{5,4},{6,7},{7,6},{8,9},{9,8},{10,11... | collective-permute-start | bytes 638984 | tf_op jit(solution)/shard_map/ppermute | solution.py:658

commit v6 on v5

--- a/solution.py
+++ b/solution.py
@@ -278,7 +278,7 @@
 
 def force_kernel(
     flags, atoms, feat, weights, mh, ml, from_second, from_first,
-    env, dinv, gate, curve, inv, rows, fsel, own, one_first, one_second, two_first, two_second, shape_store, xh, xl,
+    env, dinv, gate, curve, inv, rows, fsel, own, leaving, shape_store, xh, xl,
     square, turned, th, tl, eh, el, raw, back,
 ):
     ghost = SEND * TA
@@ -398,20 +398,17 @@
     own[0:3, CHUNK:] = tile_grads[2]
     own[3:6, 0:CHUNK] = tile_grads[0]
     own[3:6, CHUNK:] = tile_grads[3]
-    leaving = []
-    for first, ghost_grad in ((0, tile_grads[0]), (SEND, tile_grads[3])):
+    block = jnp.zeros((3, CHUNK), F32)
+    for k, (first, ghost_grad) in enumerate(((0, tile_grads[0]), (SEND, tile_grads[3]))):
         listed = paired(*(pick(tile_grads[1:3], number(SENT + first + j)) for j in range(SEND)))
-        leaving.append((listed, ghost_grad))
-    for shift, outs in ((0, (one_first, one_second)), (1, (two_first, two_second))):
-        choice = upward(shift)
-        for out, above in zip(outs, (choice, 1.0 - choice)):
-            out[...] = jnp.zeros_like(out)
-            out[0:3, :] = either(above, leaving[1][0], leaving[0][0])
-            out[3:6, :] = either(above, leaving[1][1], leaving[0][1])
+        for to in range(leaving.shape[0]):
+            leaving[to, 8 * k : 8 * k + 3, :] = listed
+            leaving[to, 8 * k + 3 : 8 * k + 6, :] = ghost_grad
+            leaving[to, 8 * k + 6 : 8 * k + 8, :] = block[0:2]
 
 
 def tangent_kernel(
-    scale, flags, atoms, weights, mh, ml, from_first, from_second, own, one_second, two_second, one_first, two_first,
+    scale, flags, atoms, weights, mh, ml, from_first, from_second, own, arriving,
     rows, env, gate, curve, inv, shape_store, xh, xl,
     forces, keep, give, small, envdot, curl, both,
     square, turned, th, tl, raw, left, right,
@@ -424,11 +421,11 @@
     others = [number(OTHER + p) for p in range(PAIRS)]
     shared = flags[SHARED : SHARED + 1, 0:1]
     mine = [own[0:3, 0:CHUNK], own[0:3, CHUNK:]]
-    up, up_two = upward(0), upward(1)
-    low_one = either(up, one_second[...], one_first[...])
-    high_one = either(up, one_first[...], one_second[...])
-    low_two = either(up_two, two_second[...], two_first[...])
-    high_two = either(up_two, two_first[...], two_second[...])
+    up = upward(0)
+    count = lax.axis_size("domain")
+    here = lax.axis_index("domain")
+    low_one, low_two = (arriving[lax.rem(here + count - k, count), 8:16, :] for k in (1, 2))
+    high_one, high_two = (arriving[lax.rem(here + k, count), 0:8, :] for k in (1, 2))
     low_tail = either(up, from_second[ghost:, :], from_first[ghost:, :])
     high_tail = either(up, from_first[ghost:, :], from_second[ghost:, :])
     arrived = [twice(low_one[3:6, :], j) for j in range(SEND)]
@@ -732,7 +729,7 @@
     )
 
     factors = (PAIRS, BASIS * TA, channels)
-    env, dinv, gate, curve, inv, rows, fsel, own, *leaving, shape_store, xh, xl = call(
+    env, dinv, gate, curve, inv, rows, fsel, own, leaving, shape_store, xh, xl = call(
         force_kernel,
         "force",
         [
@@ -744,10 +741,7 @@
             (8, CHUNK),
             (slots, channels),
             (8, atoms_here),
-            (8, CHUNK),
-            (8, CHUNK),
-            (8, CHUNK),
-            (8, CHUNK),
+            (lax.axis_size("domain"), 16, CHUNK),
             (PAIRS, 4 + BASIS, TA, CHUNK),
             (factors, BF16),
             (factors, BF16),
@@ -759,7 +753,7 @@
         flags, atoms, own_feat, weights, mh, ml, from_second, from_first,
         flops=1 << 31,
     )
-    arriving = [exchanged(leaving[i], i // 2, i % 2 == 0) for i in (1, 3, 0, 2)]
+    arriving = lax.all_to_all(leaving, "domain", 0, 0)
 
     rows_mix = 3 * channels
     total_count = 3.0 * atoms_here * lax.axis_size("domain") * lax.axis_size("batch")
@@ -779,7 +773,7 @@
         + [((PAIRS, *table), BF16)] * 2
         + [((PAIRS * COMPS * TA, channels), F32)]
         + [((2 * slots, 3 * channels), F32), ((2 * slots, channels), F32)],
-        flags, atoms, weights, mh, ml, from_first, from_second, own, *arriving,
+        flags, atoms, weights, mh, ml, from_first, from_second, own, arriving,
         rows, env, gate, curve, inv, shape_store, xh, xl,
         flops=1 << 31,
     )

time: 64.4 us -> 65.1 us (1.011)
  blocking collectives: 0 us -> 11.6 us
  starting transfers between devices: 22.8 us -> 16.5 us
  waiting for transfers between devices: 23.3 us -> 18.7 us
    all_to_all x0 -> x1, blocking collectives: none -> 11.6 us  [on_device(): arriving = lax.all_to_all(leaving, 'domain', 0, 0)]
    ppermute x6 -> x2, starting transfers between devices: 11.9 us -> 6.58 us  [exchanged(): lax.ppermute(block, 'domain', [(i, (i + step if up[i] else i - step) % co...]
    ppermute x6 -> x2, waiting for transfers between devices: 6.41 us -> 2.68 us  [exchanged(): lax.ppermute(block, 'domain', [(i, (i + step if up[i] else i - step) % co...]
    ppermute x8, starting transfers between devices: 10.8 us -> 9.83 us  [partner(): lax.ppermute(block, 'domain', [(i, i ^ mask) for i in range(lax.axis_size...]
    ppermute x8, waiting for transfers between devices: 13.7 us -> 12.9 us  [partner(): lax.ppermute(block, 'domain', [(i, i ^ mask) for i in range(lax.axis_size...]
  transfers between devices with their start and end apart: 17 -> 13, of which waited for: 12 -> 11; matrix products, arithmetic and copies ran while one was open for 0% -> 0% of each run, Pallas kernels for 10% -> 10%
where the time goes in v6:
time: 65.1 us; the launch traced here: 64.9 us
  waiting for transfers between devices  18.7 us (29%)
  Pallas kernels  17.4 us (27%)
  starting transfers between devices  16.5 us (25%)
  blocking collectives  11.6 us (18%)
  between operations  0.7 us (1%)
    pallas_call x11, Pallas kernels, call(): pl.pallas_call(kernel, name=name, out_shape=[jax.ShapeDtypeStruct(*out) f...  17.4 us
    ppermute x8, waiting for transfers between devices, partner(): lax.ppermute(block, 'domain', [(i, i ^ mask) for i in range(lax.axis_size...  12.9 us
    all_to_all x1, blocking collectives, on_device(): arriving = lax.all_to_all(leaving, 'domain', 0, 0)  11.6 us
    ppermute x8, starting transfers between devices, partner(): lax.ppermute(block, 'domain', [(i, i ^ mask) for i in range(lax.axis_size...  9.83 us
    ppermute x2, starting transfers between devices, exchanged(): lax.ppermute(block, 'domain', [(i, (i + step if up[i] else i - step) % co...  6.58 us
    ppermute x3, waiting for transfers between devices, shifted(): lax.ppermute(block, axis, [(i, (i + by) % count) for i in range(count)])  3.17 us
    ppermute x2, waiting for transfers between devices, exchanged(): lax.ppermute(block, 'domain', [(i, (i + step if up[i] else i - step) % co...  2.68 us
  transfers between devices with their start and end apart: 13, of which 11 were waited for; matrix products, arithmetic and copies ran while one was open for 0% of the time, Pallas kernels for 10%

profile of v6, /device:TPU:0, one launch (start us, length us, event | category | flops | bytes accessed | tf_op | source)
XLA Modules:
  0.0 64.9 jit_solution(2311018710293984787)
XLA Ops:
  0.6 1.2 %gather.1 = (f32[136,256]{1,0:T(8,128)S(1)}, f32[136,256]{1,0:T(8,128)S(1)}, f32[8,128]{1,0:T(8,128)S(1)}) custom-call(s32[1,4]{1,0:T(1,128)} %send.3, f32[3,1,256]{2,1,0:T(1,128)} %bitcast.5, f32[1,256,256]{2,1,0:T(8,128)} %feat.3, f32[3,1,256]{2,1,0:T(1,128)} %bitcast.7), custom_call_target="tpu_custom_call" | custom-call | bytes 1048576 | tf_op jit(solution)/shard_map/gather/pallas_call | solution.py:641
  1.8 3.0 %collective-permute-start = (f32[136,256]{1,0:T(8,128)S(1)}, f32[136,256]{1,0:T(8,128)S(1)}, u32[]{:S(2)}, u32[]{:S(2)}) collective-permute-start(f32[136,256]{1,0:T(8,128)S(1)} %get-tuple-element.49), channel_id=1, source_target_pairs={{0,2},{2,0},{4,6},{6,4},{8,10},{10,8},{12,14},{14,12},{1,3},{3,1},... | collective-permute-start | bytes 417800 | tf_op jit(solution)/shard_map/ppermute | solution.py:661
  4.8 3.5 %collective-permute-start.1 = (f32[136,256]{1,0:T(8,128)S(1)}, f32[136,256]{1,0:T(8,128)S(1)}, u32[]{:S(2)}, u32[]{:S(2)}) collective-permute-start(f32[136,256]{1,0:T(8,128)S(1)} %get-tuple-element.50), channel_id=1, source_target_pairs={{0,14},{2,4},{4,2},{6,8},{8,6},{10,12},{12,10},{14,0},{1,15},{3,5}... | collective-permute-start | bytes 417800 | tf_op jit(solution)/shard_map/ppermute | solution.py:661
  8.4 1.6 %stage.1 = (f32[16,128]{1,0:T(8,128)S(1)}, f32[8,256]{1,0:T(8,128)S(1)}, f32[256,256]{1,0:T(8,128)S(1)}, f32[16,256]{1,0:T(8,128)S(1)}, bf16[768,256]{1,0:T(8,128)(2,1)S(1)}, /*index=5*/bf16[768,256]{1,0:T(8,128)(2,1)S(1)}) custom-call(s32[1,2]{1,0:T(1,128)} %centre.1, s32[1,2]{1,0:T(1,128)} %other.1, s32[1,2]{1,0:T(1,128)} %live.1, s32[1,4]{1,0:T(1,128)} %send.3, ...), custom_call_target="tpu_custom_call" | custom-call | bytes 1048576 | tf_op jit(solution)/shard_map/stage/pallas_call | solution.py:641
  10.0 0.8 %collective-permute-done.from_first = f32[136,256]{1,0:T(8,128)S(1)} collective-permute-done((f32[136,256]{1,0:T(8,128)S(1)}, f32[136,256]{1,0:T(8,128)S(1)}, u32[]{:S(2)}, u32[]{:S(2)}) %collective-permute-start) | collective-permute-done | bytes 139296 | tf_op jit(solution)/shard_map/ppermute | solution.py:661
  10.8 1.9 %collective-permute-done.1.from_second = f32[136,256]{1,0:T(8,128)S(1)} collective-permute-done((f32[136,256]{1,0:T(8,128)S(1)}, f32[136,256]{1,0:T(8,128)S(1)}, u32[]{:S(2)}, u32[]{:S(2)}) %collective-permute-start.1) | collective-permute-done | bytes 139296 | tf_op jit(solution)/shard_map/ppermute | solution.py:661
  12.7 5.1 %force.1 = (f32[1152,256]{1,0:T(8,128)S(1)}, f32[128,768]{1,0:T(8,128)S(1)}, f32[128,256]{1,0:T(8,128)S(1)}, f32[128,256]{1,0:T(8,128)S(1)}, f32[128,768]{1,0:T(...) custom-call(f32[16,128]{1,0:T(8,128)S(1)} %get-tuple-element.44.flag, ...), custom_call_target="tpu_custom_call" | custom-call | flops 2147483648 | bytes 1048576 | tf_op jit(solution)/shard_map/force/pallas_call | solution.py:641
  17.8 11.6 %all_to_all.5.arriving = f32[8,16,128]{2,1,0:T(8,128)S(1)} all-to-all(f32[8,16,128]{2,1,0:T(8,128)S(1)} %get-tuple-element.53), channel_id=1, replica_groups=mesh['parts'=2,'domain'=8,'batch'=2] {'domain'}, dimensions={0} | all-to-all | bytes 131072 | tf_op jit(solution)/shard_map/all_to_all | solution.py:756
  29.4 3.4 %tangent.1 = (f32[3,1,256]{2,1,0:T(1,128)}, f32[768,128]{1,0:T(8,128)S(1)}, f32[768,128]{1,0:T(8,128)S(1)}, f32[8,256]{1,0:T(8,128)S(1)}, f32[1152,256]{1,0:T(8,...) custom-call(f32[16,128]{1,0:T(8,128)S(1)} %get-tuple-element.44.flags, f32[8,256]{1,0:T(8,128)S(1)} %get-tuple-element.45.atoms, ...), custom_call_target="tpu_custom_call" | custom-call | flops 2147483648 | bytes 1048576 | tf_op jit(solution)/shard_map/tangent/pallas_call | solution.py:641
  32.8 0.1 collective-permute-start.2
  32.9 1.7 %collective-permute-done.2.taken = f32[768,128]{1,0:T(8,128)S(1)} collective-permute-done((f32[768,128]{1,0:T(8,128)S(1)}, f32[768,128]{1,0:T(8,128)S(1)}, u32[]{:S(2)}, u32[]{:S(2)}) %collective-permute-start.2) | collective-permute-done | bytes 393248 | tf_op jit(solution)/shard_map/ppermute | solution.py:655
  34.6 0.1 halve.1
  34.7 0.5 collective-permute-start.3
  35.1 2.5 %radial.3.radial_1 = f32[8,256]{1,0:T(8,128)S(1)} custom-call(f32[16,128]{1,0:T(8,128)S(1)} %get-tuple-element.44.flags, f32[16,128]{1,0:T(8,128)S(1)} %get-tuple-element.67.both, f32[128,256]{1,0:T(8,128)S(1)} %get-tuple-element.68.fsel, f32[1152,256]{1,0:T(8,128)S(1)} %get-tuple-element.55.env, f32[1152,256]{1,0:T(8,128)S(1)} %get-tuple-element.69.envdot, ...), custom_call_target="tpu_custom_call" | custom-call | flops 2147483648 | bytes 1048576 | tf_op jit(solution)/shard_map/radial/pallas_call | solution.py:641
  37.6 2.5 %radial.2.radial_0 = f32[8,256]{1,0:T(8,128)S(1)} custom-call(f32[16,128]{1,0:T(8,128)S(1)} %get-tuple-element.44.flags, f32[16,128]{1,0:T(8,128)S(1)} %get-tuple-element.67.both, f32[128,256]{1,0:T(8,128)S(1)} %get-tuple-element.68.fsel, f32[1152,256]{1,0:T(8,128)S(1)} %get-tuple-element.55.env, f32[1152,256]{1,0:T(8,128)S(1)} %get-tuple-element.69.envdot, ...), custom_call_target="tpu_custom_call" | custom-call | flops 2147483648 | bytes 1048576 | tf_op jit(solution)/shard_map/radial/pallas_call | solution.py:641
  40.1 1.5 %collective-permute-done.3.taken = f32[384,128]{1,0:T(8,128)S(1)} collective-permute-done((f32[384,128]{1,0:T(8,128)S(1)}, f32[384,128]{1,0:T(8,128)S(1)}, u32[]{:S(2)}, u32[]{:S(2)}) %collective-permute-start.3) | collective-permute-done | bytes 196640 | tf_op jit(solution)/shard_map/ppermute | solution.py:665
  41.7 0.6 collective-permute-start.4
  42.3 1.1 %collective-permute-start.5 = (f32[104,128]{1,0:T(8,128)S(1)}, f32[104,128]{1,0:T(8,128)S(1)}, u32[]{:S(2)}, u32[]{:S(2)}) collective-permute-start(f32[104,128]{1,0:T(8,128)S(1)} %get-tuple-element.75), channel_id=1, source_target_pairs={{0,8},{2,10},{4,12},{6,14},{8,0},{10,2},{12,4},{14,6},{1,9},{3,11}... | collective-permute-start | bytes 159752 | tf_op jit(solution)/shard_map/ppermute | solution.py:665
  43.4 2.7 %collective-permute-start.6 = (f32[104,128]{1,0:T(8,128)S(1)}, f32[104,128]{1,0:T(8,128)S(1)}, u32[]{:S(2)}, u32[]{:S(2)}) collective-permute-start(f32[104,128]{1,0:T(8,128)S(1)} %get-tuple-element.76), channel_id=1, source_target_pairs={{0,4},{2,6},{4,0},{6,2},{8,12},{10,14},{12,8},{14,10},{1,5},{3,7},... | collective-permute-start | bytes 159752 | tf_op jit(solution)/shard_map/ppermute | solution.py:665
  46.2 1.8 %collective-permute-done.4.refs_1_ = f32[104,128]{1,0:T(8,128)S(1)} collective-permute-done((f32[104,128]{1,0:T(8,128)S(1)}, f32[104,128]{1,0:T(8,128)S(1)}, u32[]{:S(2)}, u32[]{:S(2)}) %collective-permute-start.4) | collective-permute-done | bytes 53280 | tf_op jit(solution)/shard_map/ppermute | solution.py:665
  47.9 0.9 %collective-permute-done.5.refs_2_ = f32[104,128]{1,0:T(8,128)S(1)} collective-permute-done((f32[104,128]{1,0:T(8,128)S(1)}, f32[104,128]{1,0:T(8,128)S(1)}, u32[]{:S(2)}, u32[]{:S(2)}) %collective-permute-start.5) | collective-permute-done | bytes 53280 | tf_op jit(solution)/shard_map/ppermute | solution.py:665
  48.9 1.8 %collective-permute-start.9 = (f32[104,128]{1,0:T(8,128)S(1)}, f32[104,128]{1,0:T(8,128)S(1)}, u32[]{:S(2)}, u32[]{:S(2)}) collective-permute-start(f32[104,128]{1,0:T(8,128)S(1)} %total.1.refs_0_), channel_id=1, source_target_pairs={{0,12},{2,14},{4,8},{6,10},{8,4},{10,6},{12,0},{14,2},{1,13},{3,15... | collective-permute-start | bytes 159752 | tf_op jit(solution)/shard_map/ppermute | solution.py:665
  50.7 1.1 %collective-permute-start.8 = (f32[104,128]{1,0:T(8,128)S(1)}, f32[104,128]{1,0:T(8,128)S(1)}, u32[]{:S(2)}, u32[]{:S(2)}) collective-permute-start(f32[104,128]{1,0:T(8,128)S(1)} %total.1.refs_0_), channel_id=1, source_target_pairs={{0,8},{2,10},{4,12},{6,14},{8,0},{10,2},{12,4},{14,6},{1,9},{3,11}... | collective-permute-start | bytes 159752 | tf_op jit(solution)/shard_map/ppermute | solution.py:665
  51.8 1.5 %collective-permute-start.7 = (f32[104,128]{1,0:T(8,128)S(1)}, f32[104,128]{1,0:T(8,128)S(1)}, u32[]{:S(2)}, u32[]{:S(2)}) collective-permute-start(f32[104,128]{1,0:T(8,128)S(1)} %total.1.refs_0_), channel_id=1, source_target_pairs={{0,4},{2,6},{4,0},{6,2},{8,12},{10,14},{12,8},{14,10},{1,5},{3,7},... | collective-permute-start | bytes 159752 | tf_op jit(solution)/shard_map/ppermute | solution.py:665
  53.3 1.8 %collective-permute-done.9.refs_3_ = f32[104,128]{1,0:T(8,128)S(1)} collective-permute-done((f32[104,128]{1,0:T(8,128)S(1)}, f32[104,128]{1,0:T(8,128)S(1)}, u32[]{:S(2)}, u32[]{:S(2)}) %collective-permute-start.9) | collective-permute-done | bytes 53280 | tf_op jit(solution)/shard_map/ppermute | solution.py:665
  55.1 1.2 %collective-permute-done.8.refs_2_ = f32[104,128]{1,0:T(8,128)S(1)} collective-permute-done((f32[104,128]{1,0:T(8,128)S(1)}, f32[104,128]{1,0:T(8,128)S(1)}, u32[]{:S(2)}, u32[]{:S(2)}) %collective-permute-start.8) | collective-permute-done | bytes 53280 | tf_op jit(solution)/shard_map/ppermute | solution.py:665
  56.3 0.2 collective-permute-done.7.refs_1_
  56.5 0.5 collective-permute-start.10
  57.0 5.4 %collective-permute-done.10.theirs = f32[416,128]{1,0:T(8,128)S(1)} collective-permute-done((f32[416,128]{1,0:T(8,128)S(1)}, f32[416,128]{1,0:T(8,128)S(1)}, u32[]{:S(2)}, u32[]{:S(2)}) %collective-permute-start.10) | collective-permute-done | bytes 213024 | tf_op jit(solution)/shard_map/ppermute | solution.py:665
  62.5 0.0 collective-permute-start.12
  62.5 1.5 %collective-permute-done.12.facing_theirs = f32[416,128]{1,0:T(8,128)S(1)} collective-permute-done((f32[416,128]{1,0:T(8,128)S(1)}, f32[416,128]{1,0:T(8,128)S(1)}, u32[]{:S(2)}, u32[]{:S(2)}) %collective-permute-start.12) | collective-permute-done | bytes 213024 | tf_op jit(solution)/shard_map/ppermute | solution.py:655
  63.9 1.0 %join.1 = (f32[768,256]{1,0:T(8,128)}, f32[8,256]{1,0:T(8,128)}, f32[4,256]{1,0:T(4,128)}, f32[1,256]{1,0:T(1,128)}) custom-call(f32[416,128]{1,0:T(8,128)S(1)} %grow.1.mine, f32[416,128]{1,0:T(8,128)S(1)} %collective-permute-done.10.theirs, f32[416,128]{1,0:T(8,128)S(1)} %collective-permute-done.11.facing_mine, ...), custom_call_target="tpu_custom_call" | custom-call | bytes 1048576 | tf_op jit(solution)/shard_map/join/pallas_call | solution.py:641
  (6 shorter events, 0.1 us)
Async XLA Ops:
  1.8 8.9 %collective-permute-start = (f32[136,256]{1,0:T(8,128)S(1)}, f32[136,256]{1,0:T(8,128)S(1)}, u32[]{:S(2)}, u32[]{:S(2)}) collective-permute-start(f32[136,256]{1,0:T(8,128)S(1)} %get-tuple-element.49), channel_id=1, source_target_pairs={{0,2},{2,0},{4,6},{6,4},{8,10},{10,8},{12,14},{14,12},{1,3},{3,1},... | collective-permute-start | bytes 417800 | tf_op jit(solution)/shard_map/ppermute | solution.py:661
  4.8 7.8 %collective-permute-start.1 = (f32[136,256]{1,0:T(8,128)S(1)}, f32[136,256]{1,0:T(8,128)S(1)}, u32[]{:S(2)}, u32[]{:S(2)}) collective-permute-start(f32[136,256]{1,0:T(8,128)S(1)} %get-tuple-element.50), channel_id=1, source_target_pairs={{0,14},{2,4},{4,2},{6,8},{8,6},{10,12},{12,10},{14,0},{1,15},{3,5}... | collective-permute-start | bytes 417800 | tf_op jit(solution)/shard_map/ppermute | solution.py:661
  32.8 1.8 %collective-permute-start.2 = (f32[768,128]{1,0:T(8,128)S(1)}, f32[768,128]{1,0:T(8,128)S(1)}, u32[]{:S(2)}, u32[]{:S(2)}) collective-permute-start(f32[768,128]{1,0:T(8,128)S(1)} %get-tuple-element.64), channel_id=1, source_target_pairs={{0,1},{1,0},{2,3},{3,2},{4,5},{5,4},{6,7},{7,6},{8,9},{9,8},{10,11... | collective-permute-start | bytes 1179656 | tf_op jit(solution)/shard_map/ppermute | solution.py:655
  34.7 7.0 %collective-permute-start.3 = (f32[384,128]{1,0:T(8,128)S(1)}, f32[384,128]{1,0:T(8,128)S(1)}, u32[]{:S(2)}, u32[]{:S(2)}) collective-permute-start(f32[384,128]{1,0:T(8,128)S(1)} %get-tuple-element.66), channel_id=1, source_target_pairs={{0,2},{2,0},{4,6},{6,4},{8,10},{10,8},{12,14},{14,12},{1,3},{3,1},... | collective-permute-start | bytes 589832 | tf_op jit(solution)/shard_map/ppermute | solution.py:665
  41.7 6.2 %collective-permute-start.4 = (f32[104,128]{1,0:T(8,128)S(1)}, f32[104,128]{1,0:T(8,128)S(1)}, u32[]{:S(2)}, u32[]{:S(2)}) collective-permute-start(f32[104,128]{1,0:T(8,128)S(1)} %get-tuple-element.74), channel_id=1, source_target_pairs={{0,12},{2,14},{4,8},{6,10},{8,4},{10,6},{12,0},{14,2},{1,13},{3,15... | collective-permute-start | bytes 159752 | tf_op jit(solution)/shard_map/ppermute | solution.py:665
  42.3 6.5 %collective-permute-start.5 = (f32[104,128]{1,0:T(8,128)S(1)}, f32[104,128]{1,0:T(8,128)S(1)}, u32[]{:S(2)}, u32[]{:S(2)}) collective-permute-start(f32[104,128]{1,0:T(8,128)S(1)} %get-tuple-element.75), channel_id=1, source_target_pairs={{0,8},{2,10},{4,12},{6,14},{8,0},{10,2},{12,4},{14,6},{1,9},{3,11}... | collective-permute-start | bytes 159752 | tf_op jit(solution)/shard_map/ppermute | solution.py:665
  43.4 5.4 %collective-permute-start.6 = (f32[104,128]{1,0:T(8,128)S(1)}, f32[104,128]{1,0:T(8,128)S(1)}, u32[]{:S(2)}, u32[]{:S(2)}) collective-permute-start(f32[104,128]{1,0:T(8,128)S(1)} %get-tuple-element.76), channel_id=1, source_target_pairs={{0,4},{2,6},{4,0},{6,2},{8,12},{10,14},{12,8},{14,10},{1,5},{3,7},... | collective-permute-start | bytes 159752 | tf_op jit(solution)/shard_map/ppermute | solution.py:665
  48.9 6.2 %collective-permute-start.9 = (f32[104,128]{1,0:T(8,128)S(1)}, f32[104,128]{1,0:T(8,128)S(1)}, u32[]{:S(2)}, u32[]{:S(2)}) collective-permute-start(f32[104,128]{1,0:T(8,128)S(1)} %total.1.refs_0_), channel_id=1, source_target_pairs={{0,12},{2,14},{4,8},{6,10},{8,4},{10,6},{12,0},{14,2},{1,13},{3,15... | collective-permute-start | bytes 159752 | tf_op jit(solution)/shard_map/ppermute | solution.py:665
  50.7 5.6 %collective-permute-start.8 = (f32[104,128]{1,0:T(8,128)S(1)}, f32[104,128]{1,0:T(8,128)S(1)}, u32[]{:S(2)}, u32[]{:S(2)}) collective-permute-start(f32[104,128]{1,0:T(8,128)S(1)} %total.1.refs_0_), channel_id=1, source_target_pairs={{0,8},{2,10},{4,12},{6,14},{8,0},{10,2},{12,4},{14,6},{1,9},{3,11}... | collective-permute-start | bytes 159752 | tf_op jit(solution)/shard_map/ppermute | solution.py:665
  51.8 4.7 %collective-permute-start.7 = (f32[104,128]{1,0:T(8,128)S(1)}, f32[104,128]{1,0:T(8,128)S(1)}, u32[]{:S(2)}, u32[]{:S(2)}) collective-permute-start(f32[104,128]{1,0:T(8,128)S(1)} %total.1.refs_0_), channel_id=1, source_target_pairs={{0,4},{2,6},{4,0},{6,2},{8,12},{10,14},{12,8},{14,10},{1,5},{3,7},... | collective-permute-start | bytes 159752 | tf_op jit(solution)/shard_map/ppermute | solution.py:665
  56.5 5.9 %collective-permute-start.10 = (f32[416,128]{1,0:T(8,128)S(1)}, f32[416,128]{1,0:T(8,128)S(1)}, u32[]{:S(2)}, u32[]{:S(2)}) collective-permute-start(f32[416,128]{1,0:T(8,128)S(1)} %grow.1.mine), channel_id=1, source_target_pairs={{0,2},{2,0},{4,6},{6,4},{8,10},{10,8},{12,14},{14,12},{1,3},{3,1},... | collective-permute-start | bytes 638984 | tf_op jit(solution)/shard_map/ppermute | solution.py:665
  57.0 5.4 %collective-permute-start.11 = (f32[416,128]{1,0:T(8,128)S(1)}, f32[416,128]{1,0:T(8,128)S(1)}, u32[]{:S(2)}, u32[]{:S(2)}) collective-permute-start(f32[416,128]{1,0:T(8,128)S(1)} %grow.1.mine), channel_id=1, source_target_pairs={{0,1},{1,0},{2,3},{3,2},{4,5},{5,4},{6,7},{7,6},{8,9},{9,8},{10,11... | collective-permute-start | bytes 638984 | tf_op jit(solution)/shard_map/ppermute | solution.py:655
  62.5 1.5 %collective-permute-start.12 = (f32[416,128]{1,0:T(8,128)S(1)}, f32[416,128]{1,0:T(8,128)S(1)}, u32[]{:S(2)}, u32[]{:S(2)}) collective-permute-start(f32[416,128]{1,0:T(8,128)S(1)} %collective-permute-done.10.theirs), channel_id=1, source_target_pairs={{0,1},{1,0},{2,3},{3,2},{4,5},{5,4},{6,7},{7,6},{8,9},{9,8},{10,11... | collective-permute-start | bytes 638984 | tf_op jit(solution)/shard_map/ppermute | solution.py:655

commit v7 on v5

--- a/solution.py
+++ b/solution.py
@@ -12,6 +12,7 @@
 SEND = 2
 PAIRS = 2
 COMPS = 9
+WIDE = 10 * TA
 BASIS = 8
 SPECIES = 4
 HALF = 128
@@ -278,8 +279,8 @@
 
 def force_kernel(
     flags, atoms, feat, weights, mh, ml, from_second, from_first,
-    env, dinv, gate, curve, inv, rows, fsel, own, one_first, one_second, two_first, two_second, shape_store, xh, xl,
-    square, turned, th, tl, eh, el, raw, back,
+    env, dinv, gate, curve, inv, rows, fsel, own, one_first, one_second, two_first, two_second, shape_store, xh, xl, eh, el,
+    square, turned, th, tl, raw, back,
 ):
     ghost = SEND * TA
     up = upward(0)
@@ -360,7 +361,10 @@
             hi, lo = split((2.0 * env_scale) * block * part)
             eh[p, m * TA : (m + 1) * TA, :] = hi
             el[p, m * TA : (m + 1) * TA, :] = lo
-        back[p] = product((eh[p], el[p]), (xh[p], xl[p]), NT)
+        for ref in (eh, el):
+            ref[p, COMPS * TA :, :] = jnp.zeros((WIDE - COMPS * TA, ref.shape[2]), BF16)
+        steady = (eh[p, 0 : COMPS * TA, :], el[p, 0 : COMPS * TA, :])
+        back[p] = product(steady, (xh[p], xl[p]), NT)
         d_radius = None
         d_angular = []
         for m in range(COMPS):
@@ -412,7 +416,7 @@
 
 def tangent_kernel(
     scale, flags, atoms, weights, mh, ml, from_first, from_second, own, one_second, two_second, one_first, two_first,
-    rows, env, gate, curve, inv, shape_store, xh, xl,
+    rows, env, gate, curve, inv, shape_store, xh, xl, after,
     forces, keep, give, small, envdot, curl, both,
     square, turned, th, tl, raw, left, right,
 ):
@@ -503,11 +507,10 @@
     once = 1.0 - shared * flag(lax.broadcasted_iota(jnp.int32, (half, 1), 0) >= TA)
     right[0:half, :] = bend * once
     right[half:, :] = gate[...] * weights[BASIS + SPECIES : BASIS + SPECIES + 1, :] * once
+    raw[0 : left.shape[1], :] = product(split(left[...]), split(right[...]), TN)
     core = lax.axis_index("batch")
-    left_parts = split(left[...])
     for out, part in ((keep, core), (give, 1 - core)):
-        lanes = pl.ds(pl.multiple_of(part * HALF, HALF), HALF)
-        out[...] = product(left_parts, split(right[:, lanes]), TN)
+        out[...] = raw[0 : left.shape[1], block_of_lanes(part)]
     small[...] = jnp.zeros_like(small)
     kind = turned[:, 6:7]
     for s in range(SPECIES):
@@ -515,48 +518,78 @@
     small[SPECIES : SPECIES + 1, :] = jnp.sum(gate[...] * hidden_move * once, axis=0, keepdims=True)
 
 
+def table_kernel(flags, rows, shape_store, lh, ll, token, square, turned):
+    low, high = lane_half()
+    token[...] = jnp.zeros_like(token)
+    columns_of(rows[...], square, turned)
+    for p in range(PAIRS):
+        lane_rows = [twice(rows[3 + i : 4 + i, :], p) for i in range(3)]
+        columns = [turned[p * TA : (p + 1) * TA, i : i + 1] for i in range(3)]
+        unit, inverse, weight, slope, sine, cosine = geometry(
+            lane_rows, columns, -1.0, flags[LIVE + p : LIVE + p + 1, :], flags[SAME + p : SAME + p + 1, :]
+        )
+        angular = harmonics(unit)
+        values, slopes = single_orders(sine, cosine, weight, slope)
+        for i, part in enumerate(unit + [inverse] + values + slopes):
+            shape_store[p, i] = part
+        for m in range(0, COMPS + 1, 2):
+            factor = low if m == 0 else angular[m] * low
+            if m + 1 < COMPS:
+                factor = factor + angular[m + 1] * high
+            for n in range(BASIS):
+                hi, lo = split(factor * values[n])
+                lh[p, n * TA : (n + 1) * TA, m * TA : (m + 2) * TA] = hi
+                ll[p, n * TA : (n + 1) * TA, m * TA : (m + 2) * TA] = lo
+
+
 def radial_kernel(
-    p, flags, both, fsel, env, envdot, dinv, curl, mh, ml, after,
+    p, both, shape_store, lh, ll, eh, el, fsel, env, envdot, dinv, curl, mh, ml, after,
     grad_radial,
-    square, turned, lh, ll, gh, gl, raw,
+    square, turned, sh, sl, gh, gl, raw,
 ):
     low, high = lane_half()
     columns_of(both[...], square, turned)
     here = slice(p * TA, (p + 1) * TA)
     turn_inv = product(split(curl[here, :]), (mh[...], ml[...]), NT)
-    lane_rows = [twice(both[3 + i : 4 + i, :], p) for i in range(3)]
     lane_move = [twice(both[11 + i : 12 + i, :], p) for i in range(3)]
-    columns = [turned[here, i : i + 1] for i in range(3)]
     column_move = [turned[here, 8 + i : 9 + i] for i in range(3)]
-    unit, inverse, weight, slope, sine, cosine = geometry(
-        lane_rows, columns, -1.0, flags[LIVE + p : LIVE + p + 1, :], flags[SAME + p : SAME + p + 1, :]
-    )
+    unit = [shape_store[p, i] for i in range(3)]
+    inverse = shape_store[p, 3]
     move = [b - a for a, b in zip(lane_move, column_move)]
     stretch = unit[0] * move[0] + unit[1] * move[1] + unit[2] * move[2]
     turn = [(m - v * stretch) * inverse for m, v in zip(move, unit)]
     angular, turning = harmonics(unit), harmonics_tangent(unit, turn)
-    values, slopes = single_orders(sine, cosine, weight, slope)
+    sh[:, 0:CHUNK] = lh[p, :, WIDE - CHUNK :]
+    sl[:, 0:CHUNK] = ll[p, :, WIDE - CHUNK :]
+    for m in range(0, COMPS + 1, 2):
+        if m == 0:
+            on_value, on_slope = turning[1] * high, low + angular[1] * high
+        else:
+            on_value, on_slope = turning[m] * low, angular[m] * low
+            if m + 1 < COMPS:
+                on_value = on_value + turning[m + 1] * high
+                on_slope = on_slope + angular[m + 1] * high
+        on_slope = on_slope * stretch
+        lanes = slice(CHUNK + m * TA, CHUNK + (m + 2) * TA)
+        for n in range(BASIS):
+            hi, lo = split(on_value * shape_store[p, 4 + n] + on_slope * shape_store[p, 4 + BASIS + n])
+            sh[n * TA : (n + 1) * TA, lanes] = hi
+            sl[n * TA : (n + 1) * TA, lanes] = lo
     for m in range(COMPS):
-        if m == 0:
-            on_value, on_slope = low, high * stretch
-        else:
-            on_value = angular[m] * low + turning[m] * high
-            on_slope = angular[m] * high * stretch
-        for n in range(BASIS):
-            hi, lo = split(on_value * values[n] + on_slope * slopes[n])
-            lh[n * TA : (n + 1) * TA, m * CHUNK : (m + 1) * CHUNK] = hi
-            ll[n * TA : (n + 1) * TA, m * CHUNK : (m + 1) * CHUNK] = lo
         at = slice((p * COMPS + m) * TA, (p * COMPS + m + 1) * TA)
         group = slice(GROUP[m] * 256, (GROUP[m] + 1) * 256)
         steady = (2.0 * env_scale) * dinv[here, group]
         bent = (2.0 * env_scale) * turn_inv[:, group]
         hi, lo = split(env[at, :] * bent + envdot[at, :] * steady)
-        gh[m * CHUNK : m * CHUNK + TA, :] = hi
-        gl[m * CHUNK : m * CHUNK + TA, :] = lo
-        hi, lo = split(env[at, :] * steady)
-        gh[m * CHUNK + TA : (m + 1) * CHUNK, :] = hi
-        gl[m * CHUNK + TA : (m + 1) * CHUNK, :] = lo
-    raw[...] = product((lh[...], ll[...]), (gh[...], gl[...]), NN)
+        gh[m * TA : (m + 1) * TA, :] = hi
+        gl[m * TA : (m + 1) * TA, :] = lo
+    for ref, tail in ((gh, eh), (gl, el)):
+        ref[COMPS * TA : WIDE, :] = jnp.zeros((WIDE - COMPS * TA, ref.shape[1]), BF16)
+        ref[WIDE:, :] = tail[p]
+    first = WIDE - CHUNK
+    raw[...] = product((lh[p, :, 0:first], ll[p, :, 0:first]), (gh[0:first, :], gl[0:first, :]), NN) + product(
+        (sh[...], sl[...]), (gh[first:, :], gl[first:, :]), NN
+    )
     for n in range(BASIS):
         grad_radial[n : n + 1, :] = jnp.sum(
             raw[n * TA : (n + 1) * TA, :] * fsel[here, :], axis=0, keepdims=True
@@ -732,7 +765,7 @@
     )
 
     factors = (PAIRS, BASIS * TA, channels)
-    env, dinv, gate, curve, inv, rows, fsel, own, *leaving, shape_store, xh, xl = call(
+    env, dinv, gate, curve, inv, rows, fsel, own, *leaving, shape_store, xh, xl, eh, el = call(
         force_kernel,
         "force",
         [
@@ -751,15 +784,30 @@
             (PAIRS, 4 + BASIS, TA, CHUNK),
             (factors, BF16),
             (factors, BF16),
+            ((PAIRS, WIDE, channels), BF16),
+            ((PAIRS, WIDE, channels), BF16),
         ],
         turning
         + [((PAIRS, *table), BF16)] * 2
-        + [((PAIRS, COMPS * TA, channels), BF16)] * 2
         + [((PAIRS * COMPS * TA, channels), F32), ((PAIRS, *table), F32)],
         flags, atoms, own_feat, weights, mh, ml, from_second, from_first,
         flops=1 << 31,
     )
     arriving = [exchanged(leaving[i], i // 2, i % 2 == 0) for i in (1, 3, 0, 2)]
+
+    table_shape, lh, ll, token = call(
+        table_kernel,
+        "table",
+        [
+            (PAIRS, 4 + 2 * BASIS, TA, CHUNK),
+            ((PAIRS, BASIS * TA, WIDE), BF16),
+            ((PAIRS, BASIS * TA, WIDE), BF16),
+            (8, CHUNK),
+        ],
+        turning,
+        flags, rows,
+        flops=1 << 30,
+    )
 
     rows_mix = 3 * channels
     total_count = 3.0 * atoms_here * lax.axis_size("domain") * lax.axis_size("batch")
@@ -780,7 +828,7 @@
         + [((PAIRS * COMPS * TA, channels), F32)]
         + [((2 * slots, 3 * channels), F32), ((2 * slots, channels), F32)],
         flags, atoms, weights, mh, ml, from_first, from_second, own, *arriving,
-        rows, env, gate, curve, inv, shape_store, xh, xl,
+        rows, env, gate, curve, inv, shape_store, xh, xl, token,
         flops=1 << 31,
     )
 
@@ -790,18 +838,19 @@
             "radial",
             [(BASIS, channels)],
             turning
-            + [((BASIS * TA, COMPS * CHUNK), BF16)] * 2
-            + [((COMPS * CHUNK, channels), BF16)] * 2
+            + [((BASIS * TA, CHUNK + WIDE), BF16)] * 2
+            + [((2 * WIDE, channels), BF16)] * 2
             + [((BASIS * TA, channels), F32)],
-            flags, both, fsel, env, envdot, dinv, curl, mh, ml, after,
+            both, table_shape, lh, ll, eh, el, fsel, env, envdot, dinv, curl, mh, ml, after,
             flops=1 << 31,
         )[0]
 
+    radials = [radial(0, both)]
     keep, give = call(
         halve_kernel, "halve", [(rows_mix // 2, HALF)] * 2, [], keep, shifted(give, "batch", 1)
     )
     taken = partner(give, 1)
-    radials = [radial(p, keep) for p in range(PAIRS)]
+    radials.append(radial(1, keep))
     piece = rows_mix // (2 * FOUR) + SMALL // FOUR
     blocks = call(
         spread_kernel, "spread", [(piece, HALF)] * FOUR, [((SMALL, HALF), F32)],

time: 64.4 us -> 65.5 us (1.017)
    ppermute x8, waiting for transfers between devices: 13.7 us -> 17.4 us  [partner(): lax.ppermute(block, 'domain', [(i, i ^ mask) for i in range(lax.axis_size...]
    ppermute x3, waiting for transfers between devices: 3.17 us -> 1.46 us  [shifted(): lax.ppermute(block, axis, [(i, (i + by) % count) for i in range(count)])]
    ppermute x6, waiting for transfers between devices: 6.41 us -> 5.08 us  [exchanged(): lax.ppermute(block, 'domain', [(i, (i + step if up[i] else i - step) % co...]
    pallas_call x11 -> x12, Pallas kernels: 17.4 us -> 17.8 us  [call(): pl.pallas_call(kernel, name=name, out_shape=[jax.ShapeDtypeStruct(*out) f...]
  transfers between devices with their start and end apart: 17 -> 17, of which waited for: 12 -> 10; matrix products, arithmetic and copies ran while one was open for 0% -> 0% of each run, Pallas kernels for 10% -> 11%
where the time goes in v7:
time: 65.5 us; the launch traced here: 65.3 us
  waiting for transfers between devices  23.9 us (36%)
  starting transfers between devices  22.9 us (35%)
  Pallas kernels  17.8 us (27%)
  between operations  0.73 us (1%)
    pallas_call x12, Pallas kernels, call(): pl.pallas_call(kernel, name=name, out_shape=[jax.ShapeDtypeStruct(*out) f...  17.8 us
    ppermute x8, waiting for transfers between devices, partner(): lax.ppermute(block, 'domain', [(i, i ^ mask) for i in range(lax.axis_size...  17.4 us
    ppermute x6, starting transfers between devices, exchanged(): lax.ppermute(block, 'domain', [(i, (i + step if up[i] else i - step) % co...  11.9 us
    ppermute x8, starting transfers between devices, partner(): lax.ppermute(block, 'domain', [(i, i ^ mask) for i in range(lax.axis_size...  10.8 us
    ppermute x6, waiting for transfers between devices, exchanged(): lax.ppermute(block, 'domain', [(i, (i + step if up[i] else i - step) % co...  5.08 us
    ppermute x3, waiting for transfers between devices, shifted(): lax.ppermute(block, axis, [(i, (i + by) % count) for i in range(count)])  1.46 us
  transfers between devices with their start and end apart: 17, of which 10 were waited for; matrix products, arithmetic and copies ran while one was open for 0% of the time, Pallas kernels for 11%

profile of v7, /device:TPU:0, one launch (start us, length us, event | category | flops | bytes accessed | tf_op | source)
XLA Modules:
  0.0 65.3 jit_solution(5630198366189892968)
XLA Ops:
  0.6 1.2 %gather.1 = (f32[136,256]{1,0:T(8,128)S(1)}, f32[136,256]{1,0:T(8,128)S(1)}, f32[8,128]{1,0:T(8,128)S(1)}) custom-call(s32[1,4]{1,0:T(1,128)} %send.3, f32[3,1,256]{2,1,0:T(1,128)} %bitcast.5, f32[1,256,256]{2,1,0:T(8,128)} %feat.3, f32[3,1,256]{2,1,0:T(1,128)} %bitcast.7), custom_call_target="tpu_custom_call" | custom-call | bytes 1048576 | tf_op jit(solution)/shard_map/gather/pallas_call | solution.py:677
  1.8 3.0 %collective-permute-start = (f32[136,256]{1,0:T(8,128)S(1)}, f32[136,256]{1,0:T(8,128)S(1)}, u32[]{:S(2)}, u32[]{:S(2)}) collective-permute-start(f32[136,256]{1,0:T(8,128)S(1)} %get-tuple-element.58), channel_id=1, source_target_pairs={{0,2},{2,0},{4,6},{6,4},{8,10},{10,8},{12,14},{14,12},{1,3},{3,1},... | collective-permute-start | bytes 417800 | tf_op jit(solution)/shard_map/ppermute | solution.py:697
  4.8 3.5 %collective-permute-start.1 = (f32[136,256]{1,0:T(8,128)S(1)}, f32[136,256]{1,0:T(8,128)S(1)}, u32[]{:S(2)}, u32[]{:S(2)}) collective-permute-start(f32[136,256]{1,0:T(8,128)S(1)} %get-tuple-element.59), channel_id=1, source_target_pairs={{0,14},{2,4},{4,2},{6,8},{8,6},{10,12},{12,10},{14,0},{1,15},{3,5}... | collective-permute-start | bytes 417800 | tf_op jit(solution)/shard_map/ppermute | solution.py:697
  8.4 1.6 %stage.1 = (f32[16,128]{1,0:T(8,128)S(1)}, f32[8,256]{1,0:T(8,128)S(1)}, f32[256,256]{1,0:T(8,128)S(1)}, f32[16,256]{1,0:T(8,128)S(1)}, bf16[768,256]{1,0:T(8,128)(2,1)S(1)}, /*index=5*/bf16[768,256]{1,0:T(8,128)(2,1)S(1)}) custom-call(s32[1,2]{1,0:T(1,128)} %centre.1, s32[1,2]{1,0:T(1,128)} %other.1, s32[1,2]{1,0:T(1,128)} %live.1, s32[1,4]{1,0:T(1,128)} %send.3, ...), custom_call_target="tpu_custom_call" | custom-call | bytes 1048576 | tf_op jit(solution)/shard_map/stage/pallas_call | solution.py:677
  10.0 0.8 %collective-permute-done.from_first = f32[136,256]{1,0:T(8,128)S(1)} collective-permute-done((f32[136,256]{1,0:T(8,128)S(1)}, f32[136,256]{1,0:T(8,128)S(1)}, u32[]{:S(2)}, u32[]{:S(2)}) %collective-permute-start) | collective-permute-done | bytes 139296 | tf_op jit(solution)/shard_map/ppermute | solution.py:697
  10.8 1.9 %collective-permute-done.1.from_second = f32[136,256]{1,0:T(8,128)S(1)} collective-permute-done((f32[136,256]{1,0:T(8,128)S(1)}, f32[136,256]{1,0:T(8,128)S(1)}, u32[]{:S(2)}, u32[]{:S(2)}) %collective-permute-start.1) | collective-permute-done | bytes 139296 | tf_op jit(solution)/shard_map/ppermute | solution.py:697
  12.7 5.1 %force.1 = (f32[1152,256]{1,0:T(8,128)S(1)}, f32[128,768]{1,0:T(8,128)S(1)}, f32[128,256]{1,0:T(8,128)S(1)}, f32[128,256]{1,0:T(8,128)S(1)}, f32[128,768]{1,0:T(...) custom-call(f32[16,128]{1,0:T(8,128)S(1)} %get-tuple-element.53.flag, ...), custom_call_target="tpu_custom_call" | custom-call | flops 2147483648 | bytes 1048576 | tf_op jit(solution)/shard_map/force/pallas_call | solution.py:677
  17.8 3.7 %collective-permute-start.2 = (f32[8,128]{1,0:T(8,128)S(1)}, f32[8,128]{1,0:T(8,128)S(1)}, u32[]{:S(2)}, u32[]{:S(2)}) collective-permute-start(f32[8,128]{1,0:T(8,128)S(1)} %get-tuple-element.62), channel_id=1, source_target_pairs={{0,14},{2,4},{4,2},{6,8},{8,6},{10,12},{12,10},{14,0},{1,15},{3,5}... | collective-permute-start | bytes 12296 | tf_op jit(solution)/shard_map/ppermute | solution.py:697
  21.5 0.5 collective-permute-start.3
  21.9 1.2 %collective-permute-start.4 = (f32[8,128]{1,0:T(8,128)S(1)}, f32[8,128]{1,0:T(8,128)S(1)}, u32[]{:S(2)}, u32[]{:S(2)}) collective-permute-start(f32[8,128]{1,0:T(8,128)S(1)} %get-tuple-element.64), channel_id=1, source_target_pairs={{0,2},{2,0},{4,6},{6,4},{8,10},{10,8},{12,14},{14,12},{1,3},{3,1},... | collective-permute-start | bytes 12296 | tf_op jit(solution)/shard_map/ppermute | solution.py:697
  23.2 1.3 %table.1 = (f32[2,20,64,128]{3,2,1,0:T(8,128)S(1)}, bf16[2,512,640]{2,1,0:T(8,128)(2,1)S(1)}, bf16[2,512,640]{2,1,0:T(8,128)(2,1)S(1)}, f32[8,128]{1,0:T(8,128)S(1)}) custom-call(f32[16,128]{1,0:T(8,128)S(1)} %get-tuple-element.53.flags, f32[8,128]{1,0:T(8,128)S(1)} %get-tuple-element.66.rows), custom_call_target="tpu_custom_call" | custom-call | flops 1073741824 | bytes 1048576 | tf_op jit(solution)/shard_map/table/pallas_call | solution.py:677
  24.5 2.4 %collective-permute-done.3.two_second = f32[8,128]{1,0:T(8,128)S(1)} collective-permute-done((f32[8,128]{1,0:T(8,128)S(1)}, f32[8,128]{1,0:T(8,128)S(1)}, u32[]{:S(2)}, u32[]{:S(2)}) %collective-permute-start.3) | collective-permute-done | bytes 4128 | tf_op jit(solution)/shard_map/ppermute | solution.py:697
  26.9 0.0 collective-permute-done.4.one_first
  26.9 3.5 %tangent.1 = (f32[3,1,256]{2,1,0:T(1,128)}, f32[768,128]{1,0:T(8,128)S(1)}, f32[768,128]{1,0:T(8,128)S(1)}, f32[8,256]{1,0:T(8,128)S(1)}, f32[1152,256]{1,0:T(8,...) custom-call(f32[16,128]{1,0:T(8,128)S(1)} %get-tuple-element.53.flags, f32[8,256]{1,0:T(8,128)S(1)} %get-tuple-element.54.atoms, ...), custom_call_target="tpu_custom_call" | custom-call | flops 2147483648 | bytes 1048576 | tf_op jit(solution)/shard_map/tangent/pallas_call | solution.py:677
  30.4 0.1 collective-permute-start.6
  30.5 2.0 %radial.2.radial_0 = f32[8,256]{1,0:T(8,128)S(1)} custom-call(f32[16,128]{1,0:T(8,128)S(1)} %get-tuple-element.80.both.after, f32[2,20,64,128]{3,2,1,0:T(8,128)S(1)} %get-tuple-element.81.shape_store, bf16[2,512,640]{2,1,0:T(8,128)(2,1)S(1)} %get-tuple-element.82.lh, bf16[2,512,640]{2,1,0:T(8,128)(2,1)S(1)} %get-tuple-element.83.ll, ...), custom_call_target="tpu_custom_call" | custom-call | flops 2147483648 | bytes 1048576 | tf_op jit(solution)/shard_map/radial/pallas_call | solution.py:677
  32.5 0.1 halve.1
  32.6 0.7 %collective-permute-start.7 = (f32[384,128]{1,0:T(8,128)S(1)}, f32[384,128]{1,0:T(8,128)S(1)}, u32[]{:S(2)}, u32[]{:S(2)}) collective-permute-start(f32[384,128]{1,0:T(8,128)S(1)} %get-tuple-element.79), channel_id=1, source_target_pairs={{0,2},{2,0},{4,6},{6,4},{8,10},{10,8},{12,14},{14,12},{1,3},{3,1},... | collective-permute-start | bytes 589832 | tf_op jit(solution)/shard_map/ppermute | solution.py:701
  33.3 2.0 %radial.3.radial_1 = f32[8,256]{1,0:T(8,128)S(1)} custom-call(f32[16,128]{1,0:T(8,128)S(1)} %get-tuple-element.80.both.after, f32[2,20,64,128]{3,2,1,0:T(8,128)S(1)} %get-tuple-element.81.shape_store, bf16[2,512,640]{2,1,0:T(8,128)(2,1)S(1)} %get-tuple-element.82.lh, bf16[2,512,640]{2,1,0:T(8,128)(2,1)S(1)} %get-tuple-element.83.ll, ...), custom_call_target="tpu_custom_call" | custom-call | flops 2147483648 | bytes 1048576 | tf_op jit(solution)/shard_map/radial/pallas_call | solution.py:677
  35.3 4.6 %collective-permute-done.7.taken = f32[384,128]{1,0:T(8,128)S(1)} collective-permute-done((f32[384,128]{1,0:T(8,128)S(1)}, f32[384,128]{1,0:T(8,128)S(1)}, u32[]{:S(2)}, u32[]{:S(2)}) %collective-permute-start.7) | collective-permute-done | bytes 196640 | tf_op jit(solution)/shard_map/ppermute | solution.py:701
  40.0 2.4 %collective-permute-start.8 = (f32[104,128]{1,0:T(8,128)S(1)}, f32[104,128]{1,0:T(8,128)S(1)}, u32[]{:S(2)}, u32[]{:S(2)}) collective-permute-start(f32[104,128]{1,0:T(8,128)S(1)} %get-tuple-element.92), channel_id=1, source_target_pairs={{0,12},{2,14},{4,8},{6,10},{8,4},{10,6},{12,0},{14,2},{1,13},{3,15... | collective-permute-start | bytes 159752 | tf_op jit(solution)/shard_map/ppermute | solution.py:701
  42.3 2.1 %collective-permute-start.10 = (f32[104,128]{1,0:T(8,128)S(1)}, f32[104,128]{1,0:T(8,128)S(1)}, u32[]{:S(2)}, u32[]{:S(2)}) collective-permute-start(f32[104,128]{1,0:T(8,128)S(1)} %get-tuple-element.94), channel_id=1, source_target_pairs={{0,4},{2,6},{4,0},{6,2},{8,12},{10,14},{12,8},{14,10},{1,5},{3,7},... | collective-permute-start | bytes 159752 | tf_op jit(solution)/shard_map/ppermute | solution.py:701
  44.4 1.6 %collective-permute-done.8.refs_1_ = f32[104,128]{1,0:T(8,128)S(1)} collective-permute-done((f32[104,128]{1,0:T(8,128)S(1)}, f32[104,128]{1,0:T(8,128)S(1)}, u32[]{:S(2)}, u32[]{:S(2)}) %collective-permute-start.8) | collective-permute-done | bytes 53280 | tf_op jit(solution)/shard_map/ppermute | solution.py:701
  46.0 1.7 %collective-permute-done.9.refs_2_ = f32[104,128]{1,0:T(8,128)S(1)} collective-permute-done((f32[104,128]{1,0:T(8,128)S(1)}, f32[104,128]{1,0:T(8,128)S(1)}, u32[]{:S(2)}, u32[]{:S(2)}) %collective-permute-start.9) | collective-permute-done | bytes 53280 | tf_op jit(solution)/shard_map/ppermute | solution.py:701
  47.7 2.5 %collective-permute-start.13 = (f32[104,128]{1,0:T(8,128)S(1)}, f32[104,128]{1,0:T(8,128)S(1)}, u32[]{:S(2)}, u32[]{:S(2)}) collective-permute-start(f32[104,128]{1,0:T(8,128)S(1)} %total.1.refs_0_), channel_id=1, source_target_pairs={{0,12},{2,14},{4,8},{6,10},{8,4},{10,6},{12,0},{14,2},{1,13},{3,15... | collective-permute-start | bytes 159752 | tf_op jit(solution)/shard_map/ppermute | solution.py:701
  50.2 2.0 %collective-permute-start.11 = (f32[104,128]{1,0:T(8,128)S(1)}, f32[104,128]{1,0:T(8,128)S(1)}, u32[]{:S(2)}, u32[]{:S(2)}) collective-permute-start(f32[104,128]{1,0:T(8,128)S(1)} %total.1.refs_0_), channel_id=1, source_target_pairs={{0,4},{2,6},{4,0},{6,2},{8,12},{10,14},{12,8},{14,10},{1,5},{3,7},... | collective-permute-start | bytes 159752 | tf_op jit(solution)/shard_map/ppermute | solution.py:701
  52.2 1.7 %collective-permute-done.13.refs_3_ = f32[104,128]{1,0:T(8,128)S(1)} collective-permute-done((f32[104,128]{1,0:T(8,128)S(1)}, f32[104,128]{1,0:T(8,128)S(1)}, u32[]{:S(2)}, u32[]{:S(2)}) %collective-permute-start.13) | collective-permute-done | bytes 53280 | tf_op jit(solution)/shard_map/ppermute | solution.py:701
  53.8 1.8 %collective-permute-done.12.refs_2_ = f32[104,128]{1,0:T(8,128)S(1)} collective-permute-done((f32[104,128]{1,0:T(8,128)S(1)}, f32[104,128]{1,0:T(8,128)S(1)}, u32[]{:S(2)}, u32[]{:S(2)}) %collective-permute-start.12) | collective-permute-done | bytes 53280 | tf_op jit(solution)/shard_map/ppermute | solution.py:701
  55.7 1.2 %collective-permute-start.14 = (f32[416,128]{1,0:T(8,128)S(1)}, f32[416,128]{1,0:T(8,128)S(1)}, u32[]{:S(2)}, u32[]{:S(2)}) collective-permute-start(f32[416,128]{1,0:T(8,128)S(1)} %grow.1.mine), channel_id=1, source_target_pairs={{0,2},{2,0},{4,6},{6,4},{8,10},{10,8},{12,14},{14,12},{1,3},{3,1},... | collective-permute-start | bytes 638984 | tf_op jit(solution)/shard_map/ppermute | solution.py:701
  56.9 6.0 %collective-permute-done.14.theirs = f32[416,128]{1,0:T(8,128)S(1)} collective-permute-done((f32[416,128]{1,0:T(8,128)S(1)}, f32[416,128]{1,0:T(8,128)S(1)}, u32[]{:S(2)}, u32[]{:S(2)}) %collective-permute-start.14) | collective-permute-done | bytes 213024 | tf_op jit(solution)/shard_map/ppermute | solution.py:701
  62.9 1.5 %collective-permute-done.16.facing_theirs = f32[416,128]{1,0:T(8,128)S(1)} collective-permute-done((f32[416,128]{1,0:T(8,128)S(1)}, f32[416,128]{1,0:T(8,128)S(1)}, u32[]{:S(2)}, u32[]{:S(2)}) %collective-permute-start.16) | collective-permute-done | bytes 213024 | tf_op jit(solution)/shard_map/ppermute | solution.py:691
  64.4 1.0 %join.1 = (f32[768,256]{1,0:T(8,128)}, f32[8,256]{1,0:T(8,128)}, f32[4,256]{1,0:T(4,128)}, f32[1,256]{1,0:T(1,128)}) custom-call(f32[416,128]{1,0:T(8,128)S(1)} %grow.1.mine, f32[416,128]{1,0:T(8,128)S(1)} %collective-permute-done.14.theirs, f32[416,128]{1,0:T(8,128)S(1)} %collective-permute-done.15.facing_mine, ...), custom_call_target="tpu_custom_call" | custom-call | bytes 1048576 | tf_op jit(solution)/shard_map/join/pallas_call | solution.py:677
  (14 shorter events, 0.1 us)
Async XLA Ops:
  1.8 8.9 %collective-permute-start = (f32[136,256]{1,0:T(8,128)S(1)}, f32[136,256]{1,0:T(8,128)S(1)}, u32[]{:S(2)}, u32[]{:S(2)}) collective-permute-start(f32[136,256]{1,0:T(8,128)S(1)} %get-tuple-element.58), channel_id=1, source_target_pairs={{0,2},{2,0},{4,6},{6,4},{8,10},{10,8},{12,14},{14,12},{1,3},{3,1},... | collective-permute-start | bytes 417800 | tf_op jit(solution)/shard_map/ppermute | solution.py:697
  4.8 7.8 %collective-permute-start.1 = (f32[136,256]{1,0:T(8,128)S(1)}, f32[136,256]{1,0:T(8,128)S(1)}, u32[]{:S(2)}, u32[]{:S(2)}) collective-permute-start(f32[136,256]{1,0:T(8,128)S(1)} %get-tuple-element.59), channel_id=1, source_target_pairs={{0,14},{2,4},{4,2},{6,8},{8,6},{10,12},{12,10},{14,0},{1,15},{3,5}... | collective-permute-start | bytes 417800 | tf_op jit(solution)/shard_map/ppermute | solution.py:697
  17.8 6.7 %collective-permute-start.2 = (f32[8,128]{1,0:T(8,128)S(1)}, f32[8,128]{1,0:T(8,128)S(1)}, u32[]{:S(2)}, u32[]{:S(2)}) collective-permute-start(f32[8,128]{1,0:T(8,128)S(1)} %get-tuple-element.62), channel_id=1, source_target_pairs={{0,14},{2,4},{4,2},{6,8},{8,6},{10,12},{12,10},{14,0},{1,15},{3,5}... | collective-permute-start | bytes 12296 | tf_op jit(solution)/shard_map/ppermute | solution.py:697
  21.5 5.4 %collective-permute-start.3 = (f32[8,128]{1,0:T(8,128)S(1)}, f32[8,128]{1,0:T(8,128)S(1)}, u32[]{:S(2)}, u32[]{:S(2)}) collective-permute-start(f32[8,128]{1,0:T(8,128)S(1)} %get-tuple-element.63), channel_id=1, source_target_pairs={{0,12},{2,14},{4,8},{6,10},{8,4},{10,6},{12,0},{14,2},{1,13},{3,15... | collective-permute-start | bytes 12296 | tf_op jit(solution)/shard_map/ppermute | solution.py:697
  21.9 5.0 %collective-permute-start.4 = (f32[8,128]{1,0:T(8,128)S(1)}, f32[8,128]{1,0:T(8,128)S(1)}, u32[]{:S(2)}, u32[]{:S(2)}) collective-permute-start(f32[8,128]{1,0:T(8,128)S(1)} %get-tuple-element.64), channel_id=1, source_target_pairs={{0,2},{2,0},{4,6},{6,4},{8,10},{10,8},{12,14},{14,12},{1,3},{3,1},... | collective-permute-start | bytes 12296 | tf_op jit(solution)/shard_map/ppermute | solution.py:697
  23.2 3.7 %collective-permute-start.5 = (f32[8,128]{1,0:T(8,128)S(1)}, f32[8,128]{1,0:T(8,128)S(1)}, u32[]{:S(2)}, u32[]{:S(2)}) collective-permute-start(f32[8,128]{1,0:T(8,128)S(1)} %get-tuple-element.65), channel_id=1, source_target_pairs={{0,4},{2,6},{4,0},{6,2},{8,12},{10,14},{12,8},{14,10},{1,5},{3,7},... | collective-permute-start | bytes 12296 | tf_op jit(solution)/shard_map/ppermute | solution.py:697
  30.4 2.1 %collective-permute-start.6 = (f32[768,128]{1,0:T(8,128)S(1)}, f32[768,128]{1,0:T(8,128)S(1)}, u32[]{:S(2)}, u32[]{:S(2)}) collective-permute-start(f32[768,128]{1,0:T(8,128)S(1)} %get-tuple-element.77), channel_id=1, source_target_pairs={{0,1},{1,0},{2,3},{3,2},{4,5},{5,4},{6,7},{7,6},{8,9},{9,8},{10,11... | collective-permute-start | bytes 1179656 | tf_op jit(solution)/shard_map/ppermute | solution.py:691
  32.6 7.4 %collective-permute-start.7 = (f32[384,128]{1,0:T(8,128)S(1)}, f32[384,128]{1,0:T(8,128)S(1)}, u32[]{:S(2)}, u32[]{:S(2)}) collective-permute-start(f32[384,128]{1,0:T(8,128)S(1)} %get-tuple-element.79), channel_id=1, source_target_pairs={{0,2},{2,0},{4,6},{6,4},{8,10},{10,8},{12,14},{14,12},{1,3},{3,1},... | collective-permute-start | bytes 589832 | tf_op jit(solution)/shard_map/ppermute | solution.py:701
  40.0 6.0 %collective-permute-start.8 = (f32[104,128]{1,0:T(8,128)S(1)}, f32[104,128]{1,0:T(8,128)S(1)}, u32[]{:S(2)}, u32[]{:S(2)}) collective-permute-start(f32[104,128]{1,0:T(8,128)S(1)} %get-tuple-element.92), channel_id=1, source_target_pairs={{0,12},{2,14},{4,8},{6,10},{8,4},{10,6},{12,0},{14,2},{1,13},{3,15... | collective-permute-start | bytes 159752 | tf_op jit(solution)/shard_map/ppermute | solution.py:701
  42.3 5.3 %collective-permute-start.9 = (f32[104,128]{1,0:T(8,128)S(1)}, f32[104,128]{1,0:T(8,128)S(1)}, u32[]{:S(2)}, u32[]{:S(2)}) collective-permute-start(f32[104,128]{1,0:T(8,128)S(1)} %get-tuple-element.93), channel_id=1, source_target_pairs={{0,8},{2,10},{4,12},{6,14},{8,0},{10,2},{12,4},{14,6},{1,9},{3,11}... | collective-permute-start | bytes 159752 | tf_op jit(solution)/shard_map/ppermute | solution.py:701
  42.3 5.3 %collective-permute-start.10 = (f32[104,128]{1,0:T(8,128)S(1)}, f32[104,128]{1,0:T(8,128)S(1)}, u32[]{:S(2)}, u32[]{:S(2)}) collective-permute-start(f32[104,128]{1,0:T(8,128)S(1)} %get-tuple-element.94), channel_id=1, source_target_pairs={{0,4},{2,6},{4,0},{6,2},{8,12},{10,14},{12,8},{14,10},{1,5},{3,7},... | collective-permute-start | bytes 159752 | tf_op jit(solution)/shard_map/ppermute | solution.py:701
  47.7 6.1 %collective-permute-start.13 = (f32[104,128]{1,0:T(8,128)S(1)}, f32[104,128]{1,0:T(8,128)S(1)}, u32[]{:S(2)}, u32[]{:S(2)}) collective-permute-start(f32[104,128]{1,0:T(8,128)S(1)} %total.1.refs_0_), channel_id=1, source_target_pairs={{0,12},{2,14},{4,8},{6,10},{8,4},{10,6},{12,0},{14,2},{1,13},{3,15... | collective-permute-start | bytes 159752 | tf_op jit(solution)/shard_map/ppermute | solution.py:701
  50.2 5.5 %collective-permute-start.12 = (f32[104,128]{1,0:T(8,128)S(1)}, f32[104,128]{1,0:T(8,128)S(1)}, u32[]{:S(2)}, u32[]{:S(2)}) collective-permute-start(f32[104,128]{1,0:T(8,128)S(1)} %total.1.refs_0_), channel_id=1, source_target_pairs={{0,8},{2,10},{4,12},{6,14},{8,0},{10,2},{12,4},{14,6},{1,9},{3,11}... | collective-permute-start | bytes 159752 | tf_op jit(solution)/shard_map/ppermute | solution.py:701
  50.2 5.5 %collective-permute-start.11 = (f32[104,128]{1,0:T(8,128)S(1)}, f32[104,128]{1,0:T(8,128)S(1)}, u32[]{:S(2)}, u32[]{:S(2)}) collective-permute-start(f32[104,128]{1,0:T(8,128)S(1)} %total.1.refs_0_), channel_id=1, source_target_pairs={{0,4},{2,6},{4,0},{6,2},{8,12},{10,14},{12,8},{14,10},{1,5},{3,7},... | collective-permute-start | bytes 159752 | tf_op jit(solution)/shard_map/ppermute | solution.py:701
  55.7 7.2 %collective-permute-start.14 = (f32[416,128]{1,0:T(8,128)S(1)}, f32[416,128]{1,0:T(8,128)S(1)}, u32[]{:S(2)}, u32[]{:S(2)}) collective-permute-start(f32[416,128]{1,0:T(8,128)S(1)} %grow.1.mine), channel_id=1, source_target_pairs={{0,2},{2,0},{4,6},{6,4},{8,10},{10,8},{12,14},{14,12},{1,3},{3,1},... | collective-permute-start | bytes 638984 | tf_op jit(solution)/shard_map/ppermute | solution.py:701
  56.9 6.0 %collective-permute-start.15 = (f32[416,128]{1,0:T(8,128)S(1)}, f32[416,128]{1,0:T(8,128)S(1)}, u32[]{:S(2)}, u32[]{:S(2)}) collective-permute-start(f32[416,128]{1,0:T(8,128)S(1)} %grow.1.mine), channel_id=1, source_target_pairs={{0,1},{1,0},{2,3},{3,2},{4,5},{5,4},{6,7},{7,6},{8,9},{9,8},{10,11... | collective-permute-start | bytes 638984 | tf_op jit(solution)/shard_map/ppermute | solution.py:691
  62.9 1.5 %collective-permute-start.16 = (f32[416,128]{1,0:T(8,128)S(1)}, f32[416,128]{1,0:T(8,128)S(1)}, u32[]{:S(2)}, u32[]{:S(2)}) collective-permute-start(f32[416,128]{1,0:T(8,128)S(1)} %collective-permute-done.14.theirs), channel_id=1, source_target_pairs={{0,1},{1,0},{2,3},{3,2},{4,5},{5,4},{6,7},{7,6},{8,9},{9,8},{10,11... | collective-permute-start | bytes 638984 | tf_op jit(solution)/shard_map/ppermute | solution.py:691

commit v8 on v7

--- a/solution.py
+++ b/solution.py
@@ -597,11 +597,16 @@
 
 
 SMALL = 32
+PAD = 8
 FOUR = 4
 
 
 def block_of(part, rows):
     return pl.ds(pl.multiple_of(part * rows, 8), rows)
+
+
+def block_from(start, rows):
+    return pl.ds(pl.multiple_of(start, 8), rows)
 
 
 def block_of_lanes(part):
@@ -615,49 +620,73 @@
     return total
 
 
-def halve_kernel(keep, taken, keep_out, give_out):
-    me = place(0, 2)
-    for out, part in ((keep_out, me), (give_out, 1 - me)):
-        out[...] = total_of([keep, taken], block_of(part, out.shape[0]))
-
-
-def spread_kernel(keep, taken, radial_0, radial_1, small, *refs):
-    outs, tiny = refs[:FOUR], refs[FOUR]
+def halve_kernel(keep, taken, after, *outs):
+    half, piece = keep.shape[0] // 2, keep.shape[0] // (2 * FOUR)
+    mine, me = place(0, 2), place(1, FOUR)
+    for i, out in enumerate(outs):
+        part = mine if i < 2 else 1 - mine
+        for j in range(2):
+            k = 1 + 2 * (i % 2) - j
+            at = block_from(part * half + lax.bitwise_xor(me, k) * piece, piece)
+            out[j * piece : (j + 1) * piece, :] = keep[at, :] + taken[at, :]
+        if out.shape[0] > 2 * piece:
+            out[2 * piece :, :] = jnp.zeros((out.shape[0] - 2 * piece, HALF), F32)
+
+
+def spread_kernel(first, keep, taken, radial_0, radial_1, small, after, out_0, out_1, tiny):
     for h in range(2):
         lanes = slice(h * HALF, (h + 1) * HALF)
         tiny[16 * h : 16 * h + 8, :] = radial_0[:, lanes] + radial_1[:, lanes]
         tiny[16 * h + 8 : 16 * h + 16, :] = small[:, lanes]
     me = place(1, FOUR)
-    for k, out in enumerate(outs):
-        rows, few = out.shape[0] - SMALL // FOUR, SMALL // FOUR
-        to = lax.bitwise_xor(me, k)
-        out[0:rows, :] = total_of([keep, taken], block_of(to, rows))
-        out[rows:, :] = tiny[block_of(to, few), :]
+    few = SMALL // FOUR
+    rows = keep.shape[0] // 2
+    for j, out in enumerate((out_0, out_1)):
+        out[0:rows, :] = total_of([keep, taken], slice(j * rows, (j + 1) * rows))
+        out[rows : rows + few, :] = tiny[block_of(lax.bitwise_xor(me, first - j), few), :]
+        if out.shape[0] > rows + few:
+            out[rows + few :, :] = jnp.zeros((out.shape[0] - rows - few, HALF), F32)
 
 
 def total_kernel(*refs):
-    refs[-1][...] = total_of(refs[:-1], slice(None))
-
-
-def grow_kernel(*refs):
-    parts, out = refs[:FOUR], refs[FOUR]
+    refs[-1][...] = total_of(refs[:-1], slice(0, refs[-1].shape[0]))
+
+
+def near_kernel(mine, third, out):
+    rows = mine.shape[0] - SMALL // FOUR
+    out[0:rows, :] = mine[0:rows, :]
+    out[rows : 2 * rows, :] = third[0:rows, :]
+    out[2 * rows :, :] = jnp.zeros((out.shape[0] - 2 * rows, HALF), F32)
+
+
+def rest_kernel(mine, first, second, third, after, out):
     few = SMALL // FOUR
-    rows = parts[0].shape[0] - few
+    rows = mine.shape[0] - few
+    out[0:rows, :] = second[0:rows, :]
+    out[rows : 2 * rows, :] = first[0:rows, :]
     me = place(1, FOUR)
-    for k, ref in enumerate(parts):
-        to = lax.bitwise_xor(me, k)
-        out[block_of(to, rows), :] = ref[0:rows, :]
-        out[pl.ds(pl.multiple_of(FOUR * rows + to * few, 8), few), :] = ref[rows:, :]
-
-
-def join_kernel(mine, theirs, facing_mine, facing_theirs, mix, radial, kinds, out):
-    rows = mine.shape[0] - SMALL
-    me, core = place(0, 2), lax.axis_index("batch")
-    for lane_part, pair in ((core, (mine, theirs)), (1 - core, (facing_mine, facing_theirs))):
-        lanes = block_of_lanes(lane_part)
-        for ref, part in zip(pair, (me, 1 - me)):
-            mix[block_of(part, rows), lanes] = ref[0:rows, :]
-    both = (mine[rows:, :] + theirs[rows:, :]) + (facing_mine[rows:, :] + facing_theirs[rows:, :])
+    for k, ref in enumerate((mine, first, second, third)):
+        out[block_from(2 * rows + lax.bitwise_xor(me, k) * few, few), :] = ref[rows:, :]
+
+
+def pair_kernel(near, rest, their_near, their_rest, out):
+    piece = (rest.shape[0] - SMALL) // 2
+    half = FOUR * piece
+    mine, me = place(0, 2), place(1, FOUR)
+    for refs, part in (((near, rest), mine), ((their_near, their_rest), 1 - mine)):
+        for ref, ks in zip(refs, ((0, 3), (2, 1))):
+            for j, k in enumerate(ks):
+                at = block_from(part * half + lax.bitwise_xor(me, k) * piece, piece)
+                out[at, :] = ref[j * piece : (j + 1) * piece, :]
+    out[2 * half :, :] = rest[2 * piece :, :] + their_rest[2 * piece :, :]
+
+
+def join_kernel(whole, facing, mix, radial, kinds, out):
+    rows = mix.shape[0]
+    core = lax.axis_index("batch")
+    for ref, part in ((whole, core), (facing, 1 - core)):
+        mix[:, block_of_lanes(part)] = ref[0:rows, :]
+    both = whole[rows:, :] + facing[rows:, :]
     for h in range(2):
         lanes = slice(h * HALF, (h + 1) * HALF)
         few = both[16 * h : 16 * h + 16, :]
@@ -682,7 +711,7 @@
         out_specs=[spec(pltpu.VMEM)] * len(outs),
         scratch_shapes=[pltpu.VMEM(*item) if isinstance(item, tuple) else item for item in scratch],
         compiler_params=pltpu.CompilerParams(vmem_limit_bytes=28 * 1024 * 1024),
-        cost_estimate=pl.CostEstimate(flops=flops, bytes_accessed=1 << 20, transcendentals=0),
+        cost_estimate=pl.CostEstimate(flops=flops, bytes_accessed=1 << 20 if flops else 1 << 10, transcendentals=0),
     )(*operands, *after)
 
 
@@ -842,38 +871,50 @@
             + [((2 * WIDE, channels), BF16)] * 2
             + [((BASIS * TA, channels), F32)],
             both, table_shape, lh, ll, eh, el, fsel, env, envdot, dinv, curl, mh, ml, after,
-            flops=1 << 31,
+            flops=1 << 31 if p == 0 else 0,
         )[0]
 
     radials = [radial(0, both)]
-    keep, give = call(
-        halve_kernel, "halve", [(rows_mix // 2, HALF)] * 2, [], keep, shifted(give, "batch", 1)
-    )
-    taken = partner(give, 1)
-    radials.append(radial(1, keep))
-    piece = rows_mix // (2 * FOUR) + SMALL // FOUR
-    blocks = call(
-        spread_kernel, "spread", [(piece, HALF)] * FOUR, [((SMALL, HALF), F32)],
-        keep, taken, *radials, small,
-    )
-    terms = [blocks[0]] + [partner(blocks[k], 2 * k) for k in range(FOUR - 1, 0, -1)]
-    (mine,) = call(total_kernel, "total", [(piece, HALF)], [], *terms)
+    piece = rows_mix // (2 * FOUR)
+    few = SMALL // FOUR
+    near, far, give_near, give_far = call(
+        halve_kernel, "halve", [(2 * piece, HALF)] * 3 + [(2 * piece + PAD, HALF)], [],
+        keep, shifted(give, "batch", 1), radials[0],
+    )
+    radials.append(radial(1, far))
+    blocks = []
+    after = radials[1]
+    taken_near = partner(give_near, 1)
+    taken_far = partner(give_far, 1)
+    for first, kept, taken in ((3, far, taken_far), (1, near, taken_near)):
+        blocks += call(
+            functools.partial(spread_kernel, first),
+            "spread", [(piece + few + PAD * k, HALF) for k in (first - 1, max(first - 2, 0))], [((SMALL, HALF), F32)],
+            kept, taken, *radials, small, after,
+        )
+        after = blocks[0]
+    terms = [blocks[3]] + [partner(blocks[3 - k], 2 * k) for k in range(FOUR - 1, 0, -1)]
+    (mine,) = call(total_kernel, "total", [(piece + few, HALF)], [], *terms)
     bit = 2 * FOUR
     while bit < lax.axis_size("domain"):
-        (mine,) = call(total_kernel, "total", [(piece, HALF)], [], mine, partner(mine, bit))
+        (mine,) = call(total_kernel, "total", [(piece + few, HALF)], [], mine, partner(mine, bit))
         bit *= 2
     parts = [mine] + [partner(mine, 2 * k) for k in range(1, FOUR)]
-    (mine,) = call(grow_kernel, "grow", [(rows_mix // 2 + SMALL, HALF)], [], *parts)
-    theirs = partner(mine, 1)
-    facing = [shifted(part, "batch", 1) for part in (mine, theirs)]
+    (near,) = call(near_kernel, "near", [(2 * piece + SMALL + PAD, HALF)], [], mine, parts[3])
+    their_near = partner(near, 1)
+    (rest,) = call(rest_kernel, "rest", [(2 * piece + SMALL, HALF)], [], *parts, near)
+    their_rest = partner(rest, 1)
+    (whole,) = call(
+        pair_kernel, "pair", [(rows_mix + SMALL, HALF)], [], near, rest, their_near, their_rest
+    )
+    facing = shifted(whole, "batch", 1)
     mix, radial_sum, kinds, out = call(
         join_kernel,
         "join",
         [(rows_mix, channels), (BASIS, channels), (SPECIES, channels), (1, channels)],
         [],
-        mine,
-        theirs,
-        *facing,
+        whole,
+        facing,
     )
     return forces.transpose(1, 0, 2), radial_sum, mix, kinds, out.reshape(channels)
 

time: 65.5 us -> 62.3 us (0.951)
  waiting for transfers between devices: 23.9 us -> 17.3 us
  starting transfers between devices: 22.9 us -> 26.3 us
    ppermute x8 -> x10, waiting for transfers between devices: 17.4 us -> 10.5 us  [partner(): lax.ppermute(block, 'domain', [(i, i ^ mask) for i in range(lax.axis_size...]
    ppermute x8 -> x10, starting transfers between devices: 10.8 us -> 14.2 us  [partner(): lax.ppermute(block, 'domain', [(i, i ^ mask) for i in range(lax.axis_size...]
    ppermute x3 -> x2, waiting for transfers between devices: 1.46 us -> 1.74 us  [shifted(): lax.ppermute(block, axis, [(i, (i + by) % count) for i in range(count)])]
    pallas_call x12 -> x15, Pallas kernels: 17.8 us -> 17.8 us  [call(): pl.pallas_call(kernel, name=name, out_shape=[jax.ShapeDtypeStruct(*out) f...]
  transfers between devices with their start and end apart: 17 -> 18, of which waited for: 10 -> 10; matrix products, arithmetic and copies ran while one was open for 0% -> 0% of each run, Pallas kernels for 11% -> 11%
where the time goes in v8:
time: 62.3 us; the launch traced here: 62.1 us
  starting transfers between devices  26.3 us (42%)
  Pallas kernels  17.8 us (29%)
  waiting for transfers between devices  17.3 us (28%)
  between operations  0.76 us (1%)
    pallas_call x15, Pallas kernels, call(): pl.pallas_call(kernel, name=name, out_shape=[jax.ShapeDtypeStruct(*out) f...  17.8 us
    ppermute x10, starting transfers between devices, partner(): lax.ppermute(block, 'domain', [(i, i ^ mask) for i in range(lax.axis_size...  14.2 us
    ppermute x6, starting transfers between devices, exchanged(): lax.ppermute(block, 'domain', [(i, (i + step if up[i] else i - step) % co...  11.9 us
    ppermute x10, waiting for transfers between devices, partner(): lax.ppermute(block, 'domain', [(i, i ^ mask) for i in range(lax.axis_size...  10.5 us
    ppermute x6, waiting for transfers between devices, exchanged(): lax.ppermute(block, 'domain', [(i, (i + step if up[i] else i - step) % co...  5.08 us
    ppermute x2, waiting for transfers between devices, shifted(): lax.ppermute(block, axis, [(i, (i + by) % count) for i in range(count)])  1.74 us
  transfers between devices with their start and end apart: 18, of which 10 were waited for; matrix products, arithmetic and copies ran while one was open for 0% of the time, Pallas kernels for 11%

profile of v8, /device:TPU:0, one launch (start us, length us, event | category | flops | bytes accessed | tf_op | source)
XLA Modules:
  0.0 62.1 jit_solution(12304043586907873137)
XLA Ops:
  0.6 1.2 %gather.1 = (f32[136,256]{1,0:T(8,128)S(1)}, f32[136,256]{1,0:T(8,128)S(1)}, f32[8,128]{1,0:T(8,128)S(1)}) custom-call(s32[1,4]{1,0:T(1,128)} %send.3, f32[3,1,256]{2,1,0:T(1,128)} %bitcast.5, f32[1,256,256]{2,1,0:T(8,128)} %feat.3, f32[3,1,256]{2,1,0:T(1,128)} %bitcast.7), custom_call_target="tpu_custom_call" | custom-call | bytes 1024 | tf_op jit(solution)/shard_map/gather/pallas_call | solution.py:706
  1.8 3.0 %collective-permute-start = (f32[136,256]{1,0:T(8,128)S(1)}, f32[136,256]{1,0:T(8,128)S(1)}, u32[]{:S(2)}, u32[]{:S(2)}) collective-permute-start(f32[136,256]{1,0:T(8,128)S(1)} %get-tuple-element.60), channel_id=1, source_target_pairs={{0,2},{2,0},{4,6},{6,4},{8,10},{10,8},{12,14},{14,12},{1,3},{3,1},... | collective-permute-start | bytes 417800 | tf_op jit(solution)/shard_map/ppermute | solution.py:726
  4.8 3.5 %collective-permute-start.1 = (f32[136,256]{1,0:T(8,128)S(1)}, f32[136,256]{1,0:T(8,128)S(1)}, u32[]{:S(2)}, u32[]{:S(2)}) collective-permute-start(f32[136,256]{1,0:T(8,128)S(1)} %get-tuple-element.61), channel_id=1, source_target_pairs={{0,14},{2,4},{4,2},{6,8},{8,6},{10,12},{12,10},{14,0},{1,15},{3,5}... | collective-permute-start | bytes 417800 | tf_op jit(solution)/shard_map/ppermute | solution.py:726
  8.4 1.6 %stage.1 = (f32[16,128]{1,0:T(8,128)S(1)}, f32[8,256]{1,0:T(8,128)S(1)}, f32[256,256]{1,0:T(8,128)S(1)}, f32[16,256]{1,0:T(8,128)S(1)}, bf16[768,256]{1,0:T(8,128)(2,1)S(1)}, /*index=5*/bf16[768,256]{1,0:T(8,128)(2,1)S(1)}) custom-call(s32[1,2]{1,0:T(1,128)} %centre.1, s32[1,2]{1,0:T(1,128)} %other.1, s32[1,2]{1,0:T(1,128)} %live.1, s32[1,4]{1,0:T(1,128)} %send.3, ...), custom_call_target="tpu_custom_call" | custom-call | bytes 1024 | tf_op jit(solution)/shard_map/stage/pallas_call | solution.py:706
  10.0 0.8 %collective-permute-done.from_first = f32[136,256]{1,0:T(8,128)S(1)} collective-permute-done((f32[136,256]{1,0:T(8,128)S(1)}, f32[136,256]{1,0:T(8,128)S(1)}, u32[]{:S(2)}, u32[]{:S(2)}) %collective-permute-start) | collective-permute-done | bytes 139296 | tf_op jit(solution)/shard_map/ppermute | solution.py:726
  10.8 1.9 %collective-permute-done.1.from_second = f32[136,256]{1,0:T(8,128)S(1)} collective-permute-done((f32[136,256]{1,0:T(8,128)S(1)}, f32[136,256]{1,0:T(8,128)S(1)}, u32[]{:S(2)}, u32[]{:S(2)}) %collective-permute-start.1) | collective-permute-done | bytes 139296 | tf_op jit(solution)/shard_map/ppermute | solution.py:726
  12.7 5.1 %force.1 = (f32[1152,256]{1,0:T(8,128)S(1)}, f32[128,768]{1,0:T(8,128)S(1)}, f32[128,256]{1,0:T(8,128)S(1)}, f32[128,256]{1,0:T(8,128)S(1)}, f32[128,768]{1,0:T(...) custom-call(f32[16,128]{1,0:T(8,128)S(1)} %get-tuple-element.55.flag, ...), custom_call_target="tpu_custom_call" | custom-call | flops 2147483648 | bytes 1048576 | tf_op jit(solution)/shard_map/force/pallas_call | solution.py:706
  17.7 3.7 %collective-permute-start.2 = (f32[8,128]{1,0:T(8,128)S(1)}, f32[8,128]{1,0:T(8,128)S(1)}, u32[]{:S(2)}, u32[]{:S(2)}) collective-permute-start(f32[8,128]{1,0:T(8,128)S(1)} %get-tuple-element.64), channel_id=1, source_target_pairs={{0,14},{2,4},{4,2},{6,8},{8,6},{10,12},{12,10},{14,0},{1,15},{3,5}... | collective-permute-start | bytes 12296 | tf_op jit(solution)/shard_map/ppermute | solution.py:726
  21.4 0.5 collective-permute-start.3
  21.9 1.2 %collective-permute-start.4 = (f32[8,128]{1,0:T(8,128)S(1)}, f32[8,128]{1,0:T(8,128)S(1)}, u32[]{:S(2)}, u32[]{:S(2)}) collective-permute-start(f32[8,128]{1,0:T(8,128)S(1)} %get-tuple-element.66), channel_id=1, source_target_pairs={{0,2},{2,0},{4,6},{6,4},{8,10},{10,8},{12,14},{14,12},{1,3},{3,1},... | collective-permute-start | bytes 12296 | tf_op jit(solution)/shard_map/ppermute | solution.py:726
  23.1 1.3 %table.1 = (f32[2,20,64,128]{3,2,1,0:T(8,128)S(1)}, bf16[2,512,640]{2,1,0:T(8,128)(2,1)S(1)}, bf16[2,512,640]{2,1,0:T(8,128)(2,1)S(1)}, f32[8,128]{1,0:T(8,128)S(1)}) custom-call(f32[16,128]{1,0:T(8,128)S(1)} %get-tuple-element.55.flags, f32[8,128]{1,0:T(8,128)S(1)} %get-tuple-element.68.rows), custom_call_target="tpu_custom_call" | custom-call | flops 1073741824 | bytes 1048576 | tf_op jit(solution)/shard_map/table/pallas_call | solution.py:706
  24.4 2.4 %collective-permute-done.3.two_second = f32[8,128]{1,0:T(8,128)S(1)} collective-permute-done((f32[8,128]{1,0:T(8,128)S(1)}, f32[8,128]{1,0:T(8,128)S(1)}, u32[]{:S(2)}, u32[]{:S(2)}) %collective-permute-start.3) | collective-permute-done | bytes 4128 | tf_op jit(solution)/shard_map/ppermute | solution.py:726
  26.8 3.5 %tangent.1 = (f32[3,1,256]{2,1,0:T(1,128)}, f32[768,128]{1,0:T(8,128)S(1)}, f32[768,128]{1,0:T(8,128)S(1)}, f32[8,256]{1,0:T(8,128)S(1)}, f32[1152,256]{1,0:T(8,...) custom-call(f32[16,128]{1,0:T(8,128)S(1)} %get-tuple-element.55.flags, f32[8,256]{1,0:T(8,128)S(1)} %get-tuple-element.56.atoms, ...), custom_call_target="tpu_custom_call" | custom-call | flops 2147483648 | bytes 1048576 | tf_op jit(solution)/shard_map/tangent/pallas_call | solution.py:706
  30.4 2.0 %radial.2.after.radial_0 = f32[8,256]{1,0:T(8,128)S(1)} custom-call(f32[16,128]{1,0:T(8,128)S(1)} %get-tuple-element.80.both.after, f32[2,20,64,128]{3,2,1,0:T(8,128)S(1)} %get-tuple-element.81.shape_store, bf16[2,512,640]{2,1,0:T(8,128)(2,1)S(1)} %get-tuple-element.82.lh, bf16[2,512,640]{2,1,0:T(8,128)(2,1)S(1)} %get-tuple-element.83.ll, ...), custom_call_target="tpu_custom_call" | custom-call | flops 2147483648 | bytes 1048576 | tf_op jit(solution)/shard_map/radial/pallas_call | solution.py:706
  32.5 0.7 %collective-permute-start.8 = (f32[200,128]{1,0:T(8,128)S(1)}, f32[200,128]{1,0:T(8,128)S(1)}, u32[]{:S(2)}, u32[]{:S(2)}) collective-permute-start(f32[200,128]{1,0:T(8,128)S(1)} %get-tuple-element.94), channel_id=1, source_target_pairs={{0,2},{2,0},{4,6},{6,4},{8,10},{10,8},{12,14},{14,12},{1,3},{3,1},... | collective-permute-start | bytes 307208 | tf_op jit(solution)/shard_map/ppermute | solution.py:730
  33.2 1.4 %collective-permute-start.7 = (f32[192,128]{1,0:T(8,128)S(1)}, f32[192,128]{1,0:T(8,128)S(1)}, u32[]{:S(2)}, u32[]{:S(2)}) collective-permute-start(f32[192,128]{1,0:T(8,128)S(1)} %get-tuple-element.91), channel_id=1, source_target_pairs={{0,2},{2,0},{4,6},{6,4},{8,10},{10,8},{12,14},{14,12},{1,3},{3,1},... | collective-permute-start | bytes 294920 | tf_op jit(solution)/shard_map/ppermute | solution.py:730
  34.6 2.0 %radial.3.radial_1.after = f32[8,256]{1,0:T(8,128)S(1)} custom-call(f32[16,128]{1,0:T(8,128)S(1)} %get-tuple-element.80.both.after, f32[2,20,64,128]{3,2,1,0:T(8,128)S(1)} %get-tuple-element.81.shape_store, bf16[2,512,640]{2,1,0:T(8,128)(2,1)S(1)} %get-tuple-element.82.lh, bf16[2,512,640]{2,1,0:T(8,128)(2,1)S(1)} %get-tuple-element.83.ll, ...), custom_call_target="tpu_custom_call" | custom-call | bytes 1024 | tf_op jit(solution)/shard_map/radial/pallas_call | solution.py:706
  36.6 1.6 %collective-permute-done.8.taken = f32[200,128]{1,0:T(8,128)S(1)} collective-permute-done((f32[200,128]{1,0:T(8,128)S(1)}, f32[200,128]{1,0:T(8,128)S(1)}, u32[]{:S(2)}, u32[]{:S(2)}) %collective-permute-start.8) | collective-permute-done | bytes 102432 | tf_op jit(solution)/shard_map/ppermute | solution.py:730
  38.2 2.2 %collective-permute-start.9 = (f32[120,128]{1,0:T(8,128)S(1)}, f32[120,128]{1,0:T(8,128)S(1)}, u32[]{:S(2)}, u32[]{:S(2)}) collective-permute-start(f32[120,128]{1,0:T(8,128)S(1)} %get-tuple-element.95.after), channel_id=1, source_target_pairs={{0,12},{2,14},{4,8},{6,10},{8,4},{10,6},{12,0},{14,2},{1,13},{3,15... | collective-permute-start | bytes 184328 | tf_op jit(solution)/shard_map/ppermute | solution.py:730
  40.4 2.3 %collective-permute-start.11 = (f32[104,128]{1,0:T(8,128)S(1)}, f32[104,128]{1,0:T(8,128)S(1)}, u32[]{:S(2)}, u32[]{:S(2)}) collective-permute-start(f32[104,128]{1,0:T(8,128)S(1)} %get-tuple-element.98), channel_id=1, source_target_pairs={{0,4},{2,6},{4,0},{6,2},{8,12},{10,14},{12,8},{14,10},{1,5},{3,7},... | collective-permute-start | bytes 159752 | tf_op jit(solution)/shard_map/ppermute | solution.py:730
  42.8 2.4 %collective-permute-done.11.refs_3_ = f32[104,128]{1,0:T(8,128)S(1)} collective-permute-done((f32[104,128]{1,0:T(8,128)S(1)}, f32[104,128]{1,0:T(8,128)S(1)}, u32[]{:S(2)}, u32[]{:S(2)}) %collective-permute-start.11) | collective-permute-done | bytes 53280 | tf_op jit(solution)/shard_map/ppermute | solution.py:730
  45.2 0.6 %collective-permute-done.10.refs_2_ = f32[112,128]{1,0:T(8,128)S(1)} collective-permute-done((f32[112,128]{1,0:T(8,128)S(1)}, f32[112,128]{1,0:T(8,128)S(1)}, u32[]{:S(2)}, u32[]{:S(2)}) %collective-permute-start.10) | collective-permute-done | bytes 57376 | tf_op jit(solution)/shard_map/ppermute | solution.py:730
  45.9 2.5 %collective-permute-start.12 = (f32[104,128]{1,0:T(8,128)S(1)}, f32[104,128]{1,0:T(8,128)S(1)}, u32[]{:S(2)}, u32[]{:S(2)}) collective-permute-start(f32[104,128]{1,0:T(8,128)S(1)} %total.1.mine), channel_id=1, source_target_pairs={{0,12},{2,14},{4,8},{6,10},{8,4},{10,6},{12,0},{14,2},{1,13},{3,15... | collective-permute-start | bytes 159752 | tf_op jit(solution)/shard_map/ppermute | solution.py:730
  48.4 0.1 collective-permute-start.14
  48.5 1.8 %collective-permute-start.13 = (f32[104,128]{1,0:T(8,128)S(1)}, f32[104,128]{1,0:T(8,128)S(1)}, u32[]{:S(2)}, u32[]{:S(2)}) collective-permute-start(f32[104,128]{1,0:T(8,128)S(1)} %total.1.mine), channel_id=1, source_target_pairs={{0,4},{2,6},{4,0},{6,2},{8,12},{10,14},{12,8},{14,10},{1,5},{3,7},... | collective-permute-start | bytes 159752 | tf_op jit(solution)/shard_map/ppermute | solution.py:730
  50.3 1.5 %collective-permute-done.12.third = f32[104,128]{1,0:T(8,128)S(1)} collective-permute-done((f32[104,128]{1,0:T(8,128)S(1)}, f32[104,128]{1,0:T(8,128)S(1)}, u32[]{:S(2)}, u32[]{:S(2)}) %collective-permute-start.12) | collective-permute-done | bytes 53280 | tf_op jit(solution)/shard_map/ppermute | solution.py:730
  51.9 1.8 %collective-permute-start.15 = (f32[232,128]{1,0:T(8,128)S(1)}, f32[232,128]{1,0:T(8,128)S(1)}, u32[]{:S(2)}, u32[]{:S(2)}) collective-permute-start(f32[232,128]{1,0:T(8,128)S(1)} %near.1.after), channel_id=1, source_target_pairs={{0,2},{2,0},{4,6},{6,4},{8,10},{10,8},{12,14},{14,12},{1,3},{3,1},... | collective-permute-start | bytes 356360 | tf_op jit(solution)/shard_map/ppermute | solution.py:730
  53.7 0.2 collective-permute-done.14.second
  53.9 1.4 %collective-permute-start.16 = (f32[224,128]{1,0:T(8,128)S(1)}, f32[224,128]{1,0:T(8,128)S(1)}, u32[]{:S(2)}, u32[]{:S(2)}) collective-permute-start(f32[224,128]{1,0:T(8,128)S(1)} %rest.1), channel_id=1, source_target_pairs={{0,2},{2,0},{4,6},{6,4},{8,10},{10,8},{12,14},{14,12},{1,3},{3,1},... | collective-permute-start | bytes 344072 | tf_op jit(solution)/shard_map/ppermute | solution.py:730
  55.3 4.0 %collective-permute-done.16.their_rest = f32[224,128]{1,0:T(8,128)S(1)} collective-permute-done((f32[224,128]{1,0:T(8,128)S(1)}, f32[224,128]{1,0:T(8,128)S(1)}, u32[]{:S(2)}, u32[]{:S(2)}) %collective-permute-start.16) | collective-permute-done | bytes 114720 | tf_op jit(solution)/shard_map/ppermute | solution.py:730
  59.4 1.7 %collective-permute-done.17.facing = f32[800,128]{1,0:T(8,128)S(1)} collective-permute-done((f32[800,128]{1,0:T(8,128)S(1)}, f32[800,128]{1,0:T(8,128)S(1)}, u32[]{:S(2)}, u32[]{:S(2)}) %collective-permute-start.17) | collective-permute-done | bytes 409632 | tf_op jit(solution)/shard_map/ppermute | solution.py:720
  61.1 1.0 %join.1 = (f32[768,256]{1,0:T(8,128)}, f32[8,256]{1,0:T(8,128)}, f32[4,256]{1,0:T(4,128)}, f32[1,256]{1,0:T(1,128)}) custom-call(f32[800,128]{1,0:T(8,128)S(1)} %pair.1.whole, f32[800,128]{1,0:T(8,128)S(1)} %collective-permute-done.17.facing), custom_call_target="tpu_custom_call" | custom-call | bytes 1024 | tf_op jit(solution)/shard_map/join/pallas_call | solution.py:706
  (19 shorter events, 0.3 us)
Async XLA Ops:
  1.8 8.9 %collective-permute-start = (f32[136,256]{1,0:T(8,128)S(1)}, f32[136,256]{1,0:T(8,128)S(1)}, u32[]{:S(2)}, u32[]{:S(2)}) collective-permute-start(f32[136,256]{1,0:T(8,128)S(1)} %get-tuple-element.60), channel_id=1, source_target_pairs={{0,2},{2,0},{4,6},{6,4},{8,10},{10,8},{12,14},{14,12},{1,3},{3,1},... | collective-permute-start | bytes 417800 | tf_op jit(solution)/shard_map/ppermute | solution.py:726
  4.8 7.8 %collective-permute-start.1 = (f32[136,256]{1,0:T(8,128)S(1)}, f32[136,256]{1,0:T(8,128)S(1)}, u32[]{:S(2)}, u32[]{:S(2)}) collective-permute-start(f32[136,256]{1,0:T(8,128)S(1)} %get-tuple-element.61), channel_id=1, source_target_pairs={{0,14},{2,4},{4,2},{6,8},{8,6},{10,12},{12,10},{14,0},{1,15},{3,5}... | collective-permute-start | bytes 417800 | tf_op jit(solution)/shard_map/ppermute | solution.py:726
  17.7 6.7 %collective-permute-start.2 = (f32[8,128]{1,0:T(8,128)S(1)}, f32[8,128]{1,0:T(8,128)S(1)}, u32[]{:S(2)}, u32[]{:S(2)}) collective-permute-start(f32[8,128]{1,0:T(8,128)S(1)} %get-tuple-element.64), channel_id=1, source_target_pairs={{0,14},{2,4},{4,2},{6,8},{8,6},{10,12},{12,10},{14,0},{1,15},{3,5}... | collective-permute-start | bytes 12296 | tf_op jit(solution)/shard_map/ppermute | solution.py:726
  21.4 5.4 %collective-permute-start.3 = (f32[8,128]{1,0:T(8,128)S(1)}, f32[8,128]{1,0:T(8,128)S(1)}, u32[]{:S(2)}, u32[]{:S(2)}) collective-permute-start(f32[8,128]{1,0:T(8,128)S(1)} %get-tuple-element.65), channel_id=1, source_target_pairs={{0,12},{2,14},{4,8},{6,10},{8,4},{10,6},{12,0},{14,2},{1,13},{3,15... | collective-permute-start | bytes 12296 | tf_op jit(solution)/shard_map/ppermute | solution.py:726
  21.9 5.0 %collective-permute-start.4 = (f32[8,128]{1,0:T(8,128)S(1)}, f32[8,128]{1,0:T(8,128)S(1)}, u32[]{:S(2)}, u32[]{:S(2)}) collective-permute-start(f32[8,128]{1,0:T(8,128)S(1)} %get-tuple-element.66), channel_id=1, source_target_pairs={{0,2},{2,0},{4,6},{6,4},{8,10},{10,8},{12,14},{14,12},{1,3},{3,1},... | collective-permute-start | bytes 12296 | tf_op jit(solution)/shard_map/ppermute | solution.py:726
  23.1 3.7 %collective-permute-start.5 = (f32[8,128]{1,0:T(8,128)S(1)}, f32[8,128]{1,0:T(8,128)S(1)}, u32[]{:S(2)}, u32[]{:S(2)}) collective-permute-start(f32[8,128]{1,0:T(8,128)S(1)} %get-tuple-element.67), channel_id=1, source_target_pairs={{0,4},{2,6},{4,0},{6,2},{8,12},{10,14},{12,8},{14,10},{1,5},{3,7},... | collective-permute-start | bytes 12296 | tf_op jit(solution)/shard_map/ppermute | solution.py:726
  30.3 2.1 %collective-permute-start.6 = (f32[768,128]{1,0:T(8,128)S(1)}, f32[768,128]{1,0:T(8,128)S(1)}, u32[]{:S(2)}, u32[]{:S(2)}) collective-permute-start(f32[768,128]{1,0:T(8,128)S(1)} %get-tuple-element.79), channel_id=1, source_target_pairs={{0,1},{1,0},{2,3},{3,2},{4,5},{5,4},{6,7},{7,6},{8,9},{9,8},{10,11... | collective-permute-start | bytes 1179656 | tf_op jit(solution)/shard_map/ppermute | solution.py:720
  32.5 5.7 %collective-permute-start.8 = (f32[200,128]{1,0:T(8,128)S(1)}, f32[200,128]{1,0:T(8,128)S(1)}, u32[]{:S(2)}, u32[]{:S(2)}) collective-permute-start(f32[200,128]{1,0:T(8,128)S(1)} %get-tuple-element.94), channel_id=1, source_target_pairs={{0,2},{2,0},{4,6},{6,4},{8,10},{10,8},{12,14},{14,12},{1,3},{3,1},... | collective-permute-start | bytes 307208 | tf_op jit(solution)/shard_map/ppermute | solution.py:730
  33.2 7.2 %collective-permute-start.7 = (f32[192,128]{1,0:T(8,128)S(1)}, f32[192,128]{1,0:T(8,128)S(1)}, u32[]{:S(2)}, u32[]{:S(2)}) collective-permute-start(f32[192,128]{1,0:T(8,128)S(1)} %get-tuple-element.91), channel_id=1, source_target_pairs={{0,2},{2,0},{4,6},{6,4},{8,10},{10,8},{12,14},{14,12},{1,3},{3,1},... | collective-permute-start | bytes 294920 | tf_op jit(solution)/shard_map/ppermute | solution.py:730
  38.2 7.6 %collective-permute-start.9 = (f32[120,128]{1,0:T(8,128)S(1)}, f32[120,128]{1,0:T(8,128)S(1)}, u32[]{:S(2)}, u32[]{:S(2)}) collective-permute-start(f32[120,128]{1,0:T(8,128)S(1)} %get-tuple-element.95.after), channel_id=1, source_target_pairs={{0,12},{2,14},{4,8},{6,10},{8,4},{10,6},{12,0},{14,2},{1,13},{3,15... | collective-permute-start | bytes 184328 | tf_op jit(solution)/shard_map/ppermute | solution.py:730
  40.4 5.4 %collective-permute-start.10 = (f32[112,128]{1,0:T(8,128)S(1)}, f32[112,128]{1,0:T(8,128)S(1)}, u32[]{:S(2)}, u32[]{:S(2)}) collective-permute-start(f32[112,128]{1,0:T(8,128)S(1)} %get-tuple-element.97), channel_id=1, source_target_pairs={{0,8},{2,10},{4,12},{6,14},{8,0},{10,2},{12,4},{14,6},{1,9},{3,11}... | collective-permute-start | bytes 172040 | tf_op jit(solution)/shard_map/ppermute | solution.py:730
  40.4 4.8 %collective-permute-start.11 = (f32[104,128]{1,0:T(8,128)S(1)}, f32[104,128]{1,0:T(8,128)S(1)}, u32[]{:S(2)}, u32[]{:S(2)}) collective-permute-start(f32[104,128]{1,0:T(8,128)S(1)} %get-tuple-element.98), channel_id=1, source_target_pairs={{0,4},{2,6},{4,0},{6,2},{8,12},{10,14},{12,8},{14,10},{1,5},{3,7},... | collective-permute-start | bytes 159752 | tf_op jit(solution)/shard_map/ppermute | solution.py:730
  45.9 6.0 %collective-permute-start.12 = (f32[104,128]{1,0:T(8,128)S(1)}, f32[104,128]{1,0:T(8,128)S(1)}, u32[]{:S(2)}, u32[]{:S(2)}) collective-permute-start(f32[104,128]{1,0:T(8,128)S(1)} %total.1.mine), channel_id=1, source_target_pairs={{0,12},{2,14},{4,8},{6,10},{8,4},{10,6},{12,0},{14,2},{1,13},{3,15... | collective-permute-start | bytes 159752 | tf_op jit(solution)/shard_map/ppermute | solution.py:730
  48.4 5.5 %collective-permute-start.14 = (f32[104,128]{1,0:T(8,128)S(1)}, f32[104,128]{1,0:T(8,128)S(1)}, u32[]{:S(2)}, u32[]{:S(2)}) collective-permute-start(f32[104,128]{1,0:T(8,128)S(1)} %total.1.mine), channel_id=1, source_target_pairs={{0,8},{2,10},{4,12},{6,14},{8,0},{10,2},{12,4},{14,6},{1,9},{3,11}... | collective-permute-start | bytes 159752 | tf_op jit(solution)/shard_map/ppermute | solution.py:730
  48.5 5.4 %collective-permute-start.13 = (f32[104,128]{1,0:T(8,128)S(1)}, f32[104,128]{1,0:T(8,128)S(1)}, u32[]{:S(2)}, u32[]{:S(2)}) collective-permute-start(f32[104,128]{1,0:T(8,128)S(1)} %total.1.mine), channel_id=1, source_target_pairs={{0,4},{2,6},{4,0},{6,2},{8,12},{10,14},{12,8},{14,10},{1,5},{3,7},... | collective-permute-start | bytes 159752 | tf_op jit(solution)/shard_map/ppermute | solution.py:730
  51.9 7.4 %collective-permute-start.15 = (f32[232,128]{1,0:T(8,128)S(1)}, f32[232,128]{1,0:T(8,128)S(1)}, u32[]{:S(2)}, u32[]{:S(2)}) collective-permute-start(f32[232,128]{1,0:T(8,128)S(1)} %near.1.after), channel_id=1, source_target_pairs={{0,2},{2,0},{4,6},{6,4},{8,10},{10,8},{12,14},{14,12},{1,3},{3,1},... | collective-permute-start | bytes 356360 | tf_op jit(solution)/shard_map/ppermute | solution.py:730
  53.9 5.3 %collective-permute-start.16 = (f32[224,128]{1,0:T(8,128)S(1)}, f32[224,128]{1,0:T(8,128)S(1)}, u32[]{:S(2)}, u32[]{:S(2)}) collective-permute-start(f32[224,128]{1,0:T(8,128)S(1)} %rest.1), channel_id=1, source_target_pairs={{0,2},{2,0},{4,6},{6,4},{8,10},{10,8},{12,14},{14,12},{1,3},{3,1},... | collective-permute-start | bytes 344072 | tf_op jit(solution)/shard_map/ppermute | solution.py:730
  59.3 1.8 %collective-permute-start.17 = (f32[800,128]{1,0:T(8,128)S(1)}, f32[800,128]{1,0:T(8,128)S(1)}, u32[]{:S(2)}, u32[]{:S(2)}) collective-permute-start(f32[800,128]{1,0:T(8,128)S(1)} %pair.1.whole), channel_id=1, source_target_pairs={{0,1},{1,0},{2,3},{3,2},{4,5},{5,4},{6,7},{7,6},{8,9},{9,8},{10,11... | collective-permute-start | bytes 1228808 | tf_op jit(solution)/shard_map/ppermute | solution.py:720

commit v9 on v8

--- a/solution.py
+++ b/solution.py
@@ -42,6 +42,18 @@
         return lax.dot_general(x, y, dims, preferred_element_type=F32)
 
     return one(lh, rh) + (one(lh, rl) + one(ll, rh))
+
+
+def long_product(left, right, dims):
+    return lax.dot_general(left, right, dims, preferred_element_type=F32)
+
+
+def put_left(ref, p, rows, lane, width, value):
+    hi, lo = split(value)
+    span = ref.shape[2] // 3
+    for third, part in enumerate((hi, lo, hi)):
+        at = third * span + lane
+        ref[p, rows, at : at + width] = part
 
 
 def flag(condition):
@@ -170,12 +182,14 @@
     return twice(first, p)
 
 
-def radial_feat(feat, radial, p, high_ref, low_ref):
+def radial_feat(feat, radial, p, tall, wide):
     own = feat[p * TA : (p + 1) * TA, :]
+    span, channels = BASIS * TA, feat.shape[1]
     for n in range(BASIS):
         hi, lo = split(own * radial[n : n + 1, :])
-        high_ref[n * TA : (n + 1) * TA, :] = hi
-        low_ref[n * TA : (n + 1) * TA, :] = lo
+        for third, part in enumerate((hi, hi, lo)):
+            tall[p, third * span + n * TA : third * span + (n + 1) * TA, :] = part
+            wide[p, n * TA : (n + 1) * TA, third * channels : (third + 1) * channels] = part
 
 
 OTHER, CENTRE, LIVE, SAME, SHARED, SENT = 0, 2, 4, 6, 8, 9
@@ -279,8 +293,8 @@
 
 def force_kernel(
     flags, atoms, feat, weights, mh, ml, from_second, from_first,
-    env, dinv, gate, curve, inv, rows, fsel, own, one_first, one_second, two_first, two_second, shape_store, xh, xl, eh, el,
-    square, turned, th, tl, raw, back,
+    env, dinv, gate, curve, inv, rows, fsel, own, one_first, one_second, two_first, two_second, shape_store, tall, eh, el,
+    square, turned, table, wide, steady, raw, back,
 ):
     ghost = SEND * TA
     up = upward(0)
@@ -323,11 +337,9 @@
         for m in range(COMPS):
             for k in range(BASIS // 2):
                 entry = values[k] if m == 0 else angular[m] * values[k]
-                hi, lo = split(entry)
-                th[p, m * TA : (m + 1) * TA, k * CHUNK : (k + 1) * CHUNK] = hi
-                tl[p, m * TA : (m + 1) * TA, k * CHUNK : (k + 1) * CHUNK] = lo
-        radial_feat(fsel, weights, p, xh.at[p], xl.at[p])
-        raw[p * COMPS * TA : (p + 1) * COMPS * TA, :] = product((th[p], tl[p]), (xh[p], xl[p]), NN)
+                put_left(table, p, slice(m * TA, (m + 1) * TA), k * CHUNK, CHUNK, entry)
+        radial_feat(fsel, weights, p, tall, wide)
+        raw[p * COMPS * TA : (p + 1) * COMPS * TA, :] = long_product(table[p], tall[p], NN)
 
     for m in range(COMPS):
         first = raw[m * TA : (m + 1) * TA, :]
@@ -358,13 +370,15 @@
         for m in range(COMPS):
             block = env[(p * COMPS + m) * TA : (p * COMPS + m + 1) * TA, :]
             part = dinv[p * TA : (p + 1) * TA, GROUP[m] * 256 : (GROUP[m] + 1) * 256]
+            at = slice(m * TA, (m + 1) * TA)
             hi, lo = split((2.0 * env_scale) * block * part)
-            eh[p, m * TA : (m + 1) * TA, :] = hi
-            el[p, m * TA : (m + 1) * TA, :] = lo
+            eh[p, at, :] = hi
+            el[p, at, :] = lo
+            for third, piece in enumerate((hi, lo, hi)):
+                steady[p, at, third * 256 : (third + 1) * 256] = piece
         for ref in (eh, el):
             ref[p, COMPS * TA :, :] = jnp.zeros((WIDE - COMPS * TA, ref.shape[2]), BF16)
-        steady = (eh[p, 0 : COMPS * TA, :], el[p, 0 : COMPS * TA, :])
-        back[p] = product(steady, (xh[p], xl[p]), NT)
+        back[p] = long_product(steady[p], wide[p], NT)
         d_radius = None
         d_angular = []
         for m in range(COMPS):
@@ -416,9 +430,9 @@
 
 def tangent_kernel(
     scale, flags, atoms, weights, mh, ml, from_first, from_second, own, one_second, two_second, one_first, two_first,
-    rows, env, gate, curve, inv, shape_store, xh, xl, after,
+    rows, env, gate, curve, inv, shape_store, tall, after,
     forces, keep, give, small, envdot, curl, both,
-    square, turned, th, tl, raw, left, right,
+    square, turned, table, raw, left, right,
 ):
     ghost = SEND * TA
     def number(row):
@@ -480,10 +494,8 @@
         for m in range(COMPS):
             for k in range(BASIS // 2):
                 entry = slopes[k] if m == 0 else angular[m] * slopes[k] + turning[m] * values[k]
-                hi, lo = split(entry)
-                th[p, m * TA : (m + 1) * TA, k * CHUNK : (k + 1) * CHUNK] = hi
-                tl[p, m * TA : (m + 1) * TA, k * CHUNK : (k + 1) * CHUNK] = lo
-        raw[p * COMPS * TA : (p + 1) * COMPS * TA, :] = product((th[p], tl[p]), (xh[p], xl[p]), NN)
+                put_left(table, p, slice(m * TA, (m + 1) * TA), k * CHUNK, CHUNK, entry)
+        raw[p * COMPS * TA : (p + 1) * COMPS * TA, :] = long_product(table[p], tall[p], NN)
 
     for m in range(COMPS):
         first = raw[m * TA : (m + 1) * TA, :]
@@ -681,11 +693,16 @@
     out[2 * half :, :] = rest[2 * piece :, :] + their_rest[2 * piece :, :]
 
 
-def join_kernel(whole, facing, mix, radial, kinds, out):
+def join_kernel(whole, facing, mix, radial, kinds, out, sems):
     rows = mix.shape[0]
     core = lax.axis_index("batch")
-    for ref, part in ((whole, core), (facing, 1 - core)):
-        mix[:, block_of_lanes(part)] = ref[0:rows, :]
+    copies = fetch(
+        [
+            (ref.at[0:rows, :], mix.at[:, block_of_lanes(part)])
+            for ref, part in ((whole, core), (facing, 1 - core))
+        ],
+        sems,
+    )
     both = whole[rows:, :] + facing[rows:, :]
     for h in range(2):
         lanes = slice(h * HALF, (h + 1) * HALF)
@@ -693,13 +710,15 @@
         radial[:, lanes] = few[0:BASIS]
         kinds[:, lanes] = few[BASIS : BASIS + SPECIES]
         out[:, lanes] = few[BASIS + SPECIES : BASIS + SPECIES + 1]
+    for copy in copies:
+        copy.wait()
 
 
 def spec(space):
     return pl.BlockSpec(memory_space=space)
 
 
-def call(kernel, name, outs, scratch, *operands, space=pltpu.VMEM, after=(), flops=0):
+def call(kernel, name, outs, scratch, *operands, space=pltpu.VMEM, after=(), flops=0, loose=0):
     if space is pltpu.HBM:
         operands = [pltpu.with_memory_space_constraint(operand, space) for operand in operands]
     outs = [out if len(out) == 2 and isinstance(out[0], tuple) else (out, F32) for out in outs]
@@ -708,7 +727,7 @@
         name=name,
         out_shape=[jax.ShapeDtypeStruct(*out) for out in outs],
         in_specs=[spec(space)] * len(operands) + [spec(pltpu.VMEM)] * len(after),
-        out_specs=[spec(pltpu.VMEM)] * len(outs),
+        out_specs=[spec(pl.ANY)] * loose + [spec(pltpu.VMEM)] * (len(outs) - loose),
         scratch_shapes=[pltpu.VMEM(*item) if isinstance(item, tuple) else item for item in scratch],
         compiler_params=pltpu.CompilerParams(vmem_limit_bytes=28 * 1024 * 1024),
         cost_estimate=pl.CostEstimate(flops=flops, bytes_accessed=1 << 20 if flops else 1 << 10, transcendentals=0),
@@ -793,8 +812,8 @@
         after=(token,),
     )
 
-    factors = (PAIRS, BASIS * TA, channels)
-    env, dinv, gate, curve, inv, rows, fsel, own, *leaving, shape_store, xh, xl, eh, el = call(
+    long_table = (PAIRS, COMPS * TA, 3 * BASIS * TA)
+    env, dinv, gate, curve, inv, rows, fsel, own, *leaving, shape_store, tall, eh, el = call(
         force_kernel,
         "force",
         [
@@ -811,13 +830,13 @@
             (8, CHUNK),
             (8, CHUNK),
             (PAIRS, 4 + BASIS, TA, CHUNK),
-            (factors, BF16),
-            (factors, BF16),
+            ((PAIRS, 3 * BASIS * TA, channels), BF16),
             ((PAIRS, WIDE, channels), BF16),
             ((PAIRS, WIDE, channels), BF16),
         ],
         turning
-        + [((PAIRS, *table), BF16)] * 2
+        + [(long_table, BF16), ((PAIRS, BASIS * TA, 3 * channels), BF16)]
+        + [((PAIRS, COMPS * TA, 3 * channels), BF16)]
         + [((PAIRS * COMPS * TA, channels), F32), ((PAIRS, *table), F32)],
         flags, atoms, own_feat, weights, mh, ml, from_second, from_first,
         flops=1 << 31,
@@ -853,11 +872,11 @@
             (16, CHUNK),
         ],
         turning
-        + [((PAIRS, *table), BF16)] * 2
+        + [(long_table, BF16)]
         + [((PAIRS * COMPS * TA, channels), F32)]
         + [((2 * slots, 3 * channels), F32), ((2 * slots, channels), F32)],
         flags, atoms, weights, mh, ml, from_first, from_second, own, *arriving,
-        rows, env, gate, curve, inv, shape_store, xh, xl, token,
+        rows, env, gate, curve, inv, shape_store, tall, token,
         flops=1 << 31,
     )
 
@@ -912,9 +931,10 @@
         join_kernel,
         "join",
         [(rows_mix, channels), (BASIS, channels), (SPECIES, channels), (1, channels)],
-        [],
+        [pltpu.SemaphoreType.DMA((2,))],
         whole,
         facing,
+        loose=1,
     )
     return forces.transpose(1, 0, 2), radial_sum, mix, kinds, out.reshape(channels)
 

time: 62.3 us -> 62.6 us (level)
  no operation moved by 1% of the time
where the time goes in v9:
time: 62.6 us; the launch traced here: 62.5 us
  starting transfers between devices  26.3 us (42%)
  Pallas kernels  18.1 us (29%)
  waiting for transfers between devices  17.3 us (28%)
  between operations  0.75 us (1%)
    pallas_call x15, Pallas kernels, call(): pl.pallas_call(kernel, name=name, out_shape=[jax.ShapeDtypeStruct(*out) f...  18.1 us
    ppermute x10, starting transfers between devices, partner(): lax.ppermute(block, 'domain', [(i, i ^ mask) for i in range(lax.axis_size...  14.2 us
    ppermute x6, starting transfers between devices, exchanged(): lax.ppermute(block, 'domain', [(i, (i + step if up[i] else i - step) % co...  11.9 us
    ppermute x10, waiting for transfers between devices, partner(): lax.ppermute(block, 'domain', [(i, i ^ mask) for i in range(lax.axis_size...  10.5 us
    ppermute x6, waiting for transfers between devices, exchanged(): lax.ppermute(block, 'domain', [(i, (i + step if up[i] else i - step) % co...  5.08 us
    ppermute x2, waiting for transfers between devices, shifted(): lax.ppermute(block, axis, [(i, (i + by) % count) for i in range(count)])  1.74 us
  transfers between devices with their start and end apart: 18, of which 10 were waited for; matrix products, arithmetic and copies ran while one was open for 0% of the time, Pallas kernels for 11%

profile of v9, /device:TPU:0, one launch (start us, length us, event | category | flops | bytes accessed | tf_op | source)
XLA Modules:
  0.0 62.5 jit_solution(188701686177464281)
XLA Ops:
  0.6 1.2 %gather.1 = (f32[136,256]{1,0:T(8,128)S(1)}, f32[136,256]{1,0:T(8,128)S(1)}, f32[8,128]{1,0:T(8,128)S(1)}) custom-call(s32[1,4]{1,0:T(1,128)} %send.3, f32[3,1,256]{2,1,0:T(1,128)} %bitcast.5, f32[1,256,256]{2,1,0:T(8,128)} %feat.3, f32[3,1,256]{2,1,0:T(1,128)} %bitcast.7), custom_call_target="tpu_custom_call" | custom-call | bytes 1024 | tf_op jit(solution)/shard_map/gather/pallas_call | solution.py:725
  1.8 3.0 %collective-permute-start = (f32[136,256]{1,0:T(8,128)S(1)}, f32[136,256]{1,0:T(8,128)S(1)}, u32[]{:S(2)}, u32[]{:S(2)}) collective-permute-start(f32[136,256]{1,0:T(8,128)S(1)} %get-tuple-element.59), channel_id=1, source_target_pairs={{0,2},{2,0},{4,6},{6,4},{8,10},{10,8},{12,14},{14,12},{1,3},{3,1},... | collective-permute-start | bytes 417800 | tf_op jit(solution)/shard_map/ppermute | solution.py:745
  4.8 3.5 %collective-permute-start.1 = (f32[136,256]{1,0:T(8,128)S(1)}, f32[136,256]{1,0:T(8,128)S(1)}, u32[]{:S(2)}, u32[]{:S(2)}) collective-permute-start(f32[136,256]{1,0:T(8,128)S(1)} %get-tuple-element.60), channel_id=1, source_target_pairs={{0,14},{2,4},{4,2},{6,8},{8,6},{10,12},{12,10},{14,0},{1,15},{3,5}... | collective-permute-start | bytes 417800 | tf_op jit(solution)/shard_map/ppermute | solution.py:745
  8.4 1.6 %stage.1 = (f32[16,128]{1,0:T(8,128)S(1)}, f32[8,256]{1,0:T(8,128)S(1)}, f32[256,256]{1,0:T(8,128)S(1)}, f32[16,256]{1,0:T(8,128)S(1)}, bf16[768,256]{1,0:T(8,128)(2,1)S(1)}, /*index=5*/bf16[768,256]{1,0:T(8,128)(2,1)S(1)}) custom-call(s32[1,2]{1,0:T(1,128)} %centre.1, s32[1,2]{1,0:T(1,128)} %other.1, s32[1,2]{1,0:T(1,128)} %live.1, s32[1,4]{1,0:T(1,128)} %send.3, ...), custom_call_target="tpu_custom_call" | custom-call | bytes 1024 | tf_op jit(solution)/shard_map/stage/pallas_call | solution.py:725
  10.0 0.8 %collective-permute-done.from_first = f32[136,256]{1,0:T(8,128)S(1)} collective-permute-done((f32[136,256]{1,0:T(8,128)S(1)}, f32[136,256]{1,0:T(8,128)S(1)}, u32[]{:S(2)}, u32[]{:S(2)}) %collective-permute-start) | collective-permute-done | bytes 139296 | tf_op jit(solution)/shard_map/ppermute | solution.py:745
  10.8 1.9 %collective-permute-done.1.from_second = f32[136,256]{1,0:T(8,128)S(1)} collective-permute-done((f32[136,256]{1,0:T(8,128)S(1)}, f32[136,256]{1,0:T(8,128)S(1)}, u32[]{:S(2)}, u32[]{:S(2)}) %collective-permute-start.1) | collective-permute-done | bytes 139296 | tf_op jit(solution)/shard_map/ppermute | solution.py:745
  12.7 4.9 %force.1 = (f32[1152,256]{1,0:T(8,128)S(1)}, f32[128,768]{1,0:T(8,128)S(1)}, f32[128,256]{1,0:T(8,128)S(1)}, f32[128,256]{1,0:T(8,128)S(1)}, f32[128,768]{1,0:T(...) custom-call(f32[16,128]{1,0:T(8,128)S(1)} %get-tuple-element.54.flag, ...), custom_call_target="tpu_custom_call" | custom-call | flops 2147483648 | bytes 1048576 | tf_op jit(solution)/shard_map/force/pallas_call | solution.py:725
  17.6 3.7 %collective-permute-start.2 = (f32[8,128]{1,0:T(8,128)S(1)}, f32[8,128]{1,0:T(8,128)S(1)}, u32[]{:S(2)}, u32[]{:S(2)}) collective-permute-start(f32[8,128]{1,0:T(8,128)S(1)} %get-tuple-element.63), channel_id=1, source_target_pairs={{0,14},{2,4},{4,2},{6,8},{8,6},{10,12},{12,10},{14,0},{1,15},{3,5}... | collective-permute-start | bytes 12296 | tf_op jit(solution)/shard_map/ppermute | solution.py:745
  21.3 0.5 collective-permute-start.3
  21.7 1.2 %collective-permute-start.4 = (f32[8,128]{1,0:T(8,128)S(1)}, f32[8,128]{1,0:T(8,128)S(1)}, u32[]{:S(2)}, u32[]{:S(2)}) collective-permute-start(f32[8,128]{1,0:T(8,128)S(1)} %get-tuple-element.65), channel_id=1, source_target_pairs={{0,2},{2,0},{4,6},{6,4},{8,10},{10,8},{12,14},{14,12},{1,3},{3,1},... | collective-permute-start | bytes 12296 | tf_op jit(solution)/shard_map/ppermute | solution.py:745
  23.0 1.3 %table.1 = (f32[2,20,64,128]{3,2,1,0:T(8,128)S(1)}, bf16[2,512,640]{2,1,0:T(8,128)(2,1)S(1)}, bf16[2,512,640]{2,1,0:T(8,128)(2,1)S(1)}, f32[8,128]{1,0:T(8,128)S(1)}) custom-call(f32[16,128]{1,0:T(8,128)S(1)} %get-tuple-element.54.flags, f32[8,128]{1,0:T(8,128)S(1)} %get-tuple-element.67.rows), custom_call_target="tpu_custom_call" | custom-call | flops 1073741824 | bytes 1048576 | tf_op jit(solution)/shard_map/table/pallas_call | solution.py:725
  24.3 2.4 %collective-permute-done.3.two_second = f32[8,128]{1,0:T(8,128)S(1)} collective-permute-done((f32[8,128]{1,0:T(8,128)S(1)}, f32[8,128]{1,0:T(8,128)S(1)}, u32[]{:S(2)}, u32[]{:S(2)}) %collective-permute-start.3) | collective-permute-done | bytes 4128 | tf_op jit(solution)/shard_map/ppermute | solution.py:745
  26.7 3.5 %tangent.1 = (f32[3,1,256]{2,1,0:T(1,128)}, f32[768,128]{1,0:T(8,128)S(1)}, f32[768,128]{1,0:T(8,128)S(1)}, f32[8,256]{1,0:T(8,128)S(1)}, f32[1152,256]{1,0:T(8,...) custom-call(f32[16,128]{1,0:T(8,128)S(1)} %get-tuple-element.54.flags, f32[8,256]{1,0:T(8,128)S(1)} %get-tuple-element.55.atoms, ...), custom_call_target="tpu_custom_call" | custom-call | flops 2147483648 | bytes 1048576 | tf_op jit(solution)/shard_map/tangent/pallas_call | solution.py:725
  30.2 2.0 %radial.2.after.radial_0 = f32[8,256]{1,0:T(8,128)S(1)} custom-call(f32[16,128]{1,0:T(8,128)S(1)} %get-tuple-element.78.both.after, f32[2,20,64,128]{3,2,1,0:T(8,128)S(1)} %get-tuple-element.79.shape_store, bf16[2,512,640]{2,1,0:T(8,128)(2,1)S(1)} %get-tuple-element.80.lh, bf16[2,512,640]{2,1,0:T(8,128)(2,1)S(1)} %get-tuple-element.81.ll, ...), custom_call_target="tpu_custom_call" | custom-call | flops 2147483648 | bytes 1048576 | tf_op jit(solution)/shard_map/radial/pallas_call | solution.py:725
  32.3 0.7 %collective-permute-start.8 = (f32[200,128]{1,0:T(8,128)S(1)}, f32[200,128]{1,0:T(8,128)S(1)}, u32[]{:S(2)}, u32[]{:S(2)}) collective-permute-start(f32[200,128]{1,0:T(8,128)S(1)} %get-tuple-element.92), channel_id=1, source_target_pairs={{0,2},{2,0},{4,6},{6,4},{8,10},{10,8},{12,14},{14,12},{1,3},{3,1},... | collective-permute-start | bytes 307208 | tf_op jit(solution)/shard_map/ppermute | solution.py:749
  33.1 1.4 %collective-permute-start.7 = (f32[192,128]{1,0:T(8,128)S(1)}, f32[192,128]{1,0:T(8,128)S(1)}, u32[]{:S(2)}, u32[]{:S(2)}) collective-permute-start(f32[192,128]{1,0:T(8,128)S(1)} %get-tuple-element.89), channel_id=1, source_target_pairs={{0,2},{2,0},{4,6},{6,4},{8,10},{10,8},{12,14},{14,12},{1,3},{3,1},... | collective-permute-start | bytes 294920 | tf_op jit(solution)/shard_map/ppermute | solution.py:749
  34.4 2.0 %radial.3.radial_1.after = f32[8,256]{1,0:T(8,128)S(1)} custom-call(f32[16,128]{1,0:T(8,128)S(1)} %get-tuple-element.78.both.after, f32[2,20,64,128]{3,2,1,0:T(8,128)S(1)} %get-tuple-element.79.shape_store, bf16[2,512,640]{2,1,0:T(8,128)(2,1)S(1)} %get-tuple-element.80.lh, bf16[2,512,640]{2,1,0:T(8,128)(2,1)S(1)} %get-tuple-element.81.ll, ...), custom_call_target="tpu_custom_call" | custom-call | bytes 1024 | tf_op jit(solution)/shard_map/radial/pallas_call | solution.py:725
  36.4 1.7 %collective-permute-done.8.taken = f32[200,128]{1,0:T(8,128)S(1)} collective-permute-done((f32[200,128]{1,0:T(8,128)S(1)}, f32[200,128]{1,0:T(8,128)S(1)}, u32[]{:S(2)}, u32[]{:S(2)}) %collective-permute-start.8) | collective-permute-done | bytes 102432 | tf_op jit(solution)/shard_map/ppermute | solution.py:749
  38.1 2.2 %collective-permute-start.9 = (f32[120,128]{1,0:T(8,128)S(1)}, f32[120,128]{1,0:T(8,128)S(1)}, u32[]{:S(2)}, u32[]{:S(2)}) collective-permute-start(f32[120,128]{1,0:T(8,128)S(1)} %get-tuple-element.93.after), channel_id=1, source_target_pairs={{0,12},{2,14},{4,8},{6,10},{8,4},{10,6},{12,0},{14,2},{1,13},{3,15... | collective-permute-start | bytes 184328 | tf_op jit(solution)/shard_map/ppermute | solution.py:749
  40.3 2.4 %collective-permute-start.11 = (f32[104,128]{1,0:T(8,128)S(1)}, f32[104,128]{1,0:T(8,128)S(1)}, u32[]{:S(2)}, u32[]{:S(2)}) collective-permute-start(f32[104,128]{1,0:T(8,128)S(1)} %get-tuple-element.96), channel_id=1, source_target_pairs={{0,4},{2,6},{4,0},{6,2},{8,12},{10,14},{12,8},{14,10},{1,5},{3,7},... | collective-permute-start | bytes 159752 | tf_op jit(solution)/shard_map/ppermute | solution.py:749
  42.6 2.4 %collective-permute-done.11.refs_3_ = f32[104,128]{1,0:T(8,128)S(1)} collective-permute-done((f32[104,128]{1,0:T(8,128)S(1)}, f32[104,128]{1,0:T(8,128)S(1)}, u32[]{:S(2)}, u32[]{:S(2)}) %collective-permute-start.11) | collective-permute-done | bytes 53280 | tf_op jit(solution)/shard_map/ppermute | solution.py:749
  45.1 0.6 %collective-permute-done.10.refs_2_ = f32[112,128]{1,0:T(8,128)S(1)} collective-permute-done((f32[112,128]{1,0:T(8,128)S(1)}, f32[112,128]{1,0:T(8,128)S(1)}, u32[]{:S(2)}, u32[]{:S(2)}) %collective-permute-start.10) | collective-permute-done | bytes 57376 | tf_op jit(solution)/shard_map/ppermute | solution.py:749
  45.7 2.5 %collective-permute-start.12 = (f32[104,128]{1,0:T(8,128)S(1)}, f32[104,128]{1,0:T(8,128)S(1)}, u32[]{:S(2)}, u32[]{:S(2)}) collective-permute-start(f32[104,128]{1,0:T(8,128)S(1)} %total.1.mine), channel_id=1, source_target_pairs={{0,12},{2,14},{4,8},{6,10},{8,4},{10,6},{12,0},{14,2},{1,13},{3,15... | collective-permute-start | bytes 159752 | tf_op jit(solution)/shard_map/ppermute | solution.py:749
  48.2 0.1 collective-permute-start.14
  48.3 1.8 %collective-permute-start.13 = (f32[104,128]{1,0:T(8,128)S(1)}, f32[104,128]{1,0:T(8,128)S(1)}, u32[]{:S(2)}, u32[]{:S(2)}) collective-permute-start(f32[104,128]{1,0:T(8,128)S(1)} %total.1.mine), channel_id=1, source_target_pairs={{0,4},{2,6},{4,0},{6,2},{8,12},{10,14},{12,8},{14,10},{1,5},{3,7},... | collective-permute-start | bytes 159752 | tf_op jit(solution)/shard_map/ppermute | solution.py:749
  50.2 1.5 %collective-permute-done.12.third = f32[104,128]{1,0:T(8,128)S(1)} collective-permute-done((f32[104,128]{1,0:T(8,128)S(1)}, f32[104,128]{1,0:T(8,128)S(1)}, u32[]{:S(2)}, u32[]{:S(2)}) %collective-permute-start.12) | collective-permute-done | bytes 53280 | tf_op jit(solution)/shard_map/ppermute | solution.py:749
  51.7 1.8 %collective-permute-start.15 = (f32[232,128]{1,0:T(8,128)S(1)}, f32[232,128]{1,0:T(8,128)S(1)}, u32[]{:S(2)}, u32[]{:S(2)}) collective-permute-start(f32[232,128]{1,0:T(8,128)S(1)} %near.1.after), channel_id=1, source_target_pairs={{0,2},{2,0},{4,6},{6,4},{8,10},{10,8},{12,14},{14,12},{1,3},{3,1},... | collective-permute-start | bytes 356360 | tf_op jit(solution)/shard_map/ppermute | solution.py:749
  53.5 0.2 collective-permute-done.14.second
  53.8 1.4 %collective-permute-start.16 = (f32[224,128]{1,0:T(8,128)S(1)}, f32[224,128]{1,0:T(8,128)S(1)}, u32[]{:S(2)}, u32[]{:S(2)}) collective-permute-start(f32[224,128]{1,0:T(8,128)S(1)} %rest.1), channel_id=1, source_target_pairs={{0,2},{2,0},{4,6},{6,4},{8,10},{10,8},{12,14},{14,12},{1,3},{3,1},... | collective-permute-start | bytes 344072 | tf_op jit(solution)/shard_map/ppermute | solution.py:749
  55.1 4.0 %collective-permute-done.16.their_rest = f32[224,128]{1,0:T(8,128)S(1)} collective-permute-done((f32[224,128]{1,0:T(8,128)S(1)}, f32[224,128]{1,0:T(8,128)S(1)}, u32[]{:S(2)}, u32[]{:S(2)}) %collective-permute-start.16) | collective-permute-done | bytes 114720 | tf_op jit(solution)/shard_map/ppermute | solution.py:749
  59.2 1.7 %collective-permute-done.17.facing = f32[800,128]{1,0:T(8,128)S(1)} collective-permute-done((f32[800,128]{1,0:T(8,128)S(1)}, f32[800,128]{1,0:T(8,128)S(1)}, u32[]{:S(2)}, u32[]{:S(2)}) %collective-permute-start.17) | collective-permute-done | bytes 409632 | tf_op jit(solution)/shard_map/ppermute | solution.py:739
  61.0 1.5 %join.1 = (f32[768,256]{1,0:T(8,128)}, f32[8,256]{1,0:T(8,128)}, f32[4,256]{1,0:T(4,128)}, f32[1,256]{1,0:T(1,128)}) custom-call(f32[800,128]{1,0:T(8,128)S(1)} %pair.1.whole, f32[800,128]{1,0:T(8,128)S(1)} %collective-permute-done.17.facing), custom_call_target="tpu_custom_call" | custom-call | bytes 1024 | tf_op jit(solution)/shard_map/join/pallas_call | solution.py:725
  (19 shorter events, 0.3 us)
Async XLA Ops:
  1.8 8.9 %collective-permute-start = (f32[136,256]{1,0:T(8,128)S(1)}, f32[136,256]{1,0:T(8,128)S(1)}, u32[]{:S(2)}, u32[]{:S(2)}) collective-permute-start(f32[136,256]{1,0:T(8,128)S(1)} %get-tuple-element.59), channel_id=1, source_target_pairs={{0,2},{2,0},{4,6},{6,4},{8,10},{10,8},{12,14},{14,12},{1,3},{3,1},... | collective-permute-start | bytes 417800 | tf_op jit(solution)/shard_map/ppermute | solution.py:745
  4.8 7.8 %collective-permute-start.1 = (f32[136,256]{1,0:T(8,128)S(1)}, f32[136,256]{1,0:T(8,128)S(1)}, u32[]{:S(2)}, u32[]{:S(2)}) collective-permute-start(f32[136,256]{1,0:T(8,128)S(1)} %get-tuple-element.60), channel_id=1, source_target_pairs={{0,14},{2,4},{4,2},{6,8},{8,6},{10,12},{12,10},{14,0},{1,15},{3,5}... | collective-permute-start | bytes 417800 | tf_op jit(solution)/shard_map/ppermute | solution.py:745
  17.6 6.7 %collective-permute-start.2 = (f32[8,128]{1,0:T(8,128)S(1)}, f32[8,128]{1,0:T(8,128)S(1)}, u32[]{:S(2)}, u32[]{:S(2)}) collective-permute-start(f32[8,128]{1,0:T(8,128)S(1)} %get-tuple-element.63), channel_id=1, source_target_pairs={{0,14},{2,4},{4,2},{6,8},{8,6},{10,12},{12,10},{14,0},{1,15},{3,5}... | collective-permute-start | bytes 12296 | tf_op jit(solution)/shard_map/ppermute | solution.py:745
  21.3 5.4 %collective-permute-start.3 = (f32[8,128]{1,0:T(8,128)S(1)}, f32[8,128]{1,0:T(8,128)S(1)}, u32[]{:S(2)}, u32[]{:S(2)}) collective-permute-start(f32[8,128]{1,0:T(8,128)S(1)} %get-tuple-element.64), channel_id=1, source_target_pairs={{0,12},{2,14},{4,8},{6,10},{8,4},{10,6},{12,0},{14,2},{1,13},{3,15... | collective-permute-start | bytes 12296 | tf_op jit(solution)/shard_map/ppermute | solution.py:745
  21.7 5.0 %collective-permute-start.4 = (f32[8,128]{1,0:T(8,128)S(1)}, f32[8,128]{1,0:T(8,128)S(1)}, u32[]{:S(2)}, u32[]{:S(2)}) collective-permute-start(f32[8,128]{1,0:T(8,128)S(1)} %get-tuple-element.65), channel_id=1, source_target_pairs={{0,2},{2,0},{4,6},{6,4},{8,10},{10,8},{12,14},{14,12},{1,3},{3,1},... | collective-permute-start | bytes 12296 | tf_op jit(solution)/shard_map/ppermute | solution.py:745
  23.0 3.7 %collective-permute-start.5 = (f32[8,128]{1,0:T(8,128)S(1)}, f32[8,128]{1,0:T(8,128)S(1)}, u32[]{:S(2)}, u32[]{:S(2)}) collective-permute-start(f32[8,128]{1,0:T(8,128)S(1)} %get-tuple-element.66), channel_id=1, source_target_pairs={{0,4},{2,6},{4,0},{6,2},{8,12},{10,14},{12,8},{14,10},{1,5},{3,7},... | collective-permute-start | bytes 12296 | tf_op jit(solution)/shard_map/ppermute | solution.py:745
  30.2 2.1 %collective-permute-start.6 = (f32[768,128]{1,0:T(8,128)S(1)}, f32[768,128]{1,0:T(8,128)S(1)}, u32[]{:S(2)}, u32[]{:S(2)}) collective-permute-start(f32[768,128]{1,0:T(8,128)S(1)} %get-tuple-element.77), channel_id=1, source_target_pairs={{0,1},{1,0},{2,3},{3,2},{4,5},{5,4},{6,7},{7,6},{8,9},{9,8},{10,11... | collective-permute-start | bytes 1179656 | tf_op jit(solution)/shard_map/ppermute | solution.py:739
  32.3 5.7 %collective-permute-start.8 = (f32[200,128]{1,0:T(8,128)S(1)}, f32[200,128]{1,0:T(8,128)S(1)}, u32[]{:S(2)}, u32[]{:S(2)}) collective-permute-start(f32[200,128]{1,0:T(8,128)S(1)} %get-tuple-element.92), channel_id=1, source_target_pairs={{0,2},{2,0},{4,6},{6,4},{8,10},{10,8},{12,14},{14,12},{1,3},{3,1},... | collective-permute-start | bytes 307208 | tf_op jit(solution)/shard_map/ppermute | solution.py:749
  33.1 7.2 %collective-permute-start.7 = (f32[192,128]{1,0:T(8,128)S(1)}, f32[192,128]{1,0:T(8,128)S(1)}, u32[]{:S(2)}, u32[]{:S(2)}) collective-permute-start(f32[192,128]{1,0:T(8,128)S(1)} %get-tuple-element.89), channel_id=1, source_target_pairs={{0,2},{2,0},{4,6},{6,4},{8,10},{10,8},{12,14},{14,12},{1,3},{3,1},... | collective-permute-start | bytes 294920 | tf_op jit(solution)/shard_map/ppermute | solution.py:749
  38.1 7.6 %collective-permute-start.9 = (f32[120,128]{1,0:T(8,128)S(1)}, f32[120,128]{1,0:T(8,128)S(1)}, u32[]{:S(2)}, u32[]{:S(2)}) collective-permute-start(f32[120,128]{1,0:T(8,128)S(1)} %get-tuple-element.93.after), channel_id=1, source_target_pairs={{0,12},{2,14},{4,8},{6,10},{8,4},{10,6},{12,0},{14,2},{1,13},{3,15... | collective-permute-start | bytes 184328 | tf_op jit(solution)/shard_map/ppermute | solution.py:749
  40.3 5.4 %collective-permute-start.10 = (f32[112,128]{1,0:T(8,128)S(1)}, f32[112,128]{1,0:T(8,128)S(1)}, u32[]{:S(2)}, u32[]{:S(2)}) collective-permute-start(f32[112,128]{1,0:T(8,128)S(1)} %get-tuple-element.95), channel_id=1, source_target_pairs={{0,8},{2,10},{4,12},{6,14},{8,0},{10,2},{12,4},{14,6},{1,9},{3,11}... | collective-permute-start | bytes 172040 | tf_op jit(solution)/shard_map/ppermute | solution.py:749
  40.3 4.8 %collective-permute-start.11 = (f32[104,128]{1,0:T(8,128)S(1)}, f32[104,128]{1,0:T(8,128)S(1)}, u32[]{:S(2)}, u32[]{:S(2)}) collective-permute-start(f32[104,128]{1,0:T(8,128)S(1)} %get-tuple-element.96), channel_id=1, source_target_pairs={{0,4},{2,6},{4,0},{6,2},{8,12},{10,14},{12,8},{14,10},{1,5},{3,7},... | collective-permute-start | bytes 159752 | tf_op jit(solution)/shard_map/ppermute | solution.py:749
  45.7 6.0 %collective-permute-start.12 = (f32[104,128]{1,0:T(8,128)S(1)}, f32[104,128]{1,0:T(8,128)S(1)}, u32[]{:S(2)}, u32[]{:S(2)}) collective-permute-start(f32[104,128]{1,0:T(8,128)S(1)} %total.1.mine), channel_id=1, source_target_pairs={{0,12},{2,14},{4,8},{6,10},{8,4},{10,6},{12,0},{14,2},{1,13},{3,15... | collective-permute-start | bytes 159752 | tf_op jit(solution)/shard_map/ppermute | solution.py:749
  48.2 5.5 %collective-permute-start.14 = (f32[104,128]{1,0:T(8,128)S(1)}, f32[104,128]{1,0:T(8,128)S(1)}, u32[]{:S(2)}, u32[]{:S(2)}) collective-permute-start(f32[104,128]{1,0:T(8,128)S(1)} %total.1.mine), channel_id=1, source_target_pairs={{0,8},{2,10},{4,12},{6,14},{8,0},{10,2},{12,4},{14,6},{1,9},{3,11}... | collective-permute-start | bytes 159752 | tf_op jit(solution)/shard_map/ppermute | solution.py:749
  48.3 5.4 %collective-permute-start.13 = (f32[104,128]{1,0:T(8,128)S(1)}, f32[104,128]{1,0:T(8,128)S(1)}, u32[]{:S(2)}, u32[]{:S(2)}) collective-permute-start(f32[104,128]{1,0:T(8,128)S(1)} %total.1.mine), channel_id=1, source_target_pairs={{0,4},{2,6},{4,0},{6,2},{8,12},{10,14},{12,8},{14,10},{1,5},{3,7},... | collective-permute-start | bytes 159752 | tf_op jit(solution)/shard_map/ppermute | solution.py:749
  51.7 7.4 %collective-permute-start.15 = (f32[232,128]{1,0:T(8,128)S(1)}, f32[232,128]{1,0:T(8,128)S(1)}, u32[]{:S(2)}, u32[]{:S(2)}) collective-permute-start(f32[232,128]{1,0:T(8,128)S(1)} %near.1.after), channel_id=1, source_target_pairs={{0,2},{2,0},{4,6},{6,4},{8,10},{10,8},{12,14},{14,12},{1,3},{3,1},... | collective-permute-start | bytes 356360 | tf_op jit(solution)/shard_map/ppermute | solution.py:749
  53.8 5.3 %collective-permute-start.16 = (f32[224,128]{1,0:T(8,128)S(1)}, f32[224,128]{1,0:T(8,128)S(1)}, u32[]{:S(2)}, u32[]{:S(2)}) collective-permute-start(f32[224,128]{1,0:T(8,128)S(1)} %rest.1), channel_id=1, source_target_pairs={{0,2},{2,0},{4,6},{6,4},{8,10},{10,8},{12,14},{14,12},{1,3},{3,1},... | collective-permute-start | bytes 344072 | tf_op jit(solution)/shard_map/ppermute | solution.py:749
  59.1 1.8 %collective-permute-start.17 = (f32[800,128]{1,0:T(8,128)S(1)}, f32[800,128]{1,0:T(8,128)S(1)}, u32[]{:S(2)}, u32[]{:S(2)}) collective-permute-start(f32[800,128]{1,0:T(8,128)S(1)} %pair.1.whole), channel_id=1, source_target_pairs={{0,1},{1,0},{2,3},{3,2},{4,5},{5,4},{6,7},{7,6},{8,9},{9,8},{10,11... | collective-permute-start | bytes 1228808 | tf_op jit(solution)/shard_map/ppermute | solution.py:739

commit v10 on v9

--- a/solution.py
+++ b/solution.py
@@ -12,6 +12,7 @@
 SEND = 2
 PAIRS = 2
 COMPS = 9
+STRIP = 16
 WIDE = 10 * TA
 BASIS = 8
 SPECIES = 4
@@ -95,14 +96,14 @@
     return low * flag(position == 2 * q) + high * flag(position == 2 * q + 1)
 
 
-def geometry(lane_rows, columns, sign, live, same):
+def geometry(lane_rows, columns, sign, live, same, first):
     offset = [(row - column) * sign for row, column in zip(lane_rows, columns)]
     dist_sq = offset[0] * offset[0] + offset[1] * offset[1] + offset[2] * offset[2] + soften
     distance = jnp.sqrt(dist_sq)
     inverse = 1.0 / distance
     unit = [x * inverse for x in offset]
-    row = lax.broadcasted_iota(jnp.int32, (TA, CHUNK), 0)
-    lane = lax.broadcasted_iota(jnp.int32, (TA, CHUNK), 1)
+    row = lax.broadcasted_iota(jnp.int32, (STRIP, CHUNK), 0) + first
+    lane = lax.broadcasted_iota(jnp.int32, (STRIP, CHUNK), 1)
     lane = jnp.where(lane >= TA, lane - TA, lane)
     mask = live * (1.0 - same * flag(row == lane))
     base = jnp.maximum(1.0 - dist_sq * (1.0 / (cutoff * cutoff)), 0.0)
@@ -294,7 +295,7 @@
 def force_kernel(
     flags, atoms, feat, weights, mh, ml, from_second, from_first,
     env, dinv, gate, curve, inv, rows, fsel, own, one_first, one_second, two_first, two_second, shape_store, tall, eh, el,
-    square, turned, table, wide, steady, raw, back,
+    square, turned, squares, table, wide, steady, raw, back,
 ):
     ghost = SEND * TA
     up = upward(0)
@@ -322,22 +323,23 @@
             + pick_rows(from_second.at[0:ghost], o, (SEND + 4) * (1.0 - up))
         )
 
-    shapes = []
     for p in range(PAIRS):
         lane_rows = [twice(rows[i : i + 1, :], p) for i in range(3)]
-        columns = [turned[p * TA : (p + 1) * TA, 3 + i : 4 + i] for i in range(3)]
-        unit, inverse, weight, slope, sine, cosine = geometry(
-            lane_rows, columns, 1.0, number(LIVE + p), number(SAME + p)
-        )
-        angular = harmonics(unit)
-        values, slopes = paired_orders(sine, cosine, weight, slope)
-        shapes.append((unit, inverse, angular, values, slopes))
-        for i, part in enumerate(unit + [inverse] + values + slopes):
-            shape_store[p, i] = part
-        for m in range(COMPS):
-            for k in range(BASIS // 2):
-                entry = values[k] if m == 0 else angular[m] * values[k]
-                put_left(table, p, slice(m * TA, (m + 1) * TA), k * CHUNK, CHUNK, entry)
+        for r in range(0, TA, STRIP):
+            strip = slice(p * TA + r, p * TA + r + STRIP)
+            columns = [turned[strip, 3 + i : 4 + i] for i in range(3)]
+            unit, inverse, weight, slope, sine, cosine = geometry(
+                lane_rows, columns, 1.0, number(LIVE + p), number(SAME + p), r
+            )
+            angular = harmonics(unit)
+            values, slopes = paired_orders(sine, cosine, weight, slope)
+            for i, part in enumerate(unit + [inverse] + values + slopes):
+                shape_store[p, i, r : r + STRIP, :] = part
+            for m in range(COMPS):
+                at = slice(m * TA + r, m * TA + r + STRIP)
+                for k in range(BASIS // 2):
+                    entry = values[k] if m == 0 else angular[m] * values[k]
+                    put_left(table, p, at, k * CHUNK, CHUNK, entry)
         radial_feat(fsel, weights, p, tall, wide)
         raw[p * COMPS * TA : (p + 1) * COMPS * TA, :] = long_product(table[p], tall[p], NN)
 
@@ -365,8 +367,8 @@
     dinv[...] = product(split(first_order * out_row), (mh[...], ml[...]), NT)
 
     tile_grads = [jnp.zeros((3, CHUNK), F32) for _ in range(4)]
+    other_rows = []
     for p in range(PAIRS):
-        unit, inverse, angular, values, slopes = shapes[p]
         for m in range(COMPS):
             block = env[(p * COMPS + m) * TA : (p * COMPS + m + 1) * TA, :]
             part = dinv[p * TA : (p + 1) * TA, GROUP[m] * 256 : (GROUP[m] + 1) * 256]
@@ -379,35 +381,42 @@
         for ref in (eh, el):
             ref[p, COMPS * TA :, :] = jnp.zeros((WIDE - COMPS * TA, ref.shape[2]), BF16)
         back[p] = long_product(steady[p], wide[p], NT)
-        d_radius = None
-        d_angular = []
-        for m in range(COMPS):
-            along, across = None, None
-            for k in range(BASIS // 2):
-                block = back[p, m * TA : (m + 1) * TA, k * CHUNK : (k + 1) * CHUNK]
-                along = block * slopes[k] if along is None else along + block * slopes[k]
-                across = block * values[k] if across is None else across + block * values[k]
-            d_angular.append(across)
-            term = along if m == 0 else along * angular[m]
-            d_radius = term if d_radius is None else d_radius + term
-        x, y, z = unit
-        g = d_angular
-        toward = [
-            g[1] + root_three * (y * g[4] + z * g[6] + x * g[7]) - x * g[8],
-            g[2] + root_three * (x * g[4] + z * g[5] - y * g[7]) - y * g[8],
-            g[3] + root_three * (y * g[5] + x * g[6]) + 2.0 * (z * g[8]),
-        ]
-        radial_part = d_radius - inverse * (toward[0] * x + toward[1] * y + toward[2] * z)
-        for i in range(3):
-            d_offset = inverse * toward[i] + unit[i] * radial_part
-            summed = jnp.sum(d_offset, axis=0, keepdims=True)
-            other_row = summed + pltpu.roll(summed, TA, 1)
-            square[0:TA, :] = d_offset
-            square[TA:, :] = d_offset
-            centre_row = -jnp.sum(square[...].T, axis=0, keepdims=True)
-            component = flag(lax.broadcasted_iota(jnp.int32, (3, CHUNK), 0) == i)
+        summed = [jnp.zeros((1, CHUNK), F32) for _ in range(3)]
+        for r in range(0, TA, STRIP):
+            strip = slice(r, r + STRIP)
+            x, y, z, inverse = (shape_store[p, i, strip, :] for i in range(4))
+            values = [shape_store[p, 4 + k, strip, :] for k in range(BASIS // 2)]
+            slopes = [shape_store[p, 8 + k, strip, :] for k in range(BASIS // 2)]
+            angular = harmonics((x, y, z))
+            d_radius = None
+            g = []
+            for m in range(COMPS):
+                along, across = None, None
+                for k in range(BASIS // 2):
+                    block = back[p, m * TA + r : m * TA + r + STRIP, k * CHUNK : (k + 1) * CHUNK]
+                    along = block * slopes[k] if along is None else along + block * slopes[k]
+                    across = block * values[k] if across is None else across + block * values[k]
+                g.append(across)
+                term = along if m == 0 else along * angular[m]
+                d_radius = term if d_radius is None else d_radius + term
+            toward = [
+                g[1] + root_three * (y * g[4] + z * g[6] + x * g[7]) - x * g[8],
+                g[2] + root_three * (x * g[4] + z * g[5] - y * g[7]) - y * g[8],
+                g[3] + root_three * (y * g[5] + x * g[6]) + 2.0 * (z * g[8]),
+            ]
+            radial_part = d_radius - inverse * (toward[0] * x + toward[1] * y + toward[2] * z)
+            for i, v in enumerate((x, y, z)):
+                d_offset = inverse * toward[i] + v * radial_part
+                summed[i] = summed[i] + jnp.sum(d_offset, axis=0, keepdims=True)
+                squares[i, p * TA + r : p * TA + r + STRIP, :] = d_offset
+        other_rows.append([part + pltpu.roll(part, TA, 1) for part in summed])
+    for i in range(3):
+        centre_both = -jnp.sum(squares[i].T, axis=0, keepdims=True)
+        component = flag(lax.broadcasted_iota(jnp.int32, (3, CHUNK), 0) == i)
+        for p in range(PAIRS):
+            centre_row = twice(centre_both, p)
             for q in range(4):
-                at = chunk_mask(others[p], q) * other_row
+                at = chunk_mask(others[p], q) * other_rows[p][i]
                 if q in (1, 2):
                     at = at + chunk_mask(centres[p] + SEND, q) * centre_row
                 tile_grads[q] = tile_grads[q] + at * component
@@ -481,20 +490,23 @@
 
     for p in range(PAIRS):
         lane_move = [twice(both[8 + i : 9 + i, :], p) for i in range(3)]
-        column_move = [turned[p * TA : (p + 1) * TA, 11 + i : 12 + i] for i in range(3)]
-        unit = [shape_store[p, i] for i in range(3)]
-        inverse = shape_store[p, 3]
-        values = [shape_store[p, 4 + k] for k in range(BASIS // 2)]
-        slopes = [shape_store[p, 8 + k] for k in range(BASIS // 2)]
-        move = [a - b for a, b in zip(lane_move, column_move)]
-        stretch = unit[0] * move[0] + unit[1] * move[1] + unit[2] * move[2]
-        turn = [(m - v * stretch) * inverse for m, v in zip(move, unit)]
-        angular, turning = harmonics(unit), harmonics_tangent(unit, turn)
-        slopes = [s * stretch for s in slopes]
-        for m in range(COMPS):
+        for r in range(0, TA, STRIP):
+            strip = slice(r, r + STRIP)
+            here = slice(p * TA + r, p * TA + r + STRIP)
+            column_move = [turned[here, 11 + i : 12 + i] for i in range(3)]
+            unit = [shape_store[p, i, strip, :] for i in range(3)]
+            inverse = shape_store[p, 3, strip, :]
+            move = [a - b for a, b in zip(lane_move, column_move)]
+            stretch = unit[0] * move[0] + unit[1] * move[1] + unit[2] * move[2]
+            turn = [(m - v * stretch) * inverse for m, v in zip(move, unit)]
+            angular, turning = harmonics(unit), harmonics_tangent(unit, turn)
             for k in range(BASIS // 2):
-                entry = slopes[k] if m == 0 else angular[m] * slopes[k] + turning[m] * values[k]
-                put_left(table, p, slice(m * TA, (m + 1) * TA), k * CHUNK, CHUNK, entry)
+                value = shape_store[p, 4 + k, strip, :]
+                slope = shape_store[p, 8 + k, strip, :] * stretch
+                for m in range(COMPS):
+                    at = slice(m * TA + r, m * TA + r + STRIP)
+                    entry = slope if m == 0 else angular[m] * slope + turning[m] * value
+                    put_left(table, p, at, k * CHUNK, CHUNK, entry)
         raw[p * COMPS * TA : (p + 1) * COMPS * TA, :] = long_product(table[p], tall[p], NN)
 
     for m in range(COMPS):
@@ -536,22 +548,23 @@
     columns_of(rows[...], square, turned)
     for p in range(PAIRS):
         lane_rows = [twice(rows[3 + i : 4 + i, :], p) for i in range(3)]
-        columns = [turned[p * TA : (p + 1) * TA, i : i + 1] for i in range(3)]
-        unit, inverse, weight, slope, sine, cosine = geometry(
-            lane_rows, columns, -1.0, flags[LIVE + p : LIVE + p + 1, :], flags[SAME + p : SAME + p + 1, :]
-        )
-        angular = harmonics(unit)
-        values, slopes = single_orders(sine, cosine, weight, slope)
-        for i, part in enumerate(unit + [inverse] + values + slopes):
-            shape_store[p, i] = part
-        for m in range(0, COMPS + 1, 2):
-            factor = low if m == 0 else angular[m] * low
-            if m + 1 < COMPS:
-                factor = factor + angular[m + 1] * high
-            for n in range(BASIS):
-                hi, lo = split(factor * values[n])
-                lh[p, n * TA : (n + 1) * TA, m * TA : (m + 2) * TA] = hi
-                ll[p, n * TA : (n + 1) * TA, m * TA : (m + 2) * TA] = lo
+        for r in range(0, TA, STRIP):
+            columns = [turned[p * TA + r : p * TA + r + STRIP, i : i + 1] for i in range(3)]
+            unit, inverse, weight, slope, sine, cosine = geometry(
+                lane_rows, columns, -1.0, flags[LIVE + p : LIVE + p + 1, :], flags[SAME + p : SAME + p + 1, :], r
+            )
+            angular = harmonics(unit)
+            values, slopes = single_orders(sine, cosine, weight, slope)
+            for i, part in enumerate(unit + [inverse] + values + slopes):
+                shape_store[p, i, r : r + STRIP, :] = part
+            for m in range(0, COMPS + 1, 2):
+                factor = low if m == 0 else angular[m] * low
+                if m + 1 < COMPS:
+                    factor = factor + angular[m + 1] * high
+                for n in range(BASIS):
+                    hi, lo = split(factor * values[n])
+                    lh[p, n * TA + r : n * TA + r + STRIP, m * TA : (m + 2) * TA] = hi
+                    ll[p, n * TA + r : n * TA + r + STRIP, m * TA : (m + 2) * TA] = lo
 
 
 def radial_kernel(
@@ -564,29 +577,31 @@
     here = slice(p * TA, (p + 1) * TA)
     turn_inv = product(split(curl[here, :]), (mh[...], ml[...]), NT)
     lane_move = [twice(both[11 + i : 12 + i, :], p) for i in range(3)]
-    column_move = [turned[here, 8 + i : 9 + i] for i in range(3)]
-    unit = [shape_store[p, i] for i in range(3)]
-    inverse = shape_store[p, 3]
-    move = [b - a for a, b in zip(lane_move, column_move)]
-    stretch = unit[0] * move[0] + unit[1] * move[1] + unit[2] * move[2]
-    turn = [(m - v * stretch) * inverse for m, v in zip(move, unit)]
-    angular, turning = harmonics(unit), harmonics_tangent(unit, turn)
     sh[:, 0:CHUNK] = lh[p, :, WIDE - CHUNK :]
     sl[:, 0:CHUNK] = ll[p, :, WIDE - CHUNK :]
-    for m in range(0, COMPS + 1, 2):
-        if m == 0:
-            on_value, on_slope = turning[1] * high, low + angular[1] * high
-        else:
+    for r in range(0, TA, STRIP):
+        strip = slice(r, r + STRIP)
+        column_move = [turned[p * TA + r : p * TA + r + STRIP, 8 + i : 9 + i] for i in range(3)]
+        unit = [shape_store[p, i, strip, :] for i in range(3)]
+        inverse = shape_store[p, 3, strip, :]
+        move = [b - a for a, b in zip(lane_move, column_move)]
+        stretch = unit[0] * move[0] + unit[1] * move[1] + unit[2] * move[2]
+        turn = [(m - v * stretch) * inverse for m, v in zip(move, unit)]
+        angular, turning = harmonics(unit), harmonics_tangent(unit, turn)
+        on_values, on_slopes = [turning[1] * high], [(low + angular[1] * high) * stretch]
+        for m in range(2, COMPS + 1, 2):
             on_value, on_slope = turning[m] * low, angular[m] * low
             if m + 1 < COMPS:
                 on_value = on_value + turning[m + 1] * high
                 on_slope = on_slope + angular[m + 1] * high
-        on_slope = on_slope * stretch
-        lanes = slice(CHUNK + m * TA, CHUNK + (m + 2) * TA)
+            on_values.append(on_value)
+            on_slopes.append(on_slope * stretch)
         for n in range(BASIS):
-            hi, lo = split(on_value * shape_store[p, 4 + n] + on_slope * shape_store[p, 4 + BASIS + n])
-            sh[n * TA : (n + 1) * TA, lanes] = hi
-            sl[n * TA : (n + 1) * TA, lanes] = lo
+            value, slope = shape_store[p, 4 + n, strip, :], shape_store[p, 4 + BASIS + n, strip, :]
+            for j, (on_value, on_slope) in enumerate(zip(on_values, on_slopes)):
+                hi, lo = split(on_value * value + on_slope * slope)
+                sh[n * TA + r : n * TA + r + STRIP, (j + 1) * CHUNK : (j + 2) * CHUNK] = hi
+                sl[n * TA + r : n * TA + r + STRIP, (j + 1) * CHUNK : (j + 2) * CHUNK] = lo
     for m in range(COMPS):
         at = slice((p * COMPS + m) * TA, (p * COMPS + m + 1) * TA)
         group = slice(GROUP[m] * 256, (GROUP[m] + 1) * 256)
@@ -693,16 +708,11 @@
     out[2 * half :, :] = rest[2 * piece :, :] + their_rest[2 * piece :, :]
 
 
-def join_kernel(whole, facing, mix, radial, kinds, out, sems):
+def join_kernel(whole, facing, mix, radial, kinds, out):
     rows = mix.shape[0]
     core = lax.axis_index("batch")
-    copies = fetch(
-        [
-            (ref.at[0:rows, :], mix.at[:, block_of_lanes(part)])
-            for ref, part in ((whole, core), (facing, 1 - core))
-        ],
-        sems,
-    )
+    for ref, part in ((whole, core), (facing, 1 - core)):
+        mix[:, block_of_lanes(part)] = ref[0:rows, :]
     both = whole[rows:, :] + facing[rows:, :]
     for h in range(2):
         lanes = slice(h * HALF, (h + 1) * HALF)
@@ -710,15 +720,13 @@
         radial[:, lanes] = few[0:BASIS]
         kinds[:, lanes] = few[BASIS : BASIS + SPECIES]
         out[:, lanes] = few[BASIS + SPECIES : BASIS + SPECIES + 1]
-    for copy in copies:
-        copy.wait()
 
 
 def spec(space):
     return pl.BlockSpec(memory_space=space)
 
 
-def call(kernel, name, outs, scratch, *operands, space=pltpu.VMEM, after=(), flops=0, loose=0):
+def call(kernel, name, outs, scratch, *operands, space=pltpu.VMEM, after=(), flops=0):
     if space is pltpu.HBM:
         operands = [pltpu.with_memory_space_constraint(operand, space) for operand in operands]
     outs = [out if len(out) == 2 and isinstance(out[0], tuple) else (out, F32) for out in outs]
@@ -727,7 +735,7 @@
         name=name,
         out_shape=[jax.ShapeDtypeStruct(*out) for out in outs],
         in_specs=[spec(space)] * len(operands) + [spec(pltpu.VMEM)] * len(after),
-        out_specs=[spec(pl.ANY)] * loose + [spec(pltpu.VMEM)] * (len(outs) - loose),
+        out_specs=[spec(pltpu.VMEM)] * len(outs),
         scratch_shapes=[pltpu.VMEM(*item) if isinstance(item, tuple) else item for item in scratch],
         compiler_params=pltpu.CompilerParams(vmem_limit_bytes=28 * 1024 * 1024),
         cost_estimate=pl.CostEstimate(flops=flops, bytes_accessed=1 << 20 if flops else 1 << 10, transcendentals=0),
@@ -835,6 +843,7 @@
             ((PAIRS, WIDE, channels), BF16),
         ],
         turning
+        + [((3, CHUNK, CHUNK), F32)]
         + [(long_table, BF16), ((PAIRS, BASIS * TA, 3 * channels), BF16)]
         + [((PAIRS, COMPS * TA, 3 * channels), BF16)]
         + [((PAIRS * COMPS * TA, channels), F32), ((PAIRS, *table), F32)],
@@ -931,10 +940,9 @@
         join_kernel,
         "join",
         [(rows_mix, channels), (BASIS, channels), (SPECIES, channels), (1, channels)],
-        [pltpu.SemaphoreType.DMA((2,))],
+        [],
         whole,
         facing,
-        loose=1,
     )
     return forces.transpose(1, 0, 2), radial_sum, mix, kinds, out.reshape(channels)
 

time: 62.6 us -> 62.2 us (level)
  no operation moved by 1% of the time
where the time goes in v10:
time: 62.2 us; the launch traced here: 62 us
  starting transfers between devices  26.3 us (42%)
  Pallas kernels  17.7 us (28%)
  waiting for transfers between devices  17.3 us (28%)
  between operations  0.75 us (1%)
    pallas_call x15, Pallas kernels, call(): pl.pallas_call(kernel, name=name, out_shape=[jax.ShapeDtypeStruct(*out) f...  17.7 us
    ppermute x10, starting transfers between devices, partner(): lax.ppermute(block, 'domain', [(i, i ^ mask) for i in range(lax.axis_size...  14.2 us
    ppermute x6, starting transfers between devices, exchanged(): lax.ppermute(block, 'domain', [(i, (i + step if up[i] else i - step) % co...  11.9 us
    ppermute x10, waiting for transfers between devices, partner(): lax.ppermute(block, 'domain', [(i, i ^ mask) for i in range(lax.axis_size...  10.5 us
    ppermute x6, waiting for transfers between devices, exchanged(): lax.ppermute(block, 'domain', [(i, (i + step if up[i] else i - step) % co...  5.09 us
    ppermute x2, waiting for transfers between devices, shifted(): lax.ppermute(block, axis, [(i, (i + by) % count) for i in range(count)])  1.74 us
  transfers between devices with their start and end apart: 18, of which 10 were waited for; matrix products, arithmetic and copies ran while one was open for 0% of the time, Pallas kernels for 11%

profile of v10, /device:TPU:0, one launch (start us, length us, event | category | flops | bytes accessed | tf_op | source)
XLA Modules:
  0.0 62.0 jit_solution(13345347366577241413)
XLA Ops:
  0.6 1.2 %gather.1 = (f32[136,256]{1,0:T(8,128)S(1)}, f32[136,256]{1,0:T(8,128)S(1)}, f32[8,128]{1,0:T(8,128)S(1)}) custom-call(s32[1,4]{1,0:T(1,128)} %send.3, f32[3,1,256]{2,1,0:T(1,128)} %bitcast.5, f32[1,256,256]{2,1,0:T(8,128)} %feat.3, f32[3,1,256]{2,1,0:T(1,128)} %bitcast.7), custom_call_target="tpu_custom_call" | custom-call | bytes 1024 | tf_op jit(solution)/shard_map/gather/pallas_call | solution.py:733
  1.8 3.0 %collective-permute-start = (f32[136,256]{1,0:T(8,128)S(1)}, f32[136,256]{1,0:T(8,128)S(1)}, u32[]{:S(2)}, u32[]{:S(2)}) collective-permute-start(f32[136,256]{1,0:T(8,128)S(1)} %get-tuple-element.59), channel_id=1, source_target_pairs={{0,2},{2,0},{4,6},{6,4},{8,10},{10,8},{12,14},{14,12},{1,3},{3,1},... | collective-permute-start | bytes 417800 | tf_op jit(solution)/shard_map/ppermute | solution.py:753
  4.8 3.5 %collective-permute-start.1 = (f32[136,256]{1,0:T(8,128)S(1)}, f32[136,256]{1,0:T(8,128)S(1)}, u32[]{:S(2)}, u32[]{:S(2)}) collective-permute-start(f32[136,256]{1,0:T(8,128)S(1)} %get-tuple-element.60), channel_id=1, source_target_pairs={{0,14},{2,4},{4,2},{6,8},{8,6},{10,12},{12,10},{14,0},{1,15},{3,5}... | collective-permute-start | bytes 417800 | tf_op jit(solution)/shard_map/ppermute | solution.py:753
  8.4 1.6 %stage.1 = (f32[16,128]{1,0:T(8,128)S(1)}, f32[8,256]{1,0:T(8,128)S(1)}, f32[256,256]{1,0:T(8,128)S(1)}, f32[16,256]{1,0:T(8,128)S(1)}, bf16[768,256]{1,0:T(8,128)(2,1)S(1)}, /*index=5*/bf16[768,256]{1,0:T(8,128)(2,1)S(1)}) custom-call(s32[1,2]{1,0:T(1,128)} %centre.1, s32[1,2]{1,0:T(1,128)} %other.1, s32[1,2]{1,0:T(1,128)} %live.1, s32[1,4]{1,0:T(1,128)} %send.3, ...), custom_call_target="tpu_custom_call" | custom-call | bytes 1024 | tf_op jit(solution)/shard_map/stage/pallas_call | solution.py:733
  10.0 0.8 %collective-permute-done.from_first = f32[136,256]{1,0:T(8,128)S(1)} collective-permute-done((f32[136,256]{1,0:T(8,128)S(1)}, f32[136,256]{1,0:T(8,128)S(1)}, u32[]{:S(2)}, u32[]{:S(2)}) %collective-permute-start) | collective-permute-done | bytes 139296 | tf_op jit(solution)/shard_map/ppermute | solution.py:753
  10.8 1.9 %collective-permute-done.1.from_second = f32[136,256]{1,0:T(8,128)S(1)} collective-permute-done((f32[136,256]{1,0:T(8,128)S(1)}, f32[136,256]{1,0:T(8,128)S(1)}, u32[]{:S(2)}, u32[]{:S(2)}) %collective-permute-start.1) | collective-permute-done | bytes 139296 | tf_op jit(solution)/shard_map/ppermute | solution.py:753
  12.7 5.0 %force.1 = (f32[1152,256]{1,0:T(8,128)S(1)}, f32[128,768]{1,0:T(8,128)S(1)}, f32[128,256]{1,0:T(8,128)S(1)}, f32[128,256]{1,0:T(8,128)S(1)}, f32[128,768]{1,0:T(...) custom-call(f32[16,128]{1,0:T(8,128)S(1)} %get-tuple-element.54.flag, ...), custom_call_target="tpu_custom_call" | custom-call | flops 2147483648 | bytes 1048576 | tf_op jit(solution)/shard_map/force/pallas_call | solution.py:733
  17.7 3.7 %collective-permute-start.2 = (f32[8,128]{1,0:T(8,128)S(1)}, f32[8,128]{1,0:T(8,128)S(1)}, u32[]{:S(2)}, u32[]{:S(2)}) collective-permute-start(f32[8,128]{1,0:T(8,128)S(1)} %get-tuple-element.63), channel_id=1, source_target_pairs={{0,14},{2,4},{4,2},{6,8},{8,6},{10,12},{12,10},{14,0},{1,15},{3,5}... | collective-permute-start | bytes 12296 | tf_op jit(solution)/shard_map/ppermute | solution.py:753
  21.4 0.5 collective-permute-start.3
  21.8 1.2 %collective-permute-start.4 = (f32[8,128]{1,0:T(8,128)S(1)}, f32[8,128]{1,0:T(8,128)S(1)}, u32[]{:S(2)}, u32[]{:S(2)}) collective-permute-start(f32[8,128]{1,0:T(8,128)S(1)} %get-tuple-element.65), channel_id=1, source_target_pairs={{0,2},{2,0},{4,6},{6,4},{8,10},{10,8},{12,14},{14,12},{1,3},{3,1},... | collective-permute-start | bytes 12296 | tf_op jit(solution)/shard_map/ppermute | solution.py:753
  23.0 1.3 %table.1 = (f32[2,20,64,128]{3,2,1,0:T(8,128)S(1)}, bf16[2,512,640]{2,1,0:T(8,128)(2,1)S(1)}, bf16[2,512,640]{2,1,0:T(8,128)(2,1)S(1)}, f32[8,128]{1,0:T(8,128)S(1)}) custom-call(f32[16,128]{1,0:T(8,128)S(1)} %get-tuple-element.54.flags, f32[8,128]{1,0:T(8,128)S(1)} %get-tuple-element.67.rows), custom_call_target="tpu_custom_call" | custom-call | flops 1073741824 | bytes 1048576 | tf_op jit(solution)/shard_map/table/pallas_call | solution.py:733
  24.4 2.4 %collective-permute-done.3.two_second = f32[8,128]{1,0:T(8,128)S(1)} collective-permute-done((f32[8,128]{1,0:T(8,128)S(1)}, f32[8,128]{1,0:T(8,128)S(1)}, u32[]{:S(2)}, u32[]{:S(2)}) %collective-permute-start.3) | collective-permute-done | bytes 4128 | tf_op jit(solution)/shard_map/ppermute | solution.py:753
  26.8 3.5 %tangent.1 = (f32[3,1,256]{2,1,0:T(1,128)}, f32[768,128]{1,0:T(8,128)S(1)}, f32[768,128]{1,0:T(8,128)S(1)}, f32[8,256]{1,0:T(8,128)S(1)}, f32[1152,256]{1,0:T(8,...) custom-call(f32[16,128]{1,0:T(8,128)S(1)} %get-tuple-element.54.flags, f32[8,256]{1,0:T(8,128)S(1)} %get-tuple-element.55.atoms, ...), custom_call_target="tpu_custom_call" | custom-call | flops 2147483648 | bytes 1048576 | tf_op jit(solution)/shard_map/tangent/pallas_call | solution.py:733
  30.3 2.0 %radial.2.after.radial_0 = f32[8,256]{1,0:T(8,128)S(1)} custom-call(f32[16,128]{1,0:T(8,128)S(1)} %get-tuple-element.78.both.after, f32[2,20,64,128]{3,2,1,0:T(8,128)S(1)} %get-tuple-element.79.shape_store, bf16[2,512,640]{2,1,0:T(8,128)(2,1)S(1)} %get-tuple-element.80.lh, bf16[2,512,640]{2,1,0:T(8,128)(2,1)S(1)} %get-tuple-element.81.ll, ...), custom_call_target="tpu_custom_call" | custom-call | flops 2147483648 | bytes 1048576 | tf_op jit(solution)/shard_map/radial/pallas_call | solution.py:733
  32.4 0.7 %collective-permute-start.8 = (f32[200,128]{1,0:T(8,128)S(1)}, f32[200,128]{1,0:T(8,128)S(1)}, u32[]{:S(2)}, u32[]{:S(2)}) collective-permute-start(f32[200,128]{1,0:T(8,128)S(1)} %get-tuple-element.92), channel_id=1, source_target_pairs={{0,2},{2,0},{4,6},{6,4},{8,10},{10,8},{12,14},{14,12},{1,3},{3,1},... | collective-permute-start | bytes 307208 | tf_op jit(solution)/shard_map/ppermute | solution.py:757
  33.2 1.3 %collective-permute-start.7 = (f32[192,128]{1,0:T(8,128)S(1)}, f32[192,128]{1,0:T(8,128)S(1)}, u32[]{:S(2)}, u32[]{:S(2)}) collective-permute-start(f32[192,128]{1,0:T(8,128)S(1)} %get-tuple-element.89), channel_id=1, source_target_pairs={{0,2},{2,0},{4,6},{6,4},{8,10},{10,8},{12,14},{14,12},{1,3},{3,1},... | collective-permute-start | bytes 294920 | tf_op jit(solution)/shard_map/ppermute | solution.py:757
  34.5 2.0 %radial.3.radial_1.after = f32[8,256]{1,0:T(8,128)S(1)} custom-call(f32[16,128]{1,0:T(8,128)S(1)} %get-tuple-element.78.both.after, f32[2,20,64,128]{3,2,1,0:T(8,128)S(1)} %get-tuple-element.79.shape_store, bf16[2,512,640]{2,1,0:T(8,128)(2,1)S(1)} %get-tuple-element.80.lh, bf16[2,512,640]{2,1,0:T(8,128)(2,1)S(1)} %get-tuple-element.81.ll, ...), custom_call_target="tpu_custom_call" | custom-call | bytes 1024 | tf_op jit(solution)/shard_map/radial/pallas_call | solution.py:733
  36.5 1.6 %collective-permute-done.8.taken = f32[200,128]{1,0:T(8,128)S(1)} collective-permute-done((f32[200,128]{1,0:T(8,128)S(1)}, f32[200,128]{1,0:T(8,128)S(1)}, u32[]{:S(2)}, u32[]{:S(2)}) %collective-permute-start.8) | collective-permute-done | bytes 102432 | tf_op jit(solution)/shard_map/ppermute | solution.py:757
  38.2 2.2 %collective-permute-start.9 = (f32[120,128]{1,0:T(8,128)S(1)}, f32[120,128]{1,0:T(8,128)S(1)}, u32[]{:S(2)}, u32[]{:S(2)}) collective-permute-start(f32[120,128]{1,0:T(8,128)S(1)} %get-tuple-element.93.after), channel_id=1, source_target_pairs={{0,12},{2,14},{4,8},{6,10},{8,4},{10,6},{12,0},{14,2},{1,13},{3,15... | collective-permute-start | bytes 184328 | tf_op jit(solution)/shard_map/ppermute | solution.py:757
  40.4 2.3 %collective-permute-start.11 = (f32[104,128]{1,0:T(8,128)S(1)}, f32[104,128]{1,0:T(8,128)S(1)}, u32[]{:S(2)}, u32[]{:S(2)}) collective-permute-start(f32[104,128]{1,0:T(8,128)S(1)} %get-tuple-element.96), channel_id=1, source_target_pairs={{0,4},{2,6},{4,0},{6,2},{8,12},{10,14},{12,8},{14,10},{1,5},{3,7},... | collective-permute-start | bytes 159752 | tf_op jit(solution)/shard_map/ppermute | solution.py:757
  42.7 2.4 %collective-permute-done.11.refs_3_ = f32[104,128]{1,0:T(8,128)S(1)} collective-permute-done((f32[104,128]{1,0:T(8,128)S(1)}, f32[104,128]{1,0:T(8,128)S(1)}, u32[]{:S(2)}, u32[]{:S(2)}) %collective-permute-start.11) | collective-permute-done | bytes 53280 | tf_op jit(solution)/shard_map/ppermute | solution.py:757
  45.1 0.6 %collective-permute-done.10.refs_2_ = f32[112,128]{1,0:T(8,128)S(1)} collective-permute-done((f32[112,128]{1,0:T(8,128)S(1)}, f32[112,128]{1,0:T(8,128)S(1)}, u32[]{:S(2)}, u32[]{:S(2)}) %collective-permute-start.10) | collective-permute-done | bytes 57376 | tf_op jit(solution)/shard_map/ppermute | solution.py:757
  45.8 2.5 %collective-permute-start.12 = (f32[104,128]{1,0:T(8,128)S(1)}, f32[104,128]{1,0:T(8,128)S(1)}, u32[]{:S(2)}, u32[]{:S(2)}) collective-permute-start(f32[104,128]{1,0:T(8,128)S(1)} %total.1.mine), channel_id=1, source_target_pairs={{0,12},{2,14},{4,8},{6,10},{8,4},{10,6},{12,0},{14,2},{1,13},{3,15... | collective-permute-start | bytes 159752 | tf_op jit(solution)/shard_map/ppermute | solution.py:757
  48.3 0.1 collective-permute-start.14
  48.4 1.8 %collective-permute-start.13 = (f32[104,128]{1,0:T(8,128)S(1)}, f32[104,128]{1,0:T(8,128)S(1)}, u32[]{:S(2)}, u32[]{:S(2)}) collective-permute-start(f32[104,128]{1,0:T(8,128)S(1)} %total.1.mine), channel_id=1, source_target_pairs={{0,4},{2,6},{4,0},{6,2},{8,12},{10,14},{12,8},{14,10},{1,5},{3,7},... | collective-permute-start | bytes 159752 | tf_op jit(solution)/shard_map/ppermute | solution.py:757
  50.3 1.5 %collective-permute-done.12.third = f32[104,128]{1,0:T(8,128)S(1)} collective-permute-done((f32[104,128]{1,0:T(8,128)S(1)}, f32[104,128]{1,0:T(8,128)S(1)}, u32[]{:S(2)}, u32[]{:S(2)}) %collective-permute-start.12) | collective-permute-done | bytes 53280 | tf_op jit(solution)/shard_map/ppermute | solution.py:757
  51.8 1.8 %collective-permute-start.15 = (f32[232,128]{1,0:T(8,128)S(1)}, f32[232,128]{1,0:T(8,128)S(1)}, u32[]{:S(2)}, u32[]{:S(2)}) collective-permute-start(f32[232,128]{1,0:T(8,128)S(1)} %near.1.after), channel_id=1, source_target_pairs={{0,2},{2,0},{4,6},{6,4},{8,10},{10,8},{12,14},{14,12},{1,3},{3,1},... | collective-permute-start | bytes 356360 | tf_op jit(solution)/shard_map/ppermute | solution.py:757
  53.6 0.3 collective-permute-done.14.second
  53.9 1.4 %collective-permute-start.16 = (f32[224,128]{1,0:T(8,128)S(1)}, f32[224,128]{1,0:T(8,128)S(1)}, u32[]{:S(2)}, u32[]{:S(2)}) collective-permute-start(f32[224,128]{1,0:T(8,128)S(1)} %rest.1), channel_id=1, source_target_pairs={{0,2},{2,0},{4,6},{6,4},{8,10},{10,8},{12,14},{14,12},{1,3},{3,1},... | collective-permute-start | bytes 344072 | tf_op jit(solution)/shard_map/ppermute | solution.py:757
  55.2 4.0 %collective-permute-done.16.their_rest = f32[224,128]{1,0:T(8,128)S(1)} collective-permute-done((f32[224,128]{1,0:T(8,128)S(1)}, f32[224,128]{1,0:T(8,128)S(1)}, u32[]{:S(2)}, u32[]{:S(2)}) %collective-permute-start.16) | collective-permute-done | bytes 114720 | tf_op jit(solution)/shard_map/ppermute | solution.py:757
  59.3 1.7 %collective-permute-done.17.facing = f32[800,128]{1,0:T(8,128)S(1)} collective-permute-done((f32[800,128]{1,0:T(8,128)S(1)}, f32[800,128]{1,0:T(8,128)S(1)}, u32[]{:S(2)}, u32[]{:S(2)}) %collective-permute-start.17) | collective-permute-done | bytes 409632 | tf_op jit(solution)/shard_map/ppermute | solution.py:747
  61.0 1.0 %join.1 = (f32[768,256]{1,0:T(8,128)}, f32[8,256]{1,0:T(8,128)}, f32[4,256]{1,0:T(4,128)}, f32[1,256]{1,0:T(1,128)}) custom-call(f32[800,128]{1,0:T(8,128)S(1)} %pair.1.whole, f32[800,128]{1,0:T(8,128)S(1)} %collective-permute-done.17.facing), custom_call_target="tpu_custom_call" | custom-call | bytes 1024 | tf_op jit(solution)/shard_map/join/pallas_call | solution.py:733
  (19 shorter events, 0.3 us)
Async XLA Ops:
  1.8 8.9 %collective-permute-start = (f32[136,256]{1,0:T(8,128)S(1)}, f32[136,256]{1,0:T(8,128)S(1)}, u32[]{:S(2)}, u32[]{:S(2)}) collective-permute-start(f32[136,256]{1,0:T(8,128)S(1)} %get-tuple-element.59), channel_id=1, source_target_pairs={{0,2},{2,0},{4,6},{6,4},{8,10},{10,8},{12,14},{14,12},{1,3},{3,1},... | collective-permute-start | bytes 417800 | tf_op jit(solution)/shard_map/ppermute | solution.py:753
  4.8 7.8 %collective-permute-start.1 = (f32[136,256]{1,0:T(8,128)S(1)}, f32[136,256]{1,0:T(8,128)S(1)}, u32[]{:S(2)}, u32[]{:S(2)}) collective-permute-start(f32[136,256]{1,0:T(8,128)S(1)} %get-tuple-element.60), channel_id=1, source_target_pairs={{0,14},{2,4},{4,2},{6,8},{8,6},{10,12},{12,10},{14,0},{1,15},{3,5}... | collective-permute-start | bytes 417800 | tf_op jit(solution)/shard_map/ppermute | solution.py:753
  17.7 6.7 %collective-permute-start.2 = (f32[8,128]{1,0:T(8,128)S(1)}, f32[8,128]{1,0:T(8,128)S(1)}, u32[]{:S(2)}, u32[]{:S(2)}) collective-permute-start(f32[8,128]{1,0:T(8,128)S(1)} %get-tuple-element.63), channel_id=1, source_target_pairs={{0,14},{2,4},{4,2},{6,8},{8,6},{10,12},{12,10},{14,0},{1,15},{3,5}... | collective-permute-start | bytes 12296 | tf_op jit(solution)/shard_map/ppermute | solution.py:753
  21.4 5.4 %collective-permute-start.3 = (f32[8,128]{1,0:T(8,128)S(1)}, f32[8,128]{1,0:T(8,128)S(1)}, u32[]{:S(2)}, u32[]{:S(2)}) collective-permute-start(f32[8,128]{1,0:T(8,128)S(1)} %get-tuple-element.64), channel_id=1, source_target_pairs={{0,12},{2,14},{4,8},{6,10},{8,4},{10,6},{12,0},{14,2},{1,13},{3,15... | collective-permute-start | bytes 12296 | tf_op jit(solution)/shard_map/ppermute | solution.py:753
  21.8 5.0 %collective-permute-start.4 = (f32[8,128]{1,0:T(8,128)S(1)}, f32[8,128]{1,0:T(8,128)S(1)}, u32[]{:S(2)}, u32[]{:S(2)}) collective-permute-start(f32[8,128]{1,0:T(8,128)S(1)} %get-tuple-element.65), channel_id=1, source_target_pairs={{0,2},{2,0},{4,6},{6,4},{8,10},{10,8},{12,14},{14,12},{1,3},{3,1},... | collective-permute-start | bytes 12296 | tf_op jit(solution)/shard_map/ppermute | solution.py:753
  23.0 3.7 %collective-permute-start.5 = (f32[8,128]{1,0:T(8,128)S(1)}, f32[8,128]{1,0:T(8,128)S(1)}, u32[]{:S(2)}, u32[]{:S(2)}) collective-permute-start(f32[8,128]{1,0:T(8,128)S(1)} %get-tuple-element.66), channel_id=1, source_target_pairs={{0,4},{2,6},{4,0},{6,2},{8,12},{10,14},{12,8},{14,10},{1,5},{3,7},... | collective-permute-start | bytes 12296 | tf_op jit(solution)/shard_map/ppermute | solution.py:753
  30.3 2.1 %collective-permute-start.6 = (f32[768,128]{1,0:T(8,128)S(1)}, f32[768,128]{1,0:T(8,128)S(1)}, u32[]{:S(2)}, u32[]{:S(2)}) collective-permute-start(f32[768,128]{1,0:T(8,128)S(1)} %get-tuple-element.77), channel_id=1, source_target_pairs={{0,1},{1,0},{2,3},{3,2},{4,5},{5,4},{6,7},{7,6},{8,9},{9,8},{10,11... | collective-permute-start | bytes 1179656 | tf_op jit(solution)/shard_map/ppermute | solution.py:747
  32.4 5.7 %collective-permute-start.8 = (f32[200,128]{1,0:T(8,128)S(1)}, f32[200,128]{1,0:T(8,128)S(1)}, u32[]{:S(2)}, u32[]{:S(2)}) collective-permute-start(f32[200,128]{1,0:T(8,128)S(1)} %get-tuple-element.92), channel_id=1, source_target_pairs={{0,2},{2,0},{4,6},{6,4},{8,10},{10,8},{12,14},{14,12},{1,3},{3,1},... | collective-permute-start | bytes 307208 | tf_op jit(solution)/shard_map/ppermute | solution.py:757
  33.2 7.2 %collective-permute-start.7 = (f32[192,128]{1,0:T(8,128)S(1)}, f32[192,128]{1,0:T(8,128)S(1)}, u32[]{:S(2)}, u32[]{:S(2)}) collective-permute-start(f32[192,128]{1,0:T(8,128)S(1)} %get-tuple-element.89), channel_id=1, source_target_pairs={{0,2},{2,0},{4,6},{6,4},{8,10},{10,8},{12,14},{14,12},{1,3},{3,1},... | collective-permute-start | bytes 294920 | tf_op jit(solution)/shard_map/ppermute | solution.py:757
  38.2 7.6 %collective-permute-start.9 = (f32[120,128]{1,0:T(8,128)S(1)}, f32[120,128]{1,0:T(8,128)S(1)}, u32[]{:S(2)}, u32[]{:S(2)}) collective-permute-start(f32[120,128]{1,0:T(8,128)S(1)} %get-tuple-element.93.after), channel_id=1, source_target_pairs={{0,12},{2,14},{4,8},{6,10},{8,4},{10,6},{12,0},{14,2},{1,13},{3,15... | collective-permute-start | bytes 184328 | tf_op jit(solution)/shard_map/ppermute | solution.py:757
  40.3 5.4 %collective-permute-start.10 = (f32[112,128]{1,0:T(8,128)S(1)}, f32[112,128]{1,0:T(8,128)S(1)}, u32[]{:S(2)}, u32[]{:S(2)}) collective-permute-start(f32[112,128]{1,0:T(8,128)S(1)} %get-tuple-element.95), channel_id=1, source_target_pairs={{0,8},{2,10},{4,12},{6,14},{8,0},{10,2},{12,4},{14,6},{1,9},{3,11}... | collective-permute-start | bytes 172040 | tf_op jit(solution)/shard_map/ppermute | solution.py:757
  40.4 4.8 %collective-permute-start.11 = (f32[104,128]{1,0:T(8,128)S(1)}, f32[104,128]{1,0:T(8,128)S(1)}, u32[]{:S(2)}, u32[]{:S(2)}) collective-permute-start(f32[104,128]{1,0:T(8,128)S(1)} %get-tuple-element.96), channel_id=1, source_target_pairs={{0,4},{2,6},{4,0},{6,2},{8,12},{10,14},{12,8},{14,10},{1,5},{3,7},... | collective-permute-start | bytes 159752 | tf_op jit(solution)/shard_map/ppermute | solution.py:757
  45.8 6.0 %collective-permute-start.12 = (f32[104,128]{1,0:T(8,128)S(1)}, f32[104,128]{1,0:T(8,128)S(1)}, u32[]{:S(2)}, u32[]{:S(2)}) collective-permute-start(f32[104,128]{1,0:T(8,128)S(1)} %total.1.mine), channel_id=1, source_target_pairs={{0,12},{2,14},{4,8},{6,10},{8,4},{10,6},{12,0},{14,2},{1,13},{3,15... | collective-permute-start | bytes 159752 | tf_op jit(solution)/shard_map/ppermute | solution.py:757
  48.3 5.5 %collective-permute-start.14 = (f32[104,128]{1,0:T(8,128)S(1)}, f32[104,128]{1,0:T(8,128)S(1)}, u32[]{:S(2)}, u32[]{:S(2)}) collective-permute-start(f32[104,128]{1,0:T(8,128)S(1)} %total.1.mine), channel_id=1, source_target_pairs={{0,8},{2,10},{4,12},{6,14},{8,0},{10,2},{12,4},{14,6},{1,9},{3,11}... | collective-permute-start | bytes 159752 | tf_op jit(solution)/shard_map/ppermute | solution.py:757
  48.4 5.4 %collective-permute-start.13 = (f32[104,128]{1,0:T(8,128)S(1)}, f32[104,128]{1,0:T(8,128)S(1)}, u32[]{:S(2)}, u32[]{:S(2)}) collective-permute-start(f32[104,128]{1,0:T(8,128)S(1)} %total.1.mine), channel_id=1, source_target_pairs={{0,4},{2,6},{4,0},{6,2},{8,12},{10,14},{12,8},{14,10},{1,5},{3,7},... | collective-permute-start | bytes 159752 | tf_op jit(solution)/shard_map/ppermute | solution.py:757
  51.8 7.4 %collective-permute-start.15 = (f32[232,128]{1,0:T(8,128)S(1)}, f32[232,128]{1,0:T(8,128)S(1)}, u32[]{:S(2)}, u32[]{:S(2)}) collective-permute-start(f32[232,128]{1,0:T(8,128)S(1)} %near.1.after), channel_id=1, source_target_pairs={{0,2},{2,0},{4,6},{6,4},{8,10},{10,8},{12,14},{14,12},{1,3},{3,1},... | collective-permute-start | bytes 356360 | tf_op jit(solution)/shard_map/ppermute | solution.py:757
  53.9 5.3 %collective-permute-start.16 = (f32[224,128]{1,0:T(8,128)S(1)}, f32[224,128]{1,0:T(8,128)S(1)}, u32[]{:S(2)}, u32[]{:S(2)}) collective-permute-start(f32[224,128]{1,0:T(8,128)S(1)} %rest.1), channel_id=1, source_target_pairs={{0,2},{2,0},{4,6},{6,4},{8,10},{10,8},{12,14},{14,12},{1,3},{3,1},... | collective-permute-start | bytes 344072 | tf_op jit(solution)/shard_map/ppermute | solution.py:757
  59.2 1.8 %collective-permute-start.17 = (f32[800,128]{1,0:T(8,128)S(1)}, f32[800,128]{1,0:T(8,128)S(1)}, u32[]{:S(2)}, u32[]{:S(2)}) collective-permute-start(f32[800,128]{1,0:T(8,128)S(1)} %pair.1.whole), channel_id=1, source_target_pairs={{0,1},{1,0},{2,3},{3,2},{4,5},{5,4},{6,7},{7,6},{8,9},{9,8},{10,11... | collective-permute-start | bytes 1228808 | tf_op jit(solution)/shard_map/ppermute | solution.py:747

commit v11 on v10

--- a/solution.py
+++ b/solution.py
@@ -96,11 +96,21 @@
     return low * flag(position == 2 * q) + high * flag(position == 2 * q + 1)
 
 
+def series(angle):
+    square = angle * angle
+    sine, cosine = 1.0 / math.factorial(13), -1.0 / math.factorial(14)
+    for order in range(11, 0, -2):
+        sine = sine * square + (-1.0) ** (order // 2) / math.factorial(order)
+    for order in range(12, -1, -2):
+        cosine = cosine * square + (-1.0) ** (order // 2) / math.factorial(order)
+    return sine * angle, cosine
+
+
 def geometry(lane_rows, columns, sign, live, same, first):
     offset = [(row - column) * sign for row, column in zip(lane_rows, columns)]
     dist_sq = offset[0] * offset[0] + offset[1] * offset[1] + offset[2] * offset[2] + soften
-    distance = jnp.sqrt(dist_sq)
-    inverse = 1.0 / distance
+    inverse = lax.rsqrt(dist_sq)
+    inverse = inverse * (1.5 - 0.5 * dist_sq * inverse * inverse)
     unit = [x * inverse for x in offset]
     row = lax.broadcasted_iota(jnp.int32, (STRIP, CHUNK), 0) + first
     lane = lax.broadcasted_iota(jnp.int32, (STRIP, CHUNK), 1)
@@ -109,8 +119,9 @@
     base = jnp.maximum(1.0 - dist_sq * (1.0 / (cutoff * cutoff)), 0.0)
     weight = base * base * base * mask * inverse
     slope = -(6.0 / (cutoff * cutoff)) * base * base * mask - weight * inverse
-    angle = distance * (math.pi / cutoff)
-    return unit, inverse, weight, slope, jnp.sin(angle), jnp.cos(angle)
+    turned = jnp.minimum(dist_sq * inverse, cutoff) * (math.pi / cutoff) - 0.5 * math.pi
+    sine, cosine = series(turned)
+    return unit, inverse, weight, slope, cosine, -sine
 
 
 def harmonics(v):

time: 62.2 us -> 62 us (level)
  no operation moved by 1% of the time
where the time goes in v11:
time: 62 us; the launch traced here: 61.8 us
  starting transfers between devices  26.3 us (42%)
  waiting for transfers between devices  17.5 us (28%)
  Pallas kernels  17.3 us (28%)
  between operations  0.75 us (1%)
    pallas_call x15, Pallas kernels, call(): pl.pallas_call(kernel, name=name, out_shape=[jax.ShapeDtypeStruct(*out) f...  17.3 us
    ppermute x10, starting transfers between devices, partner(): lax.ppermute(block, 'domain', [(i, i ^ mask) for i in range(lax.axis_size...  14.2 us
    ppermute x6, starting transfers between devices, exchanged(): lax.ppermute(block, 'domain', [(i, (i + step if up[i] else i - step) % co...  11.9 us
    ppermute x10, waiting for transfers between devices, partner(): lax.ppermute(block, 'domain', [(i, i ^ mask) for i in range(lax.axis_size...  10.5 us
    ppermute x6, waiting for transfers between devices, exchanged(): lax.ppermute(block, 'domain', [(i, (i + step if up[i] else i - step) % co...  5.31 us
    ppermute x2, waiting for transfers between devices, shifted(): lax.ppermute(block, axis, [(i, (i + by) % count) for i in range(count)])  1.74 us
  transfers between devices with their start and end apart: 18, of which 10 were waited for; matrix products, arithmetic and copies ran while one was open for 0% of the time, Pallas kernels for 11%

profile of v11, /device:TPU:0, one launch (start us, length us, event | category | flops | bytes accessed | tf_op | source)
XLA Modules:
  0.0 61.8 jit_solution(13001861404815566693)
XLA Ops:
  0.6 1.2 %gather.1 = (f32[136,256]{1,0:T(8,128)S(1)}, f32[136,256]{1,0:T(8,128)S(1)}, f32[8,128]{1,0:T(8,128)S(1)}) custom-call(s32[1,4]{1,0:T(1,128)} %send.3, f32[3,1,256]{2,1,0:T(1,128)} %bitcast.5, f32[1,256,256]{2,1,0:T(8,128)} %feat.3, f32[3,1,256]{2,1,0:T(1,128)} %bitcast.7), custom_call_target="tpu_custom_call" | custom-call | bytes 1024 | tf_op jit(solution)/shard_map/gather/pallas_call | solution.py:744
  1.8 3.0 %collective-permute-start = (f32[136,256]{1,0:T(8,128)S(1)}, f32[136,256]{1,0:T(8,128)S(1)}, u32[]{:S(2)}, u32[]{:S(2)}) collective-permute-start(f32[136,256]{1,0:T(8,128)S(1)} %get-tuple-element.59), channel_id=1, source_target_pairs={{0,2},{2,0},{4,6},{6,4},{8,10},{10,8},{12,14},{14,12},{1,3},{3,1},... | collective-permute-start | bytes 417800 | tf_op jit(solution)/shard_map/ppermute | solution.py:764
  4.8 3.5 %collective-permute-start.1 = (f32[136,256]{1,0:T(8,128)S(1)}, f32[136,256]{1,0:T(8,128)S(1)}, u32[]{:S(2)}, u32[]{:S(2)}) collective-permute-start(f32[136,256]{1,0:T(8,128)S(1)} %get-tuple-element.60), channel_id=1, source_target_pairs={{0,14},{2,4},{4,2},{6,8},{8,6},{10,12},{12,10},{14,0},{1,15},{3,5}... | collective-permute-start | bytes 417800 | tf_op jit(solution)/shard_map/ppermute | solution.py:764
  8.4 1.6 %stage.1 = (f32[16,128]{1,0:T(8,128)S(1)}, f32[8,256]{1,0:T(8,128)S(1)}, f32[256,256]{1,0:T(8,128)S(1)}, f32[16,256]{1,0:T(8,128)S(1)}, bf16[768,256]{1,0:T(8,128)(2,1)S(1)}, /*index=5*/bf16[768,256]{1,0:T(8,128)(2,1)S(1)}) custom-call(s32[1,2]{1,0:T(1,128)} %centre.1, s32[1,2]{1,0:T(1,128)} %other.1, s32[1,2]{1,0:T(1,128)} %live.1, s32[1,4]{1,0:T(1,128)} %send.3, ...), custom_call_target="tpu_custom_call" | custom-call | bytes 1024 | tf_op jit(solution)/shard_map/stage/pallas_call | solution.py:744
  10.0 0.8 %collective-permute-done.from_first = f32[136,256]{1,0:T(8,128)S(1)} collective-permute-done((f32[136,256]{1,0:T(8,128)S(1)}, f32[136,256]{1,0:T(8,128)S(1)}, u32[]{:S(2)}, u32[]{:S(2)}) %collective-permute-start) | collective-permute-done | bytes 139296 | tf_op jit(solution)/shard_map/ppermute | solution.py:764
  10.8 1.9 %collective-permute-done.1.from_second = f32[136,256]{1,0:T(8,128)S(1)} collective-permute-done((f32[136,256]{1,0:T(8,128)S(1)}, f32[136,256]{1,0:T(8,128)S(1)}, u32[]{:S(2)}, u32[]{:S(2)}) %collective-permute-start.1) | collective-permute-done | bytes 139296 | tf_op jit(solution)/shard_map/ppermute | solution.py:764
  12.7 4.8 %force.1 = (f32[1152,256]{1,0:T(8,128)S(1)}, f32[128,768]{1,0:T(8,128)S(1)}, f32[128,256]{1,0:T(8,128)S(1)}, f32[128,256]{1,0:T(8,128)S(1)}, f32[128,768]{1,0:T(...) custom-call(f32[16,128]{1,0:T(8,128)S(1)} %get-tuple-element.54.flag, ...), custom_call_target="tpu_custom_call" | custom-call | flops 2147483648 | bytes 1048576 | tf_op jit(solution)/shard_map/force/pallas_call | solution.py:744
  17.5 3.7 %collective-permute-start.2 = (f32[8,128]{1,0:T(8,128)S(1)}, f32[8,128]{1,0:T(8,128)S(1)}, u32[]{:S(2)}, u32[]{:S(2)}) collective-permute-start(f32[8,128]{1,0:T(8,128)S(1)} %get-tuple-element.63), channel_id=1, source_target_pairs={{0,14},{2,4},{4,2},{6,8},{8,6},{10,12},{12,10},{14,0},{1,15},{3,5}... | collective-permute-start | bytes 12296 | tf_op jit(solution)/shard_map/ppermute | solution.py:764
  21.1 0.5 collective-permute-start.3
  21.6 1.2 %collective-permute-start.4 = (f32[8,128]{1,0:T(8,128)S(1)}, f32[8,128]{1,0:T(8,128)S(1)}, u32[]{:S(2)}, u32[]{:S(2)}) collective-permute-start(f32[8,128]{1,0:T(8,128)S(1)} %get-tuple-element.65), channel_id=1, source_target_pairs={{0,2},{2,0},{4,6},{6,4},{8,10},{10,8},{12,14},{14,12},{1,3},{3,1},... | collective-permute-start | bytes 12296 | tf_op jit(solution)/shard_map/ppermute | solution.py:764
  22.8 1.1 %table.1 = (f32[2,20,64,128]{3,2,1,0:T(8,128)S(1)}, bf16[2,512,640]{2,1,0:T(8,128)(2,1)S(1)}, bf16[2,512,640]{2,1,0:T(8,128)(2,1)S(1)}, f32[8,128]{1,0:T(8,128)S(1)}) custom-call(f32[16,128]{1,0:T(8,128)S(1)} %get-tuple-element.54.flags, f32[8,128]{1,0:T(8,128)S(1)} %get-tuple-element.67.rows), custom_call_target="tpu_custom_call" | custom-call | flops 1073741824 | bytes 1048576 | tf_op jit(solution)/shard_map/table/pallas_call | solution.py:744
  23.9 2.6 %collective-permute-done.3.two_second = f32[8,128]{1,0:T(8,128)S(1)} collective-permute-done((f32[8,128]{1,0:T(8,128)S(1)}, f32[8,128]{1,0:T(8,128)S(1)}, u32[]{:S(2)}, u32[]{:S(2)}) %collective-permute-start.3) | collective-permute-done | bytes 4128 | tf_op jit(solution)/shard_map/ppermute | solution.py:764
  26.5 3.5 %tangent.1 = (f32[3,1,256]{2,1,0:T(1,128)}, f32[768,128]{1,0:T(8,128)S(1)}, f32[768,128]{1,0:T(8,128)S(1)}, f32[8,256]{1,0:T(8,128)S(1)}, f32[1152,256]{1,0:T(8,...) custom-call(f32[16,128]{1,0:T(8,128)S(1)} %get-tuple-element.54.flags, f32[8,256]{1,0:T(8,128)S(1)} %get-tuple-element.55.atoms, ...), custom_call_target="tpu_custom_call" | custom-call | flops 2147483648 | bytes 1048576 | tf_op jit(solution)/shard_map/tangent/pallas_call | solution.py:744
  30.1 2.0 %radial.2.after.radial_0 = f32[8,256]{1,0:T(8,128)S(1)} custom-call(f32[16,128]{1,0:T(8,128)S(1)} %get-tuple-element.78.both.after, f32[2,20,64,128]{3,2,1,0:T(8,128)S(1)} %get-tuple-element.79.shape_store, bf16[2,512,640]{2,1,0:T(8,128)(2,1)S(1)} %get-tuple-element.80.lh, bf16[2,512,640]{2,1,0:T(8,128)(2,1)S(1)} %get-tuple-element.81.ll, ...), custom_call_target="tpu_custom_call" | custom-call | flops 2147483648 | bytes 1048576 | tf_op jit(solution)/shard_map/radial/pallas_call | solution.py:744
  32.2 0.7 %collective-permute-start.8 = (f32[200,128]{1,0:T(8,128)S(1)}, f32[200,128]{1,0:T(8,128)S(1)}, u32[]{:S(2)}, u32[]{:S(2)}) collective-permute-start(f32[200,128]{1,0:T(8,128)S(1)} %get-tuple-element.92), channel_id=1, source_target_pairs={{0,2},{2,0},{4,6},{6,4},{8,10},{10,8},{12,14},{14,12},{1,3},{3,1},... | collective-permute-start | bytes 307208 | tf_op jit(solution)/shard_map/ppermute | solution.py:768
  32.9 1.3 %collective-permute-start.7 = (f32[192,128]{1,0:T(8,128)S(1)}, f32[192,128]{1,0:T(8,128)S(1)}, u32[]{:S(2)}, u32[]{:S(2)}) collective-permute-start(f32[192,128]{1,0:T(8,128)S(1)} %get-tuple-element.89), channel_id=1, source_target_pairs={{0,2},{2,0},{4,6},{6,4},{8,10},{10,8},{12,14},{14,12},{1,3},{3,1},... | collective-permute-start | bytes 294920 | tf_op jit(solution)/shard_map/ppermute | solution.py:768
  34.3 2.0 %radial.3.radial_1.after = f32[8,256]{1,0:T(8,128)S(1)} custom-call(f32[16,128]{1,0:T(8,128)S(1)} %get-tuple-element.78.both.after, f32[2,20,64,128]{3,2,1,0:T(8,128)S(1)} %get-tuple-element.79.shape_store, bf16[2,512,640]{2,1,0:T(8,128)(2,1)S(1)} %get-tuple-element.80.lh, bf16[2,512,640]{2,1,0:T(8,128)(2,1)S(1)} %get-tuple-element.81.ll, ...), custom_call_target="tpu_custom_call" | custom-call | bytes 1024 | tf_op jit(solution)/shard_map/radial/pallas_call | solution.py:744
  36.3 1.6 %collective-permute-done.8.taken = f32[200,128]{1,0:T(8,128)S(1)} collective-permute-done((f32[200,128]{1,0:T(8,128)S(1)}, f32[200,128]{1,0:T(8,128)S(1)}, u32[]{:S(2)}, u32[]{:S(2)}) %collective-permute-start.8) | collective-permute-done | bytes 102432 | tf_op jit(solution)/shard_map/ppermute | solution.py:768
  38.0 2.2 %collective-permute-start.9 = (f32[120,128]{1,0:T(8,128)S(1)}, f32[120,128]{1,0:T(8,128)S(1)}, u32[]{:S(2)}, u32[]{:S(2)}) collective-permute-start(f32[120,128]{1,0:T(8,128)S(1)} %get-tuple-element.93.after), channel_id=1, source_target_pairs={{0,12},{2,14},{4,8},{6,10},{8,4},{10,6},{12,0},{14,2},{1,13},{3,15... | collective-permute-start | bytes 184328 | tf_op jit(solution)/shard_map/ppermute | solution.py:768
  40.1 2.3 %collective-permute-start.11 = (f32[104,128]{1,0:T(8,128)S(1)}, f32[104,128]{1,0:T(8,128)S(1)}, u32[]{:S(2)}, u32[]{:S(2)}) collective-permute-start(f32[104,128]{1,0:T(8,128)S(1)} %get-tuple-element.96), channel_id=1, source_target_pairs={{0,4},{2,6},{4,0},{6,2},{8,12},{10,14},{12,8},{14,10},{1,5},{3,7},... | collective-permute-start | bytes 159752 | tf_op jit(solution)/shard_map/ppermute | solution.py:768
  42.5 2.4 %collective-permute-done.11.refs_3_ = f32[104,128]{1,0:T(8,128)S(1)} collective-permute-done((f32[104,128]{1,0:T(8,128)S(1)}, f32[104,128]{1,0:T(8,128)S(1)}, u32[]{:S(2)}, u32[]{:S(2)}) %collective-permute-start.11) | collective-permute-done | bytes 53280 | tf_op jit(solution)/shard_map/ppermute | solution.py:768
  44.9 0.6 %collective-permute-done.10.refs_2_ = f32[112,128]{1,0:T(8,128)S(1)} collective-permute-done((f32[112,128]{1,0:T(8,128)S(1)}, f32[112,128]{1,0:T(8,128)S(1)}, u32[]{:S(2)}, u32[]{:S(2)}) %collective-permute-start.10) | collective-permute-done | bytes 57376 | tf_op jit(solution)/shard_map/ppermute | solution.py:768
  45.6 2.5 %collective-permute-start.12 = (f32[104,128]{1,0:T(8,128)S(1)}, f32[104,128]{1,0:T(8,128)S(1)}, u32[]{:S(2)}, u32[]{:S(2)}) collective-permute-start(f32[104,128]{1,0:T(8,128)S(1)} %total.1.mine), channel_id=1, source_target_pairs={{0,12},{2,14},{4,8},{6,10},{8,4},{10,6},{12,0},{14,2},{1,13},{3,15... | collective-permute-start | bytes 159752 | tf_op jit(solution)/shard_map/ppermute | solution.py:768
  48.1 0.1 collective-permute-start.14
  48.2 1.9 %collective-permute-start.13 = (f32[104,128]{1,0:T(8,128)S(1)}, f32[104,128]{1,0:T(8,128)S(1)}, u32[]{:S(2)}, u32[]{:S(2)}) collective-permute-start(f32[104,128]{1,0:T(8,128)S(1)} %total.1.mine), channel_id=1, source_target_pairs={{0,4},{2,6},{4,0},{6,2},{8,12},{10,14},{12,8},{14,10},{1,5},{3,7},... | collective-permute-start | bytes 159752 | tf_op jit(solution)/shard_map/ppermute | solution.py:768
  50.0 1.5 %collective-permute-done.12.third = f32[104,128]{1,0:T(8,128)S(1)} collective-permute-done((f32[104,128]{1,0:T(8,128)S(1)}, f32[104,128]{1,0:T(8,128)S(1)}, u32[]{:S(2)}, u32[]{:S(2)}) %collective-permute-start.12) | collective-permute-done | bytes 53280 | tf_op jit(solution)/shard_map/ppermute | solution.py:768
  51.6 1.8 %collective-permute-start.15 = (f32[232,128]{1,0:T(8,128)S(1)}, f32[232,128]{1,0:T(8,128)S(1)}, u32[]{:S(2)}, u32[]{:S(2)}) collective-permute-start(f32[232,128]{1,0:T(8,128)S(1)} %near.1.after), channel_id=1, source_target_pairs={{0,2},{2,0},{4,6},{6,4},{8,10},{10,8},{12,14},{14,12},{1,3},{3,1},... | collective-permute-start | bytes 356360 | tf_op jit(solution)/shard_map/ppermute | solution.py:768
  53.4 0.3 collective-permute-done.14.second
  53.6 1.4 %collective-permute-start.16 = (f32[224,128]{1,0:T(8,128)S(1)}, f32[224,128]{1,0:T(8,128)S(1)}, u32[]{:S(2)}, u32[]{:S(2)}) collective-permute-start(f32[224,128]{1,0:T(8,128)S(1)} %rest.1), channel_id=1, source_target_pairs={{0,2},{2,0},{4,6},{6,4},{8,10},{10,8},{12,14},{14,12},{1,3},{3,1},... | collective-permute-start | bytes 344072 | tf_op jit(solution)/shard_map/ppermute | solution.py:768
  55.0 4.0 %collective-permute-done.16.their_rest = f32[224,128]{1,0:T(8,128)S(1)} collective-permute-done((f32[224,128]{1,0:T(8,128)S(1)}, f32[224,128]{1,0:T(8,128)S(1)}, u32[]{:S(2)}, u32[]{:S(2)}) %collective-permute-start.16) | collective-permute-done | bytes 114720 | tf_op jit(solution)/shard_map/ppermute | solution.py:768
  59.1 1.7 %collective-permute-done.17.facing = f32[800,128]{1,0:T(8,128)S(1)} collective-permute-done((f32[800,128]{1,0:T(8,128)S(1)}, f32[800,128]{1,0:T(8,128)S(1)}, u32[]{:S(2)}, u32[]{:S(2)}) %collective-permute-start.17) | collective-permute-done | bytes 409632 | tf_op jit(solution)/shard_map/ppermute | solution.py:758
  60.8 1.0 %join.1 = (f32[768,256]{1,0:T(8,128)}, f32[8,256]{1,0:T(8,128)}, f32[4,256]{1,0:T(4,128)}, f32[1,256]{1,0:T(1,128)}) custom-call(f32[800,128]{1,0:T(8,128)S(1)} %pair.1.whole, f32[800,128]{1,0:T(8,128)S(1)} %collective-permute-done.17.facing), custom_call_target="tpu_custom_call" | custom-call | bytes 1024 | tf_op jit(solution)/shard_map/join/pallas_call | solution.py:744
  (19 shorter events, 0.3 us)
Async XLA Ops:
  1.8 8.9 %collective-permute-start = (f32[136,256]{1,0:T(8,128)S(1)}, f32[136,256]{1,0:T(8,128)S(1)}, u32[]{:S(2)}, u32[]{:S(2)}) collective-permute-start(f32[136,256]{1,0:T(8,128)S(1)} %get-tuple-element.59), channel_id=1, source_target_pairs={{0,2},{2,0},{4,6},{6,4},{8,10},{10,8},{12,14},{14,12},{1,3},{3,1},... | collective-permute-start | bytes 417800 | tf_op jit(solution)/shard_map/ppermute | solution.py:764
  4.8 7.8 %collective-permute-start.1 = (f32[136,256]{1,0:T(8,128)S(1)}, f32[136,256]{1,0:T(8,128)S(1)}, u32[]{:S(2)}, u32[]{:S(2)}) collective-permute-start(f32[136,256]{1,0:T(8,128)S(1)} %get-tuple-element.60), channel_id=1, source_target_pairs={{0,14},{2,4},{4,2},{6,8},{8,6},{10,12},{12,10},{14,0},{1,15},{3,5}... | collective-permute-start | bytes 417800 | tf_op jit(solution)/shard_map/ppermute | solution.py:764
  17.5 6.4 %collective-permute-start.2 = (f32[8,128]{1,0:T(8,128)S(1)}, f32[8,128]{1,0:T(8,128)S(1)}, u32[]{:S(2)}, u32[]{:S(2)}) collective-permute-start(f32[8,128]{1,0:T(8,128)S(1)} %get-tuple-element.63), channel_id=1, source_target_pairs={{0,14},{2,4},{4,2},{6,8},{8,6},{10,12},{12,10},{14,0},{1,15},{3,5}... | collective-permute-start | bytes 12296 | tf_op jit(solution)/shard_map/ppermute | solution.py:764
  21.1 5.4 %collective-permute-start.3 = (f32[8,128]{1,0:T(8,128)S(1)}, f32[8,128]{1,0:T(8,128)S(1)}, u32[]{:S(2)}, u32[]{:S(2)}) collective-permute-start(f32[8,128]{1,0:T(8,128)S(1)} %get-tuple-element.64), channel_id=1, source_target_pairs={{0,12},{2,14},{4,8},{6,10},{8,4},{10,6},{12,0},{14,2},{1,13},{3,15... | collective-permute-start | bytes 12296 | tf_op jit(solution)/shard_map/ppermute | solution.py:764
  21.6 5.0 %collective-permute-start.4 = (f32[8,128]{1,0:T(8,128)S(1)}, f32[8,128]{1,0:T(8,128)S(1)}, u32[]{:S(2)}, u32[]{:S(2)}) collective-permute-start(f32[8,128]{1,0:T(8,128)S(1)} %get-tuple-element.65), channel_id=1, source_target_pairs={{0,2},{2,0},{4,6},{6,4},{8,10},{10,8},{12,14},{14,12},{1,3},{3,1},... | collective-permute-start | bytes 12296 | tf_op jit(solution)/shard_map/ppermute | solution.py:764
  22.8 3.7 %collective-permute-start.5 = (f32[8,128]{1,0:T(8,128)S(1)}, f32[8,128]{1,0:T(8,128)S(1)}, u32[]{:S(2)}, u32[]{:S(2)}) collective-permute-start(f32[8,128]{1,0:T(8,128)S(1)} %get-tuple-element.66), channel_id=1, source_target_pairs={{0,4},{2,6},{4,0},{6,2},{8,12},{10,14},{12,8},{14,10},{1,5},{3,7},... | collective-permute-start | bytes 12296 | tf_op jit(solution)/shard_map/ppermute | solution.py:764
  30.0 2.1 %collective-permute-start.6 = (f32[768,128]{1,0:T(8,128)S(1)}, f32[768,128]{1,0:T(8,128)S(1)}, u32[]{:S(2)}, u32[]{:S(2)}) collective-permute-start(f32[768,128]{1,0:T(8,128)S(1)} %get-tuple-element.77), channel_id=1, source_target_pairs={{0,1},{1,0},{2,3},{3,2},{4,5},{5,4},{6,7},{7,6},{8,9},{9,8},{10,11... | collective-permute-start | bytes 1179656 | tf_op jit(solution)/shard_map/ppermute | solution.py:758
  32.2 5.7 %collective-permute-start.8 = (f32[200,128]{1,0:T(8,128)S(1)}, f32[200,128]{1,0:T(8,128)S(1)}, u32[]{:S(2)}, u32[]{:S(2)}) collective-permute-start(f32[200,128]{1,0:T(8,128)S(1)} %get-tuple-element.92), channel_id=1, source_target_pairs={{0,2},{2,0},{4,6},{6,4},{8,10},{10,8},{12,14},{14,12},{1,3},{3,1},... | collective-permute-start | bytes 307208 | tf_op jit(solution)/shard_map/ppermute | solution.py:768
  32.9 7.2 %collective-permute-start.7 = (f32[192,128]{1,0:T(8,128)S(1)}, f32[192,128]{1,0:T(8,128)S(1)}, u32[]{:S(2)}, u32[]{:S(2)}) collective-permute-start(f32[192,128]{1,0:T(8,128)S(1)} %get-tuple-element.89), channel_id=1, source_target_pairs={{0,2},{2,0},{4,6},{6,4},{8,10},{10,8},{12,14},{14,12},{1,3},{3,1},... | collective-permute-start | bytes 294920 | tf_op jit(solution)/shard_map/ppermute | solution.py:768
  38.0 7.6 %collective-permute-start.9 = (f32[120,128]{1,0:T(8,128)S(1)}, f32[120,128]{1,0:T(8,128)S(1)}, u32[]{:S(2)}, u32[]{:S(2)}) collective-permute-start(f32[120,128]{1,0:T(8,128)S(1)} %get-tuple-element.93.after), channel_id=1, source_target_pairs={{0,12},{2,14},{4,8},{6,10},{8,4},{10,6},{12,0},{14,2},{1,13},{3,15... | collective-permute-start | bytes 184328 | tf_op jit(solution)/shard_map/ppermute | solution.py:768
  40.1 5.4 %collective-permute-start.10 = (f32[112,128]{1,0:T(8,128)S(1)}, f32[112,128]{1,0:T(8,128)S(1)}, u32[]{:S(2)}, u32[]{:S(2)}) collective-permute-start(f32[112,128]{1,0:T(8,128)S(1)} %get-tuple-element.95), channel_id=1, source_target_pairs={{0,8},{2,10},{4,12},{6,14},{8,0},{10,2},{12,4},{14,6},{1,9},{3,11}... | collective-permute-start | bytes 172040 | tf_op jit(solution)/shard_map/ppermute | solution.py:768
  40.1 4.8 %collective-permute-start.11 = (f32[104,128]{1,0:T(8,128)S(1)}, f32[104,128]{1,0:T(8,128)S(1)}, u32[]{:S(2)}, u32[]{:S(2)}) collective-permute-start(f32[104,128]{1,0:T(8,128)S(1)} %get-tuple-element.96), channel_id=1, source_target_pairs={{0,4},{2,6},{4,0},{6,2},{8,12},{10,14},{12,8},{14,10},{1,5},{3,7},... | collective-permute-start | bytes 159752 | tf_op jit(solution)/shard_map/ppermute | solution.py:768
  45.6 6.0 %collective-permute-start.12 = (f32[104,128]{1,0:T(8,128)S(1)}, f32[104,128]{1,0:T(8,128)S(1)}, u32[]{:S(2)}, u32[]{:S(2)}) collective-permute-start(f32[104,128]{1,0:T(8,128)S(1)} %total.1.mine), channel_id=1, source_target_pairs={{0,12},{2,14},{4,8},{6,10},{8,4},{10,6},{12,0},{14,2},{1,13},{3,15... | collective-permute-start | bytes 159752 | tf_op jit(solution)/shard_map/ppermute | solution.py:768
  48.1 5.5 %collective-permute-start.14 = (f32[104,128]{1,0:T(8,128)S(1)}, f32[104,128]{1,0:T(8,128)S(1)}, u32[]{:S(2)}, u32[]{:S(2)}) collective-permute-start(f32[104,128]{1,0:T(8,128)S(1)} %total.1.mine), channel_id=1, source_target_pairs={{0,8},{2,10},{4,12},{6,14},{8,0},{10,2},{12,4},{14,6},{1,9},{3,11}... | collective-permute-start | bytes 159752 | tf_op jit(solution)/shard_map/ppermute | solution.py:768
  48.2 5.4 %collective-permute-start.13 = (f32[104,128]{1,0:T(8,128)S(1)}, f32[104,128]{1,0:T(8,128)S(1)}, u32[]{:S(2)}, u32[]{:S(2)}) collective-permute-start(f32[104,128]{1,0:T(8,128)S(1)} %total.1.mine), channel_id=1, source_target_pairs={{0,4},{2,6},{4,0},{6,2},{8,12},{10,14},{12,8},{14,10},{1,5},{3,7},... | collective-permute-start | bytes 159752 | tf_op jit(solution)/shard_map/ppermute | solution.py:768
  51.6 7.4 %collective-permute-start.15 = (f32[232,128]{1,0:T(8,128)S(1)}, f32[232,128]{1,0:T(8,128)S(1)}, u32[]{:S(2)}, u32[]{:S(2)}) collective-permute-start(f32[232,128]{1,0:T(8,128)S(1)} %near.1.after), channel_id=1, source_target_pairs={{0,2},{2,0},{4,6},{6,4},{8,10},{10,8},{12,14},{14,12},{1,3},{3,1},... | collective-permute-start | bytes 356360 | tf_op jit(solution)/shard_map/ppermute | solution.py:768
  53.6 5.3 %collective-permute-start.16 = (f32[224,128]{1,0:T(8,128)S(1)}, f32[224,128]{1,0:T(8,128)S(1)}, u32[]{:S(2)}, u32[]{:S(2)}) collective-permute-start(f32[224,128]{1,0:T(8,128)S(1)} %rest.1), channel_id=1, source_target_pairs={{0,2},{2,0},{4,6},{6,4},{8,10},{10,8},{12,14},{14,12},{1,3},{3,1},... | collective-permute-start | bytes 344072 | tf_op jit(solution)/shard_map/ppermute | solution.py:768
  59.0 1.8 %collective-permute-start.17 = (f32[800,128]{1,0:T(8,128)S(1)}, f32[800,128]{1,0:T(8,128)S(1)}, u32[]{:S(2)}, u32[]{:S(2)}) collective-permute-start(f32[800,128]{1,0:T(8,128)S(1)} %pair.1.whole), channel_id=1, source_target_pairs={{0,1},{1,0},{2,3},{3,2},{4,5},{5,4},{6,7},{7,6},{8,9},{9,8},{10,11... | collective-permute-start | bytes 1228808 | tf_op jit(solution)/shard_map/ppermute | solution.py:758

commit v12 on v11

--- a/solution.py
+++ b/solution.py
@@ -51,9 +51,8 @@
 
 def put_left(ref, p, rows, lane, width, value):
     hi, lo = split(value)
-    span = ref.shape[2] // 3
     for third, part in enumerate((hi, lo, hi)):
-        at = third * span + lane
+        at = third * (ref.shape[2] // 3) + lane
         ref[p, rows, at : at + width] = part
 
 
@@ -75,6 +74,23 @@
     low, high = lane_half()
     swapped = pltpu.roll(chunk, TA, 1)
     return chunk * low + swapped * high if half == 0 else swapped * low + chunk * high
+
+
+def twice_at(chunk, p):
+    first = flag(p == 0)
+    return twice(chunk, 0) * first + twice(chunk, 1) * (1.0 - first)
+
+
+def slots(body):
+    def step(p, carry):
+        body(p)
+        return carry
+
+    lax.fori_loop(0, PAIRS, step, 0)
+
+
+def span(start, size):
+    return pl.ds(pl.multiple_of(start, 16), size)
 
 
 def pick(chunks, position):
@@ -195,12 +211,12 @@
 
 
 def radial_feat(feat, radial, p, tall, wide):
-    own = feat[p * TA : (p + 1) * TA, :]
-    span, channels = BASIS * TA, feat.shape[1]
+    own = feat[span(p * TA, TA), :]
+    third_rows, channels = BASIS * TA, feat.shape[1]
     for n in range(BASIS):
         hi, lo = split(own * radial[n : n + 1, :])
         for third, part in enumerate((hi, hi, lo)):
-            tall[p, third * span + n * TA : third * span + (n + 1) * TA, :] = part
+            tall[p, third * third_rows + n * TA : third * third_rows + (n + 1) * TA, :] = part
             wide[p, n * TA : (n + 1) * TA, third * channels : (third + 1) * channels] = part
 
 
@@ -306,7 +322,7 @@
 def force_kernel(
     flags, atoms, feat, weights, mh, ml, from_second, from_first,
     env, dinv, gate, curve, inv, rows, fsel, own, one_first, one_second, two_first, two_second, shape_store, tall, eh, el,
-    square, turned, squares, table, wide, steady, raw, back,
+    square, turned, squares, others_sum, table, wide, steady, raw, back,
 ):
     ghost = SEND * TA
     up = upward(0)
@@ -334,14 +350,13 @@
             + pick_rows(from_second.at[0:ghost], o, (SEND + 4) * (1.0 - up))
         )
 
-    for p in range(PAIRS):
-        lane_rows = [twice(rows[i : i + 1, :], p) for i in range(3)]
+    def forward(p):
+        lane_rows = [twice_at(rows[i : i + 1, :], p) for i in range(3)]
+        live, same = flags[pl.ds(LIVE + p, 1), :], flags[pl.ds(SAME + p, 1), :]
         for r in range(0, TA, STRIP):
-            strip = slice(p * TA + r, p * TA + r + STRIP)
+            strip = span(p * TA + r, STRIP)
             columns = [turned[strip, 3 + i : 4 + i] for i in range(3)]
-            unit, inverse, weight, slope, sine, cosine = geometry(
-                lane_rows, columns, 1.0, number(LIVE + p), number(SAME + p), r
-            )
+            unit, inverse, weight, slope, sine, cosine = geometry(lane_rows, columns, 1.0, live, same, r)
             angular = harmonics(unit)
             values, slopes = paired_orders(sine, cosine, weight, slope)
             for i, part in enumerate(unit + [inverse] + values + slopes):
@@ -352,7 +367,9 @@
                     entry = values[k] if m == 0 else angular[m] * values[k]
                     put_left(table, p, at, k * CHUNK, CHUNK, entry)
         radial_feat(fsel, weights, p, tall, wide)
-        raw[p * COMPS * TA : (p + 1) * COMPS * TA, :] = long_product(table[p], tall[p], NN)
+        raw[span(p * COMPS * TA, COMPS * TA), :] = long_product(table[p], tall[p], NN)
+
+    slots(forward)
 
     for m in range(COMPS):
         first = raw[m * TA : (m + 1) * TA, :]
@@ -378,11 +395,12 @@
     dinv[...] = product(split(first_order * out_row), (mh[...], ml[...]), NT)
 
     tile_grads = [jnp.zeros((3, CHUNK), F32) for _ in range(4)]
-    other_rows = []
-    for p in range(PAIRS):
+
+    def backward(p):
+        here = span(p * TA, TA)
         for m in range(COMPS):
-            block = env[(p * COMPS + m) * TA : (p * COMPS + m + 1) * TA, :]
-            part = dinv[p * TA : (p + 1) * TA, GROUP[m] * 256 : (GROUP[m] + 1) * 256]
+            block = env[span((p * COMPS + m) * TA, TA), :]
+            part = dinv[here, GROUP[m] * 256 : (GROUP[m] + 1) * 256]
             at = slice(m * TA, (m + 1) * TA)
             hi, lo = split((2.0 * env_scale) * block * part)
             eh[p, at, :] = hi
@@ -419,15 +437,18 @@
             for i, v in enumerate((x, y, z)):
                 d_offset = inverse * toward[i] + v * radial_part
                 summed[i] = summed[i] + jnp.sum(d_offset, axis=0, keepdims=True)
-                squares[i, p * TA + r : p * TA + r + STRIP, :] = d_offset
-        other_rows.append([part + pltpu.roll(part, TA, 1) for part in summed])
+                squares[i, span(p * TA + r, STRIP), :] = d_offset
+        for i, part in enumerate(summed):
+            others_sum[p, i : i + 1, :] = part + pltpu.roll(part, TA, 1)
+
+    slots(backward)
     for i in range(3):
         centre_both = -jnp.sum(squares[i].T, axis=0, keepdims=True)
         component = flag(lax.broadcasted_iota(jnp.int32, (3, CHUNK), 0) == i)
         for p in range(PAIRS):
             centre_row = twice(centre_both, p)
             for q in range(4):
-                at = chunk_mask(others[p], q) * other_rows[p][i]
+                at = chunk_mask(others[p], q) * others_sum[p, i : i + 1, :]
                 if q in (1, 2):
                     at = at + chunk_mask(centres[p] + SEND, q) * centre_row
                 tile_grads[q] = tile_grads[q] + at * component
@@ -499,11 +520,11 @@
     both[11:14, :] = paired(*(pick(error[1:3], centres[p]) for p in range(PAIRS)))
     columns_of(both[...], square, turned)
 
-    for p in range(PAIRS):
-        lane_move = [twice(both[8 + i : 9 + i, :], p) for i in range(3)]
+    def moved(p):
+        lane_move = [twice_at(both[8 + i : 9 + i, :], p) for i in range(3)]
         for r in range(0, TA, STRIP):
             strip = slice(r, r + STRIP)
-            here = slice(p * TA + r, p * TA + r + STRIP)
+            here = span(p * TA + r, STRIP)
             column_move = [turned[here, 11 + i : 12 + i] for i in range(3)]
             unit = [shape_store[p, i, strip, :] for i in range(3)]
             inverse = shape_store[p, 3, strip, :]
@@ -518,7 +539,9 @@
                     at = slice(m * TA + r, m * TA + r + STRIP)
                     entry = slope if m == 0 else angular[m] * slope + turning[m] * value
                     put_left(table, p, at, k * CHUNK, CHUNK, entry)
-        raw[p * COMPS * TA : (p + 1) * COMPS * TA, :] = long_product(table[p], tall[p], NN)
+        raw[span(p * COMPS * TA, COMPS * TA), :] = long_product(table[p], tall[p], NN)
+
+    slots(moved)
 
     for m in range(COMPS):
         first = raw[m * TA : (m + 1) * TA, :]
@@ -854,7 +877,7 @@
             ((PAIRS, WIDE, channels), BF16),
         ],
         turning
-        + [((3, CHUNK, CHUNK), F32)]
+        + [((3, CHUNK, CHUNK), F32), ((PAIRS, 8, CHUNK), F32)]
         + [(long_table, BF16), ((PAIRS, BASIS * TA, 3 * channels), BF16)]
         + [((PAIRS, COMPS * TA, 3 * channels), BF16)]
         + [((PAIRS * COMPS * TA, channels), F32), ((PAIRS, *table), F32)],

time: 62 us -> 62.7 us (1.011)
  Pallas kernels: 17.3 us -> 18 us
    pallas_call x15, Pallas kernels: 17.3 us -> 18 us  [call(): pl.pallas_call(kernel, name=name, out_shape=[jax.ShapeDtypeStruct(*out) f...]
where the time goes in v12:
time: 62.7 us; the launch traced here: 62.5 us
  starting transfers between devices  26.3 us (42%)
  Pallas kernels  18 us (29%)
  waiting for transfers between devices  17.5 us (28%)
  between operations  0.75 us (1%)
    pallas_call x15, Pallas kernels, call(): pl.pallas_call(kernel, name=name, out_shape=[jax.ShapeDtypeStruct(*out) f...  18 us
    ppermute x10, starting transfers between devices, partner(): lax.ppermute(block, 'domain', [(i, i ^ mask) for i in range(lax.axis_size...  14.2 us
    ppermute x6, starting transfers between devices, exchanged(): lax.ppermute(block, 'domain', [(i, (i + step if up[i] else i - step) % co...  11.9 us
    ppermute x10, waiting for transfers between devices, partner(): lax.ppermute(block, 'domain', [(i, i ^ mask) for i in range(lax.axis_size...  10.5 us
    ppermute x6, waiting for transfers between devices, exchanged(): lax.ppermute(block, 'domain', [(i, (i + step if up[i] else i - step) % co...  5.31 us
    ppermute x2, waiting for transfers between devices, shifted(): lax.ppermute(block, axis, [(i, (i + by) % count) for i in range(count)])  1.74 us
  transfers between devices with their start and end apart: 18, of which 10 were waited for; matrix products, arithmetic and copies ran while one was open for 0% of the time, Pallas kernels for 11%

profile of v12, /device:TPU:0, one launch (start us, length us, event | category | flops | bytes accessed | tf_op | source)
XLA Modules:
  0.0 62.5 jit_solution(15897694236645518215)
XLA Ops:
  0.6 1.2 %gather.1 = (f32[136,256]{1,0:T(8,128)S(1)}, f32[136,256]{1,0:T(8,128)S(1)}, f32[8,128]{1,0:T(8,128)S(1)}) custom-call(s32[1,4]{1,0:T(1,128)} %send.3, f32[3,1,256]{2,1,0:T(1,128)} %bitcast.5, f32[1,256,256]{2,1,0:T(8,128)} %feat.3, f32[3,1,256]{2,1,0:T(1,128)} %bitcast.7), custom_call_target="tpu_custom_call" | custom-call | bytes 1024 | tf_op jit(solution)/shard_map/gather/pallas_call | solution.py:767
  1.8 3.0 %collective-permute-start = (f32[136,256]{1,0:T(8,128)S(1)}, f32[136,256]{1,0:T(8,128)S(1)}, u32[]{:S(2)}, u32[]{:S(2)}) collective-permute-start(f32[136,256]{1,0:T(8,128)S(1)} %get-tuple-element.59), channel_id=1, source_target_pairs={{0,2},{2,0},{4,6},{6,4},{8,10},{10,8},{12,14},{14,12},{1,3},{3,1},... | collective-permute-start | bytes 417800 | tf_op jit(solution)/shard_map/ppermute | solution.py:787
  4.8 3.5 %collective-permute-start.1 = (f32[136,256]{1,0:T(8,128)S(1)}, f32[136,256]{1,0:T(8,128)S(1)}, u32[]{:S(2)}, u32[]{:S(2)}) collective-permute-start(f32[136,256]{1,0:T(8,128)S(1)} %get-tuple-element.60), channel_id=1, source_target_pairs={{0,14},{2,4},{4,2},{6,8},{8,6},{10,12},{12,10},{14,0},{1,15},{3,5}... | collective-permute-start | bytes 417800 | tf_op jit(solution)/shard_map/ppermute | solution.py:787
  8.4 1.6 %stage.1 = (f32[16,128]{1,0:T(8,128)S(1)}, f32[8,256]{1,0:T(8,128)S(1)}, f32[256,256]{1,0:T(8,128)S(1)}, f32[16,256]{1,0:T(8,128)S(1)}, bf16[768,256]{1,0:T(8,128)(2,1)S(1)}, /*index=5*/bf16[768,256]{1,0:T(8,128)(2,1)S(1)}) custom-call(s32[1,2]{1,0:T(1,128)} %centre.1, s32[1,2]{1,0:T(1,128)} %other.1, s32[1,2]{1,0:T(1,128)} %live.1, s32[1,4]{1,0:T(1,128)} %send.3, ...), custom_call_target="tpu_custom_call" | custom-call | bytes 1024 | tf_op jit(solution)/shard_map/stage/pallas_call | solution.py:767
  10.0 0.8 %collective-permute-done.from_first = f32[136,256]{1,0:T(8,128)S(1)} collective-permute-done((f32[136,256]{1,0:T(8,128)S(1)}, f32[136,256]{1,0:T(8,128)S(1)}, u32[]{:S(2)}, u32[]{:S(2)}) %collective-permute-start) | collective-permute-done | bytes 139296 | tf_op jit(solution)/shard_map/ppermute | solution.py:787
  10.8 1.9 %collective-permute-done.1.from_second = f32[136,256]{1,0:T(8,128)S(1)} collective-permute-done((f32[136,256]{1,0:T(8,128)S(1)}, f32[136,256]{1,0:T(8,128)S(1)}, u32[]{:S(2)}, u32[]{:S(2)}) %collective-permute-start.1) | collective-permute-done | bytes 139296 | tf_op jit(solution)/shard_map/ppermute | solution.py:787
  12.7 5.4 %force.1 = (f32[1152,256]{1,0:T(8,128)S(1)}, f32[128,768]{1,0:T(8,128)S(1)}, f32[128,256]{1,0:T(8,128)S(1)}, f32[128,256]{1,0:T(8,128)S(1)}, f32[128,768]{1,0:T(...) custom-call(f32[16,128]{1,0:T(8,128)S(1)} %get-tuple-element.54.flag, ...), custom_call_target="tpu_custom_call" | custom-call | flops 2147483648 | bytes 1048576 | tf_op jit(solution)/shard_map/force/pallas_call | solution.py:767
  18.1 3.7 %collective-permute-start.2 = (f32[8,128]{1,0:T(8,128)S(1)}, f32[8,128]{1,0:T(8,128)S(1)}, u32[]{:S(2)}, u32[]{:S(2)}) collective-permute-start(f32[8,128]{1,0:T(8,128)S(1)} %get-tuple-element.63), channel_id=1, source_target_pairs={{0,14},{2,4},{4,2},{6,8},{8,6},{10,12},{12,10},{14,0},{1,15},{3,5}... | collective-permute-start | bytes 12296 | tf_op jit(solution)/shard_map/ppermute | solution.py:787
  21.8 0.5 collective-permute-start.3
  22.2 1.2 %collective-permute-start.4 = (f32[8,128]{1,0:T(8,128)S(1)}, f32[8,128]{1,0:T(8,128)S(1)}, u32[]{:S(2)}, u32[]{:S(2)}) collective-permute-start(f32[8,128]{1,0:T(8,128)S(1)} %get-tuple-element.65), channel_id=1, source_target_pairs={{0,2},{2,0},{4,6},{6,4},{8,10},{10,8},{12,14},{14,12},{1,3},{3,1},... | collective-permute-start | bytes 12296 | tf_op jit(solution)/shard_map/ppermute | solution.py:787
  23.4 1.1 %table.1 = (f32[2,20,64,128]{3,2,1,0:T(8,128)S(1)}, bf16[2,512,640]{2,1,0:T(8,128)(2,1)S(1)}, bf16[2,512,640]{2,1,0:T(8,128)(2,1)S(1)}, f32[8,128]{1,0:T(8,128)S(1)}) custom-call(f32[16,128]{1,0:T(8,128)S(1)} %get-tuple-element.54.flags, f32[8,128]{1,0:T(8,128)S(1)} %get-tuple-element.67.rows), custom_call_target="tpu_custom_call" | custom-call | flops 1073741824 | bytes 1048576 | tf_op jit(solution)/shard_map/table/pallas_call | solution.py:767
  24.5 2.6 %collective-permute-done.3.two_second = f32[8,128]{1,0:T(8,128)S(1)} collective-permute-done((f32[8,128]{1,0:T(8,128)S(1)}, f32[8,128]{1,0:T(8,128)S(1)}, u32[]{:S(2)}, u32[]{:S(2)}) %collective-permute-start.3) | collective-permute-done | bytes 4128 | tf_op jit(solution)/shard_map/ppermute | solution.py:787
  27.2 3.6 %tangent.1 = (f32[3,1,256]{2,1,0:T(1,128)}, f32[768,128]{1,0:T(8,128)S(1)}, f32[768,128]{1,0:T(8,128)S(1)}, f32[8,256]{1,0:T(8,128)S(1)}, f32[1152,256]{1,0:T(8,...) custom-call(f32[16,128]{1,0:T(8,128)S(1)} %get-tuple-element.54.flags, f32[8,256]{1,0:T(8,128)S(1)} %get-tuple-element.55.atoms, ...), custom_call_target="tpu_custom_call" | custom-call | flops 2147483648 | bytes 1048576 | tf_op jit(solution)/shard_map/tangent/pallas_call | solution.py:767
  30.8 2.0 %radial.2.after.radial_0 = f32[8,256]{1,0:T(8,128)S(1)} custom-call(f32[16,128]{1,0:T(8,128)S(1)} %get-tuple-element.78.both.after, f32[2,20,64,128]{3,2,1,0:T(8,128)S(1)} %get-tuple-element.79.shape_store, bf16[2,512,640]{2,1,0:T(8,128)(2,1)S(1)} %get-tuple-element.80.lh, bf16[2,512,640]{2,1,0:T(8,128)(2,1)S(1)} %get-tuple-element.81.ll, ...), custom_call_target="tpu_custom_call" | custom-call | flops 2147483648 | bytes 1048576 | tf_op jit(solution)/shard_map/radial/pallas_call | solution.py:767
  32.9 0.8 %collective-permute-start.8 = (f32[200,128]{1,0:T(8,128)S(1)}, f32[200,128]{1,0:T(8,128)S(1)}, u32[]{:S(2)}, u32[]{:S(2)}) collective-permute-start(f32[200,128]{1,0:T(8,128)S(1)} %get-tuple-element.92), channel_id=1, source_target_pairs={{0,2},{2,0},{4,6},{6,4},{8,10},{10,8},{12,14},{14,12},{1,3},{3,1},... | collective-permute-start | bytes 307208 | tf_op jit(solution)/shard_map/ppermute | solution.py:791
  33.6 1.3 %collective-permute-start.7 = (f32[192,128]{1,0:T(8,128)S(1)}, f32[192,128]{1,0:T(8,128)S(1)}, u32[]{:S(2)}, u32[]{:S(2)}) collective-permute-start(f32[192,128]{1,0:T(8,128)S(1)} %get-tuple-element.89), channel_id=1, source_target_pairs={{0,2},{2,0},{4,6},{6,4},{8,10},{10,8},{12,14},{14,12},{1,3},{3,1},... | collective-permute-start | bytes 294920 | tf_op jit(solution)/shard_map/ppermute | solution.py:791
  35.0 2.0 %radial.3.radial_1.after = f32[8,256]{1,0:T(8,128)S(1)} custom-call(f32[16,128]{1,0:T(8,128)S(1)} %get-tuple-element.78.both.after, f32[2,20,64,128]{3,2,1,0:T(8,128)S(1)} %get-tuple-element.79.shape_store, bf16[2,512,640]{2,1,0:T(8,128)(2,1)S(1)} %get-tuple-element.80.lh, bf16[2,512,640]{2,1,0:T(8,128)(2,1)S(1)} %get-tuple-element.81.ll, ...), custom_call_target="tpu_custom_call" | custom-call | bytes 1024 | tf_op jit(solution)/shard_map/radial/pallas_call | solution.py:767
  37.0 1.6 %collective-permute-done.8.taken = f32[200,128]{1,0:T(8,128)S(1)} collective-permute-done((f32[200,128]{1,0:T(8,128)S(1)}, f32[200,128]{1,0:T(8,128)S(1)}, u32[]{:S(2)}, u32[]{:S(2)}) %collective-permute-start.8) | collective-permute-done | bytes 102432 | tf_op jit(solution)/shard_map/ppermute | solution.py:791
  38.7 2.2 %collective-permute-start.9 = (f32[120,128]{1,0:T(8,128)S(1)}, f32[120,128]{1,0:T(8,128)S(1)}, u32[]{:S(2)}, u32[]{:S(2)}) collective-permute-start(f32[120,128]{1,0:T(8,128)S(1)} %get-tuple-element.93.after), channel_id=1, source_target_pairs={{0,12},{2,14},{4,8},{6,10},{8,4},{10,6},{12,0},{14,2},{1,13},{3,15... | collective-permute-start | bytes 184328 | tf_op jit(solution)/shard_map/ppermute | solution.py:791
  40.9 2.3 %collective-permute-start.11 = (f32[104,128]{1,0:T(8,128)S(1)}, f32[104,128]{1,0:T(8,128)S(1)}, u32[]{:S(2)}, u32[]{:S(2)}) collective-permute-start(f32[104,128]{1,0:T(8,128)S(1)} %get-tuple-element.96), channel_id=1, source_target_pairs={{0,4},{2,6},{4,0},{6,2},{8,12},{10,14},{12,8},{14,10},{1,5},{3,7},... | collective-permute-start | bytes 159752 | tf_op jit(solution)/shard_map/ppermute | solution.py:791
  43.2 2.4 %collective-permute-done.11.refs_3_ = f32[104,128]{1,0:T(8,128)S(1)} collective-permute-done((f32[104,128]{1,0:T(8,128)S(1)}, f32[104,128]{1,0:T(8,128)S(1)}, u32[]{:S(2)}, u32[]{:S(2)}) %collective-permute-start.11) | collective-permute-done | bytes 53280 | tf_op jit(solution)/shard_map/ppermute | solution.py:791
  45.6 0.7 %collective-permute-done.10.refs_2_ = f32[112,128]{1,0:T(8,128)S(1)} collective-permute-done((f32[112,128]{1,0:T(8,128)S(1)}, f32[112,128]{1,0:T(8,128)S(1)}, u32[]{:S(2)}, u32[]{:S(2)}) %collective-permute-start.10) | collective-permute-done | bytes 57376 | tf_op jit(solution)/shard_map/ppermute | solution.py:791
  46.3 2.5 %collective-permute-start.12 = (f32[104,128]{1,0:T(8,128)S(1)}, f32[104,128]{1,0:T(8,128)S(1)}, u32[]{:S(2)}, u32[]{:S(2)}) collective-permute-start(f32[104,128]{1,0:T(8,128)S(1)} %total.1.mine), channel_id=1, source_target_pairs={{0,12},{2,14},{4,8},{6,10},{8,4},{10,6},{12,0},{14,2},{1,13},{3,15... | collective-permute-start | bytes 159752 | tf_op jit(solution)/shard_map/ppermute | solution.py:791
  48.8 0.1 collective-permute-start.14
  48.9 1.9 %collective-permute-start.13 = (f32[104,128]{1,0:T(8,128)S(1)}, f32[104,128]{1,0:T(8,128)S(1)}, u32[]{:S(2)}, u32[]{:S(2)}) collective-permute-start(f32[104,128]{1,0:T(8,128)S(1)} %total.1.mine), channel_id=1, source_target_pairs={{0,4},{2,6},{4,0},{6,2},{8,12},{10,14},{12,8},{14,10},{1,5},{3,7},... | collective-permute-start | bytes 159752 | tf_op jit(solution)/shard_map/ppermute | solution.py:791
  50.7 1.5 %collective-permute-done.12.third = f32[104,128]{1,0:T(8,128)S(1)} collective-permute-done((f32[104,128]{1,0:T(8,128)S(1)}, f32[104,128]{1,0:T(8,128)S(1)}, u32[]{:S(2)}, u32[]{:S(2)}) %collective-permute-start.12) | collective-permute-done | bytes 53280 | tf_op jit(solution)/shard_map/ppermute | solution.py:791
  52.3 1.8 %collective-permute-start.15 = (f32[232,128]{1,0:T(8,128)S(1)}, f32[232,128]{1,0:T(8,128)S(1)}, u32[]{:S(2)}, u32[]{:S(2)}) collective-permute-start(f32[232,128]{1,0:T(8,128)S(1)} %near.1.after), channel_id=1, source_target_pairs={{0,2},{2,0},{4,6},{6,4},{8,10},{10,8},{12,14},{14,12},{1,3},{3,1},... | collective-permute-start | bytes 356360 | tf_op jit(solution)/shard_map/ppermute | solution.py:791
  54.1 0.2 collective-permute-done.14.second
  54.4 1.4 %collective-permute-start.16 = (f32[224,128]{1,0:T(8,128)S(1)}, f32[224,128]{1,0:T(8,128)S(1)}, u32[]{:S(2)}, u32[]{:S(2)}) collective-permute-start(f32[224,128]{1,0:T(8,128)S(1)} %rest.1), channel_id=1, source_target_pairs={{0,2},{2,0},{4,6},{6,4},{8,10},{10,8},{12,14},{14,12},{1,3},{3,1},... | collective-permute-start | bytes 344072 | tf_op jit(solution)/shard_map/ppermute | solution.py:791
  55.7 4.0 %collective-permute-done.16.their_rest = f32[224,128]{1,0:T(8,128)S(1)} collective-permute-done((f32[224,128]{1,0:T(8,128)S(1)}, f32[224,128]{1,0:T(8,128)S(1)}, u32[]{:S(2)}, u32[]{:S(2)}) %collective-permute-start.16) | collective-permute-done | bytes 114720 | tf_op jit(solution)/shard_map/ppermute | solution.py:791
  59.8 1.7 %collective-permute-done.17.facing = f32[800,128]{1,0:T(8,128)S(1)} collective-permute-done((f32[800,128]{1,0:T(8,128)S(1)}, f32[800,128]{1,0:T(8,128)S(1)}, u32[]{:S(2)}, u32[]{:S(2)}) %collective-permute-start.17) | collective-permute-done | bytes 409632 | tf_op jit(solution)/shard_map/ppermute | solution.py:781
  61.5 1.0 %join.1 = (f32[768,256]{1,0:T(8,128)}, f32[8,256]{1,0:T(8,128)}, f32[4,256]{1,0:T(4,128)}, f32[1,256]{1,0:T(1,128)}) custom-call(f32[800,128]{1,0:T(8,128)S(1)} %pair.1.whole, f32[800,128]{1,0:T(8,128)S(1)} %collective-permute-done.17.facing), custom_call_target="tpu_custom_call" | custom-call | bytes 1024 | tf_op jit(solution)/shard_map/join/pallas_call | solution.py:767
  (19 shorter events, 0.3 us)
Async XLA Ops:
  1.8 8.9 %collective-permute-start = (f32[136,256]{1,0:T(8,128)S(1)}, f32[136,256]{1,0:T(8,128)S(1)}, u32[]{:S(2)}, u32[]{:S(2)}) collective-permute-start(f32[136,256]{1,0:T(8,128)S(1)} %get-tuple-element.59), channel_id=1, source_target_pairs={{0,2},{2,0},{4,6},{6,4},{8,10},{10,8},{12,14},{14,12},{1,3},{3,1},... | collective-permute-start | bytes 417800 | tf_op jit(solution)/shard_map/ppermute | solution.py:787
  4.8 7.8 %collective-permute-start.1 = (f32[136,256]{1,0:T(8,128)S(1)}, f32[136,256]{1,0:T(8,128)S(1)}, u32[]{:S(2)}, u32[]{:S(2)}) collective-permute-start(f32[136,256]{1,0:T(8,128)S(1)} %get-tuple-element.60), channel_id=1, source_target_pairs={{0,14},{2,4},{4,2},{6,8},{8,6},{10,12},{12,10},{14,0},{1,15},{3,5}... | collective-permute-start | bytes 417800 | tf_op jit(solution)/shard_map/ppermute | solution.py:787
  18.1 6.4 %collective-permute-start.2 = (f32[8,128]{1,0:T(8,128)S(1)}, f32[8,128]{1,0:T(8,128)S(1)}, u32[]{:S(2)}, u32[]{:S(2)}) collective-permute-start(f32[8,128]{1,0:T(8,128)S(1)} %get-tuple-element.63), channel_id=1, source_target_pairs={{0,14},{2,4},{4,2},{6,8},{8,6},{10,12},{12,10},{14,0},{1,15},{3,5}... | collective-permute-start | bytes 12296 | tf_op jit(solution)/shard_map/ppermute | solution.py:787
  21.8 5.4 %collective-permute-start.3 = (f32[8,128]{1,0:T(8,128)S(1)}, f32[8,128]{1,0:T(8,128)S(1)}, u32[]{:S(2)}, u32[]{:S(2)}) collective-permute-start(f32[8,128]{1,0:T(8,128)S(1)} %get-tuple-element.64), channel_id=1, source_target_pairs={{0,12},{2,14},{4,8},{6,10},{8,4},{10,6},{12,0},{14,2},{1,13},{3,15... | collective-permute-start | bytes 12296 | tf_op jit(solution)/shard_map/ppermute | solution.py:787
  22.2 4.9 %collective-permute-start.4 = (f32[8,128]{1,0:T(8,128)S(1)}, f32[8,128]{1,0:T(8,128)S(1)}, u32[]{:S(2)}, u32[]{:S(2)}) collective-permute-start(f32[8,128]{1,0:T(8,128)S(1)} %get-tuple-element.65), channel_id=1, source_target_pairs={{0,2},{2,0},{4,6},{6,4},{8,10},{10,8},{12,14},{14,12},{1,3},{3,1},... | collective-permute-start | bytes 12296 | tf_op jit(solution)/shard_map/ppermute | solution.py:787
  23.4 3.7 %collective-permute-start.5 = (f32[8,128]{1,0:T(8,128)S(1)}, f32[8,128]{1,0:T(8,128)S(1)}, u32[]{:S(2)}, u32[]{:S(2)}) collective-permute-start(f32[8,128]{1,0:T(8,128)S(1)} %get-tuple-element.66), channel_id=1, source_target_pairs={{0,4},{2,6},{4,0},{6,2},{8,12},{10,14},{12,8},{14,10},{1,5},{3,7},... | collective-permute-start | bytes 12296 | tf_op jit(solution)/shard_map/ppermute | solution.py:787
  30.7 2.1 %collective-permute-start.6 = (f32[768,128]{1,0:T(8,128)S(1)}, f32[768,128]{1,0:T(8,128)S(1)}, u32[]{:S(2)}, u32[]{:S(2)}) collective-permute-start(f32[768,128]{1,0:T(8,128)S(1)} %get-tuple-element.77), channel_id=1, source_target_pairs={{0,1},{1,0},{2,3},{3,2},{4,5},{5,4},{6,7},{7,6},{8,9},{9,8},{10,11... | collective-permute-start | bytes 1179656 | tf_op jit(solution)/shard_map/ppermute | solution.py:781
  32.9 5.7 %collective-permute-start.8 = (f32[200,128]{1,0:T(8,128)S(1)}, f32[200,128]{1,0:T(8,128)S(1)}, u32[]{:S(2)}, u32[]{:S(2)}) collective-permute-start(f32[200,128]{1,0:T(8,128)S(1)} %get-tuple-element.92), channel_id=1, source_target_pairs={{0,2},{2,0},{4,6},{6,4},{8,10},{10,8},{12,14},{14,12},{1,3},{3,1},... | collective-permute-start | bytes 307208 | tf_op jit(solution)/shard_map/ppermute | solution.py:791
  33.6 7.2 %collective-permute-start.7 = (f32[192,128]{1,0:T(8,128)S(1)}, f32[192,128]{1,0:T(8,128)S(1)}, u32[]{:S(2)}, u32[]{:S(2)}) collective-permute-start(f32[192,128]{1,0:T(8,128)S(1)} %get-tuple-element.89), channel_id=1, source_target_pairs={{0,2},{2,0},{4,6},{6,4},{8,10},{10,8},{12,14},{14,12},{1,3},{3,1},... | collective-permute-start | bytes 294920 | tf_op jit(solution)/shard_map/ppermute | solution.py:791
  38.7 7.6 %collective-permute-start.9 = (f32[120,128]{1,0:T(8,128)S(1)}, f32[120,128]{1,0:T(8,128)S(1)}, u32[]{:S(2)}, u32[]{:S(2)}) collective-permute-start(f32[120,128]{1,0:T(8,128)S(1)} %get-tuple-element.93.after), channel_id=1, source_target_pairs={{0,12},{2,14},{4,8},{6,10},{8,4},{10,6},{12,0},{14,2},{1,13},{3,15... | collective-permute-start | bytes 184328 | tf_op jit(solution)/shard_map/ppermute | solution.py:791
  40.8 5.4 %collective-permute-start.10 = (f32[112,128]{1,0:T(8,128)S(1)}, f32[112,128]{1,0:T(8,128)S(1)}, u32[]{:S(2)}, u32[]{:S(2)}) collective-permute-start(f32[112,128]{1,0:T(8,128)S(1)} %get-tuple-element.95), channel_id=1, source_target_pairs={{0,8},{2,10},{4,12},{6,14},{8,0},{10,2},{12,4},{14,6},{1,9},{3,11}... | collective-permute-start | bytes 172040 | tf_op jit(solution)/shard_map/ppermute | solution.py:791
  40.9 4.8 %collective-permute-start.11 = (f32[104,128]{1,0:T(8,128)S(1)}, f32[104,128]{1,0:T(8,128)S(1)}, u32[]{:S(2)}, u32[]{:S(2)}) collective-permute-start(f32[104,128]{1,0:T(8,128)S(1)} %get-tuple-element.96), channel_id=1, source_target_pairs={{0,4},{2,6},{4,0},{6,2},{8,12},{10,14},{12,8},{14,10},{1,5},{3,7},... | collective-permute-start | bytes 159752 | tf_op jit(solution)/shard_map/ppermute | solution.py:791
  46.3 6.0 %collective-permute-start.12 = (f32[104,128]{1,0:T(8,128)S(1)}, f32[104,128]{1,0:T(8,128)S(1)}, u32[]{:S(2)}, u32[]{:S(2)}) collective-permute-start(f32[104,128]{1,0:T(8,128)S(1)} %total.1.mine), channel_id=1, source_target_pairs={{0,12},{2,14},{4,8},{6,10},{8,4},{10,6},{12,0},{14,2},{1,13},{3,15... | collective-permute-start | bytes 159752 | tf_op jit(solution)/shard_map/ppermute | solution.py:791
  48.8 5.5 %collective-permute-start.14 = (f32[104,128]{1,0:T(8,128)S(1)}, f32[104,128]{1,0:T(8,128)S(1)}, u32[]{:S(2)}, u32[]{:S(2)}) collective-permute-start(f32[104,128]{1,0:T(8,128)S(1)} %total.1.mine), channel_id=1, source_target_pairs={{0,8},{2,10},{4,12},{6,14},{8,0},{10,2},{12,4},{14,6},{1,9},{3,11}... | collective-permute-start | bytes 159752 | tf_op jit(solution)/shard_map/ppermute | solution.py:791
  48.9 5.4 %collective-permute-start.13 = (f32[104,128]{1,0:T(8,128)S(1)}, f32[104,128]{1,0:T(8,128)S(1)}, u32[]{:S(2)}, u32[]{:S(2)}) collective-permute-start(f32[104,128]{1,0:T(8,128)S(1)} %total.1.mine), channel_id=1, source_target_pairs={{0,4},{2,6},{4,0},{6,2},{8,12},{10,14},{12,8},{14,10},{1,5},{3,7},... | collective-permute-start | bytes 159752 | tf_op jit(solution)/shard_map/ppermute | solution.py:791
  52.3 7.4 %collective-permute-start.15 = (f32[232,128]{1,0:T(8,128)S(1)}, f32[232,128]{1,0:T(8,128)S(1)}, u32[]{:S(2)}, u32[]{:S(2)}) collective-permute-start(f32[232,128]{1,0:T(8,128)S(1)} %near.1.after), channel_id=1, source_target_pairs={{0,2},{2,0},{4,6},{6,4},{8,10},{10,8},{12,14},{14,12},{1,3},{3,1},... | collective-permute-start | bytes 356360 | tf_op jit(solution)/shard_map/ppermute | solution.py:791
  54.4 5.3 %collective-permute-start.16 = (f32[224,128]{1,0:T(8,128)S(1)}, f32[224,128]{1,0:T(8,128)S(1)}, u32[]{:S(2)}, u32[]{:S(2)}) collective-permute-start(f32[224,128]{1,0:T(8,128)S(1)} %rest.1), channel_id=1, source_target_pairs={{0,2},{2,0},{4,6},{6,4},{8,10},{10,8},{12,14},{14,12},{1,3},{3,1},... | collective-permute-start | bytes 344072 | tf_op jit(solution)/shard_map/ppermute | solution.py:791
  59.7 1.8 %collective-permute-start.17 = (f32[800,128]{1,0:T(8,128)S(1)}, f32[800,128]{1,0:T(8,128)S(1)}, u32[]{:S(2)}, u32[]{:S(2)}) collective-permute-start(f32[800,128]{1,0:T(8,128)S(1)} %pair.1.whole), channel_id=1, source_target_pairs={{0,1},{1,0},{2,3},{3,2},{4,5},{5,4},{6,7},{7,6},{8,9},{9,8},{10,11... | collective-permute-start | bytes 1228808 | tf_op jit(solution)/shard_map/ppermute | solution.py:781

commit v13 on v11

--- a/solution.py
+++ b/solution.py
@@ -260,7 +260,7 @@
 
 def stage_kernel(
     centre, other, live, send, pos, ref, species, feat, radial_w, mix_w, species_w, out_w, after,
-    flags, atoms, own_feat, weights, mh, ml,
+    flags, atoms, own_feat, weights, mh, ml, nh, nl,
     centre_v, other_v, live_v, send_v, pos_v, ref_v, species_v, radial_v, mix_v, species_w_v, out_v, sems,
 ):
     copies = fetch(
@@ -298,13 +298,14 @@
     weights[BASIS : BASIS + SPECIES, :] = species_w_v[...]
     weights[BASIS + SPECIES : BASIS + SPECIES + 1, :] = out_v[...]
     copies[-1].wait()
-    hi, lo = split(mix_v[...])
-    mh[...] = hi
-    ml[...] = lo
+    for value, (high_part, low_part) in ((mix_v[...], (mh, ml)), (mix_v[...].T, (nh, nl))):
+        hi, lo = split(value)
+        high_part[...] = hi
+        low_part[...] = lo
 
 
 def force_kernel(
-    flags, atoms, feat, weights, mh, ml, from_second, from_first,
+    flags, atoms, feat, weights, mh, ml, nh, nl, from_second, from_first,
     env, dinv, gate, curve, inv, rows, fsel, own, one_first, one_second, two_first, two_second, shape_store, tall, eh, el,
     square, turned, squares, table, wide, steady, raw, back,
 ):
@@ -375,7 +376,7 @@
     first_order = sigma * (1.0 + hidden * (1.0 - sigma))
     gate[...] = first_order
     curve[...] = sigma * (1.0 - sigma) * (2.0 + hidden * (1.0 - 2.0 * sigma)) * out_row
-    dinv[...] = product(split(first_order * out_row), (mh[...], ml[...]), NT)
+    dinv[...] = product(split(first_order * out_row), (nh[...], nl[...]), NN)
 
     tile_grads = [jnp.zeros((3, CHUNK), F32) for _ in range(4)]
     other_rows = []
@@ -450,9 +451,9 @@
 
 def tangent_kernel(
     scale, flags, atoms, weights, mh, ml, from_first, from_second, own, one_second, two_second, one_first, two_first,
-    rows, env, gate, curve, inv, shape_store, tall, after,
+    rows, env, gate, curve, inv_high, inv_low, shape_store, tall,
     forces, keep, give, small, envdot, curl, both,
-    square, turned, table, raw, left, right,
+    square, turned, table, raw, invdot, left_high, left_low, right,
 ):
     ghost = SEND * TA
     def number(row):
@@ -525,7 +526,6 @@
         second = raw[(COMPS + m) * TA : (COMPS + m + 1) * TA, :]
         envdot[m * TA : (m + 1) * TA, :] = env_scale * (first + shared * second)
         envdot[(COMPS + m) * TA : (COMPS + m + 1) * TA, :] = env_scale * (second + shared * first)
-    invdot = left
     half = PAIRS * TA
     for p in range(PAIRS):
         sums = [None] * 3
@@ -534,18 +534,21 @@
             term = 2.0 * env[at, :] * envdot[at, :]
             sums[GROUP[m]] = term if sums[GROUP[m]] is None else sums[GROUP[m]] + term
         for g in range(3):
-            invdot[half + p * TA : half + (p + 1) * TA, g * 256 : (g + 1) * 256] = sums[g]
-    invdot[0:half, :] = inv[...]
-    hidden_move = product(split(invdot[half:, :]), (mh[...], ml[...]), NN)
+            invdot[p * TA : (p + 1) * TA, g * 256 : (g + 1) * 256] = sums[g]
+    hidden_move = product(split(invdot[...]), (mh[...], ml[...]), NN)
     bend = curve[...] * hidden_move
     curl[...] = bend
     once = 1.0 - shared * flag(lax.broadcasted_iota(jnp.int32, (half, 1), 0) >= TA)
     right[0:half, :] = bend * once
     right[half:, :] = gate[...] * weights[BASIS + SPECIES : BASIS + SPECIES + 1, :] * once
-    raw[0 : left.shape[1], :] = product(split(left[...]), split(right[...]), TN)
+    hi, lo = split(invdot[...].T)
+    for ref, given, made in ((left_high, inv_high, hi), (left_low, inv_low, lo)):
+        ref[:, 0:half] = given[...]
+        ref[:, half:] = made
+    raw[0 : left_high.shape[0], :] = product((left_high[...], left_low[...]), split(right[...]), NN)
     core = lax.axis_index("batch")
     for out, part in ((keep, core), (give, 1 - core)):
-        out[...] = raw[0 : left.shape[1], block_of_lanes(part)]
+        out[...] = raw[0 : left_high.shape[0], block_of_lanes(part)]
     small[...] = jnp.zeros_like(small)
     kind = turned[:, 6:7]
     for s in range(SPECIES):
@@ -553,9 +556,11 @@
     small[SPECIES : SPECIES + 1, :] = jnp.sum(gate[...] * hidden_move * once, axis=0, keepdims=True)
 
 
-def table_kernel(flags, rows, shape_store, lh, ll, token, square, turned):
+def table_kernel(flags, rows, inv, shape_store, lh, ll, inv_high, inv_low, square, turned):
     low, high = lane_half()
-    token[...] = jnp.zeros_like(token)
+    hi, lo = split(inv[...].T)
+    inv_high[...] = hi
+    inv_low[...] = lo
     columns_of(rows[...], square, turned)
     for p in range(PAIRS):
         lane_rows = [twice(rows[3 + i : 4 + i, :], p) for i in range(3)]
@@ -579,14 +584,14 @@
 
 
 def radial_kernel(
-    p, both, shape_store, lh, ll, eh, el, fsel, env, envdot, dinv, curl, mh, ml, after,
+    p, both, shape_store, lh, ll, eh, el, fsel, env, envdot, dinv, curl, nh, nl, after,
     grad_radial,
     square, turned, sh, sl, gh, gl, raw,
 ):
     low, high = lane_half()
     columns_of(both[...], square, turned)
     here = slice(p * TA, (p + 1) * TA)
-    turn_inv = product(split(curl[here, :]), (mh[...], ml[...]), NT)
+    turn_inv = product(split(curl[here, :]), (nh[...], nl[...]), NN)
     lane_move = [twice(both[11 + i : 12 + i, :], p) for i in range(3)]
     sh[:, 0:CHUNK] = lh[p, :, WIDE - CHUNK :]
     sl[:, 0:CHUNK] = ll[p, :, WIDE - CHUNK :]
@@ -810,7 +815,7 @@
     )
     from_second = exchanged(to_second, 0, False)
     from_first = exchanged(to_first, 0, True)
-    flags, atoms, own_feat, weights, mh, ml = call(
+    flags, atoms, own_feat, weights, mh, ml, nh, nl = call(
         stage_kernel,
         "stage",
         [
@@ -820,6 +825,8 @@
             (16, channels),
             (mix_w.shape, BF16),
             (mix_w.shape, BF16),
+            (mix_w.shape[::-1], BF16),
+            (mix_w.shape[::-1], BF16),
         ],
         ints
         + [(line, F32), (line, F32), ((1, atoms_here), jnp.int32)]
@@ -858,22 +865,23 @@
         + [(long_table, BF16), ((PAIRS, BASIS * TA, 3 * channels), BF16)]
         + [((PAIRS, COMPS * TA, 3 * channels), BF16)]
         + [((PAIRS * COMPS * TA, channels), F32), ((PAIRS, *table), F32)],
-        flags, atoms, own_feat, weights, mh, ml, from_second, from_first,
+        flags, atoms, own_feat, weights, mh, ml, nh, nl, from_second, from_first,
         flops=1 << 31,
     )
     arriving = [exchanged(leaving[i], i // 2, i % 2 == 0) for i in (1, 3, 0, 2)]
 
-    table_shape, lh, ll, token = call(
+    table_shape, lh, ll, inv_high, inv_low = call(
         table_kernel,
         "table",
         [
             (PAIRS, 4 + 2 * BASIS, TA, CHUNK),
             ((PAIRS, BASIS * TA, WIDE), BF16),
             ((PAIRS, BASIS * TA, WIDE), BF16),
-            (8, CHUNK),
+            ((3 * channels, slots), BF16),
+            ((3 * channels, slots), BF16),
         ],
         turning,
-        flags, rows,
+        flags, rows, inv,
         flops=1 << 30,
     )
 
@@ -894,9 +902,11 @@
         turning
         + [(long_table, BF16)]
         + [((PAIRS * COMPS * TA, channels), F32)]
-        + [((2 * slots, 3 * channels), F32), ((2 * slots, channels), F32)],
+        + [((slots, 3 * channels), F32)]
+        + [((3 * channels, 2 * slots), BF16)] * 2
+        + [((2 * slots, channels), F32)],
         flags, atoms, weights, mh, ml, from_first, from_second, own, *arriving,
-        rows, env, gate, curve, inv, shape_store, tall, token,
+        rows, env, gate, curve, inv_high, inv_low, shape_store, tall,
         flops=1 << 31,
     )
 
@@ -909,7 +919,7 @@
             + [((BASIS * TA, CHUNK + WIDE), BF16)] * 2
             + [((2 * WIDE, channels), BF16)] * 2
             + [((BASIS * TA, channels), F32)],
-            both, table_shape, lh, ll, eh, el, fsel, env, envdot, dinv, curl, mh, ml, after,
+            both, table_shape, lh, ll, eh, el, fsel, env, envdot, dinv, curl, nh, nl, after,
             flops=1 << 31 if p == 0 else 0,
         )[0]
 

time: 62 us -> 61.4 us (level)
  no operation moved by 1% of the time
where the time goes in v13:
time: 61.4 us; the launch traced here: 61.3 us
  starting transfers between devices  26.3 us (43%)
  waiting for transfers between devices  17.5 us (29%)
  Pallas kernels  16.8 us (27%)
  between operations  0.75 us (1%)
    pallas_call x15, Pallas kernels, call(): pl.pallas_call(kernel, name=name, out_shape=[jax.ShapeDtypeStruct(*out) f...  16.8 us
    ppermute x10, starting transfers between devices, partner(): lax.ppermute(block, 'domain', [(i, i ^ mask) for i in range(lax.axis_size...  14.2 us
    ppermute x6, starting transfers between devices, exchanged(): lax.ppermute(block, 'domain', [(i, (i + step if up[i] else i - step) % co...  11.9 us
    ppermute x10, waiting for transfers between devices, partner(): lax.ppermute(block, 'domain', [(i, i ^ mask) for i in range(lax.axis_size...  10.7 us
    ppermute x6, waiting for transfers between devices, exchanged(): lax.ppermute(block, 'domain', [(i, (i + step if up[i] else i - step) % co...  5.02 us
    ppermute x2, waiting for transfers between devices, shifted(): lax.ppermute(block, axis, [(i, (i + by) % count) for i in range(count)])  1.74 us
  transfers between devices with their start and end apart: 18, of which 10 were waited for; matrix products, arithmetic and copies ran while one was open for 0% of the time, Pallas kernels for 11%

profile of v13, /device:TPU:0, one launch (start us, length us, event | category | flops | bytes accessed | tf_op | source)
XLA Modules:
  0.0 61.3 jit_solution(14897782762379095512)
XLA Ops:
  0.6 1.2 %gather.1 = (f32[136,256]{1,0:T(8,128)S(1)}, f32[136,256]{1,0:T(8,128)S(1)}, f32[8,128]{1,0:T(8,128)S(1)}) custom-call(s32[1,4]{1,0:T(1,128)} %send.3, f32[3,1,256]{2,1,0:T(1,128)} %bitcast.5, f32[1,256,256]{2,1,0:T(8,128)} %feat.3, f32[3,1,256]{2,1,0:T(1,128)} %bitcast.7), custom_call_target="tpu_custom_call" | custom-call | bytes 1024 | tf_op jit(solution)/shard_map/gather/pallas_call | solution.py:749
  1.8 3.0 %collective-permute-start = (f32[136,256]{1,0:T(8,128)S(1)}, f32[136,256]{1,0:T(8,128)S(1)}, u32[]{:S(2)}, u32[]{:S(2)}) collective-permute-start(f32[136,256]{1,0:T(8,128)S(1)} %get-tuple-element.62), channel_id=1, source_target_pairs={{0,2},{2,0},{4,6},{6,4},{8,10},{10,8},{12,14},{14,12},{1,3},{3,1},... | collective-permute-start | bytes 417800 | tf_op jit(solution)/shard_map/ppermute | solution.py:769
  4.8 3.5 %collective-permute-start.1 = (f32[136,256]{1,0:T(8,128)S(1)}, f32[136,256]{1,0:T(8,128)S(1)}, u32[]{:S(2)}, u32[]{:S(2)}) collective-permute-start(f32[136,256]{1,0:T(8,128)S(1)} %get-tuple-element.63), channel_id=1, source_target_pairs={{0,14},{2,4},{4,2},{6,8},{8,6},{10,12},{12,10},{14,0},{1,15},{3,5}... | collective-permute-start | bytes 417800 | tf_op jit(solution)/shard_map/ppermute | solution.py:769
  8.4 1.7 %stage.1 = (f32[16,128]{1,0:T(8,128)S(1)}, f32[8,256]{1,0:T(8,128)S(1)}, f32[256,256]{1,0:T(8,128)S(1)}, f32[16,256]{1,0:T(8,128)S(1)}, bf16[768,256]{1,0:T(8,12...) custom-call(s32[1,2]{1,0:T(1,128)} %centre.1, ...), custom_call_target="tpu_custom_call" | custom-call | bytes 1024 | tf_op jit(solution)/shard_map/stage/pallas_call | solution.py:749
  10.1 0.6 %collective-permute-done.from_first = f32[136,256]{1,0:T(8,128)S(1)} collective-permute-done((f32[136,256]{1,0:T(8,128)S(1)}, f32[136,256]{1,0:T(8,128)S(1)}, u32[]{:S(2)}, u32[]{:S(2)}) %collective-permute-start) | collective-permute-done | bytes 139296 | tf_op jit(solution)/shard_map/ppermute | solution.py:769
  10.8 1.9 %collective-permute-done.1.from_second = f32[136,256]{1,0:T(8,128)S(1)} collective-permute-done((f32[136,256]{1,0:T(8,128)S(1)}, f32[136,256]{1,0:T(8,128)S(1)}, u32[]{:S(2)}, u32[]{:S(2)}) %collective-permute-start.1) | collective-permute-done | bytes 139296 | tf_op jit(solution)/shard_map/ppermute | solution.py:769
  12.7 4.5 %force.1 = (f32[1152,256]{1,0:T(8,128)S(1)}, f32[128,768]{1,0:T(8,128)S(1)}, f32[128,256]{1,0:T(8,128)S(1)}, f32[128,256]{1,0:T(8,128)S(1)}, f32[128,768]{1,0:T(...) custom-call(f32[16,128]{1,0:T(8,128)S(1)} %get-tuple-element.57.flag, ...), custom_call_target="tpu_custom_call" | custom-call | flops 2147483648 | bytes 1048576 | tf_op jit(solution)/shard_map/force/pallas_call | solution.py:749
  17.2 3.7 %collective-permute-start.2 = (f32[8,128]{1,0:T(8,128)S(1)}, f32[8,128]{1,0:T(8,128)S(1)}, u32[]{:S(2)}, u32[]{:S(2)}) collective-permute-start(f32[8,128]{1,0:T(8,128)S(1)} %get-tuple-element.68), channel_id=1, source_target_pairs={{0,14},{2,4},{4,2},{6,8},{8,6},{10,12},{12,10},{14,0},{1,15},{3,5}... | collective-permute-start | bytes 12296 | tf_op jit(solution)/shard_map/ppermute | solution.py:769
  20.9 0.5 collective-permute-start.3
  21.3 1.2 %collective-permute-start.4 = (f32[8,128]{1,0:T(8,128)S(1)}, f32[8,128]{1,0:T(8,128)S(1)}, u32[]{:S(2)}, u32[]{:S(2)}) collective-permute-start(f32[8,128]{1,0:T(8,128)S(1)} %get-tuple-element.70), channel_id=1, source_target_pairs={{0,2},{2,0},{4,6},{6,4},{8,10},{10,8},{12,14},{14,12},{1,3},{3,1},... | collective-permute-start | bytes 12296 | tf_op jit(solution)/shard_map/ppermute | solution.py:769
  22.6 1.2 %table.1 = (f32[2,20,64,128]{3,2,1,0:T(8,128)S(1)}, bf16[2,512,640]{2,1,0:T(8,128)(2,1)S(1)}, bf16[2,512,640]{2,1,0:T(8,128)(2,1)S(1)}, bf16[768,128]{1,0:T(8,128)(2,1)S(1)}, bf16[768,128]{1,0:T(8,128)(2,1)S(1)}) custom-call(f32[16,128]{1,0:T(8,128)S(1)} %get-tuple-element.57.flags, f32[8,128]{1,0:T(8,128)S(1)} %get-tuple-element.72.rows, ...), custom_call_target="tpu_custom_call" | custom-call | flops 1073741824 | bytes 1048576 | tf_op jit(solution)/shard_map/table/pallas_call | solution.py:749
  23.8 2.5 %collective-permute-done.3.two_second = f32[8,128]{1,0:T(8,128)S(1)} collective-permute-done((f32[8,128]{1,0:T(8,128)S(1)}, f32[8,128]{1,0:T(8,128)S(1)}, u32[]{:S(2)}, u32[]{:S(2)}) %collective-permute-start.3) | collective-permute-done | bytes 4128 | tf_op jit(solution)/shard_map/ppermute | solution.py:769
  26.3 3.5 %tangent.1 = (f32[3,1,256]{2,1,0:T(1,128)}, f32[768,128]{1,0:T(8,128)S(1)}, f32[768,128]{1,0:T(8,128)S(1)}, f32[8,256]{1,0:T(8,128)S(1)}, f32[1152,256]{1,0:T(8,...) custom-call(f32[16,128]{1,0:T(8,128)S(1)} %get-tuple-element.57.flags, f32[8,256]{1,0:T(8,128)S(1)} %get-tuple-element.58.atoms, ...), custom_call_target="tpu_custom_call" | custom-call | flops 2147483648 | bytes 1048576 | tf_op jit(solution)/shard_map/tangent/pallas_call | solution.py:749
  29.9 1.7 %radial.2.after.radial_0 = f32[8,256]{1,0:T(8,128)S(1)} custom-call(f32[16,128]{1,0:T(8,128)S(1)} %get-tuple-element.84.both.after, f32[2,20,64,128]{3,2,1,0:T(8,128)S(1)} %get-tuple-element.85.shape_store, bf16[2,512,640]{2,1,0:T(8,128)(2,1)S(1)} %get-tuple-element.86.lh, bf16[2,512,640]{2,1,0:T(8,128)(2,1)S(1)} %get-tuple-element.87.ll, ...), custom_call_target="tpu_custom_call" | custom-call | flops 2147483648 | bytes 1048576 | tf_op jit(solution)/shard_map/radial/pallas_call | solution.py:749
  31.7 0.7 %collective-permute-start.8 = (f32[200,128]{1,0:T(8,128)S(1)}, f32[200,128]{1,0:T(8,128)S(1)}, u32[]{:S(2)}, u32[]{:S(2)}) collective-permute-start(f32[200,128]{1,0:T(8,128)S(1)} %get-tuple-element.98), channel_id=1, source_target_pairs={{0,2},{2,0},{4,6},{6,4},{8,10},{10,8},{12,14},{14,12},{1,3},{3,1},... | collective-permute-start | bytes 307208 | tf_op jit(solution)/shard_map/ppermute | solution.py:773
  32.4 1.4 %collective-permute-start.7 = (f32[192,128]{1,0:T(8,128)S(1)}, f32[192,128]{1,0:T(8,128)S(1)}, u32[]{:S(2)}, u32[]{:S(2)}) collective-permute-start(f32[192,128]{1,0:T(8,128)S(1)} %get-tuple-element.95), channel_id=1, source_target_pairs={{0,2},{2,0},{4,6},{6,4},{8,10},{10,8},{12,14},{14,12},{1,3},{3,1},... | collective-permute-start | bytes 294920 | tf_op jit(solution)/shard_map/ppermute | solution.py:773
  33.8 1.7 %radial.3.radial_1.after = f32[8,256]{1,0:T(8,128)S(1)} custom-call(f32[16,128]{1,0:T(8,128)S(1)} %get-tuple-element.84.both.after, f32[2,20,64,128]{3,2,1,0:T(8,128)S(1)} %get-tuple-element.85.shape_store, bf16[2,512,640]{2,1,0:T(8,128)(2,1)S(1)} %get-tuple-element.86.lh, bf16[2,512,640]{2,1,0:T(8,128)(2,1)S(1)} %get-tuple-element.87.ll, ...), custom_call_target="tpu_custom_call" | custom-call | bytes 1024 | tf_op jit(solution)/shard_map/radial/pallas_call | solution.py:749
  35.5 1.9 %collective-permute-done.8.taken = f32[200,128]{1,0:T(8,128)S(1)} collective-permute-done((f32[200,128]{1,0:T(8,128)S(1)}, f32[200,128]{1,0:T(8,128)S(1)}, u32[]{:S(2)}, u32[]{:S(2)}) %collective-permute-start.8) | collective-permute-done | bytes 102432 | tf_op jit(solution)/shard_map/ppermute | solution.py:773
  37.4 2.2 %collective-permute-start.9 = (f32[120,128]{1,0:T(8,128)S(1)}, f32[120,128]{1,0:T(8,128)S(1)}, u32[]{:S(2)}, u32[]{:S(2)}) collective-permute-start(f32[120,128]{1,0:T(8,128)S(1)} %get-tuple-element.99.after), channel_id=1, source_target_pairs={{0,12},{2,14},{4,8},{6,10},{8,4},{10,6},{12,0},{14,2},{1,13},{3,15... | collective-permute-start | bytes 184328 | tf_op jit(solution)/shard_map/ppermute | solution.py:773
  39.6 2.3 %collective-permute-start.11 = (f32[104,128]{1,0:T(8,128)S(1)}, f32[104,128]{1,0:T(8,128)S(1)}, u32[]{:S(2)}, u32[]{:S(2)}) collective-permute-start(f32[104,128]{1,0:T(8,128)S(1)} %get-tuple-element.102), channel_id=1, source_target_pairs={{0,4},{2,6},{4,0},{6,2},{8,12},{10,14},{12,8},{14,10},{1,5},{3,7},... | collective-permute-start | bytes 159752 | tf_op jit(solution)/shard_map/ppermute | solution.py:773
  42.0 2.4 %collective-permute-done.11.refs_3_ = f32[104,128]{1,0:T(8,128)S(1)} collective-permute-done((f32[104,128]{1,0:T(8,128)S(1)}, f32[104,128]{1,0:T(8,128)S(1)}, u32[]{:S(2)}, u32[]{:S(2)}) %collective-permute-start.11) | collective-permute-done | bytes 53280 | tf_op jit(solution)/shard_map/ppermute | solution.py:773
  44.4 0.6 %collective-permute-done.10.refs_2_ = f32[112,128]{1,0:T(8,128)S(1)} collective-permute-done((f32[112,128]{1,0:T(8,128)S(1)}, f32[112,128]{1,0:T(8,128)S(1)}, u32[]{:S(2)}, u32[]{:S(2)}) %collective-permute-start.10) | collective-permute-done | bytes 57376 | tf_op jit(solution)/shard_map/ppermute | solution.py:773
  45.0 2.5 %collective-permute-start.12 = (f32[104,128]{1,0:T(8,128)S(1)}, f32[104,128]{1,0:T(8,128)S(1)}, u32[]{:S(2)}, u32[]{:S(2)}) collective-permute-start(f32[104,128]{1,0:T(8,128)S(1)} %total.1.mine), channel_id=1, source_target_pairs={{0,12},{2,14},{4,8},{6,10},{8,4},{10,6},{12,0},{14,2},{1,13},{3,15... | collective-permute-start | bytes 159752 | tf_op jit(solution)/shard_map/ppermute | solution.py:773
  47.6 0.1 collective-permute-start.14
  47.7 1.8 %collective-permute-start.13 = (f32[104,128]{1,0:T(8,128)S(1)}, f32[104,128]{1,0:T(8,128)S(1)}, u32[]{:S(2)}, u32[]{:S(2)}) collective-permute-start(f32[104,128]{1,0:T(8,128)S(1)} %total.1.mine), channel_id=1, source_target_pairs={{0,4},{2,6},{4,0},{6,2},{8,12},{10,14},{12,8},{14,10},{1,5},{3,7},... | collective-permute-start | bytes 159752 | tf_op jit(solution)/shard_map/ppermute | solution.py:773
  49.5 1.5 %collective-permute-done.12.third = f32[104,128]{1,0:T(8,128)S(1)} collective-permute-done((f32[104,128]{1,0:T(8,128)S(1)}, f32[104,128]{1,0:T(8,128)S(1)}, u32[]{:S(2)}, u32[]{:S(2)}) %collective-permute-start.12) | collective-permute-done | bytes 53280 | tf_op jit(solution)/shard_map/ppermute | solution.py:773
  51.1 1.8 %collective-permute-start.15 = (f32[232,128]{1,0:T(8,128)S(1)}, f32[232,128]{1,0:T(8,128)S(1)}, u32[]{:S(2)}, u32[]{:S(2)}) collective-permute-start(f32[232,128]{1,0:T(8,128)S(1)} %near.1.after), channel_id=1, source_target_pairs={{0,2},{2,0},{4,6},{6,4},{8,10},{10,8},{12,14},{14,12},{1,3},{3,1},... | collective-permute-start | bytes 356360 | tf_op jit(solution)/shard_map/ppermute | solution.py:773
  52.8 0.3 collective-permute-done.14.second
  53.1 1.4 %collective-permute-start.16 = (f32[224,128]{1,0:T(8,128)S(1)}, f32[224,128]{1,0:T(8,128)S(1)}, u32[]{:S(2)}, u32[]{:S(2)}) collective-permute-start(f32[224,128]{1,0:T(8,128)S(1)} %rest.1), channel_id=1, source_target_pairs={{0,2},{2,0},{4,6},{6,4},{8,10},{10,8},{12,14},{14,12},{1,3},{3,1},... | collective-permute-start | bytes 344072 | tf_op jit(solution)/shard_map/ppermute | solution.py:773
  54.5 4.0 %collective-permute-done.16.their_rest = f32[224,128]{1,0:T(8,128)S(1)} collective-permute-done((f32[224,128]{1,0:T(8,128)S(1)}, f32[224,128]{1,0:T(8,128)S(1)}, u32[]{:S(2)}, u32[]{:S(2)}) %collective-permute-start.16) | collective-permute-done | bytes 114720 | tf_op jit(solution)/shard_map/ppermute | solution.py:773
  58.6 1.7 %collective-permute-done.17.facing = f32[800,128]{1,0:T(8,128)S(1)} collective-permute-done((f32[800,128]{1,0:T(8,128)S(1)}, f32[800,128]{1,0:T(8,128)S(1)}, u32[]{:S(2)}, u32[]{:S(2)}) %collective-permute-start.17) | collective-permute-done | bytes 409632 | tf_op jit(solution)/shard_map/ppermute | solution.py:763
  60.3 1.0 %join.1 = (f32[768,256]{1,0:T(8,128)}, f32[8,256]{1,0:T(8,128)}, f32[4,256]{1,0:T(4,128)}, f32[1,256]{1,0:T(1,128)}) custom-call(f32[800,128]{1,0:T(8,128)S(1)} %pair.1.whole, f32[800,128]{1,0:T(8,128)S(1)} %collective-permute-done.17.facing), custom_call_target="tpu_custom_call" | custom-call | bytes 1024 | tf_op jit(solution)/shard_map/join/pallas_call | solution.py:749
  (19 shorter events, 0.4 us)
Async XLA Ops:
  1.8 8.9 %collective-permute-start = (f32[136,256]{1,0:T(8,128)S(1)}, f32[136,256]{1,0:T(8,128)S(1)}, u32[]{:S(2)}, u32[]{:S(2)}) collective-permute-start(f32[136,256]{1,0:T(8,128)S(1)} %get-tuple-element.62), channel_id=1, source_target_pairs={{0,2},{2,0},{4,6},{6,4},{8,10},{10,8},{12,14},{14,12},{1,3},{3,1},... | collective-permute-start | bytes 417800 | tf_op jit(solution)/shard_map/ppermute | solution.py:769
  4.8 7.8 %collective-permute-start.1 = (f32[136,256]{1,0:T(8,128)S(1)}, f32[136,256]{1,0:T(8,128)S(1)}, u32[]{:S(2)}, u32[]{:S(2)}) collective-permute-start(f32[136,256]{1,0:T(8,128)S(1)} %get-tuple-element.63), channel_id=1, source_target_pairs={{0,14},{2,4},{4,2},{6,8},{8,6},{10,12},{12,10},{14,0},{1,15},{3,5}... | collective-permute-start | bytes 417800 | tf_op jit(solution)/shard_map/ppermute | solution.py:769
  17.2 6.6 %collective-permute-start.2 = (f32[8,128]{1,0:T(8,128)S(1)}, f32[8,128]{1,0:T(8,128)S(1)}, u32[]{:S(2)}, u32[]{:S(2)}) collective-permute-start(f32[8,128]{1,0:T(8,128)S(1)} %get-tuple-element.68), channel_id=1, source_target_pairs={{0,14},{2,4},{4,2},{6,8},{8,6},{10,12},{12,10},{14,0},{1,15},{3,5}... | collective-permute-start | bytes 12296 | tf_op jit(solution)/shard_map/ppermute | solution.py:769
  20.9 5.4 %collective-permute-start.3 = (f32[8,128]{1,0:T(8,128)S(1)}, f32[8,128]{1,0:T(8,128)S(1)}, u32[]{:S(2)}, u32[]{:S(2)}) collective-permute-start(f32[8,128]{1,0:T(8,128)S(1)} %get-tuple-element.69), channel_id=1, source_target_pairs={{0,12},{2,14},{4,8},{6,10},{8,4},{10,6},{12,0},{14,2},{1,13},{3,15... | collective-permute-start | bytes 12296 | tf_op jit(solution)/shard_map/ppermute | solution.py:769
  21.3 5.0 %collective-permute-start.4 = (f32[8,128]{1,0:T(8,128)S(1)}, f32[8,128]{1,0:T(8,128)S(1)}, u32[]{:S(2)}, u32[]{:S(2)}) collective-permute-start(f32[8,128]{1,0:T(8,128)S(1)} %get-tuple-element.70), channel_id=1, source_target_pairs={{0,2},{2,0},{4,6},{6,4},{8,10},{10,8},{12,14},{14,12},{1,3},{3,1},... | collective-permute-start | bytes 12296 | tf_op jit(solution)/shard_map/ppermute | solution.py:769
  22.5 3.7 %collective-permute-start.5 = (f32[8,128]{1,0:T(8,128)S(1)}, f32[8,128]{1,0:T(8,128)S(1)}, u32[]{:S(2)}, u32[]{:S(2)}) collective-permute-start(f32[8,128]{1,0:T(8,128)S(1)} %get-tuple-element.71), channel_id=1, source_target_pairs={{0,4},{2,6},{4,0},{6,2},{8,12},{10,14},{12,8},{14,10},{1,5},{3,7},... | collective-permute-start | bytes 12296 | tf_op jit(solution)/shard_map/ppermute | solution.py:769
  29.8 1.8 %collective-permute-start.6 = (f32[768,128]{1,0:T(8,128)S(1)}, f32[768,128]{1,0:T(8,128)S(1)}, u32[]{:S(2)}, u32[]{:S(2)}) collective-permute-start(f32[768,128]{1,0:T(8,128)S(1)} %get-tuple-element.83), channel_id=1, source_target_pairs={{0,1},{1,0},{2,3},{3,2},{4,5},{5,4},{6,7},{7,6},{8,9},{9,8},{10,11... | collective-permute-start | bytes 1179656 | tf_op jit(solution)/shard_map/ppermute | solution.py:763
  31.7 5.7 %collective-permute-start.8 = (f32[200,128]{1,0:T(8,128)S(1)}, f32[200,128]{1,0:T(8,128)S(1)}, u32[]{:S(2)}, u32[]{:S(2)}) collective-permute-start(f32[200,128]{1,0:T(8,128)S(1)} %get-tuple-element.98), channel_id=1, source_target_pairs={{0,2},{2,0},{4,6},{6,4},{8,10},{10,8},{12,14},{14,12},{1,3},{3,1},... | collective-permute-start | bytes 307208 | tf_op jit(solution)/shard_map/ppermute | solution.py:773
  32.4 7.2 %collective-permute-start.7 = (f32[192,128]{1,0:T(8,128)S(1)}, f32[192,128]{1,0:T(8,128)S(1)}, u32[]{:S(2)}, u32[]{:S(2)}) collective-permute-start(f32[192,128]{1,0:T(8,128)S(1)} %get-tuple-element.95), channel_id=1, source_target_pairs={{0,2},{2,0},{4,6},{6,4},{8,10},{10,8},{12,14},{14,12},{1,3},{3,1},... | collective-permute-start | bytes 294920 | tf_op jit(solution)/shard_map/ppermute | solution.py:773
  37.4 7.6 %collective-permute-start.9 = (f32[120,128]{1,0:T(8,128)S(1)}, f32[120,128]{1,0:T(8,128)S(1)}, u32[]{:S(2)}, u32[]{:S(2)}) collective-permute-start(f32[120,128]{1,0:T(8,128)S(1)} %get-tuple-element.99.after), channel_id=1, source_target_pairs={{0,12},{2,14},{4,8},{6,10},{8,4},{10,6},{12,0},{14,2},{1,13},{3,15... | collective-permute-start | bytes 184328 | tf_op jit(solution)/shard_map/ppermute | solution.py:773
  39.6 5.4 %collective-permute-start.10 = (f32[112,128]{1,0:T(8,128)S(1)}, f32[112,128]{1,0:T(8,128)S(1)}, u32[]{:S(2)}, u32[]{:S(2)}) collective-permute-start(f32[112,128]{1,0:T(8,128)S(1)} %get-tuple-element.101), channel_id=1, source_target_pairs={{0,8},{2,10},{4,12},{6,14},{8,0},{10,2},{12,4},{14,6},{1,9},{3,11}... | collective-permute-start | bytes 172040 | tf_op jit(solution)/shard_map/ppermute | solution.py:773
  39.6 4.8 %collective-permute-start.11 = (f32[104,128]{1,0:T(8,128)S(1)}, f32[104,128]{1,0:T(8,128)S(1)}, u32[]{:S(2)}, u32[]{:S(2)}) collective-permute-start(f32[104,128]{1,0:T(8,128)S(1)} %get-tuple-element.102), channel_id=1, source_target_pairs={{0,4},{2,6},{4,0},{6,2},{8,12},{10,14},{12,8},{14,10},{1,5},{3,7},... | collective-permute-start | bytes 159752 | tf_op jit(solution)/shard_map/ppermute | solution.py:773
  45.0 6.0 %collective-permute-start.12 = (f32[104,128]{1,0:T(8,128)S(1)}, f32[104,128]{1,0:T(8,128)S(1)}, u32[]{:S(2)}, u32[]{:S(2)}) collective-permute-start(f32[104,128]{1,0:T(8,128)S(1)} %total.1.mine), channel_id=1, source_target_pairs={{0,12},{2,14},{4,8},{6,10},{8,4},{10,6},{12,0},{14,2},{1,13},{3,15... | collective-permute-start | bytes 159752 | tf_op jit(solution)/shard_map/ppermute | solution.py:773
  47.6 5.5 %collective-permute-start.14 = (f32[104,128]{1,0:T(8,128)S(1)}, f32[104,128]{1,0:T(8,128)S(1)}, u32[]{:S(2)}, u32[]{:S(2)}) collective-permute-start(f32[104,128]{1,0:T(8,128)S(1)} %total.1.mine), channel_id=1, source_target_pairs={{0,8},{2,10},{4,12},{6,14},{8,0},{10,2},{12,4},{14,6},{1,9},{3,11}... | collective-permute-start | bytes 159752 | tf_op jit(solution)/shard_map/ppermute | solution.py:773
  47.7 5.4 %collective-permute-start.13 = (f32[104,128]{1,0:T(8,128)S(1)}, f32[104,128]{1,0:T(8,128)S(1)}, u32[]{:S(2)}, u32[]{:S(2)}) collective-permute-start(f32[104,128]{1,0:T(8,128)S(1)} %total.1.mine), channel_id=1, source_target_pairs={{0,4},{2,6},{4,0},{6,2},{8,12},{10,14},{12,8},{14,10},{1,5},{3,7},... | collective-permute-start | bytes 159752 | tf_op jit(solution)/shard_map/ppermute | solution.py:773
  51.1 7.4 %collective-permute-start.15 = (f32[232,128]{1,0:T(8,128)S(1)}, f32[232,128]{1,0:T(8,128)S(1)}, u32[]{:S(2)}, u32[]{:S(2)}) collective-permute-start(f32[232,128]{1,0:T(8,128)S(1)} %near.1.after), channel_id=1, source_target_pairs={{0,2},{2,0},{4,6},{6,4},{8,10},{10,8},{12,14},{14,12},{1,3},{3,1},... | collective-permute-start | bytes 356360 | tf_op jit(solution)/shard_map/ppermute | solution.py:773
  53.1 5.3 %collective-permute-start.16 = (f32[224,128]{1,0:T(8,128)S(1)}, f32[224,128]{1,0:T(8,128)S(1)}, u32[]{:S(2)}, u32[]{:S(2)}) collective-permute-start(f32[224,128]{1,0:T(8,128)S(1)} %rest.1), channel_id=1, source_target_pairs={{0,2},{2,0},{4,6},{6,4},{8,10},{10,8},{12,14},{14,12},{1,3},{3,1},... | collective-permute-start | bytes 344072 | tf_op jit(solution)/shard_map/ppermute | solution.py:773
  58.5 1.8 %collective-permute-start.17 = (f32[800,128]{1,0:T(8,128)S(1)}, f32[800,128]{1,0:T(8,128)S(1)}, u32[]{:S(2)}, u32[]{:S(2)}) collective-permute-start(f32[800,128]{1,0:T(8,128)S(1)} %pair.1.whole), channel_id=1, source_target_pairs={{0,1},{1,0},{2,3},{3,2},{4,5},{5,4},{6,7},{7,6},{8,9},{9,8},{10,11... | collective-permute-start | bytes 1228808 | tf_op jit(solution)/shard_map/ppermute | solution.py:763

commit v14 on v11

--- a/solution.py
+++ b/solution.py
@@ -194,14 +194,18 @@
     return twice(first, p)
 
 
-def radial_feat(feat, radial, p, tall, wide):
+def radial_feat(feat, turned_feat, radial, spread_w, p, tall, flat):
     own = feat[p * TA : (p + 1) * TA, :]
     span, channels = BASIS * TA, feat.shape[1]
     for n in range(BASIS):
         hi, lo = split(own * radial[n : n + 1, :])
         for third, part in enumerate((hi, hi, lo)):
             tall[p, third * span + n * TA : third * span + (n + 1) * TA, :] = part
-            wide[p, n * TA : (n + 1) * TA, third * channels : (third + 1) * channels] = part
+    both = twice(turned_feat, p)
+    for k in range(BASIS // 2):
+        hi, lo = split(both * spread_w[k])
+        for third, part in enumerate((hi, hi, lo)):
+            flat[p, third * channels : (third + 1) * channels, k * CHUNK : (k + 1) * CHUNK] = part
 
 
 OTHER, CENTRE, LIVE, SAME, SHARED, SENT = 0, 2, 4, 6, 8, 9
@@ -260,8 +264,8 @@
 
 def stage_kernel(
     centre, other, live, send, pos, ref, species, feat, radial_w, mix_w, species_w, out_w, after,
-    flags, atoms, own_feat, weights, mh, ml,
-    centre_v, other_v, live_v, send_v, pos_v, ref_v, species_v, radial_v, mix_v, species_w_v, out_v, sems,
+    flags, atoms, own_feat, weights, spread_w, mh, ml, nh, nl,
+    centre_v, other_v, live_v, send_v, pos_v, ref_v, species_v, radial_v, mix_v, species_w_v, out_v, square, sems,
 ):
     copies = fetch(
         [
@@ -297,16 +301,23 @@
     weights[0:BASIS, :] = radial_v[...]
     weights[BASIS : BASIS + SPECIES, :] = species_w_v[...]
     weights[BASIS + SPECIES : BASIS + SPECIES + 1, :] = out_v[...]
+    square[...] = jnp.zeros_like(square)
+    square[0:BASIS, :] = radial_v[...]
+    turned = square[...].T
+    low, high = lane_half()
+    for k in range(BASIS // 2):
+        spread_w[k] = turned[:, 2 * k : 2 * k + 1] * low + turned[:, 2 * k + 1 : 2 * k + 2] * high
     copies[-1].wait()
-    hi, lo = split(mix_v[...])
-    mh[...] = hi
-    ml[...] = lo
+    for value, (high_part, low_part) in ((mix_v[...], (mh, ml)), (mix_v[...].T, (nh, nl))):
+        hi, lo = split(value)
+        high_part[...] = hi
+        low_part[...] = lo
 
 
 def force_kernel(
-    flags, atoms, feat, weights, mh, ml, from_second, from_first,
+    flags, atoms, feat, weights, spread_w, mh, ml, nh, nl, from_second, from_first,
     env, dinv, gate, curve, inv, rows, fsel, own, one_first, one_second, two_first, two_second, shape_store, tall, eh, el,
-    square, turned, squares, table, wide, steady, raw, back,
+    square, turned, squares, table, flat, steady, raw, back,
 ):
     ghost = SEND * TA
     up = upward(0)
@@ -334,6 +345,7 @@
             + pick_rows(from_second.at[0:ghost], o, (SEND + 4) * (1.0 - up))
         )
 
+    turned_feat = fsel[...].T
     for p in range(PAIRS):
         lane_rows = [twice(rows[i : i + 1, :], p) for i in range(3)]
         for r in range(0, TA, STRIP):
@@ -351,7 +363,7 @@
                 for k in range(BASIS // 2):
                     entry = values[k] if m == 0 else angular[m] * values[k]
                     put_left(table, p, at, k * CHUNK, CHUNK, entry)
-        radial_feat(fsel, weights, p, tall, wide)
+        radial_feat(fsel, turned_feat, weights, spread_w, p, tall, flat)
         raw[p * COMPS * TA : (p + 1) * COMPS * TA, :] = long_product(table[p], tall[p], NN)
 
     for m in range(COMPS):
@@ -375,7 +387,7 @@
     first_order = sigma * (1.0 + hidden * (1.0 - sigma))
     gate[...] = first_order
     curve[...] = sigma * (1.0 - sigma) * (2.0 + hidden * (1.0 - 2.0 * sigma)) * out_row
-    dinv[...] = product(split(first_order * out_row), (mh[...], ml[...]), NT)
+    dinv[...] = product(split(first_order * out_row), (nh[...], nl[...]), NN)
 
     tile_grads = [jnp.zeros((3, CHUNK), F32) for _ in range(4)]
     other_rows = []
@@ -391,7 +403,7 @@
                 steady[p, at, third * 256 : (third + 1) * 256] = piece
         for ref in (eh, el):
             ref[p, COMPS * TA :, :] = jnp.zeros((WIDE - COMPS * TA, ref.shape[2]), BF16)
-        back[p] = long_product(steady[p], wide[p], NT)
+        back[p] = long_product(steady[p], flat[p], NN)
         summed = [jnp.zeros((1, CHUNK), F32) for _ in range(3)]
         for r in range(0, TA, STRIP):
             strip = slice(r, r + STRIP)
@@ -525,7 +537,6 @@
         second = raw[(COMPS + m) * TA : (COMPS + m + 1) * TA, :]
         envdot[m * TA : (m + 1) * TA, :] = env_scale * (first + shared * second)
         envdot[(COMPS + m) * TA : (COMPS + m + 1) * TA, :] = env_scale * (second + shared * first)
-    invdot = left
     half = PAIRS * TA
     for p in range(PAIRS):
         sums = [None] * 3
@@ -534,9 +545,9 @@
             term = 2.0 * env[at, :] * envdot[at, :]
             sums[GROUP[m]] = term if sums[GROUP[m]] is None else sums[GROUP[m]] + term
         for g in range(3):
-            invdot[half + p * TA : half + (p + 1) * TA, g * 256 : (g + 1) * 256] = sums[g]
-    invdot[0:half, :] = inv[...]
-    hidden_move = product(split(invdot[half:, :]), (mh[...], ml[...]), NN)
+            left[half + p * TA : half + (p + 1) * TA, g * 256 : (g + 1) * 256] = sums[g]
+    left[0:half, :] = inv[...]
+    hidden_move = product(split(left[half:, :]), (mh[...], ml[...]), NN)
     bend = curve[...] * hidden_move
     curl[...] = bend
     once = 1.0 - shared * flag(lax.broadcasted_iota(jnp.int32, (half, 1), 0) >= TA)
@@ -579,14 +590,14 @@
 
 
 def radial_kernel(
-    p, both, shape_store, lh, ll, eh, el, fsel, env, envdot, dinv, curl, mh, ml, after,
+    p, both, shape_store, lh, ll, eh, el, fsel, env, envdot, dinv, curl, nh, nl, after,
     grad_radial,
     square, turned, sh, sl, gh, gl, raw,
 ):
     low, high = lane_half()
     columns_of(both[...], square, turned)
     here = slice(p * TA, (p + 1) * TA)
-    turn_inv = product(split(curl[here, :]), (mh[...], ml[...]), NT)
+    turn_inv = product(split(curl[here, :]), (nh[...], nl[...]), NN)
     lane_move = [twice(both[11 + i : 12 + i, :], p) for i in range(3)]
     sh[:, 0:CHUNK] = lh[p, :, WIDE - CHUNK :]
     sl[:, 0:CHUNK] = ll[p, :, WIDE - CHUNK :]
@@ -810,7 +821,7 @@
     )
     from_second = exchanged(to_second, 0, False)
     from_first = exchanged(to_first, 0, True)
-    flags, atoms, own_feat, weights, mh, ml = call(
+    flags, atoms, own_feat, weights, spread_w, mh, ml, nh, nl = call(
         stage_kernel,
         "stage",
         [
@@ -818,13 +829,16 @@
             (8, atoms_here),
             (atoms_here, channels),
             (16, channels),
+            (BASIS // 2, channels, CHUNK),
             (mix_w.shape, BF16),
             (mix_w.shape, BF16),
+            (mix_w.shape[::-1], BF16),
+            (mix_w.shape[::-1], BF16),
         ],
         ints
         + [(line, F32), (line, F32), ((1, atoms_here), jnp.int32)]
         + [(radial_w.shape, F32), (mix_w.shape, F32), (species_w.shape, F32), (out_row.shape, F32)]
-        + [pltpu.SemaphoreType.DMA((12,))],
+        + [((CHUNK, channels), F32), pltpu.SemaphoreType.DMA((12,))],
         centre_tile, other_tile, pair_live, send_tiles, positions, ref_forces, species, features,
         radial_w, mix_w, species_w, out_row,
         space=pltpu.HBM,
@@ -855,10 +869,10 @@
         ],
         turning
         + [((3, CHUNK, CHUNK), F32)]
-        + [(long_table, BF16), ((PAIRS, BASIS * TA, 3 * channels), BF16)]
+        + [(long_table, BF16), ((PAIRS, 3 * channels, BASIS * TA), BF16)]
         + [((PAIRS, COMPS * TA, 3 * channels), BF16)]
         + [((PAIRS * COMPS * TA, channels), F32), ((PAIRS, *table), F32)],
-        flags, atoms, own_feat, weights, mh, ml, from_second, from_first,
+        flags, atoms, own_feat, weights, spread_w, mh, ml, nh, nl, from_second, from_first,
         flops=1 << 31,
     )
     arriving = [exchanged(leaving[i], i // 2, i % 2 == 0) for i in (1, 3, 0, 2)]
@@ -909,7 +923,7 @@
             + [((BASIS * TA, CHUNK + WIDE), BF16)] * 2
             + [((2 * WIDE, channels), BF16)] * 2
             + [((BASIS * TA, channels), F32)],
-            both, table_shape, lh, ll, eh, el, fsel, env, envdot, dinv, curl, mh, ml, after,
+            both, table_shape, lh, ll, eh, el, fsel, env, envdot, dinv, curl, nh, nl, after,
             flops=1 << 31 if p == 0 else 0,
         )[0]
 

time: 62 us -> 61.5 us (level)
  no operation moved by 1% of the time
where the time goes in v14:
time: 61.5 us; the launch traced here: 61.3 us
  starting transfers between devices  26.3 us (43%)
  waiting for transfers between devices  17.4 us (28%)
  Pallas kernels  16.9 us (27%)
  between operations  0.75 us (1%)
    pallas_call x15, Pallas kernels, call(): pl.pallas_call(kernel, name=name, out_shape=[jax.ShapeDtypeStruct(*out) f...  16.9 us
    ppermute x10, starting transfers between devices, partner(): lax.ppermute(block, 'domain', [(i, i ^ mask) for i in range(lax.axis_size...  14.2 us
    ppermute x6, starting transfers between devices, exchanged(): lax.ppermute(block, 'domain', [(i, (i + step if up[i] else i - step) % co...  11.9 us
    ppermute x10, waiting for transfers between devices, partner(): lax.ppermute(block, 'domain', [(i, i ^ mask) for i in range(lax.axis_size...  10.7 us
    ppermute x6, waiting for transfers between devices, exchanged(): lax.ppermute(block, 'domain', [(i, (i + step if up[i] else i - step) % co...  4.96 us
    ppermute x2, waiting for transfers between devices, shifted(): lax.ppermute(block, axis, [(i, (i + by) % count) for i in range(count)])  1.74 us
  transfers between devices with their start and end apart: 18, of which 10 were waited for; matrix products, arithmetic and copies ran while one was open for 0% of the time, Pallas kernels for 11%

profile of v14, /device:TPU:0, one launch (start us, length us, event | category | flops | bytes accessed | tf_op | source)
XLA Modules:
  0.0 61.3 jit_solution(7587044421718840565)
XLA Ops:
  0.6 1.2 %gather.1 = (f32[136,256]{1,0:T(8,128)S(1)}, f32[136,256]{1,0:T(8,128)S(1)}, f32[8,128]{1,0:T(8,128)S(1)}) custom-call(s32[1,4]{1,0:T(1,128)} %send.3, f32[3,1,256]{2,1,0:T(1,128)} %bitcast.5, f32[1,256,256]{2,1,0:T(8,128)} %feat.3, f32[3,1,256]{2,1,0:T(1,128)} %bitcast.7), custom_call_target="tpu_custom_call" | custom-call | bytes 1024 | tf_op jit(solution)/shard_map/gather/pallas_call | solution.py:755
  1.8 3.0 %collective-permute-start = (f32[136,256]{1,0:T(8,128)S(1)}, f32[136,256]{1,0:T(8,128)S(1)}, u32[]{:S(2)}, u32[]{:S(2)}) collective-permute-start(f32[136,256]{1,0:T(8,128)S(1)} %get-tuple-element.62), channel_id=1, source_target_pairs={{0,2},{2,0},{4,6},{6,4},{8,10},{10,8},{12,14},{14,12},{1,3},{3,1},... | collective-permute-start | bytes 417800 | tf_op jit(solution)/shard_map/ppermute | solution.py:775
  4.8 3.5 %collective-permute-start.1 = (f32[136,256]{1,0:T(8,128)S(1)}, f32[136,256]{1,0:T(8,128)S(1)}, u32[]{:S(2)}, u32[]{:S(2)}) collective-permute-start(f32[136,256]{1,0:T(8,128)S(1)} %get-tuple-element.63), channel_id=1, source_target_pairs={{0,14},{2,4},{4,2},{6,8},{8,6},{10,12},{12,10},{14,0},{1,15},{3,5}... | collective-permute-start | bytes 417800 | tf_op jit(solution)/shard_map/ppermute | solution.py:775
  8.4 1.9 %stage.1 = (f32[16,128]{1,0:T(8,128)S(1)}, f32[8,256]{1,0:T(8,128)S(1)}, f32[256,256]{1,0:T(8,128)S(1)}, f32[16,256]{1,0:T(8,128)S(1)}, f32[4,256,128]{2,1,0:T(8...) custom-call(s32[1,2]{1,0:T(1,128)} %centre.1, ...), custom_call_target="tpu_custom_call" | custom-call | bytes 1024 | tf_op jit(solution)/shard_map/stage/pallas_call | solution.py:755
  10.3 0.4 collective-permute-done.from_first
  10.8 1.9 %collective-permute-done.1.from_second = f32[136,256]{1,0:T(8,128)S(1)} collective-permute-done((f32[136,256]{1,0:T(8,128)S(1)}, f32[136,256]{1,0:T(8,128)S(1)}, u32[]{:S(2)}, u32[]{:S(2)}) %collective-permute-start.1) | collective-permute-done | bytes 139296 | tf_op jit(solution)/shard_map/ppermute | solution.py:775
  12.7 4.6 %force.1 = (f32[1152,256]{1,0:T(8,128)S(1)}, f32[128,768]{1,0:T(8,128)S(1)}, f32[128,256]{1,0:T(8,128)S(1)}, f32[128,256]{1,0:T(8,128)S(1)}, f32[128,768]{1,0:T(...) custom-call(f32[16,128]{1,0:T(8,128)S(1)} %get-tuple-element.57.flag, ...), custom_call_target="tpu_custom_call" | custom-call | flops 2147483648 | bytes 1048576 | tf_op jit(solution)/shard_map/force/pallas_call | solution.py:755
  17.3 3.7 %collective-permute-start.2 = (f32[8,128]{1,0:T(8,128)S(1)}, f32[8,128]{1,0:T(8,128)S(1)}, u32[]{:S(2)}, u32[]{:S(2)}) collective-permute-start(f32[8,128]{1,0:T(8,128)S(1)} %get-tuple-element.69), channel_id=1, source_target_pairs={{0,14},{2,4},{4,2},{6,8},{8,6},{10,12},{12,10},{14,0},{1,15},{3,5}... | collective-permute-start | bytes 12296 | tf_op jit(solution)/shard_map/ppermute | solution.py:775
  21.0 0.5 collective-permute-start.3
  21.4 1.2 %collective-permute-start.4 = (f32[8,128]{1,0:T(8,128)S(1)}, f32[8,128]{1,0:T(8,128)S(1)}, u32[]{:S(2)}, u32[]{:S(2)}) collective-permute-start(f32[8,128]{1,0:T(8,128)S(1)} %get-tuple-element.71), channel_id=1, source_target_pairs={{0,2},{2,0},{4,6},{6,4},{8,10},{10,8},{12,14},{14,12},{1,3},{3,1},... | collective-permute-start | bytes 12296 | tf_op jit(solution)/shard_map/ppermute | solution.py:775
  22.6 1.1 %table.1 = (f32[2,20,64,128]{3,2,1,0:T(8,128)S(1)}, bf16[2,512,640]{2,1,0:T(8,128)(2,1)S(1)}, bf16[2,512,640]{2,1,0:T(8,128)(2,1)S(1)}, f32[8,128]{1,0:T(8,128)S(1)}) custom-call(f32[16,128]{1,0:T(8,128)S(1)} %get-tuple-element.57.flags, f32[8,128]{1,0:T(8,128)S(1)} %get-tuple-element.73.rows), custom_call_target="tpu_custom_call" | custom-call | flops 1073741824 | bytes 1048576 | tf_op jit(solution)/shard_map/table/pallas_call | solution.py:755
  23.8 2.6 %collective-permute-done.3.two_second = f32[8,128]{1,0:T(8,128)S(1)} collective-permute-done((f32[8,128]{1,0:T(8,128)S(1)}, f32[8,128]{1,0:T(8,128)S(1)}, u32[]{:S(2)}, u32[]{:S(2)}) %collective-permute-start.3) | collective-permute-done | bytes 4128 | tf_op jit(solution)/shard_map/ppermute | solution.py:775
  26.4 3.5 %tangent.1 = (f32[3,1,256]{2,1,0:T(1,128)}, f32[768,128]{1,0:T(8,128)S(1)}, f32[768,128]{1,0:T(8,128)S(1)}, f32[8,256]{1,0:T(8,128)S(1)}, f32[1152,256]{1,0:T(8,...) custom-call(f32[16,128]{1,0:T(8,128)S(1)} %get-tuple-element.57.flags, f32[8,256]{1,0:T(8,128)S(1)} %get-tuple-element.58.atoms, ...), custom_call_target="tpu_custom_call" | custom-call | flops 2147483648 | bytes 1048576 | tf_op jit(solution)/shard_map/tangent/pallas_call | solution.py:755
  29.9 1.7 %radial.2.after.radial_0 = f32[8,256]{1,0:T(8,128)S(1)} custom-call(f32[16,128]{1,0:T(8,128)S(1)} %get-tuple-element.84.both.after, f32[2,20,64,128]{3,2,1,0:T(8,128)S(1)} %get-tuple-element.85.shape_store, bf16[2,512,640]{2,1,0:T(8,128)(2,1)S(1)} %get-tuple-element.86.lh, bf16[2,512,640]{2,1,0:T(8,128)(2,1)S(1)} %get-tuple-element.87.ll, ...), custom_call_target="tpu_custom_call" | custom-call | flops 2147483648 | bytes 1048576 | tf_op jit(solution)/shard_map/radial/pallas_call | solution.py:755
  31.7 0.7 %collective-permute-start.8 = (f32[200,128]{1,0:T(8,128)S(1)}, f32[200,128]{1,0:T(8,128)S(1)}, u32[]{:S(2)}, u32[]{:S(2)}) collective-permute-start(f32[200,128]{1,0:T(8,128)S(1)} %get-tuple-element.98), channel_id=1, source_target_pairs={{0,2},{2,0},{4,6},{6,4},{8,10},{10,8},{12,14},{14,12},{1,3},{3,1},... | collective-permute-start | bytes 307208 | tf_op jit(solution)/shard_map/ppermute | solution.py:779
  32.5 1.3 %collective-permute-start.7 = (f32[192,128]{1,0:T(8,128)S(1)}, f32[192,128]{1,0:T(8,128)S(1)}, u32[]{:S(2)}, u32[]{:S(2)}) collective-permute-start(f32[192,128]{1,0:T(8,128)S(1)} %get-tuple-element.95), channel_id=1, source_target_pairs={{0,2},{2,0},{4,6},{6,4},{8,10},{10,8},{12,14},{14,12},{1,3},{3,1},... | collective-permute-start | bytes 294920 | tf_op jit(solution)/shard_map/ppermute | solution.py:779
  33.8 1.7 %radial.3.radial_1.after = f32[8,256]{1,0:T(8,128)S(1)} custom-call(f32[16,128]{1,0:T(8,128)S(1)} %get-tuple-element.84.both.after, f32[2,20,64,128]{3,2,1,0:T(8,128)S(1)} %get-tuple-element.85.shape_store, bf16[2,512,640]{2,1,0:T(8,128)(2,1)S(1)} %get-tuple-element.86.lh, bf16[2,512,640]{2,1,0:T(8,128)(2,1)S(1)} %get-tuple-element.87.ll, ...), custom_call_target="tpu_custom_call" | custom-call | bytes 1024 | tf_op jit(solution)/shard_map/radial/pallas_call | solution.py:755
  35.6 1.9 %collective-permute-done.8.taken = f32[200,128]{1,0:T(8,128)S(1)} collective-permute-done((f32[200,128]{1,0:T(8,128)S(1)}, f32[200,128]{1,0:T(8,128)S(1)}, u32[]{:S(2)}, u32[]{:S(2)}) %collective-permute-start.8) | collective-permute-done | bytes 102432 | tf_op jit(solution)/shard_map/ppermute | solution.py:779
  37.5 2.2 %collective-permute-start.9 = (f32[120,128]{1,0:T(8,128)S(1)}, f32[120,128]{1,0:T(8,128)S(1)}, u32[]{:S(2)}, u32[]{:S(2)}) collective-permute-start(f32[120,128]{1,0:T(8,128)S(1)} %get-tuple-element.99.after), channel_id=1, source_target_pairs={{0,12},{2,14},{4,8},{6,10},{8,4},{10,6},{12,0},{14,2},{1,13},{3,15... | collective-permute-start | bytes 184328 | tf_op jit(solution)/shard_map/ppermute | solution.py:779
  39.7 2.3 %collective-permute-start.11 = (f32[104,128]{1,0:T(8,128)S(1)}, f32[104,128]{1,0:T(8,128)S(1)}, u32[]{:S(2)}, u32[]{:S(2)}) collective-permute-start(f32[104,128]{1,0:T(8,128)S(1)} %get-tuple-element.102), channel_id=1, source_target_pairs={{0,4},{2,6},{4,0},{6,2},{8,12},{10,14},{12,8},{14,10},{1,5},{3,7},... | collective-permute-start | bytes 159752 | tf_op jit(solution)/shard_map/ppermute | solution.py:779
  42.0 2.4 %collective-permute-done.11.refs_3_ = f32[104,128]{1,0:T(8,128)S(1)} collective-permute-done((f32[104,128]{1,0:T(8,128)S(1)}, f32[104,128]{1,0:T(8,128)S(1)}, u32[]{:S(2)}, u32[]{:S(2)}) %collective-permute-start.11) | collective-permute-done | bytes 53280 | tf_op jit(solution)/shard_map/ppermute | solution.py:779
  44.5 0.6 %collective-permute-done.10.refs_2_ = f32[112,128]{1,0:T(8,128)S(1)} collective-permute-done((f32[112,128]{1,0:T(8,128)S(1)}, f32[112,128]{1,0:T(8,128)S(1)}, u32[]{:S(2)}, u32[]{:S(2)}) %collective-permute-start.10) | collective-permute-done | bytes 57376 | tf_op jit(solution)/shard_map/ppermute | solution.py:779
  45.1 2.5 %collective-permute-start.12 = (f32[104,128]{1,0:T(8,128)S(1)}, f32[104,128]{1,0:T(8,128)S(1)}, u32[]{:S(2)}, u32[]{:S(2)}) collective-permute-start(f32[104,128]{1,0:T(8,128)S(1)} %total.1.mine), channel_id=1, source_target_pairs={{0,12},{2,14},{4,8},{6,10},{8,4},{10,6},{12,0},{14,2},{1,13},{3,15... | collective-permute-start | bytes 159752 | tf_op jit(solution)/shard_map/ppermute | solution.py:779
  47.6 0.1 collective-permute-start.14
  47.7 1.8 %collective-permute-start.13 = (f32[104,128]{1,0:T(8,128)S(1)}, f32[104,128]{1,0:T(8,128)S(1)}, u32[]{:S(2)}, u32[]{:S(2)}) collective-permute-start(f32[104,128]{1,0:T(8,128)S(1)} %total.1.mine), channel_id=1, source_target_pairs={{0,4},{2,6},{4,0},{6,2},{8,12},{10,14},{12,8},{14,10},{1,5},{3,7},... | collective-permute-start | bytes 159752 | tf_op jit(solution)/shard_map/ppermute | solution.py:779
  49.6 1.5 %collective-permute-done.12.third = f32[104,128]{1,0:T(8,128)S(1)} collective-permute-done((f32[104,128]{1,0:T(8,128)S(1)}, f32[104,128]{1,0:T(8,128)S(1)}, u32[]{:S(2)}, u32[]{:S(2)}) %collective-permute-start.12) | collective-permute-done | bytes 53280 | tf_op jit(solution)/shard_map/ppermute | solution.py:779
  51.1 1.8 %collective-permute-start.15 = (f32[232,128]{1,0:T(8,128)S(1)}, f32[232,128]{1,0:T(8,128)S(1)}, u32[]{:S(2)}, u32[]{:S(2)}) collective-permute-start(f32[232,128]{1,0:T(8,128)S(1)} %near.1.after), channel_id=1, source_target_pairs={{0,2},{2,0},{4,6},{6,4},{8,10},{10,8},{12,14},{14,12},{1,3},{3,1},... | collective-permute-start | bytes 356360 | tf_op jit(solution)/shard_map/ppermute | solution.py:779
  52.9 0.2 collective-permute-done.14.second
  53.2 1.4 %collective-permute-start.16 = (f32[224,128]{1,0:T(8,128)S(1)}, f32[224,128]{1,0:T(8,128)S(1)}, u32[]{:S(2)}, u32[]{:S(2)}) collective-permute-start(f32[224,128]{1,0:T(8,128)S(1)} %rest.1), channel_id=1, source_target_pairs={{0,2},{2,0},{4,6},{6,4},{8,10},{10,8},{12,14},{14,12},{1,3},{3,1},... | collective-permute-start | bytes 344072 | tf_op jit(solution)/shard_map/ppermute | solution.py:779
  54.5 4.0 %collective-permute-done.16.their_rest = f32[224,128]{1,0:T(8,128)S(1)} collective-permute-done((f32[224,128]{1,0:T(8,128)S(1)}, f32[224,128]{1,0:T(8,128)S(1)}, u32[]{:S(2)}, u32[]{:S(2)}) %collective-permute-start.16) | collective-permute-done | bytes 114720 | tf_op jit(solution)/shard_map/ppermute | solution.py:779
  58.6 1.7 %collective-permute-done.17.facing = f32[800,128]{1,0:T(8,128)S(1)} collective-permute-done((f32[800,128]{1,0:T(8,128)S(1)}, f32[800,128]{1,0:T(8,128)S(1)}, u32[]{:S(2)}, u32[]{:S(2)}) %collective-permute-start.17) | collective-permute-done | bytes 409632 | tf_op jit(solution)/shard_map/ppermute | solution.py:769
  60.4 1.0 %join.1 = (f32[768,256]{1,0:T(8,128)}, f32[8,256]{1,0:T(8,128)}, f32[4,256]{1,0:T(4,128)}, f32[1,256]{1,0:T(1,128)}) custom-call(f32[800,128]{1,0:T(8,128)S(1)} %pair.1.whole, f32[800,128]{1,0:T(8,128)S(1)} %collective-permute-done.17.facing), custom_call_target="tpu_custom_call" | custom-call | bytes 1024 | tf_op jit(solution)/shard_map/join/pallas_call | solution.py:755
  (19 shorter events, 0.3 us)
Async XLA Ops:
  1.8 8.9 %collective-permute-start = (f32[136,256]{1,0:T(8,128)S(1)}, f32[136,256]{1,0:T(8,128)S(1)}, u32[]{:S(2)}, u32[]{:S(2)}) collective-permute-start(f32[136,256]{1,0:T(8,128)S(1)} %get-tuple-element.62), channel_id=1, source_target_pairs={{0,2},{2,0},{4,6},{6,4},{8,10},{10,8},{12,14},{14,12},{1,3},{3,1},... | collective-permute-start | bytes 417800 | tf_op jit(solution)/shard_map/ppermute | solution.py:775
  4.8 7.8 %collective-permute-start.1 = (f32[136,256]{1,0:T(8,128)S(1)}, f32[136,256]{1,0:T(8,128)S(1)}, u32[]{:S(2)}, u32[]{:S(2)}) collective-permute-start(f32[136,256]{1,0:T(8,128)S(1)} %get-tuple-element.63), channel_id=1, source_target_pairs={{0,14},{2,4},{4,2},{6,8},{8,6},{10,12},{12,10},{14,0},{1,15},{3,5}... | collective-permute-start | bytes 417800 | tf_op jit(solution)/shard_map/ppermute | solution.py:775
  17.3 6.4 %collective-permute-start.2 = (f32[8,128]{1,0:T(8,128)S(1)}, f32[8,128]{1,0:T(8,128)S(1)}, u32[]{:S(2)}, u32[]{:S(2)}) collective-permute-start(f32[8,128]{1,0:T(8,128)S(1)} %get-tuple-element.69), channel_id=1, source_target_pairs={{0,14},{2,4},{4,2},{6,8},{8,6},{10,12},{12,10},{14,0},{1,15},{3,5}... | collective-permute-start | bytes 12296 | tf_op jit(solution)/shard_map/ppermute | solution.py:775
  21.0 5.4 %collective-permute-start.3 = (f32[8,128]{1,0:T(8,128)S(1)}, f32[8,128]{1,0:T(8,128)S(1)}, u32[]{:S(2)}, u32[]{:S(2)}) collective-permute-start(f32[8,128]{1,0:T(8,128)S(1)} %get-tuple-element.70), channel_id=1, source_target_pairs={{0,12},{2,14},{4,8},{6,10},{8,4},{10,6},{12,0},{14,2},{1,13},{3,15... | collective-permute-start | bytes 12296 | tf_op jit(solution)/shard_map/ppermute | solution.py:775
  21.4 5.0 %collective-permute-start.4 = (f32[8,128]{1,0:T(8,128)S(1)}, f32[8,128]{1,0:T(8,128)S(1)}, u32[]{:S(2)}, u32[]{:S(2)}) collective-permute-start(f32[8,128]{1,0:T(8,128)S(1)} %get-tuple-element.71), channel_id=1, source_target_pairs={{0,2},{2,0},{4,6},{6,4},{8,10},{10,8},{12,14},{14,12},{1,3},{3,1},... | collective-permute-start | bytes 12296 | tf_op jit(solution)/shard_map/ppermute | solution.py:775
  22.6 3.7 %collective-permute-start.5 = (f32[8,128]{1,0:T(8,128)S(1)}, f32[8,128]{1,0:T(8,128)S(1)}, u32[]{:S(2)}, u32[]{:S(2)}) collective-permute-start(f32[8,128]{1,0:T(8,128)S(1)} %get-tuple-element.72), channel_id=1, source_target_pairs={{0,4},{2,6},{4,0},{6,2},{8,12},{10,14},{12,8},{14,10},{1,5},{3,7},... | collective-permute-start | bytes 12296 | tf_op jit(solution)/shard_map/ppermute | solution.py:775
  29.9 1.8 %collective-permute-start.6 = (f32[768,128]{1,0:T(8,128)S(1)}, f32[768,128]{1,0:T(8,128)S(1)}, u32[]{:S(2)}, u32[]{:S(2)}) collective-permute-start(f32[768,128]{1,0:T(8,128)S(1)} %get-tuple-element.83), channel_id=1, source_target_pairs={{0,1},{1,0},{2,3},{3,2},{4,5},{5,4},{6,7},{7,6},{8,9},{9,8},{10,11... | collective-permute-start | bytes 1179656 | tf_op jit(solution)/shard_map/ppermute | solution.py:769
  31.7 5.7 %collective-permute-start.8 = (f32[200,128]{1,0:T(8,128)S(1)}, f32[200,128]{1,0:T(8,128)S(1)}, u32[]{:S(2)}, u32[]{:S(2)}) collective-permute-start(f32[200,128]{1,0:T(8,128)S(1)} %get-tuple-element.98), channel_id=1, source_target_pairs={{0,2},{2,0},{4,6},{6,4},{8,10},{10,8},{12,14},{14,12},{1,3},{3,1},... | collective-permute-start | bytes 307208 | tf_op jit(solution)/shard_map/ppermute | solution.py:779
  32.5 7.2 %collective-permute-start.7 = (f32[192,128]{1,0:T(8,128)S(1)}, f32[192,128]{1,0:T(8,128)S(1)}, u32[]{:S(2)}, u32[]{:S(2)}) collective-permute-start(f32[192,128]{1,0:T(8,128)S(1)} %get-tuple-element.95), channel_id=1, source_target_pairs={{0,2},{2,0},{4,6},{6,4},{8,10},{10,8},{12,14},{14,12},{1,3},{3,1},... | collective-permute-start | bytes 294920 | tf_op jit(solution)/shard_map/ppermute | solution.py:779
  37.5 7.6 %collective-permute-start.9 = (f32[120,128]{1,0:T(8,128)S(1)}, f32[120,128]{1,0:T(8,128)S(1)}, u32[]{:S(2)}, u32[]{:S(2)}) collective-permute-start(f32[120,128]{1,0:T(8,128)S(1)} %get-tuple-element.99.after), channel_id=1, source_target_pairs={{0,12},{2,14},{4,8},{6,10},{8,4},{10,6},{12,0},{14,2},{1,13},{3,15... | collective-permute-start | bytes 184328 | tf_op jit(solution)/shard_map/ppermute | solution.py:779
  39.7 5.4 %collective-permute-start.10 = (f32[112,128]{1,0:T(8,128)S(1)}, f32[112,128]{1,0:T(8,128)S(1)}, u32[]{:S(2)}, u32[]{:S(2)}) collective-permute-start(f32[112,128]{1,0:T(8,128)S(1)} %get-tuple-element.101), channel_id=1, source_target_pairs={{0,8},{2,10},{4,12},{6,14},{8,0},{10,2},{12,4},{14,6},{1,9},{3,11}... | collective-permute-start | bytes 172040 | tf_op jit(solution)/shard_map/ppermute | solution.py:779
  39.7 4.8 %collective-permute-start.11 = (f32[104,128]{1,0:T(8,128)S(1)}, f32[104,128]{1,0:T(8,128)S(1)}, u32[]{:S(2)}, u32[]{:S(2)}) collective-permute-start(f32[104,128]{1,0:T(8,128)S(1)} %get-tuple-element.102), channel_id=1, source_target_pairs={{0,4},{2,6},{4,0},{6,2},{8,12},{10,14},{12,8},{14,10},{1,5},{3,7},... | collective-permute-start | bytes 159752 | tf_op jit(solution)/shard_map/ppermute | solution.py:779
  45.1 6.0 %collective-permute-start.12 = (f32[104,128]{1,0:T(8,128)S(1)}, f32[104,128]{1,0:T(8,128)S(1)}, u32[]{:S(2)}, u32[]{:S(2)}) collective-permute-start(f32[104,128]{1,0:T(8,128)S(1)} %total.1.mine), channel_id=1, source_target_pairs={{0,12},{2,14},{4,8},{6,10},{8,4},{10,6},{12,0},{14,2},{1,13},{3,15... | collective-permute-start | bytes 159752 | tf_op jit(solution)/shard_map/ppermute | solution.py:779
  47.6 5.5 %collective-permute-start.14 = (f32[104,128]{1,0:T(8,128)S(1)}, f32[104,128]{1,0:T(8,128)S(1)}, u32[]{:S(2)}, u32[]{:S(2)}) collective-permute-start(f32[104,128]{1,0:T(8,128)S(1)} %total.1.mine), channel_id=1, source_target_pairs={{0,8},{2,10},{4,12},{6,14},{8,0},{10,2},{12,4},{14,6},{1,9},{3,11}... | collective-permute-start | bytes 159752 | tf_op jit(solution)/shard_map/ppermute | solution.py:779
  47.7 5.4 %collective-permute-start.13 = (f32[104,128]{1,0:T(8,128)S(1)}, f32[104,128]{1,0:T(8,128)S(1)}, u32[]{:S(2)}, u32[]{:S(2)}) collective-permute-start(f32[104,128]{1,0:T(8,128)S(1)} %total.1.mine), channel_id=1, source_target_pairs={{0,4},{2,6},{4,0},{6,2},{8,12},{10,14},{12,8},{14,10},{1,5},{3,7},... | collective-permute-start | bytes 159752 | tf_op jit(solution)/shard_map/ppermute | solution.py:779
  51.1 7.4 %collective-permute-start.15 = (f32[232,128]{1,0:T(8,128)S(1)}, f32[232,128]{1,0:T(8,128)S(1)}, u32[]{:S(2)}, u32[]{:S(2)}) collective-permute-start(f32[232,128]{1,0:T(8,128)S(1)} %near.1.after), channel_id=1, source_target_pairs={{0,2},{2,0},{4,6},{6,4},{8,10},{10,8},{12,14},{14,12},{1,3},{3,1},... | collective-permute-start | bytes 356360 | tf_op jit(solution)/shard_map/ppermute | solution.py:779
  53.2 5.3 %collective-permute-start.16 = (f32[224,128]{1,0:T(8,128)S(1)}, f32[224,128]{1,0:T(8,128)S(1)}, u32[]{:S(2)}, u32[]{:S(2)}) collective-permute-start(f32[224,128]{1,0:T(8,128)S(1)} %rest.1), channel_id=1, source_target_pairs={{0,2},{2,0},{4,6},{6,4},{8,10},{10,8},{12,14},{14,12},{1,3},{3,1},... | collective-permute-start | bytes 344072 | tf_op jit(solution)/shard_map/ppermute | solution.py:779
  58.5 1.8 %collective-permute-start.17 = (f32[800,128]{1,0:T(8,128)S(1)}, f32[800,128]{1,0:T(8,128)S(1)}, u32[]{:S(2)}, u32[]{:S(2)}) collective-permute-start(f32[800,128]{1,0:T(8,128)S(1)} %pair.1.whole), channel_id=1, source_target_pairs={{0,1},{1,0},{2,3},{3,2},{4,5},{5,4},{6,7},{7,6},{8,9},{9,8},{10,11... | collective-permute-start | bytes 1228808 | tf_op jit(solution)/shard_map/ppermute | solution.py:769
